TPU v7x, 32 devices: a whole 2x2x4 slice. The times are simulated.
32 devices in a mesh: group: 2 (over y), ctx: 4 (over z), exp: 2 (over x), tp: 2 (over core).
Axes of the slice: x: 2, y: 2, z: 4, core: 2. Of those that a mesh axis runs over, the one named last changes fastest.
Arguments:
- queries: bfloat16 [256, 2, 2048], P(('group', 'ctx'), 'tp', 'exp'), parts along dimension 0, may hold values from -5 to 5
- cached_keys: bfloat16 [16384, 2, 128], P(('group', 'ctx'), 'tp'), parts along dimension 0, may hold values from -5 to 5
- cached_values: bfloat16 [16384, 2, 128], P(('group', 'ctx'), 'tp'), parts along dimension 0, may hold values from -5 to 5
- key_seg: int32 [16384], P(('group', 'ctx')), parts along dimension 0, may hold values from 0 to 63, as said below
- query_seg: int32 [256], P(('group', 'ctx')), parts along dimension 0, may hold values from 0 to 63, as said below
- parent: int32 [128], P('group'), parts along dimension 0, may hold values from 0 to 62, as said below
- out_weight: bfloat16 [2, 2048, 2048], P('tp', 'exp'), may hold values from -0.09375 to 0.09375
- residual: bfloat16 [256, 2048], P(('group', 'ctx'), ('exp', 'tp')), parts along dimension 0, may hold values from -15 to 15
- norm_gain: bfloat16 [2048], P(('exp', 'tp')), may hold values from 0.25 to 1.75
- gate_up_weight: bfloat16 [64, 2048, 1536], P('ctx', ('exp', 'tp')), may hold values from -0.125 to 0.125
- down_weight: bfloat16 [64, 768, 2048], P('ctx', None, ('exp', 'tp')), may hold values from -0.21875 to 0.21875
- expert_ids: int32 [256, 8], P(('group', 'ctx')), parts along dimension 0, may hold values from 0 to 63, all different within a row; in each aligned block of 32 rows (0 to 31, 32 to 63, ...) at most 8 rows name the same one
- route_weight: float32 [256, 8], P(('group', 'ctx')), parts along dimension 0, may hold values from 0.05 to 0.5
Outputs:
- layer_out: bfloat16 [256, 2048], P(('group', 'ctx'), ('exp', 'tp')), parts along dimension 0
There are 2 independent parts, one for each index of `group`. A program takes and returns all parts, laid end to end along the dimension named above; an argument that names none is the same for every part. Nothing has to cross between parts.
Inputs may be any that keep to these rules, and one draw needn't show every extreme that they name: `key_seg`: never falls along the prompt; the first 16 positions are in segment 0; every one of the 64 segments has at least one position. `query_seg`: equals key_seg at the last 128 positions of the prompt, in order. parent[0] = 0 and parent[s] < s for s > 0; every segment reaches 0 within 6 applications of parent, and segment 64 - 1 needs exactly 6. `expert_ids`: each row names 8 different experts; among the 32 rows of one device no expert is named more than 8 times.
All inputs are finite; a program needn't handle non-finite values.
Results may differ from a plain program's by a relative error of at most 0.0085.
Values may be sent and summed in bfloat16 or wider, within the bound.
No kernel may reach another device: no remote copies, remote signals or barrier semaphores. Data moves between devices by JAX's collectives and lax.ppermute only.
A program may use at most 128 MiB of HBM per device.

v0:
```python
import math

import jax
import jax.numpy as jnp
from jax import lax
from jax.sharding import PartitionSpec as P

MOST = 8
DEPTH = 6


epsilon = 1e-06
masked_score = -1e30


def shifted(value, axis, steps):
    count = lax.axis_size(axis)
    pairs = [(source, (source + steps) % count) for source in range(count)]
    return lax.ppermute(value, axis, pairs)


def ancestor_mask(segments, parent):
    labels = jnp.arange(parent.shape[0], dtype=jnp.int32)
    current = segments
    seen = current[:, None] == labels[None, :]
    for level in range(DEPTH):
        current = jnp.sum(
            jnp.where(current[:, None] == labels[None, :], parent[None, :], 0), axis=1
        )
        seen = seen | (current[:, None] == labels[None, :])
    return seen.astype(jnp.bfloat16)


def attend_tile(carried, home_block, cached_keys, cached_values, key_onehot, key_pos, first_query):
    queries, visible, running_total, highest, weight_sum = carried
    query_rows = queries.shape[0]
    inverse_root = 1.0 / math.sqrt(queries.shape[3])
    query_pos = first_query + home_block * query_rows + jnp.arange(query_rows, dtype=jnp.int32)
    seg_match = jnp.dot(visible, key_onehot, preferred_element_type=jnp.float32) > 0.5
    allowed = seg_match & (key_pos[None, :] <= query_pos[:, None])
    state = (running_total, highest, weight_sum)
    old_total, old_high, old_sum = state
    scores = (
        jnp.einsum("qghd,cgd->qghc", queries, cached_keys, preferred_element_type=jnp.float32)
        * inverse_root
    )
    keep = allowed[:, None, None, :]
    scores = jnp.where(keep, scores, masked_score)
    new_high = jnp.maximum(old_high, jnp.max(scores, axis=-1))
    factor = jnp.exp(old_high - new_high)
    probs = jnp.where(keep, jnp.exp(scores - new_high[..., None]), 0.0)
    new_sum = old_sum * factor + jnp.sum(probs, axis=-1)
    update = jnp.einsum(
        "qghc,cgd->qghd",
        probs.astype(jnp.bfloat16),
        cached_values,
        preferred_element_type=jnp.float32,
    )
    state = (old_total * factor[..., None] + update, new_high, new_sum)
    return (queries, visible, state[0], state[1], state[2])


def body(
    queries,
    cached_keys,
    cached_values,
    key_seg,
    query_seg,
    parent,
    out_weight,
    residual,
    norm_gain,
    gate_up_weight,
    down_weight,
    expert_ids,
    route_weight,
):
    ctx_count = lax.axis_size("ctx")
    own_index = lax.axis_index("ctx")
    query_rows = queries.shape[0]
    key_count = cached_keys.shape[0]
    head_size = cached_keys.shape[2]
    local_groups = cached_keys.shape[1]
    local_heads = queries.shape[2] // head_size
    seg_count = parent.shape[0]
    grouped = queries.reshape(query_rows, local_groups, local_heads, head_size)
    visible = ancestor_mask(query_seg, parent)
    key_onehot = (key_seg[None, :] == jnp.arange(seg_count, dtype=jnp.int32)[:, None]).astype(
        jnp.bfloat16
    )
    key_pos = own_index * key_count + jnp.arange(key_count, dtype=jnp.int32)
    first_query = ctx_count * key_count - ctx_count * query_rows

    def visit(carried, home_block):
        return attend_tile(
            carried, home_block, cached_keys, cached_values, key_onehot, key_pos, first_query
        )

    def advance(carried, index):
        moved = visit(carried, (own_index - index) % ctx_count)
        return (
            shifted(moved[0].astype(jnp.float32), "ctx", 1).astype(jnp.bfloat16),
            shifted(moved[1].astype(jnp.float32), "ctx", 1).astype(jnp.bfloat16),
            shifted(moved[2], "ctx", 1),
            shifted(moved[3], "ctx", 1),
            shifted(moved[4], "ctx", 1),
        )

    def two_steps(turn, carried):
        carried = advance(carried, 2 * turn)
        return advance(carried, 2 * turn + 1)

    shape = grouped.shape[:3]
    final = lax.fori_loop(
        0,
        ctx_count // 2,
        two_steps,
        (
            grouped,
            visible,
            jnp.zeros(grouped.shape, jnp.float32),
            jnp.full(shape, masked_score, jnp.float32),
            jnp.zeros(shape, jnp.float32),
        ),
    )
    running_total = final[2]
    weight_sum = final[4]
    attention = (running_total / weight_sum[..., None]).astype(jnp.bfloat16).reshape(query_rows, -1)
    model_width = out_weight.shape[-1]
    projected = jnp.dot(
        attention, out_weight.reshape(-1, model_width), preferred_element_type=jnp.float32
    )
    piece_width = residual.shape[1]
    piece_index = lax.axis_index("exp") * lax.axis_size("tp") + lax.axis_index("tp")
    offset = piece_index * piece_width
    placed = lax.dynamic_update_slice_in_dim(
        jnp.zeros_like(projected), residual.astype(jnp.float32), offset, 1
    )
    whole_state = lax.psum(projected + placed, ("exp", "tp"))
    mean_square = jnp.mean(whole_state * whole_state, axis=1, keepdims=True)
    mixed_in = lax.dynamic_slice_in_dim(whole_state, offset, piece_width, 1)
    normed = (mixed_in * lax.rsqrt(mean_square + epsilon) * norm_gain.astype(jnp.float32)).astype(
        jnp.bfloat16
    )
    local_experts = gate_up_weight.shape[0]
    expert_total = local_experts * ctx_count
    capacity = MOST
    flat_ids = expert_ids.reshape(-1)
    expert_labels = jnp.arange(expert_total, dtype=jnp.int32)
    onehot = (flat_ids[:, None] == expert_labels[None, :]).astype(jnp.int32)
    earlier = jnp.cumsum(onehot, axis=0) - onehot
    slot_index = jnp.sum(earlier * onehot, axis=1)
    target = (flat_ids * capacity + slot_index).reshape(expert_ids.shape)
    slot_labels = jnp.arange(expert_total * capacity, dtype=jnp.int32)
    matches = target[:, :, None] == slot_labels[None, None, :]
    pick_matrix = jnp.any(matches, axis=1).astype(jnp.bfloat16)
    combine = jnp.sum(jnp.where(matches, route_weight[:, :, None], 0.0), axis=1)
    outgoing = jnp.einsum(
        "qr,qd->rd", pick_matrix, normed, preferred_element_type=jnp.float32
    ).astype(jnp.bfloat16)
    outgoing = outgoing.reshape(ctx_count, local_experts, capacity, piece_width)
    ff_width = down_weight.shape[1]
    gate_up = jnp.einsum(
        "cesd,edf->cesf",
        lax.all_to_all(outgoing, "ctx", split_axis=0, concat_axis=0, tiled=True),
        gate_up_weight,
        preferred_element_type=jnp.float32,
    )
    summed = lax.psum(gate_up, ("exp", "tp"))
    hidden = (jax.nn.silu(summed[..., :ff_width]) * summed[..., ff_width:]).astype(jnp.bfloat16)
    produced = jnp.einsum(
        "cesf,efd->cesd", hidden, down_weight, preferred_element_type=jnp.float32
    ).astype(jnp.bfloat16)
    returned = lax.all_to_all(produced, "ctx", split_axis=0, concat_axis=0, tiled=True)
    moe_sum = jnp.dot(
        combine,
        returned.reshape(-1, piece_width).astype(jnp.float32),
        precision=lax.Precision.HIGHEST,
    )
    return (mixed_in + moe_sum).astype(jnp.bfloat16)


def solution(mesh):
    in_specs = (
        P(("group", "ctx"), "tp", "exp"),
        P(("group", "ctx"), "tp", None),
        P(("group", "ctx"), "tp", None),
        P(("group", "ctx")),
        P(("group", "ctx")),
        P("group"),
        P("tp", "exp", None),
        P(("group", "ctx"), ("exp", "tp")),
        P(("exp", "tp")),
        P("ctx", ("exp", "tp"), None),
        P("ctx", None, ("exp", "tp")),
        P(("group", "ctx"), None),
        P(("group", "ctx"), None),
    )
    out_specs = P(("group", "ctx"), ("exp", "tp"))
    return jax.shard_map(body, mesh=mesh, in_specs=in_specs, out_specs=out_specs, check_vma=False)
```

profile of v0, /device:TPU:0, one launch (start us, length us, event | category | flops | bytes accessed | tf_op | source)
XLA Modules:
  0.0 231.2 jit_solution(11961990887068566452)
XLA Ops:
  12.5 47.1 %while.24 = (s32[]{:T(128)}, bf16[32,1,8,128]{3,0,2,1:T(8,128)(2,1)S(1)}, bf16[32,64]{1,0:T(8,128)(2,1)S(1)}, f32[32,1,8,128]{3,0,2,1:T(8,128)S(1)}, f32[32,1,8]...) while((s32[]{:T(128)}, ...), condition=%wide.region_11.12_spmd.clone, body=%wide.region_6.11_spmd.clone.sunk | while | flops 564137600 | bytes 21788112 | solution.py:114
  12.5 3.1 %collective-permute-start.2 = (bf16[32,64]{1,0:T(8,128)(2,1)S(1)}, bf16[32,64]{1,0:T(8,128)(2,1)S(1)}, u32[]{:S(2)}, u32[]{:S(2)}) collective-permute-start(bf16[32,64]{1,0:T(8,128)(2,1)S(1)} %get-tuple-element.477), channel_id=1, source_target_pairs={{0,4},{4,8},{8,12},{12,0},{1,5},{5,9},{9,13},{13,1},{2,6},{6,10},{... | collective-permute-start | bytes 12296 | tf_op jit(solution)/shard_map/while/body/eval_jaxpr/ppermute | solution.py:19
  15.6 1.6 collective-permute-start
  18.0 1.6 fusion.118
  19.6 1.6 collective-permute-start.5
  22.4 1.8 collective-permute-start.4
  24.2 1.6 collective-permute-start.3
  26.6 1.6 collective-permute-start.7
  31.1 1.6 collective-permute-start.9
  32.8 3.9 %collective-permute-done.9 = f32[32,1,8]{0,2,1:T(8,128)S(1)} collective-permute-done((f32[32,1,8]{0,2,1:T(8,128)S(1)}, f32[32,1,8]{0,2,1:T(8,128)S(1)}, u32[]{:S(2)}, u32[]{:S(2)}) %collective-permute-start.9) | collective-permute-done | bytes 1056 | tf_op jit(solution)/shard_map/while/body/eval_jaxpr/ppermute | solution.py:19
  38.8 1.6 fusion.118
  42.4 2.4 %collective-permute-start.8 = (f32[32,1,8]{0,2,1:T(8,128)S(1)}, f32[32,1,8]{0,2,1:T(8,128)S(1)}, u32[]{:S(2)}, u32[]{:S(2)}) collective-permute-start(f32[32,1,8]{0,2,1:T(8,128)S(1)} %bitcast_add_fusion.4), channel_id=1, source_target_pairs={{0,4},{4,8},{8,12},{12,0},{1,5},{5,9},{9,13},{13,1},{2,6},{6,10},{... | collective-permute-start | bytes 3080 | tf_op jit(solution)/shard_map/while/body/eval_jaxpr/ppermute | solution.py:19
  47.4 1.4 collective-permute-start.7
  48.8 2.4 %collective-permute-start.1 = (bf16[32,1,8,128]{3,0,2,1:T(8,128)(2,1)S(1)}, bf16[32,1,8,128]{3,0,2,1:T(8,128)(2,1)S(1)}, u32[]{:S(2)}, u32[]{:S(2)}) collective-permute-start(bf16[32,1,8,128]{3,0,2,1:T(8,128)(2,1)S(1)} %collective-permute-done), channel_id=1, source_target_pairs={{0,4},{4,8},{8,12},{12,0},{1,5},{5,9},{9,13},{13,1},{2,6},{6,10},{... | collective-permute-start | bytes 196616 | tf_op jit(solution)/shard_map/while/body/eval_jaxpr/ppermute | solution.py:19
  53.6 5.9 %collective-permute-done.9 = f32[32,1,8]{0,2,1:T(8,128)S(1)} collective-permute-done((f32[32,1,8]{0,2,1:T(8,128)S(1)}, f32[32,1,8]{0,2,1:T(8,128)S(1)}, u32[]{:S(2)}, u32[]{:S(2)}) %collective-permute-start.9) | collective-permute-done | bytes 1056 | tf_op jit(solution)/shard_map/while/body/eval_jaxpr/ppermute | solution.py:19
  59.8 3.0 %fusion.50 = f32[32,2048]{1,0:T(8,128)S(1)} fusion(bf16[1,1024,2048]{2,1,0:T(8,128)(2,1)} %param.21, bf16[4,8,8,128]{3,2,1,0:T(8,128)(2,1)S(1)} %bitcast.183), kind=kOutput, calls=%fused_computation.61 | convolution fusion | flops 134217728 | bytes 4521984 | tf_op jit(solution)/shard_map/dot_general | solution.py:130
  65.2 29.0 %all-reduce.3.cloned.1.call-done = f32[32,2048]{1,0:T(8,128)} async-done(((f32[32,2048]{1,0:T(8,128)}), f32[32,2048]{1,0:T(8,128)}) %all-reduce.3.cloned.1.call-update) | async-done | bytes 262160 | tf_op jit(solution)/shard_map/psum | solution.py:139
  96.4 17.8 %all_to_all.10 = bf16[4,16,8,512]{3,2,1,0:T(8,128)(2,1)S(1)} all-to-all(bf16[4,16,8,512]{3,2,1,0:T(8,128)(2,1)S(1)} %bitcast.178), channel_id=1, replica_groups=mesh['group'=2,'ctx'=4,'exp'=2,'tp'=2] {'ctx'}, dimensions={0} | all-to-all | bytes 1048576 | tf_op jit(solution)/shard_map/all_to_all | solution.py:165
  114.2 14.1 %fusion.52 = f32[4,16,8,1536]{3,2,0,1:T(8,128)} fusion(bf16[16,512,1536]{2,1,0:T(8,128)(2,1)} %param.24, bf16[4,16,8,512]{3,2,1,0:T(8,128)(2,1)S(1)} %all_to_all.10), kind=kOutput, calls=%fused_computation.63 | convolution fusion | flops 805306368 | bytes 28835840 | tf_op jit(solution)/shard_map/cesd,edf->cesf/dot_general | solution.py:163
  128.3 67.0 %all-reduce.5.cloned.1.call-done = f32[4,16,8,1536]{3,2,0,1:T(8,128)} async-done(((f32[4,16,8,1536]{3,2,0,1:T(8,128)}), f32[4,16,8,1536]{3,2,0,1:T(8,128)}) %all-reduce.5.cloned.1.call-update) | async-done | bytes 3145744 | tf_op jit(solution)/shard_map/psum | solution.py:169
  195.4 7.3 %fusion.59 = bf16[4,16,8,512]{3,2,0,1:T(8,128)(2,1)S(1)} fusion(bf16[16,768,512]{2,1,0:T(8,128)(2,1)} %param.25, f32[4,16,8,1536]{3,2,0,1:T(8,128)} %all-reduce.5.cloned.1.call-done), kind=kOutput, calls=%fused_computation.68 | convolution fusion | flops 405274624 | bytes 16252928 | tf_op jit(solution)/shard_map/cesf,efd->cesd/dot_general | solution.py:171
  203.6 4.6 %all-to-all-start.1 = ((bf16[4,16,8,512]{3,2,1,0:T(8,128)(2,1)}), bf16[4,16,8,512]{3,2,1,0:T(8,128)(2,1)S(1)}, u32[]{:S(2)}, u32[]{:S(2)}) async-start(bf16[4,16,8,512]{3,2,1,0:T(8,128)(2,1)} %copy.60), calls=%async_computation.1 | async-start | bytes 1048576 | tf_op jit(solution)/shard_map/all_to_all | solution.py:174
  208.5 14.1 %all-to-all-done.1 = bf16[4,16,8,512]{3,2,1,0:T(8,128)(2,1)S(1)} async-done(((bf16[4,16,8,512]{3,2,1,0:T(8,128)(2,1)}), bf16[4,16,8,512]{3,2,1,0:T(8,128)(2,1)S(1)}, u32[]{:S(2)}, u32[]{:S(2)}) %all-to-all-start.1) | async-done | bytes 524320 | tf_op jit(solution)/shard_map/all_to_all | solution.py:174
  222.6 1.8 fusion.62
  (117 shorter events, 26.5 us)
Async XLA Ops:
  6.5 5.9 %copy-start = (bf16[32,1,1024]{2,0,1:T(8,128)(2,1)S(1)}, bf16[32,1,1024]{2,0,1:T(8,128)(2,1)}, u32[]{:S(2)}) copy-start(bf16[32,1,1024]{2,0,1:T(8,128)(2,1)} %param.15) | copy-start | bytes 196612
  6.5 87.6 %all-reduce.3.cloned.1.call-start = ((), (), s32[]{:S(2)}) async-start(), calls=%async_computation.2 | async-start | bytes 524288 | tf_op jit(solution)/shard_map/psum | solution.py:139
  12.5 11.8 %collective-permute-start.2 = (bf16[32,64]{1,0:T(8,128)(2,1)S(1)}, bf16[32,64]{1,0:T(8,128)(2,1)S(1)}, u32[]{:S(2)}, u32[]{:S(2)}) collective-permute-start(bf16[32,64]{1,0:T(8,128)(2,1)S(1)} %get-tuple-element.477), channel_id=1, source_target_pairs={{0,4},{4,8},{8,12},{12,0},{1,5},{5,9},{9,13},{13,1},{2,6},{6,10},{... | collective-permute-start | bytes 12296 | tf_op jit(solution)/shard_map/while/body/eval_jaxpr/ppermute | solution.py:19
  15.6 10.4 %collective-permute-start = (bf16[32,1,8,128]{3,0,2,1:T(8,128)(2,1)S(1)}, bf16[32,1,8,128]{3,0,2,1:T(8,128)(2,1)S(1)}, u32[]{:S(2)}, u32[]{:S(2)}) collective-permute-start(bf16[32,1,8,128]{3,0,2,1:T(8,128)(2,1)S(1)} %get-tuple-element.476), channel_id=1, source_target_pairs={{0,4},{4,8},{8,12},{12,0},{1,5},{5,9},{9,13},{13,1},{2,6},{6,10},{... | collective-permute-start | bytes 196616 | tf_op jit(solution)/shard_map/while/body/eval_jaxpr/ppermute | solution.py:19
  19.6 6.9 %collective-permute-start.5 = (f32[32,1,8]{0,2,1:T(8,128)S(1)}, f32[32,1,8]{0,2,1:T(8,128)S(1)}, u32[]{:S(2)}, u32[]{:S(2)}) collective-permute-start(f32[32,1,8]{0,2,1:T(8,128)S(1)} %get-tuple-element.451), channel_id=1, source_target_pairs={{0,4},{4,8},{8,12},{12,0},{1,5},{5,9},{9,13},{13,1},{2,6},{6,10},{... | collective-permute-start | bytes 3080 | tf_op jit(solution)/shard_map/while/body/eval_jaxpr/ppermute | solution.py:19
  21.8 9.3 %collective-permute-start.8 = (f32[32,1,8]{0,2,1:T(8,128)S(1)}, f32[32,1,8]{0,2,1:T(8,128)S(1)}, u32[]{:S(2)}, u32[]{:S(2)}) collective-permute-start(f32[32,1,8]{0,2,1:T(8,128)S(1)} %bitcast_add_fusion.4), channel_id=1, source_target_pairs={{0,4},{4,8},{8,12},{12,0},{1,5},{5,9},{9,13},{13,1},{2,6},{6,10},{... | collective-permute-start | bytes 3080 | tf_op jit(solution)/shard_map/while/body/eval_jaxpr/ppermute | solution.py:19
  22.4 6.9 %collective-permute-start.4 = (f32[32,1,8,128]{3,0,2,1:T(8,128)S(1)}, f32[32,1,8,128]{3,0,2,1:T(8,128)S(1)}, u32[]{:S(2)}, u32[]{:S(2)}) collective-permute-start(f32[32,1,8,128]{3,0,2,1:T(8,128)S(1)} %fusion.120), channel_id=1, source_target_pairs={{0,4},{4,8},{8,12},{12,0},{1,5},{5,9},{9,13},{13,1},{2,6},{6,10},{... | collective-permute-start | bytes 393224 | tf_op jit(solution)/shard_map/while/body/eval_jaxpr/ppermute | solution.py:19
  24.2 8.5 %collective-permute-start.3 = (bf16[32,64]{1,0:T(8,128)(2,1)S(1)}, bf16[32,64]{1,0:T(8,128)(2,1)S(1)}, u32[]{:S(2)}, u32[]{:S(2)}) collective-permute-start(bf16[32,64]{1,0:T(8,128)(2,1)S(1)} %collective-permute-done.2), channel_id=1, source_target_pairs={{0,4},{4,8},{8,12},{12,0},{1,5},{5,9},{9,13},{13,1},{2,6},{6,10},{... | collective-permute-start | bytes 12296 | tf_op jit(solution)/shard_map/while/body/eval_jaxpr/ppermute | solution.py:19
  26.6 6.2 %collective-permute-start.7 = (f32[32,1,8]{0,2,1:T(8,128)S(1)}, f32[32,1,8]{0,2,1:T(8,128)S(1)}, u32[]{:S(2)}, u32[]{:S(2)}) collective-permute-start(f32[32,1,8]{0,2,1:T(8,128)S(1)} %get-tuple-element.456), channel_id=1, source_target_pairs={{0,4},{4,8},{8,12},{12,0},{1,5},{5,9},{9,13},{13,1},{2,6},{6,10},{... | collective-permute-start | bytes 3080 | tf_op jit(solution)/shard_map/while/body/eval_jaxpr/ppermute | solution.py:19
  28.2 8.5 %collective-permute-start.1 = (bf16[32,1,8,128]{3,0,2,1:T(8,128)(2,1)S(1)}, bf16[32,1,8,128]{3,0,2,1:T(8,128)(2,1)S(1)}, u32[]{:S(2)}, u32[]{:S(2)}) collective-permute-start(bf16[32,1,8,128]{3,0,2,1:T(8,128)(2,1)S(1)} %collective-permute-done), channel_id=1, source_target_pairs={{0,4},{4,8},{8,12},{12,0},{1,5},{5,9},{9,13},{13,1},{2,6},{6,10},{... | collective-permute-start | bytes 196616 | tf_op jit(solution)/shard_map/while/body/eval_jaxpr/ppermute | solution.py:19
  29.8 6.9 %collective-permute-start.6 = (f32[32,1,8,128]{3,0,2,1:T(8,128)S(1)}, f32[32,1,8,128]{3,0,2,1:T(8,128)S(1)}, u32[]{:S(2)}, u32[]{:S(2)}) collective-permute-start(f32[32,1,8,128]{3,0,2,1:T(8,128)S(1)} %multiply_add_fusion.3), channel_id=1, source_target_pairs={{0,4},{4,8},{8,12},{12,0},{1,5},{5,9},{9,13},{13,1},{2,6},{6,10},{... | collective-permute-start | bytes 393224 | tf_op jit(solution)/shard_map/while/body/eval_jaxpr/ppermute | solution.py:19
  31.1 5.6 %collective-permute-start.9 = (f32[32,1,8]{0,2,1:T(8,128)S(1)}, f32[32,1,8]{0,2,1:T(8,128)S(1)}, u32[]{:S(2)}, u32[]{:S(2)}) collective-permute-start(f32[32,1,8]{0,2,1:T(8,128)S(1)} %bitcast_add_fusion.5), channel_id=1, source_target_pairs={{0,4},{4,8},{8,12},{12,0},{1,5},{5,9},{9,13},{13,1},{2,6},{6,10},{... | collective-permute-start | bytes 3080 | tf_op jit(solution)/shard_map/while/body/eval_jaxpr/ppermute | solution.py:19
  36.7 8.7 %collective-permute-start.2 = (bf16[32,64]{1,0:T(8,128)(2,1)S(1)}, bf16[32,64]{1,0:T(8,128)(2,1)S(1)}, u32[]{:S(2)}, u32[]{:S(2)}) collective-permute-start(bf16[32,64]{1,0:T(8,128)(2,1)S(1)} %get-tuple-element.477), channel_id=1, source_target_pairs={{0,4},{4,8},{8,12},{12,0},{1,5},{5,9},{9,13},{13,1},{2,6},{6,10},{... | collective-permute-start | bytes 12296 | tf_op jit(solution)/shard_map/while/body/eval_jaxpr/ppermute | solution.py:19
  36.7 10.1 %collective-permute-start = (bf16[32,1,8,128]{3,0,2,1:T(8,128)(2,1)S(1)}, bf16[32,1,8,128]{3,0,2,1:T(8,128)(2,1)S(1)}, u32[]{:S(2)}, u32[]{:S(2)}) collective-permute-start(bf16[32,1,8,128]{3,0,2,1:T(8,128)(2,1)S(1)} %get-tuple-element.476), channel_id=1, source_target_pairs={{0,4},{4,8},{8,12},{12,0},{1,5},{5,9},{9,13},{13,1},{2,6},{6,10},{... | collective-permute-start | bytes 196616 | tf_op jit(solution)/shard_map/while/body/eval_jaxpr/ppermute | solution.py:19
  40.4 6.9 %collective-permute-start.5 = (f32[32,1,8]{0,2,1:T(8,128)S(1)}, f32[32,1,8]{0,2,1:T(8,128)S(1)}, u32[]{:S(2)}, u32[]{:S(2)}) collective-permute-start(f32[32,1,8]{0,2,1:T(8,128)S(1)} %get-tuple-element.451), channel_id=1, source_target_pairs={{0,4},{4,8},{8,12},{12,0},{1,5},{5,9},{9,13},{13,1},{2,6},{6,10},{... | collective-permute-start | bytes 3080 | tf_op jit(solution)/shard_map/while/body/eval_jaxpr/ppermute | solution.py:19
  42.4 10.4 %collective-permute-start.8 = (f32[32,1,8]{0,2,1:T(8,128)S(1)}, f32[32,1,8]{0,2,1:T(8,128)S(1)}, u32[]{:S(2)}, u32[]{:S(2)}) collective-permute-start(f32[32,1,8]{0,2,1:T(8,128)S(1)} %bitcast_add_fusion.4), channel_id=1, source_target_pairs={{0,4},{4,8},{8,12},{12,0},{1,5},{5,9},{9,13},{13,1},{2,6},{6,10},{... | collective-permute-start | bytes 3080 | tf_op jit(solution)/shard_map/while/body/eval_jaxpr/ppermute | solution.py:19
  45.3 6.8 %collective-permute-start.4 = (f32[32,1,8,128]{3,0,2,1:T(8,128)S(1)}, f32[32,1,8,128]{3,0,2,1:T(8,128)S(1)}, u32[]{:S(2)}, u32[]{:S(2)}) collective-permute-start(f32[32,1,8,128]{3,0,2,1:T(8,128)S(1)} %fusion.120), channel_id=1, source_target_pairs={{0,4},{4,8},{8,12},{12,0},{1,5},{5,9},{9,13},{13,1},{2,6},{6,10},{... | collective-permute-start | bytes 393224 | tf_op jit(solution)/shard_map/while/body/eval_jaxpr/ppermute | solution.py:19
  45.5 8.2 %collective-permute-start.3 = (bf16[32,64]{1,0:T(8,128)(2,1)S(1)}, bf16[32,64]{1,0:T(8,128)(2,1)S(1)}, u32[]{:S(2)}, u32[]{:S(2)}) collective-permute-start(bf16[32,64]{1,0:T(8,128)(2,1)S(1)} %collective-permute-done.2), channel_id=1, source_target_pairs={{0,4},{4,8},{8,12},{12,0},{1,5},{5,9},{9,13},{13,1},{2,6},{6,10},{... | collective-permute-start | bytes 12296 | tf_op jit(solution)/shard_map/while/body/eval_jaxpr/ppermute | solution.py:19
  47.4 6.2 %collective-permute-start.7 = (f32[32,1,8]{0,2,1:T(8,128)S(1)}, f32[32,1,8]{0,2,1:T(8,128)S(1)}, u32[]{:S(2)}, u32[]{:S(2)}) collective-permute-start(f32[32,1,8]{0,2,1:T(8,128)S(1)} %get-tuple-element.456), channel_id=1, source_target_pairs={{0,4},{4,8},{8,12},{12,0},{1,5},{5,9},{9,13},{13,1},{2,6},{6,10},{... | collective-permute-start | bytes 3080 | tf_op jit(solution)/shard_map/while/body/eval_jaxpr/ppermute | solution.py:19
  48.8 10.7 %collective-permute-start.1 = (bf16[32,1,8,128]{3,0,2,1:T(8,128)(2,1)S(1)}, bf16[32,1,8,128]{3,0,2,1:T(8,128)(2,1)S(1)}, u32[]{:S(2)}, u32[]{:S(2)}) collective-permute-start(bf16[32,1,8,128]{3,0,2,1:T(8,128)(2,1)S(1)} %collective-permute-done), channel_id=1, source_target_pairs={{0,4},{4,8},{8,12},{12,0},{1,5},{5,9},{9,13},{13,1},{2,6},{6,10},{... | collective-permute-start | bytes 196616 | tf_op jit(solution)/shard_map/while/body/eval_jaxpr/ppermute | solution.py:19
  52.7 6.9 %collective-permute-start.6 = (f32[32,1,8,128]{3,0,2,1:T(8,128)S(1)}, f32[32,1,8,128]{3,0,2,1:T(8,128)S(1)}, u32[]{:S(2)}, u32[]{:S(2)}) collective-permute-start(f32[32,1,8,128]{3,0,2,1:T(8,128)S(1)} %multiply_add_fusion.3), channel_id=1, source_target_pairs={{0,4},{4,8},{8,12},{12,0},{1,5},{5,9},{9,13},{13,1},{2,6},{6,10},{... | collective-permute-start | bytes 393224 | tf_op jit(solution)/shard_map/while/body/eval_jaxpr/ppermute | solution.py:19
  52.8 6.8 %collective-permute-start.9 = (f32[32,1,8]{0,2,1:T(8,128)S(1)}, f32[32,1,8]{0,2,1:T(8,128)S(1)}, u32[]{:S(2)}, u32[]{:S(2)}) collective-permute-start(f32[32,1,8]{0,2,1:T(8,128)S(1)} %bitcast_add_fusion.5), channel_id=1, source_target_pairs={{0,4},{4,8},{8,12},{12,0},{1,5},{5,9},{9,13},{13,1},{2,6},{6,10},{... | collective-permute-start | bytes 3080 | tf_op jit(solution)/shard_map/while/body/eval_jaxpr/ppermute | solution.py:19
  63.5 131.9 %all-reduce.5.cloned.1.call-start = ((), (), s32[]{:S(2)}) async-start(), calls=%async_computation.3 | async-start | bytes 6291456 | tf_op jit(solution)/shard_map/psum | solution.py:169
  203.6 19.0 %all-to-all-start.1 = ((bf16[4,16,8,512]{3,2,1,0:T(8,128)(2,1)}), bf16[4,16,8,512]{3,2,1,0:T(8,128)(2,1)S(1)}, u32[]{:S(2)}, u32[]{:S(2)}) async-start(bf16[4,16,8,512]{3,2,1,0:T(8,128)(2,1)} %copy.60), calls=%async_computation.1 | async-start | bytes 1048576 | tf_op jit(solution)/shard_map/all_to_all | solution.py:174
  (11 other events, 41.9 us)
Sparse Core Ops, SparseCore 0:
  63.6 30.4 all-reduce.2
  128.5 66.8 all-reduce.4
where the time goes:
time: 232 us; the launch traced here: 231 us
  waiting for transfers between devices  121 us (52%)
  matrix products  35.9 us (15%)
  starting transfers between devices  30 us (13%)
  blocking collectives  17.8 us (8%)
  between operations  13.6 us (6%)
  other arithmetic  10.4 us (4%)
    psum x1, waiting for transfers between devices, body(): summed = lax.psum(gate_up, ('exp', 'tp'))  67 us
    psum x1, waiting for transfers between devices, body(): whole_state = lax.psum(projected + placed, ('exp', 'tp'))  29 us
    ppermute x20, starting transfers between devices, shifted(): return lax.ppermute(value, axis, pairs)  25.4 us
    all_to_all x1, blocking collectives, body(): lax.all_to_all(outgoing, 'ctx', split_axis=0, concat_axis=0, tiled=True)  17.8 us
    dot_general x1, matrix products, body(): jnp.einsum('cesd,edf->cesf', lax.all_to_all(outgoing, 'ctx', split_axis=0...  14.1 us
    all_to_all x1, waiting for transfers between devices, body(): lax.all_to_all(produced, 'ctx', split_axis=0, concat_axis=0, tiled=True)  14.1 us
    ppermute x20, waiting for transfers between devices, shifted(): return lax.ppermute(value, axis, pairs)  10.8 us
    dot_general x1, matrix products, body(): jnp.einsum('cesf,efd->cesd', hidden, down_weight, preferred_element_type=...  7.33 us
  transfers between devices with their start and end apart: 23, of which 7 were waited for; matrix products, arithmetic and copies ran while one was open for 5% of the time, Pallas kernels for 0%

commit v1 on v0

v1 whole, which is shorter than its diff:
```python
import functools
import math

import jax
import jax.numpy as jnp
from jax import lax
from jax.experimental import pallas as pl
from jax.experimental.pallas import tpu as pltpu
from jax.sharding import PartitionSpec as P

MOST = 8
DEPTH = 6
LANES = 128

epsilon = 1e-06
masked_score = -1e30
least_high = -1e20

f32 = jnp.float32
bf16 = jnp.bfloat16


def params(megabytes, steps=0):
    semantics = ("arbitrary",) * steps if steps else None
    return pltpu.CompilerParams(
        vmem_limit_bytes=megabytes * 1024 * 1024, dimension_semantics=semantics
    )


def lane_ids(shape):
    return lax.broadcasted_iota(jnp.int32, shape, len(shape) - 1)


def row_ids(shape):
    return lax.broadcasted_iota(jnp.int32, shape, len(shape) - 2)


def dot(left, right, dims=((1,), (0,))):
    return lax.dot_general(left, right, (dims, ((), ())), preferred_element_type=f32)


def in_two(value):
    high = value.astype(bf16).astype(f32)
    return high, value - high


def exchange(pieces, axes):
    return lax.all_to_all(pieces, axes, split_axis=0, concat_axis=0, tiled=True)


def collect(value, axis):
    count = lax.axis_size(axis)
    return exchange(jnp.broadcast_to(value[None], (count,) + value.shape), axis)


def shifted(value, axis, steps):
    count = lax.axis_size(axis)
    pairs = [(source, (source + steps) % count) for source in range(count)]
    return lax.ppermute(value, axis, pairs)


def sight_kernel(parent_ref, key_seg_ref, sight_ref):
    seg_count, key_count = sight_ref.shape
    square = (seg_count, seg_count)
    same = row_ids(square) == lane_ids(square)
    step = (parent_ref[...] == row_ids(square)) | same
    one = step.astype(f32).astype(bf16)
    two = (dot(one, one) > 0.5).astype(f32).astype(bf16)
    four = (dot(two, two) > 0.5).astype(f32).astype(bf16)
    six = (dot(four, two) > 0.5).astype(f32).astype(bf16)
    keys = (key_seg_ref[...] == row_ids((seg_count, key_count))).astype(f32).astype(bf16)
    sight_ref[...] = dot(six, keys, ((0,), (0,))).astype(bf16)


def sight_of(parent, key_seg):
    assert DEPTH == 6
    return pl.pallas_call(
        sight_kernel,
        out_shape=jax.ShapeDtypeStruct((parent.shape[0], key_seg.shape[0]), bf16),
        compiler_params=params(16),
        name="sight",
    )(parent[None, :], key_seg[None, :])


def attend_kernel(heads, scale, lead_ref, queries_ref, keys_ref, values_ref, sight_ref, out_ref):
    rows = queries_ref.shape[0]
    key_count, head_size = keys_ref.shape
    seg_count = sight_ref.shape[0]
    width = heads * head_size
    info = queries_ref[:, width : width + LANES].astype(f32)
    own_seg = info[:, :1].astype(jnp.int32)
    onehot = (own_seg == lane_ids((rows, seg_count))).astype(f32).astype(bf16)
    seen = dot(onehot, sight_ref[...]) > 0.5
    place = (rows, key_count)
    lead = lead_ref[0] + pl.program_id(0) * rows
    causal = lane_ids(place) - row_ids(place) <= lead
    bias = jnp.where(seen & causal, 0.0, masked_score)
    stats = jnp.zeros((rows, LANES), f32)
    lane = lane_ids((rows, LANES))
    for head in range(heads):
        columns = slice(head * head_size, (head + 1) * head_size)
        scores = dot(queries_ref[:, columns], keys_ref[...], ((1,), (1,))) + bias
        high = jnp.maximum(jnp.max(scores, axis=1, keepdims=True), least_high)
        high = high.astype(bf16).astype(f32)
        probs = jnp.exp2((scores - high) * scale)
        total_high, total_low = in_two(jnp.sum(probs, axis=1, keepdims=True))
        out_ref[:, columns] = dot(probs.astype(bf16), values_ref[...]).astype(bf16)
        stats = jnp.where(lane == head, high, stats)
        stats = jnp.where(lane == heads + head, total_high, stats)
        stats = jnp.where(lane == 2 * heads + head, total_low, stats)
    out_ref[:, width : width + LANES] = stats.astype(bf16)


def attend(lead, queries, keys, values, sight, heads, scale):
    token_count, columns = queries.shape
    block = min(token_count, 128)
    key_count, head_size = keys.shape
    work = token_count * heads * key_count
    return pl.pallas_call(
        functools.partial(attend_kernel, heads, scale),
        grid=(token_count // block,),
        in_specs=[
            pl.BlockSpec(memory_space=pltpu.SMEM),
            pl.BlockSpec((block, columns), lambda index: (index, 0)),
            pl.BlockSpec(keys.shape, lambda index: (0, 0)),
            pl.BlockSpec(values.shape, lambda index: (0, 0)),
            pl.BlockSpec(sight.shape, lambda index: (0, 0)),
        ],
        out_specs=pl.BlockSpec((block, columns), lambda index: (index, 0)),
        out_shape=jax.ShapeDtypeStruct((token_count, columns), bf16),
        compiler_params=params(40, 1),
        cost_estimate=pl.CostEstimate(
            flops=4 * work * head_size, bytes_accessed=2**21, transcendentals=work
        ),
        name="attend",
    )(lead, queries, keys, values, sight)


def project_kernel(heads, scale, parts_ref, weight_ref, out_ref, attention_ref):
    source_count = parts_ref.shape[0]
    width = attention_ref.shape[1]
    head_size = width // heads

    @pl.when(pl.program_id(0) == 0)
    def merge():
        stats = [parts_ref[i, :, width : width + LANES].astype(f32) for i in range(source_count)]
        top = functools.reduce(jnp.maximum, stats)
        factors = [jnp.exp2(jnp.minimum((stat - top) * scale, 0.0)) for stat in stats]
        total = 0.0
        for stat, factor in zip(stats, factors):
            high = pltpu.roll(stat, LANES - heads, 1)
            low = pltpu.roll(stat, LANES - 2 * heads, 1)
            total = total + factor * (high + low)
        shares = [factor / total for factor in factors]
        for head in range(heads):
            columns = slice(head * head_size, (head + 1) * head_size)
            merged = 0.0
            for i in range(source_count):
                part = parts_ref[i, :, columns].astype(f32)
                merged = merged + part * shares[i][:, head : head + 1]
            attention_ref[:, columns] = merged.astype(bf16)

    out_ref[0] = dot(attention_ref[...], weight_ref[...]).astype(bf16)


def project(parts, weight, heads, scale, piece_count):
    source_count, rows, columns = parts.shape
    width, model_width = weight.shape
    piece_width = model_width // piece_count
    return pl.pallas_call(
        functools.partial(project_kernel, heads, scale),
        grid=(piece_count,),
        in_specs=[
            pl.BlockSpec(parts.shape, lambda index: (0, 0, 0)),
            pl.BlockSpec((width, piece_width), lambda index: (0, index)),
        ],
        out_specs=pl.BlockSpec((1, rows, piece_width), lambda index: (index, 0, 0)),
        out_shape=jax.ShapeDtypeStruct((piece_count, rows, piece_width), bf16),
        scratch_shapes=[pltpu.VMEM((rows, width), bf16)],
        compiler_params=params(32, 1),
        cost_estimate=pl.CostEstimate(
            flops=2 * rows * width * model_width,
            bytes_accessed=2 * width * model_width,
            transcendentals=0,
        ),
        name="project",
    )(parts, weight)


def mix_kernel(parts_ref, residual_ref, gain_ref, mixed_ref, sent_ref):
    rows, width = mixed_ref.shape
    mixed = residual_ref[...].astype(f32)
    for i in range(parts_ref.shape[0]):
        mixed = mixed + parts_ref[i].astype(f32)
    mixed_ref[...] = mixed
    sent_ref[:, :width] = (mixed * gain_ref[...].astype(f32)).astype(bf16)
    high, low = in_two(jnp.sum(mixed * mixed, axis=1, keepdims=True))
    lane = lane_ids((rows, LANES))
    squares = jnp.where(lane == 0, high, jnp.where(lane == 1, low, 0.0))
    sent_ref[:, width:] = squares.astype(bf16)


def mix(parts, residual, gain):
    rows, width = residual.shape
    return pl.pallas_call(
        mix_kernel,
        out_shape=(
            jax.ShapeDtypeStruct((rows, width), f32),
            jax.ShapeDtypeStruct((rows, width + LANES), bf16),
        ),
        compiler_params=params(16),
        name="mix",
    )(parts, residual, gain[None, :])


def route_kernel(local_experts, choices, first_ref, info_ref, place_ref, high_ref, low_ref):
    piece_count, tokens, slots = place_ref.shape
    info = info_ref[...].astype(f32)
    expert = (lane_ids((tokens, local_experts)) + first_ref[0]).astype(f32)
    member = jnp.zeros((tokens, local_experts), f32)
    weight_high = jnp.zeros((tokens, local_experts), f32)
    weight_low = jnp.zeros((tokens, local_experts), f32)
    for k in range(choices):
        chosen = info[:, 1 + k : 2 + k] == expert
        high = info[:, 1 + choices + k : 2 + choices + k]
        low = info[:, 1 + 2 * choices + k : 2 + 2 * choices + k]
        member = jnp.where(chosen, 1.0, member)
        weight_high = jnp.where(chosen, high, weight_high)
        weight_low = jnp.where(chosen, low, weight_low)
    square = (tokens, tokens)
    earlier = (lane_ids(square) < row_ids(square)).astype(f32).astype(bf16)
    member = member.astype(bf16)
    rank = jnp.where(member > 0.5, dot(earlier, member), -1.0).astype(bf16)
    weight_high = weight_high.astype(bf16)
    weight_low = weight_low.astype(bf16)
    capacity = piece_count * slots // local_experts
    for piece in range(piece_count):
        slot = lane_ids((local_experts, slots)) + piece * slots
        spread = (slot // capacity == row_ids((local_experts, slots))).astype(f32).astype(bf16)
        wanted = (lane_ids((tokens, slots)) + piece * slots) % capacity
        placed = dot(rank, spread) == wanted.astype(f32)
        place_ref[piece] = jnp.where(placed, 1.0, 0.0).astype(bf16)
        high_ref[piece] = jnp.where(placed, dot(weight_high, spread), 0.0).astype(bf16)
        low_ref[piece] = jnp.where(placed, dot(weight_low, spread), 0.0).astype(bf16)


def route(first, info, local_experts, choices, piece_count, slots):
    shape = jax.ShapeDtypeStruct((piece_count, info.shape[0], slots), bf16)
    return pl.pallas_call(
        functools.partial(route_kernel, local_experts, choices),
        in_specs=[
            pl.BlockSpec(memory_space=pltpu.SMEM),
            pl.BlockSpec(memory_space=pltpu.VMEM),
        ],
        out_shape=(shape, shape, shape),
        compiler_params=params(32),
        name="route",
    )(first, info)


def gate_up_kernel(per_step, with_sum, piece_ref, rows_ref, place_ref, weight_ref, *rest):
    added_ref = rest[0] if with_sum else None
    out_ref, picked_ref = rest[-2:]
    width = weight_ref.shape[1]
    ff_pair = weight_ref.shape[2]
    step = pl.program_id(0)

    @pl.when(step == 0)
    def pick():
        picked_ref[...] = dot(place_ref[0], rows_ref[...], ((0,), (0,))).astype(bf16)

    count = weight_ref.shape[0]
    rows = per_step // count
    for i in range(count):
        start = pl.multiple_of(step * per_step + i * rows, rows)
        picked = picked_ref[pl.ds(start, rows), :]
        product = dot(picked[:, :width], weight_ref[i])
        squares = picked[:, width:].astype(f32)
        here = slice(i * rows, (i + 1) * rows)
        if with_sum:
            product = product + added_ref[here, :ff_pair].astype(f32)
            squares = squares + added_ref[here, ff_pair:].astype(f32)
            high, low = in_two(squares[:, :1] + squares[:, 1:2])
            lane = lane_ids((rows, LANES))
            squares = jnp.where(lane == 0, high, jnp.where(lane == 1, low, 0.0))
        out_ref[here, :ff_pair] = product.astype(bf16)
        out_ref[here, ff_pair:] = squares.astype(bf16)


def gate_up(piece, rows, place, weight, added=None):
    piece_count, tokens, slots = place.shape
    local_experts, width, ff_pair = weight.shape
    capacity = piece_count * slots // local_experts
    experts = max(1, slots // capacity)
    count = 2 if experts % 2 == 0 else 1
    steps = experts // count
    per_step = slots // steps
    columns = ff_pair + LANES

    def weight_block(step, piece_ref):
        return ((piece_ref[0] * slots // capacity) // count + step, 0, 0)

    in_specs = [
        pl.BlockSpec(rows.shape, lambda step, piece_ref: (0, 0)),
        pl.BlockSpec((1, tokens, slots), lambda step, piece_ref: (piece_ref[0], 0, 0)),
        pl.BlockSpec((count, width, ff_pair), weight_block),
    ]
    operands = [rows, place, weight]
    if added is not None:
        in_specs.append(pl.BlockSpec((per_step, columns), lambda step, piece_ref: (step, 0)))
        operands.append(added)
    return pl.pallas_call(
        functools.partial(gate_up_kernel, per_step, added is not None),
        grid_spec=pltpu.PrefetchScalarGridSpec(
            num_scalar_prefetch=1,
            grid=(steps,),
            in_specs=in_specs,
            out_specs=pl.BlockSpec((per_step, columns), lambda step, piece_ref: (step, 0)),
            scratch_shapes=[pltpu.VMEM((slots, rows.shape[1]), bf16)],
        ),
        out_shape=jax.ShapeDtypeStruct((slots, columns), bf16),
        compiler_params=params(32, 1),
        cost_estimate=pl.CostEstimate(
            flops=2 * slots * width * ff_pair,
            bytes_accessed=2 * experts * width * ff_pair,
            transcendentals=0,
        ),
        name="gate_up_sum" if added is not None else "gate_up",
    )(piece, *operands)


def hidden_kernel(part_count, model_width, *refs):
    out_ref = refs[-1]
    ff_width = out_ref.shape[1]
    total = refs[0][...].astype(f32)
    for ref in refs[1:part_count]:
        total = total + ref[...].astype(f32)
    squares = total[:, 2 * ff_width : 2 * ff_width + 1] + total[:, 2 * ff_width + 1 : 2 * ff_width + 2]
    norm = lax.rsqrt(squares / model_width + epsilon)
    gate = total[:, :ff_width] * norm
    up = total[:, ff_width : 2 * ff_width] * norm
    out_ref[...] = (gate / (1.0 + jnp.exp(-gate)) * up).astype(bf16)


def hidden_of(parts, ff_width, model_width):
    return pl.pallas_call(
        functools.partial(hidden_kernel, len(parts), model_width),
        out_shape=jax.ShapeDtypeStruct((parts[0].shape[0], ff_width), bf16),
        compiler_params=params(16),
        name="hidden",
    )(*parts)


def down_kernel(piece_ref, hidden_ref, weight_ref, high_ref, low_ref, out_ref, total_ref, held_ref):
    piece, step = pl.program_id(0), pl.program_id(1)
    rows = hidden_ref.shape[1]
    count = weight_ref.shape[0]
    each = rows // count
    for i in range(count):
        here = slice(i * each, (i + 1) * each)
        product = dot(hidden_ref[0, here, :], weight_ref[i]).astype(bf16)
        start = pl.multiple_of(step * rows + i * each, each)
        held_ref[pl.ds(start, each), :] = product

    @pl.when(step == pl.num_programs(1) - 1)
    def combine():
        held = held_ref[...]
        part = dot(high_ref[0], held) + dot(low_ref[0], held)

        @pl.when(piece == 0)
        def first():
            total_ref[...] = part

        @pl.when(piece > 0)
        def later():
            total_ref[...] += part

        @pl.when(piece == pl.num_programs(0) - 1)
        def last():
            out_ref[...] = total_ref[...].astype(bf16)


def down(pieces, hidden, weight, high, low):
    held_count, slots, ff_width = hidden.shape
    piece_count, tokens, _ = high.shape
    local_experts, _, piece_width = weight.shape
    capacity = piece_count * slots // local_experts
    experts = max(1, slots // capacity)
    count = 2 if experts % 2 == 0 else 1
    steps = experts // count
    per_step = slots // steps

    def weight_block(piece, step, piece_ref):
        return ((piece_ref[piece] * slots // capacity) // count + step, 0, 0)

    def route_block(piece, step, piece_ref):
        return (piece_ref[piece], 0, 0)

    return pl.pallas_call(
        down_kernel,
        grid_spec=pltpu.PrefetchScalarGridSpec(
            num_scalar_prefetch=1,
            grid=(held_count, steps),
            in_specs=[
                pl.BlockSpec((1, per_step, ff_width), lambda piece, step, piece_ref: (piece, step, 0)),
                pl.BlockSpec((count, ff_width, piece_width), weight_block),
                pl.BlockSpec((1, tokens, slots), route_block),
                pl.BlockSpec((1, tokens, slots), route_block),
            ],
            out_specs=pl.BlockSpec((tokens, piece_width), lambda piece, step, piece_ref: (0, 0)),
            scratch_shapes=[
                pltpu.VMEM((tokens, piece_width), f32),
                pltpu.VMEM((slots, piece_width), bf16),
            ],
        ),
        out_shape=jax.ShapeDtypeStruct((tokens, piece_width), bf16),
        compiler_params=params(32, 2),
        cost_estimate=pl.CostEstimate(
            flops=2 * held_count * slots * ff_width * piece_width,
            bytes_accessed=2 * held_count * experts * ff_width * piece_width,
            transcendentals=0,
        ),
        name="down",
    )(pieces, hidden, weight, high, low)


def body(
    queries,
    cached_keys,
    cached_values,
    key_seg,
    query_seg,
    parent,
    out_weight,
    residual,
    norm_gain,
    gate_up_weight,
    down_weight,
    expert_ids,
    route_weight,
):
    ctx_count, exp_count, tp_count = (lax.axis_size(axis) for axis in ("ctx", "exp", "tp"))
    own_ctx, own_exp, own_tp = (lax.axis_index(axis) for axis in ("ctx", "exp", "tp"))
    assert tp_count == 2 and cached_keys.shape[1] == 1
    piece_count = exp_count * tp_count
    query_rows = queries.shape[0]
    key_count, _, head_size = cached_keys.shape
    heads = queries.shape[2] // head_size
    width = heads * head_size
    model_width = out_weight.shape[2]
    local_experts, piece_width, _ = gate_up_weight.shape
    ff_width = down_weight.shape[1]
    choices = expert_ids.shape[1]
    token_count = ctx_count * query_rows
    slots = local_experts * ctx_count * MOST // piece_count
    scale = math.log2(math.e) / math.sqrt(head_size)

    route_high = route_weight.astype(bf16)
    route_low = (route_weight - lax.reduce_precision(route_weight, 8, 7)).astype(bf16)
    info = jnp.concatenate(
        [query_seg[:, None].astype(bf16), expert_ids.astype(bf16), route_high, route_low], axis=1
    )
    info = jnp.pad(info, ((0, 0), (0, LANES - info.shape[1])))
    packed = jnp.concatenate([queries.reshape(query_rows, width), info], axis=1)
    gathered = collect(packed, "ctx").reshape(token_count, width + LANES)

    sight = sight_of(parent, key_seg)
    lead = ctx_count * (key_count - query_rows) - own_ctx * key_count
    attended = attend(
        lead.astype(jnp.int32)[None],
        gathered,
        cached_keys.reshape(key_count, head_size),
        cached_values.reshape(key_count, head_size),
        sight,
        heads,
        scale,
    )
    parts = exchange(attended.reshape(ctx_count, query_rows, width + LANES), "ctx")
    place, combine_high, combine_low = route(
        (own_ctx * local_experts).astype(jnp.int32)[None],
        gathered[:, width:],
        local_experts,
        choices,
        piece_count,
        slots,
    )
    projected = project(
        parts, out_weight.reshape(width, model_width), heads, scale, piece_count
    )
    mixed, sent = mix(exchange(projected, ("exp", "tp")), residual, norm_gain)
    rows = collect(sent, "ctx").reshape(token_count, piece_width + LANES)

    def piece_at(tp_index, exp_index):
        return (tp_index * exp_count + exp_index).astype(jnp.int32)[None]

    steps = list(range(1, exp_count)) + [0]
    targets = [(own_exp + step) % exp_count for step in steps]
    away = [gate_up(piece_at(1 - own_tp, at), rows, place, gate_up_weight) for at in targets]
    arrived = [shifted(value, "tp", 1) for value in away]
    summed = [
        gate_up(piece_at(own_tp, at), rows, place, gate_up_weight, value)
        for at, value in zip(targets, arrived)
    ]
    finals = [shifted(value, "exp", step) for value, step in zip(summed[:-1], steps[:-1])]
    own_hidden = hidden_of([summed[-1]] + finals, ff_width, model_width)

    here = [own_hidden] + [shifted(own_hidden, "exp", step) for step in range(1, exp_count)]
    sources = [(own_exp - step) % exp_count for step in range(exp_count)]
    here = jnp.stack(here)
    there = shifted(here, "tp", 1)
    pieces = jnp.concatenate(
        [piece_at(own_tp, at) for at in sources] + [piece_at(1 - own_tp, at) for at in sources]
    )
    moe_part = down(
        pieces, jnp.concatenate([here, there]), down_weight, combine_high, combine_low
    )
    returned = exchange(moe_part.reshape(ctx_count, query_rows, piece_width), "ctx")
    return (mixed + jnp.sum(returned.astype(f32), axis=0)).astype(bf16)


def solution(mesh):
    in_specs = (
        P(("group", "ctx"), "tp", "exp"),
        P(("group", "ctx"), "tp", None),
        P(("group", "ctx"), "tp", None),
        P(("group", "ctx")),
        P(("group", "ctx")),
        P("group"),
        P("tp", "exp", None),
        P(("group", "ctx"), ("exp", "tp")),
        P(("exp", "tp")),
        P("ctx", ("exp", "tp"), None),
        P("ctx", None, ("exp", "tp")),
        P(("group", "ctx"), None),
        P(("group", "ctx"), None),
    )
    out_specs = P(("group", "ctx"), ("exp", "tp"))
    return jax.shard_map(body, mesh=mesh, in_specs=in_specs, out_specs=out_specs, check_vma=False)
```

time: 232 us -> 113 us (0.49)
  waiting for transfers between devices: 121 us -> 31.9 us
  matrix products: 35.9 us -> 0 us
  Pallas kernels: 0 us -> 27.6 us
  starting transfers between devices: 30 us -> 14.9 us
  between operations: 13.6 us -> 0.18 us
  local copies, waits for them, and re-layouts: 2.23 us -> 13.2 us
  other arithmetic: 10.4 us -> 3.81 us
  blocking collectives: 17.8 us -> 20.2 us
    psum x2 -> x0, waiting for transfers between devices: 96 us -> none  [the longest x1 67 us: body(): summed = lax.psum(gate_up, ('exp', 'tp'))]
    dot_general x17 -> x0, matrix products: 35.9 us -> none  [the longest x1 14.1 us: body(): jnp.einsum('cesd,edf->cesf', lax.all_to_all(outgoing, 'ctx', split_axis=0...]
    pallas_call x0 -> x11, Pallas kernels: none -> 27.6 us  [the longest x4 14 us: gate_up(): pl.pallas_call(functools.partial(gate_up_kernel, per_step, added is not N...]
    ppermute x20 -> x5, starting transfers between devices: 25.4 us -> 1.96 us  [shifted(): return lax.ppermute(value, axis, pairs)]
    unnamed x15, local copies, waits for them, and re-layouts: 0.88 us -> 11 us
    reduce_sum x13 -> x1, other arithmetic: 8.54 us -> 0.02 us  [body(): return (mixed + jnp.sum(returned.astype(f32), axis=0)).astype(bf16)]
    all_to_all x1 -> x3, starting transfers between devices: 4.6 us -> 13 us  [exchange(): return lax.all_to_all(pieces, axes, split_axis=0, concat_axis=0, tiled=True)]
    ppermute x20 -> x5, waiting for transfers between devices: 10.8 us -> 14.7 us  [shifted(): return lax.ppermute(value, axis, pairs)]
  transfers between devices with their start and end apart: 23 -> 8, of which waited for: 7 -> 6; matrix products, arithmetic and copies ran while one was open for 5% -> 1% of each run, Pallas kernels for 0% -> 10%
where the time goes in v1:
time: 113 us; the launch traced here: 112 us
  waiting for transfers between devices  31.9 us (28%)
  Pallas kernels  27.6 us (24%)
  blocking collectives  20.2 us (18%)
  starting transfers between devices  14.9 us (13%)
  local copies, waits for them, and re-layouts  13.2 us (12%)
  other arithmetic  3.81 us (3%)
    all_to_all x2, blocking collectives, exchange(): return lax.all_to_all(pieces, axes, split_axis=0, concat_axis=0, tiled=True)  20.2 us
    all_to_all x3, waiting for transfers between devices, exchange(): return lax.all_to_all(pieces, axes, split_axis=0, concat_axis=0, tiled=True)  17.3 us
    ppermute x5, waiting for transfers between devices, shifted(): return lax.ppermute(value, axis, pairs)  14.7 us
    pallas_call x4, Pallas kernels, gate_up(): pl.pallas_call(functools.partial(gate_up_kernel, per_step, added is not N...  14 us
    all_to_all x3, starting transfers between devices, exchange(): return lax.all_to_all(pieces, axes, split_axis=0, concat_axis=0, tiled=True)  13 us
    unnamed x15, local copies, waits for them, and re-layouts  11 us
    pallas_call x1, Pallas kernels, down(): pl.pallas_call(down_kernel, grid_spec=pltpu.PrefetchScalarGridSpec(num_sc...  4.64 us
    pallas_call x1, Pallas kernels, attend(): pl.pallas_call(functools.partial(attend_kernel, heads, scale), grid=(toke...  4.63 us
  transfers between devices with their start and end apart: 8, of which 6 were waited for; matrix products, arithmetic and copies ran while one was open for 1% of the time, Pallas kernels for 10%

profile of v1, /device:TPU:0, one launch (start us, length us, event | category | flops | bytes accessed | tf_op | source)
XLA Modules:
  0.0 111.8 jit_solution(10806128244522831348)
XLA Ops:
  0.0 0.8 fusion.3
  2.2 0.8 fusion.1
  3.8 6.3 %all-to-all-start = ((bf16[4,32,1152]{2,1,0:T(8,128)(2,1)}), bf16[4,32,1152]{2,1,0:T(8,128)(2,1)S(1)}, u32[]{:S(2)}, u32[]{:S(2)}) async-start(bf16[4,32,1152]{2,1,0:T(8,128)(2,1)} %broadcast_in_dim.49), calls=%async_computation | async-start | bytes 589824 | tf_op jit(solution)/shard_map/all_to_all | solution.py:48
  12.1 7.6 %all-to-all-done = bf16[4,32,1152]{2,1,0:T(8,128)(2,1)S(1)} async-done(((bf16[4,32,1152]{2,1,0:T(8,128)(2,1)}), bf16[4,32,1152]{2,1,0:T(8,128)(2,1)S(1)}, u32[]{:S(2)}, u32[]{:S(2)}) %all-to-all-start) | async-done | bytes 294944 | tf_op jit(solution)/shard_map/all_to_all | solution.py:48
  19.7 1.0 copy-done.5
  20.8 1.0 copy-done.6
  21.8 4.6 %attend.1 = bf16[128,1152]{1,0:T(8,128)(2,1)S(1)} custom-call(s32[1]{0:T(128)} %bitcast.lead_ref, bf16[128,1152]{1,0:T(8,128)(2,1)S(1)} %bitcast.30, bf16[2048,128]{1,0:T(8,128)(2,1)S(1)} %bitcast.35, bf16[2048,128]{1,0:T(8,128)(2,1)S(1)} %bitcast.36, bf16[64,2048]{1,0:T(8,128)(2,1)S(1)} %sight.1.sight_ref), custom_call_target="tpu_custom_call" | custom-call | flops 1073741824 | bytes 2097152 | tf_op jit(solution)/shard_map/attend/pallas_call | solution.py:119
  26.5 11.2 %all_to_all.25.parts_ref = bf16[4,32,1152]{2,1,0:T(8,128)(2,1)S(1)} all-to-all(bf16[4,32,1152]{2,1,0:T(8,128)(2,1)S(1)} %bitcast.32), channel_id=1, replica_groups=mesh['group'=2,'ctx'=4,'exp'=2,'tp'=2] {'ctx'}, dimensions={0} | all-to-all | bytes 589824 | tf_op jit(solution)/shard_map/all_to_all | solution.py:48
  37.7 2.2 %copy-done.1 = bf16[1,1024,2048]{2,1,0:T(8,128)(2,1)S(1)} copy-done((bf16[1,1024,2048]{2,1,0:T(8,128)(2,1)S(1)}, bf16[1,1024,2048]{2,1,0:T(8,128)(2,1)}, u32[]{:S(2)}) %copy-start.1) | copy-done | bytes 4194328
  39.9 2.7 %project.1 = bf16[4,32,512]{2,1,0:T(8,128)(2,1)} custom-call(bf16[4,32,1152]{2,1,0:T(8,128)(2,1)S(1)} %all_to_all.25.parts_ref, bf16[1024,2048]{1,0:T(8,128)(2,1)S(1)} %bitcast.22), custom_call_target="tpu_custom_call" | custom-call | flops 134217728 | bytes 4194304 | tf_op jit(solution)/shard_map/project/pallas_call | solution.py:170
  42.6 3.3 %all-to-all-start.2 = ((bf16[4,32,512]{2,1,0:T(8,128)(2,1)}), bf16[4,32,512]{2,1,0:T(8,128)(2,1)S(1)}, u32[]{:S(2)}, u32[]{:S(2)}) async-start(bf16[4,32,512]{2,1,0:T(8,128)(2,1)} %project.1), calls=%async_computation.2 | async-start | bytes 262144 | tf_op jit(solution)/shard_map/all_to_all | solution.py:48
  46.6 3.9 %all-to-all-done.2.parts_ref = bf16[4,32,512]{2,1,0:T(8,128)(2,1)S(1)} async-done(((bf16[4,32,512]{2,1,0:T(8,128)(2,1)}), bf16[4,32,512]{2,1,0:T(8,128)(2,1)S(1)}, u32[]{:S(2)}, u32[]{:S(2)}) %all-to-all-start.2) | async-done | bytes 131104 | tf_op jit(solution)/shard_map/all_to_all | solution.py:48
  52.1 3.3 %all-to-all-start.3 = ((bf16[4,32,640]{2,1,0:T(8,128)(2,1)}), bf16[4,32,640]{2,1,0:T(8,128)(2,1)S(1)}, u32[]{:S(2)}, u32[]{:S(2)}) async-start(bf16[4,32,640]{2,1,0:T(8,128)(2,1)} %broadcast_in_dim.57), calls=%async_computation.3 | async-start | bytes 327680 | tf_op jit(solution)/shard_map/all_to_all | solution.py:48
  56.1 5.7 %all-to-all-done.3 = bf16[4,32,640]{2,1,0:T(8,128)(2,1)S(1)} async-done(((bf16[4,32,640]{2,1,0:T(8,128)(2,1)}), bf16[4,32,640]{2,1,0:T(8,128)(2,1)S(1)}, u32[]{:S(2)}, u32[]{:S(2)}) %all-to-all-start.3) | async-done | bytes 163872 | tf_op jit(solution)/shard_map/all_to_all | solution.py:48
  61.8 3.5 %gate_up.3 = bf16[128,1664]{1,0:T(8,128)(2,1)S(1)} custom-call(s32[1]{0:T(128)} %bitcast.17.piece_ref, bf16[128,640]{1,0:T(8,128)(2,1)S(1)} %bitcast.23, bf16[4,128,128]{2,1,0:T(8,128)(2,1)S(1)} %get-tuple-element.12.place_ref, bf16[16,512,1536]{2,1,0:T(8,128)(2,1)} %weight_ref.8), custom_call_target="tpu_custom_call" | custom-call | flops 201326592 | bytes 6291456 | tf_op jit(solution)/shard_map/gate_up/pallas_call | solution.py:312
  65.3 3.5 %gate_up.2 = bf16[128,1664]{1,0:T(8,128)(2,1)S(1)} custom-call(s32[1]{0:T(128)} %bitcast.12.piece_ref, bf16[128,640]{1,0:T(8,128)(2,1)S(1)} %bitcast.24, bf16[4,128,128]{2,1,0:T(8,128)(2,1)S(1)} %get-tuple-element.12.place_ref, bf16[16,512,1536]{2,1,0:T(8,128)(2,1)} %weight_ref.8), custom_call_target="tpu_custom_call" | custom-call | flops 201326592 | bytes 6291456 | tf_op jit(solution)/shard_map/gate_up/pallas_call | solution.py:312
  69.3 3.5 %gate_up_sum.3 = bf16[128,1664]{1,0:T(8,128)(2,1)S(1)} custom-call(s32[1]{0:T(128)} %bitcast.16.piece_ref, bf16[128,640]{1,0:T(8,128)(2,1)S(1)} %bitcast.25, bf16[4,128,128]{2,1,0:T(8,128)(2,1)S(1)} %get-tuple-element.12.place_ref, bf16[16,512,1536]{2,1,0:T(8,128)(2,1)} %weight_ref.8, bf16[128,1664]{1,0:T(8,128)(2,1)S(1)} %collective-permute-done.1.rest_0_), custom_call_target="tpu_custom_call" | custom-call | flops 201326592 | bytes 6291456 | tf_op jit(solution)/shard_map/gate_up_sum/pallas_call | solution.py:312
  73.5 3.5 %gate_up_sum.2.refs_0_ = bf16[128,1664]{1,0:T(8,128)(2,1)S(1)} custom-call(s32[1]{0:T(128)} %bitcast.10.piece_ref, bf16[128,640]{1,0:T(8,128)(2,1)S(1)} %bitcast.26, bf16[4,128,128]{2,1,0:T(8,128)(2,1)S(1)} %get-tuple-element.12.place_ref, bf16[16,512,1536]{2,1,0:T(8,128)(2,1)} %weight_ref.8, bf16[128,1664]{1,0:T(8,128)(2,1)S(1)} %collective-permute-done.rest_0_), custom_call_target="tpu_custom_call" | custom-call | flops 201326592 | bytes 6291456 | tf_op jit(solution)/shard_map/gate_up_sum/pallas_call | solution.py:312
  77.0 7.7 %collective-permute-done.2.refs_1_ = bf16[128,1664]{1,0:T(8,128)(2,1)S(1)} collective-permute-done((bf16[128,1664]{1,0:T(8,128)(2,1)S(1)}, bf16[128,1664]{1,0:T(8,128)(2,1)S(1)}, u32[]{:S(2)}, u32[]{:S(2)}) %collective-permute-start.2) | collective-permute-done | bytes 426016 | tf_op jit(solution)/shard_map/ppermute | solution.py:59
  85.7 5.4 %collective-permute-done.3 = bf16[128,768]{1,0:T(8,128)(2,1)S(1)} collective-permute-done((bf16[128,768]{1,0:T(8,128)(2,1)S(1)}, bf16[128,768]{1,0:T(8,128)(2,1)S(1)}, u32[]{:S(2)}, u32[]{:S(2)}) %collective-permute-start.3) | collective-permute-done | bytes 196640 | tf_op jit(solution)/shard_map/ppermute | solution.py:59
  91.3 1.6 %collective-permute-done.4 = bf16[2,128,768]{2,1,0:T(8,128)(2,1)S(1)} collective-permute-done((bf16[2,128,768]{2,1,0:T(8,128)(2,1)S(1)}, bf16[2,128,768]{2,1,0:T(8,128)(2,1)S(1)}, u32[]{:S(2)}, u32[]{:S(2)}) %collective-permute-start.4) | collective-permute-done | bytes 393248 | tf_op jit(solution)/shard_map/ppermute | solution.py:59
  93.0 4.6 %copy-done = bf16[16,768,512]{2,1,0:T(8,128)(2,1)S(1)} copy-done((bf16[16,768,512]{2,1,0:T(8,128)(2,1)S(1)}, bf16[16,768,512]{2,1,0:T(8,128)(2,1)}, u32[]{:S(2)}) %copy-start) | copy-done | bytes 12582936
  97.5 4.6 %down.1 = bf16[128,512]{1,0:T(8,128)(2,1)S(1)} custom-call(s32[4]{0:T(128)S(1)} %pad_add_fusion.piece_ref, bf16[4,128,768]{2,1,0:T(8,128)(2,1)S(1)} %pad_maximum_fusion.hidden_ref, bf16[16,768,512]{2,1,0:T(8,128)(2,1)S(1)} %copy-done, bf16[4,128,128]{2,1,0:T(8,128)(2,1)S(1)} %get-tuple-element.13.high_ref, bf16[4,128,128]{2,1,0:T(8,128)(2,1)S(1)} %get-tuple-element.14.low_ref), custom_call_target="tpu_custom_call" | custom-call | flops 402653184 | bytes 12582912 | tf_op jit(solution)/shard_map/down/pallas_call | solution.py:399
  102.2 9.0 %all_to_all.26 = bf16[4,32,512]{2,1,0:T(8,128)(2,1)S(1)} all-to-all(bf16[4,32,512]{2,1,0:T(8,128)(2,1)S(1)} %bitcast.29), channel_id=1, replica_groups=mesh['group'=2,'ctx'=4,'exp'=2,'tp'=2] {'ctx'}, dimensions={0} | all-to-all | bytes 262144 | tf_op jit(solution)/shard_map/all_to_all | solution.py:48
  (34 shorter events, 10.1 us)
Async XLA Ops:
  3.8 15.9 %all-to-all-start = ((bf16[4,32,1152]{2,1,0:T(8,128)(2,1)}), bf16[4,32,1152]{2,1,0:T(8,128)(2,1)S(1)}, u32[]{:S(2)}, u32[]{:S(2)}) async-start(bf16[4,32,1152]{2,1,0:T(8,128)(2,1)} %broadcast_in_dim.49), calls=%async_computation | async-start | bytes 589824 | tf_op jit(solution)/shard_map/all_to_all | solution.py:48
  10.1 0.7 copy-start.3
  10.8 0.7 copy-start.4
  19.7 1.0 copy-start.5
  20.8 1.0 copy-start.6
  37.7 2.2 %copy-start.1 = (bf16[1,1024,2048]{2,1,0:T(8,128)(2,1)S(1)}, bf16[1,1024,2048]{2,1,0:T(8,128)(2,1)}, u32[]{:S(2)}) copy-start(bf16[1,1024,2048]{2,1,0:T(8,128)(2,1)} %param.19) | copy-start | bytes 12582916
  42.6 7.9 %all-to-all-start.2 = ((bf16[4,32,512]{2,1,0:T(8,128)(2,1)}), bf16[4,32,512]{2,1,0:T(8,128)(2,1)S(1)}, u32[]{:S(2)}, u32[]{:S(2)}) async-start(bf16[4,32,512]{2,1,0:T(8,128)(2,1)} %project.1), calls=%async_computation.2 | async-start | bytes 262144 | tf_op jit(solution)/shard_map/all_to_all | solution.py:48
  50.5 0.8 copy-start.2
  52.1 9.7 %all-to-all-start.3 = ((bf16[4,32,640]{2,1,0:T(8,128)(2,1)}), bf16[4,32,640]{2,1,0:T(8,128)(2,1)S(1)}, u32[]{:S(2)}, u32[]{:S(2)}) async-start(bf16[4,32,640]{2,1,0:T(8,128)(2,1)} %broadcast_in_dim.57), calls=%async_computation.3 | async-start | bytes 327680 | tf_op jit(solution)/shard_map/all_to_all | solution.py:48
  65.3 4.1 %collective-permute-start.1 = (bf16[128,1664]{1,0:T(8,128)(2,1)S(1)}, bf16[128,1664]{1,0:T(8,128)(2,1)S(1)}, u32[]{:S(2)}, u32[]{:S(2)}) collective-permute-start(bf16[128,1664]{1,0:T(8,128)(2,1)S(1)} %gate_up.3), channel_id=1, source_target_pairs={{0,1},{1,0},{2,3},{3,2},{4,5},{5,4},{6,7},{7,6},{8,9},{9,8},{10,11... | collective-permute-start | bytes 1277960 | tf_op jit(solution)/shard_map/ppermute | solution.py:59
  68.8 4.7 %collective-permute-start = (bf16[128,1664]{1,0:T(8,128)(2,1)S(1)}, bf16[128,1664]{1,0:T(8,128)(2,1)S(1)}, u32[]{:S(2)}, u32[]{:S(2)}) collective-permute-start(bf16[128,1664]{1,0:T(8,128)(2,1)S(1)} %gate_up.2), channel_id=1, source_target_pairs={{0,1},{1,0},{2,3},{3,2},{4,5},{5,4},{6,7},{7,6},{8,9},{9,8},{10,11... | collective-permute-start | bytes 1277960 | tf_op jit(solution)/shard_map/ppermute | solution.py:59
  72.8 11.8 %collective-permute-start.2 = (bf16[128,1664]{1,0:T(8,128)(2,1)S(1)}, bf16[128,1664]{1,0:T(8,128)(2,1)S(1)}, u32[]{:S(2)}, u32[]{:S(2)}) collective-permute-start(bf16[128,1664]{1,0:T(8,128)(2,1)S(1)} %gate_up_sum.3), channel_id=1, source_target_pairs={{0,2},{2,0},{1,3},{3,1},{4,6},{6,4},{5,7},{7,5},{8,10},{10,8},{9,1... | collective-permute-start | bytes 1277960 | tf_op jit(solution)/shard_map/ppermute | solution.py:59
  85.0 6.1 %collective-permute-start.3 = (bf16[128,768]{1,0:T(8,128)(2,1)S(1)}, bf16[128,768]{1,0:T(8,128)(2,1)S(1)}, u32[]{:S(2)}, u32[]{:S(2)}) collective-permute-start(bf16[128,768]{1,0:T(8,128)(2,1)S(1)} %hidden.1), channel_id=1, source_target_pairs={{0,2},{2,0},{1,3},{3,1},{4,6},{6,4},{5,7},{7,5},{8,10},{10,8},{9,1... | collective-permute-start | bytes 589832 | tf_op jit(solution)/shard_map/ppermute | solution.py:59
  91.1 1.8 %collective-permute-start.4 = (bf16[2,128,768]{2,1,0:T(8,128)(2,1)S(1)}, bf16[2,128,768]{2,1,0:T(8,128)(2,1)S(1)}, u32[]{:S(2)}, u32[]{:S(2)}) collective-permute-start(bf16[2,128,768]{2,1,0:T(8,128)(2,1)S(1)} %pad_maximum_fusion.1), channel_id=1, source_target_pairs={{0,1},{1,0},{2,3},{3,2},{4,5},{5,4},{6,7},{7,6},{8,9},{9,8},{10,11... | collective-permute-start | bytes 1179656 | tf_op jit(solution)/shard_map/ppermute | solution.py:59
  93.0 4.6 %copy-start = (bf16[16,768,512]{2,1,0:T(8,128)(2,1)S(1)}, bf16[16,768,512]{2,1,0:T(8,128)(2,1)}, u32[]{:S(2)}) copy-start(bf16[16,768,512]{2,1,0:T(8,128)(2,1)} %weight_ref.9) | copy-start | bytes 37748740

commit v2 on v1

v2 whole, which is shorter than its diff:
```python
import functools
import math

import jax
import jax.numpy as jnp
from jax import lax
from jax.experimental import pallas as pl
from jax.experimental.pallas import tpu as pltpu
from jax.sharding import PartitionSpec as P

MOST = 8
DEPTH = 6
LANES = 128

epsilon = 1e-06
masked_score = -1e30
least_high = -1e20

f32 = jnp.float32
bf16 = jnp.bfloat16


def params(megabytes, steps=0):
    semantics = ("arbitrary",) * steps if steps else None
    return pltpu.CompilerParams(
        vmem_limit_bytes=megabytes * 1024 * 1024, dimension_semantics=semantics
    )


def cost(flops, bytes_accessed, transcendentals=0):
    return pl.CostEstimate(
        flops=flops, bytes_accessed=bytes_accessed, transcendentals=transcendentals
    )


def whole(memory_space=pltpu.VMEM):
    return pl.BlockSpec(memory_space=memory_space)


def lane_ids(shape):
    return lax.broadcasted_iota(jnp.int32, shape, len(shape) - 1)


def row_ids(shape):
    return lax.broadcasted_iota(jnp.int32, shape, len(shape) - 2)


def as_bf16(mask):
    return mask.astype(f32).astype(bf16)


def dot(left, right, dims=((1,), (0,))):
    return lax.dot_general(left, right, (dims, ((), ())), preferred_element_type=f32)


def in_two(value):
    high = value.astype(bf16).astype(f32)
    return high, value - high


def swapped(value, axes, mask):
    count = lax.axis_size(axes)
    pairs = [(source, source ^ mask) for source in range(count)]
    return lax.ppermute(value, axes, pairs)


def far_first(count):
    return list(range(count - 1, 0, -1))


def pack_kernel(width, queries_ref, seg_ref, ids_ref, weight_ref, out_ref):
    rows = out_ref.shape[0]
    choices = ids_ref.shape[0]
    out_ref[:, :width] = queries_ref[...]
    shape = (choices, LANES)

    def placed(value, first, last):
        to_lane = (lane_ids(shape) == row_ids(shape) + first) & (row_ids(shape) <= last)
        return dot(value.astype(bf16), as_bf16(to_lane), ((0,), (0,)))

    segs = jnp.broadcast_to(seg_ref[...], (choices, rows)).astype(f32)
    high, low = in_two(weight_ref[...])
    info = placed(segs, 0, 0) + placed(ids_ref[...].astype(f32), 1, choices)
    info = info + placed(high, 1 + choices, choices) + placed(low, 1 + 2 * choices, choices)
    out_ref[:, width:] = info.astype(bf16)


def pack(queries, query_seg, expert_ids, route_weight):
    rows, width = queries.shape
    return pl.pallas_call(
        functools.partial(pack_kernel, width),
        out_shape=jax.ShapeDtypeStruct((rows, width + LANES), bf16),
        compiler_params=params(4),
        name="pack",
    )(queries, query_seg[None, :], expert_ids.T, route_weight.T)


def sight_kernel(parent_ref, key_seg_ref, sight_ref):
    seg_count, key_count = sight_ref.shape
    square = (seg_count, seg_count)
    same = row_ids(square) == lane_ids(square)
    one = as_bf16((parent_ref[...] == row_ids(square)) | same)
    two = as_bf16(dot(one, one) > 0.5)
    four = as_bf16(dot(two, two) > 0.5)
    six = as_bf16(dot(four, two) > 0.5)
    keys = as_bf16(key_seg_ref[...] == row_ids((seg_count, key_count)))
    sight_ref[...] = dot(six, keys, ((0,), (0,))).astype(bf16)


def sight_of(parent, key_seg):
    assert DEPTH == 6
    return pl.pallas_call(
        sight_kernel,
        out_shape=jax.ShapeDtypeStruct((parent.shape[0], key_seg.shape[0]), bf16),
        compiler_params=params(4),
        cost_estimate=cost(2**24, 2**19),
        name="sight",
    )(parent[None, :], key_seg[None, :])


def attend_kernel(
    heads, scale, lead_at, plan_ref, queries_ref, keys_ref, values_ref, sight_ref, out_ref,
    stacked_ref, probs_ref,
):
    rows = queries_ref.shape[0]
    key_count, head_size = keys_ref.shape
    seg_count = sight_ref.shape[0]
    width = heads * head_size
    info = queries_ref[:, width:].astype(f32)
    own_seg = info[:, :1].astype(jnp.int32)
    onehot = as_bf16(own_seg == lane_ids((rows, seg_count)))
    seen = dot(onehot, sight_ref[...]) > 0.5
    place = (rows, key_count)
    causal = lane_ids(place) - row_ids(place) <= plan_ref[lead_at]
    bias = jnp.where(seen & causal, 0.0, masked_score)
    for head in range(heads):
        columns = slice(head * head_size, (head + 1) * head_size)
        stacked_ref[head * rows : (head + 1) * rows, :] = queries_ref[:, columns]
    scores = dot(stacked_ref[...], keys_ref[...], ((1,), (1,)))
    stats = jnp.zeros((rows, LANES), f32)
    lane = lane_ids((rows, LANES))
    for head in range(heads):
        here = slice(head * rows, (head + 1) * rows)
        biased = scores[here, :] + bias
        high = jnp.maximum(jnp.max(biased, axis=1, keepdims=True), least_high)
        high = high.astype(bf16).astype(f32)
        probs = jnp.exp2((biased - high) * scale)
        total_high, total_low = in_two(jnp.sum(probs, axis=1, keepdims=True))
        probs_ref[here, :] = probs.astype(bf16)
        stats = jnp.where(lane == head, high, stats)
        stats = jnp.where(lane == heads + head, total_high, stats)
        stats = jnp.where(lane == 2 * heads + head, total_low, stats)
    out_ref[:, width:] = stats.astype(bf16)
    sums = dot(probs_ref[...], values_ref[...])
    for head in range(heads):
        columns = slice(head * head_size, (head + 1) * head_size)
        out_ref[:, columns] = sums[head * rows : (head + 1) * rows, :].astype(bf16)


def attend(plan, lead_at, queries, keys, values, sight, heads, scale):
    rows, columns = queries.shape
    key_count, head_size = keys.shape
    work = rows * heads * key_count
    return pl.pallas_call(
        functools.partial(attend_kernel, heads, scale, lead_at),
        in_specs=[whole(pltpu.SMEM)] + [whole()] * 4,
        out_shape=jax.ShapeDtypeStruct((rows, columns), bf16),
        scratch_shapes=[
            pltpu.VMEM((rows * heads, head_size), bf16),
            pltpu.VMEM((rows * heads, key_count), bf16),
        ],
        compiler_params=params(12),
        cost_estimate=cost(8 * work * head_size, 2**20, work),
        name="attend",
    )(plan, queries, keys, values, sight)


def project_kernel(heads, scale, order_at, source_count, plan_ref, *refs):
    parts_refs, weight_ref = refs[:source_count], refs[source_count]
    out_refs, attention_ref = refs[source_count + 1 : -1], refs[-1]
    width = attention_ref.shape[1]
    head_size = width // heads
    stats = [ref[:, width:].astype(f32) for ref in parts_refs]
    top = functools.reduce(jnp.maximum, stats)
    factors = [jnp.exp2(jnp.minimum((stat - top) * scale, 0.0)) for stat in stats]
    total = 0.0
    for stat, factor in zip(stats, factors):
        high = pltpu.roll(stat, LANES - heads, 1)
        low = pltpu.roll(stat, LANES - 2 * heads, 1)
        total = total + factor * (high + low)
    shares = [factor / total for factor in factors]
    for head in range(heads):
        columns = slice(head * head_size, (head + 1) * head_size)
        merged = 0.0
        for ref, share in zip(parts_refs, shares):
            merged = merged + ref[:, columns].astype(f32) * share[:, head : head + 1]
        attention_ref[:, columns] = merged.astype(bf16)
    for i, out_ref in enumerate(out_refs):
        piece_width = out_ref.shape[1]
        start = pl.multiple_of(plan_ref[order_at + i] * piece_width, piece_width)
        out_ref[...] = dot(attention_ref[...], weight_ref[:, pl.ds(start, piece_width)]).astype(bf16)


def project(plan, order_at, parts, weight, heads, scale, piece_count):
    rows = parts[0].shape[0]
    width, model_width = weight.shape
    piece_width = model_width // piece_count
    return pl.pallas_call(
        functools.partial(project_kernel, heads, scale, order_at, len(parts)),
        in_specs=[whole(pltpu.SMEM)] + [whole()] * (len(parts) + 1),
        out_shape=[jax.ShapeDtypeStruct((rows, piece_width), bf16)] * piece_count,
        scratch_shapes=[pltpu.VMEM((rows, width), bf16)],
        compiler_params=params(8),
        cost_estimate=cost(2 * rows * width * model_width, 2 * width * model_width),
        name="project",
    )(plan, *parts, weight)


def mix_kernel(residual_ref, gain_ref, *refs):
    parts_refs, (mixed_ref, sent_ref) = refs[:-2], refs[-2:]
    rows, width = mixed_ref.shape
    mixed = residual_ref[...].astype(f32)
    for ref in parts_refs:
        mixed = mixed + ref[...].astype(f32)
    mixed_ref[...] = mixed
    sent_ref[:, :width] = (mixed * gain_ref[...].astype(f32)).astype(bf16)
    high, low = in_two(jnp.sum(mixed * mixed, axis=1, keepdims=True))
    lane = lane_ids((rows, LANES))
    squares = jnp.where(lane == 0, high, jnp.where(lane == 1, low, 0.0))
    sent_ref[:, width:] = squares.astype(bf16)


def mix(residual, gain, parts):
    rows, width = residual.shape
    return pl.pallas_call(
        mix_kernel,
        out_shape=(
            jax.ShapeDtypeStruct((rows, width), f32),
            jax.ShapeDtypeStruct((rows, width + LANES), bf16),
        ),
        compiler_params=params(4),
        name="mix",
    )(residual, gain[None, :], *parts)


def route_kernel(local_experts, choices, width, first_at, plan_ref, *refs):
    info_refs, (place_ref, high_ref, low_ref) = refs[:-3], refs[-3:]
    piece_count, tokens, slots = place_ref.shape
    info = jnp.concatenate([ref[:, width:] for ref in info_refs], axis=0).astype(f32)
    expert = (lane_ids((tokens, local_experts)) + plan_ref[first_at]).astype(f32)
    member = jnp.zeros((tokens, local_experts), f32)
    weight_high = jnp.zeros((tokens, local_experts), f32)
    weight_low = jnp.zeros((tokens, local_experts), f32)
    for k in range(choices):
        chosen = info[:, 1 + k : 2 + k] == expert
        high = info[:, 1 + choices + k : 2 + choices + k]
        low = info[:, 1 + 2 * choices + k : 2 + 2 * choices + k]
        member = jnp.where(chosen, 1.0, member)
        weight_high = jnp.where(chosen, high, weight_high)
        weight_low = jnp.where(chosen, low, weight_low)
    square = (tokens, tokens)
    earlier = as_bf16(lane_ids(square) < row_ids(square))
    rank = jnp.where(member > 0.5, dot(earlier, member.astype(bf16)), -1.0).astype(bf16)
    weight_high = weight_high.astype(bf16)
    weight_low = weight_low.astype(bf16)
    capacity = piece_count * slots // local_experts
    for piece in range(piece_count):
        slot = lane_ids((local_experts, slots)) + piece * slots
        spread = as_bf16(slot // capacity == row_ids((local_experts, slots)))
        wanted = (lane_ids((tokens, slots)) + piece * slots) % capacity
        placed = dot(rank, spread) == wanted.astype(f32)
        place_ref[piece] = jnp.where(placed, 1.0, 0.0).astype(bf16)
        high_ref[piece] = jnp.where(placed, dot(weight_high, spread), 0.0).astype(bf16)
        low_ref[piece] = jnp.where(placed, dot(weight_low, spread), 0.0).astype(bf16)


def route(plan, first_at, packed, width, local_experts, choices, piece_count, slots):
    tokens = sum(value.shape[0] for value in packed)
    shape = jax.ShapeDtypeStruct((piece_count, tokens, slots), bf16)
    return pl.pallas_call(
        functools.partial(route_kernel, local_experts, choices, width, first_at),
        in_specs=[whole(pltpu.SMEM)] + [whole()] * len(packed),
        out_shape=(shape, shape, shape),
        compiler_params=params(16),
        cost_estimate=cost(2**25, 2**20),
        name="route",
    )(plan, *packed)


def pick_kernel(place_ref, *refs):
    rows_refs, (out_ref, rows_ref) = refs[:-2], refs[-2:]
    rows = rows_refs[0].shape[0]
    for i, ref in enumerate(rows_refs):
        rows_ref[i * rows : (i + 1) * rows, :] = ref[...]
    for piece in range(out_ref.shape[0]):
        out_ref[piece] = dot(place_ref[piece], rows_ref[...], ((0,), (0,))).astype(bf16)


def pick(place, rows):
    piece_count, tokens, slots = place.shape
    columns = rows[0].shape[1]
    return pl.pallas_call(
        pick_kernel,
        out_shape=jax.ShapeDtypeStruct((piece_count, slots, columns), bf16),
        scratch_shapes=[pltpu.VMEM((tokens, columns), bf16)],
        compiler_params=params(8),
        cost_estimate=cost(2**26, 2**20),
        name="pick",
    )(place, *rows)


def gate_up_kernel(plan_ref, picked_ref, weight_ref, *rest):
    added_refs, out_ref = rest[:-1], rest[-1]
    _, width, ff_pair = weight_ref.shape
    picked = picked_ref[0]
    product = dot(picked[:, :width], weight_ref[0])
    squares = picked[:, width:].astype(f32)
    for ref in added_refs:
        product = product + ref[:, :ff_pair].astype(f32)
        squares = squares + ref[:, ff_pair:].astype(f32)
        high, low = in_two(squares[:, :1] + squares[:, 1:2])
        lane = lane_ids(squares.shape)
        squares = jnp.where(lane == 0, high, jnp.where(lane == 1, low, 0.0))
    out_ref[:, :ff_pair] = product.astype(bf16)
    out_ref[:, ff_pair:] = squares.astype(bf16)


def gate_up(plan, piece_at, picked, weight, added=None):
    piece_count, slots, picked_columns = picked.shape
    local_experts, width, ff_pair = weight.shape
    capacity = piece_count * slots // local_experts
    steps = max(1, slots // capacity)
    per_step = slots // steps
    columns = ff_pair + LANES

    def weight_block(step, plan_ref):
        return (plan_ref[piece_at] * slots // capacity + step, 0, 0)

    in_specs = [
        pl.BlockSpec(
            (1, per_step, picked_columns),
            lambda step, plan_ref: (plan_ref[piece_at], step, 0),
        ),
        pl.BlockSpec((1, width, ff_pair), weight_block),
    ]
    operands = [picked, weight]
    if added is not None:
        in_specs.append(pl.BlockSpec((per_step, columns), lambda step, plan_ref: (step, 0)))
        operands.append(added)
    return pl.pallas_call(
        gate_up_kernel,
        grid_spec=pltpu.PrefetchScalarGridSpec(
            num_scalar_prefetch=1,
            grid=(steps,),
            in_specs=in_specs,
            out_specs=pl.BlockSpec((per_step, columns), lambda step, plan_ref: (step, 0)),
        ),
        out_shape=jax.ShapeDtypeStruct((slots, columns), bf16),
        compiler_params=params(8, 1),
        cost_estimate=cost(2 * slots * width * ff_pair, 2 * steps * width * ff_pair),
        name="gate_up_sum" if added is not None else "gate_up",
    )(plan, *operands)


def hidden_kernel(part_count, model_width, *refs):
    out_ref = refs[-1]
    ff_width = out_ref.shape[1]
    total = refs[0][...].astype(f32)
    for ref in refs[1:part_count]:
        total = total + ref[...].astype(f32)
    squares = total[:, 2 * ff_width : 2 * ff_width + 1] + total[:, 2 * ff_width + 1 : 2 * ff_width + 2]
    norm = lax.rsqrt(squares / model_width + epsilon)
    gate = total[:, :ff_width] * norm
    up = total[:, ff_width : 2 * ff_width] * norm
    out_ref[...] = (gate / (1.0 + jnp.exp(-gate)) * up).astype(bf16)


def hidden_of(parts, ff_width, model_width):
    return pl.pallas_call(
        functools.partial(hidden_kernel, len(parts), model_width),
        out_shape=jax.ShapeDtypeStruct((parts[0].shape[0], ff_width), bf16),
        compiler_params=params(8),
        name="hidden",
    )(*parts)


def down_kernel(source_count, plan_ref, hidden_ref, weight_ref, high_ref, low_ref, *refs):
    total_ref = refs[0] if source_count else None
    *out_refs, held_ref = refs[source_count:]
    step = pl.program_id(0)
    each = hidden_ref.shape[0]
    start = pl.multiple_of(step * each, each)
    held_ref[pl.ds(start, each), :] = dot(hidden_ref[...], weight_ref[0]).astype(bf16)

    @pl.when(step == pl.num_programs(0) - 1)
    def combine():
        held = held_ref[...]
        total = dot(high_ref[0], held) + dot(low_ref[0], held)
        if total_ref is not None:
            total = total + total_ref[...]
        rows = out_refs[0].shape[0]
        for i, ref in enumerate(out_refs):
            ref[...] = total[i * rows : (i + 1) * rows, :].astype(ref.dtype)


def down(plan, piece_at, hidden, weight, high, low, total=None, out_count=1):
    slots, ff_width = hidden.shape
    piece_count, tokens, _ = high.shape
    local_experts, _, piece_width = weight.shape
    capacity = piece_count * slots // local_experts
    steps = max(1, slots // capacity)
    per_step = slots // steps
    rows = tokens // out_count

    def weight_block(step, plan_ref):
        return (plan_ref[piece_at] * slots // capacity + step, 0, 0)

    def route_block(step, plan_ref):
        return (plan_ref[piece_at], 0, 0)

    def fixed(step, plan_ref):
        return (0, 0)

    in_specs = [
        pl.BlockSpec((per_step, ff_width), lambda step, plan_ref: (step, 0)),
        pl.BlockSpec((1, ff_width, piece_width), weight_block),
        pl.BlockSpec((1, tokens, slots), route_block),
        pl.BlockSpec((1, tokens, slots), route_block),
    ]
    operands = [hidden, weight, high, low]
    if total is not None:
        in_specs.append(pl.BlockSpec((tokens, piece_width), fixed))
        operands.append(total)
    out_type = f32 if out_count == 1 else bf16
    return pl.pallas_call(
        functools.partial(down_kernel, 0 if total is None else 1),
        grid_spec=pltpu.PrefetchScalarGridSpec(
            num_scalar_prefetch=1,
            grid=(steps,),
            in_specs=in_specs,
            out_specs=[pl.BlockSpec((rows, piece_width), fixed)] * out_count,
            scratch_shapes=[pltpu.VMEM((slots, piece_width), bf16)],
        ),
        out_shape=[jax.ShapeDtypeStruct((rows, piece_width), out_type)] * out_count,
        compiler_params=params(8, 1),
        cost_estimate=cost(2 * slots * ff_width * piece_width, 2 * steps * ff_width * piece_width),
        name="down",
    )(plan, *operands)


def finish_kernel(mixed_ref, *refs):
    total = mixed_ref[...]
    for ref in refs[:-1]:
        total = total + ref[...].astype(f32)
    refs[-1][...] = total.astype(bf16)


def finish(mixed, parts):
    return pl.pallas_call(
        finish_kernel,
        out_shape=jax.ShapeDtypeStruct(mixed.shape, bf16),
        compiler_params=params(4),
        name="finish",
    )(mixed, *parts)


def body(
    queries,
    cached_keys,
    cached_values,
    key_seg,
    query_seg,
    parent,
    out_weight,
    residual,
    norm_gain,
    gate_up_weight,
    down_weight,
    expert_ids,
    route_weight,
):
    ctx_count, exp_count, tp_count = (lax.axis_size(axis) for axis in ("ctx", "exp", "tp"))
    own_ctx, own_exp, own_tp = (lax.axis_index(axis) for axis in ("ctx", "exp", "tp"))
    assert tp_count == 2 and cached_keys.shape[1] == 1
    assert ctx_count & (ctx_count - 1) == 0 and exp_count & (exp_count - 1) == 0
    piece_count = exp_count * tp_count
    query_rows = queries.shape[0]
    key_count, _, head_size = cached_keys.shape
    heads = queries.shape[2] // head_size
    width = heads * head_size
    model_width = out_weight.shape[2]
    local_experts, piece_width, _ = gate_up_weight.shape
    ff_width = down_weight.shape[1]
    choices = expert_ids.shape[1]
    slots = local_experts * ctx_count * MOST // piece_count
    scale = math.log2(math.e) / math.sqrt(head_size)

    last = ctx_count * (key_count - query_rows) - own_ctx * key_count
    leads = [last + (own_ctx ^ k) * query_rows for k in range(ctx_count)]
    own_piece = own_exp * tp_count + own_tp
    column_pieces = [own_piece ^ k for k in range(piece_count)]
    slot_pieces = [
        (own_tp ^ flip) * exp_count + (own_exp ^ k) for flip in (0, 1) for k in range(exp_count)
    ]
    scalars = [own_ctx * local_experts] + leads + column_pieces + slot_pieces
    plan = jnp.stack([jnp.asarray(value, jnp.int32) for value in scalars])
    lead_at = 1
    order_at = lead_at + ctx_count
    mine_at = order_at + piece_count
    away_at = mine_at + exp_count

    packed = pack(queries.reshape(query_rows, width), query_seg, expert_ids, route_weight)
    gathered = {0: packed}
    for k in far_first(ctx_count):
        gathered[k] = swapped(packed, "ctx", k)
    sight = sight_of(parent, key_seg)
    keys = cached_keys.reshape(key_count, head_size)
    values = cached_values.reshape(key_count, head_size)
    parts = []
    for k in range(ctx_count):
        part = attend(plan, lead_at + k, gathered[k], keys, values, sight, heads, scale)
        parts.append(swapped(part, "ctx", k) if k else part)
    place, combine_high, combine_low = route(
        plan,
        0,
        [gathered[k] for k in range(ctx_count)],
        width,
        local_experts,
        choices,
        piece_count,
        slots,
    )
    projected = project(
        plan, order_at, parts, out_weight.reshape(width, model_width), heads, scale, piece_count
    )
    pieces = [projected[0]] + [
        swapped(projected[k], ("exp", "tp"), k) for k in far_first(piece_count)
    ]
    mixed, sent = mix(residual, norm_gain, pieces)
    rows = {0: sent}
    for k in far_first(ctx_count):
        rows[k] = swapped(sent, "ctx", k)
    picked = pick(place, [rows[k] for k in range(ctx_count)])

    finals = []
    for k in far_first(exp_count) + [0]:
        away = gate_up(plan, away_at + k, picked, gate_up_weight)
        summed = gate_up(plan, mine_at + k, picked, gate_up_weight, swapped(away, "tp", 1))
        finals.append(swapped(summed, "exp", k) if k else summed)
    own_hidden = hidden_of(finals, ff_width, model_width)

    total = None
    for k in range(exp_count):
        here = swapped(own_hidden, "exp", k) if k else own_hidden
        there = swapped(here, "tp", 1)
        for piece_at, hidden in ((mine_at + k, here), (away_at + k, there)):
            ends = piece_at == away_at + exp_count - 1
            totals = down(
                plan,
                piece_at,
                hidden,
                down_weight,
                combine_high,
                combine_low,
                total,
                ctx_count if ends else 1,
            )
            total = totals[0]
    returned = [totals[0]] + [swapped(totals[k], "ctx", k) for k in far_first(ctx_count)]
    return finish(mixed, returned)


def solution(mesh):
    in_specs = (
        P(("group", "ctx"), "tp", "exp"),
        P(("group", "ctx"), "tp", None),
        P(("group", "ctx"), "tp", None),
        P(("group", "ctx")),
        P(("group", "ctx")),
        P("group"),
        P("tp", "exp", None),
        P(("group", "ctx"), ("exp", "tp")),
        P(("exp", "tp")),
        P("ctx", ("exp", "tp"), None),
        P("ctx", None, ("exp", "tp")),
        P(("group", "ctx"), None),
        P(("group", "ctx"), None),
    )
    out_specs = P(("group", "ctx"), ("exp", "tp"))
    return jax.shard_map(body, mesh=mesh, in_specs=in_specs, out_specs=out_specs, check_vma=False)
```

time: 113 us -> 93.1 us (0.82)
  blocking collectives: 20.2 us -> 0 us
  starting transfers between devices: 14.9 us -> 24 us
  waiting for transfers between devices: 31.9 us -> 24.1 us
  other arithmetic: 3.81 us -> 0.01 us
  local copies, waits for them, and re-layouts: 13.2 us -> 16.8 us
    ppermute x5 -> x21, starting transfers between devices: 1.96 us -> 24 us  [swapped(): return lax.ppermute(value, axes, pairs)]
    all_to_all x2 -> x0, blocking collectives: 20.2 us -> none  [exchange(): return lax.all_to_all(pieces, axes, split_axis=0, concat_axis=0, tiled=True)]
    all_to_all x3 -> x0, waiting for transfers between devices: 17.3 us -> none  [exchange(): return lax.all_to_all(pieces, axes, split_axis=0, concat_axis=0, tiled=True)]
    all_to_all x3 -> x0, starting transfers between devices: 13 us -> none  [exchange(): return lax.all_to_all(pieces, axes, split_axis=0, concat_axis=0, tiled=True)]
    ppermute x5 -> x21, waiting for transfers between devices: 14.7 us -> 24.1 us  [swapped(): return lax.ppermute(value, axes, pairs)]
    unnamed x15 -> x30, local copies, waits for them, and re-layouts: 11 us -> 16.7 us
    convert_element_type x4 -> x0, other arithmetic: 2.74 us -> none  [the longest x1 0.77 us: body(): route_high = route_weight.astype(bf16)]
    broadcast_in_dim x2 -> x0, local copies, waits for them, and re-layouts: 1.43 us -> none  [collect(): return exchange(jnp.broadcast_to(value[None], (count,) + value.shape), axis)]
  transfers between devices with their start and end apart: 8 -> 21, of which waited for: 6 -> 11; matrix products, arithmetic and copies ran while one was open for 1% -> 0% of each run, Pallas kernels for 10% -> 22%
where the time goes in v2:
time: 93.1 us; the launch traced here: 92.6 us
  Pallas kernels  27.5 us (30%)
  waiting for transfers between devices  24.1 us (26%)
  starting transfers between devices  24 us (26%)
  local copies, waits for them, and re-layouts  16.8 us (18%)
    ppermute x21, waiting for transfers between devices, swapped(): return lax.ppermute(value, axes, pairs)  24.1 us
    ppermute x21, starting transfers between devices, swapped(): return lax.ppermute(value, axes, pairs)  24 us
    unnamed x30, local copies, waits for them, and re-layouts  16.7 us
    pallas_call x4, Pallas kernels, gate_up(): pl.pallas_call(gate_up_kernel, grid_spec=pltpu.PrefetchScalarGridSpec(num...  8.29 us
    pallas_call x4, Pallas kernels, attend(): pl.pallas_call(functools.partial(attend_kernel, heads, scale, lead_at), i...  7.24 us
    pallas_call x4, Pallas kernels, down(): pl.pallas_call(functools.partial(down_kernel, 0 if total is None else 1),...  7.08 us
  transfers between devices with their start and end apart: 21, of which 11 were waited for; matrix products, arithmetic and copies ran while one was open for 0% of the time, Pallas kernels for 22%

profile of v2, /device:TPU:0, one launch (start us, length us, event | category | flops | bytes accessed | tf_op | source)
XLA Modules:
  0.0 92.6 jit_solution(13965134276682617208)
XLA Ops:
  3.1 3.0 %collective-permute-start = (bf16[32,1152]{1,0:T(8,128)(2,1)S(1)}, bf16[32,1152]{1,0:T(8,128)(2,1)S(1)}, u32[]{:S(2)}, u32[]{:S(2)}) collective-permute-start(bf16[32,1152]{1,0:T(8,128)(2,1)S(1)} %pack.1.queries_ref.refs_0_), channel_id=1, source_target_pairs={{0,4},{4,0},{8,12},{12,8},{1,5},{5,1},{9,13},{13,9},{2,6},{6,2},{1... | collective-permute-start | bytes 221192 | tf_op jit(solution)/shard_map/ppermute | solution.py:64
  6.1 2.6 %collective-permute-start.2 = (bf16[32,1152]{1,0:T(8,128)(2,1)S(1)}, bf16[32,1152]{1,0:T(8,128)(2,1)S(1)}, u32[]{:S(2)}, u32[]{:S(2)}) collective-permute-start(bf16[32,1152]{1,0:T(8,128)(2,1)S(1)} %pack.1.queries_ref.refs_0_), channel_id=1, source_target_pairs={{0,8},{4,12},{8,0},{12,4},{1,9},{5,13},{9,1},{13,5},{2,10},{6,14},... | collective-permute-start | bytes 221192 | tf_op jit(solution)/shard_map/ppermute | solution.py:64
  12.9 1.8 %attend.5 = bf16[32,1152]{1,0:T(8,128)(2,1)S(1)} custom-call(s32[13]{0:T(128)S(1)} %stack.55.plan_ref, bf16[32,1152]{1,0:T(8,128)(2,1)S(1)} %collective-permute-done.queries_ref.refs_1_, bf16[2048,128]{1,0:T(8,128)(2,1)S(1)} %bitcast.31, bf16[2048,128]{1,0:T(8,128)(2,1)S(1)} %bitcast.35, bf16[64,2048]{1,0:T(8,128)(2,1)S(1)} %sight.1.sight_ref), custom_call_target="tpu_custom_call" | custom-call | flops 536870912 | bytes 1048576 | tf_op jit(solution)/shard_map/attend/pallas_call | solution.py:164
  15.6 1.8 %attend.6 = bf16[32,1152]{1,0:T(8,128)(2,1)S(1)} custom-call(s32[13]{0:T(128)S(1)} %stack.55.plan_ref, bf16[32,1152]{1,0:T(8,128)(2,1)S(1)} %collective-permute-done.2.queries_ref.refs_2_, bf16[2048,128]{1,0:T(8,128)(2,1)S(1)} %bitcast.32, bf16[2048,128]{1,0:T(8,128)(2,1)S(1)} %bitcast.36, bf16[64,2048]{1,0:T(8,128)(2,1)S(1)} %sight.1.sight_ref), custom_call_target="tpu_custom_call" | custom-call | flops 536870912 | bytes 1048576 | tf_op jit(solution)/shard_map/attend/pallas_call | solution.py:164
  17.5 3.5 %collective-permute-start.3 = (bf16[32,1152]{1,0:T(8,128)(2,1)S(1)}, bf16[32,1152]{1,0:T(8,128)(2,1)S(1)}, u32[]{:S(2)}, u32[]{:S(2)}) collective-permute-start(bf16[32,1152]{1,0:T(8,128)(2,1)S(1)} %attend.6), channel_id=1, source_target_pairs={{0,8},{4,12},{8,0},{12,4},{1,9},{5,13},{9,1},{13,5},{2,10},{6,14},... | collective-permute-start | bytes 221192 | tf_op jit(solution)/shard_map/ppermute | solution.py:64
  21.0 1.8 %attend.7 = bf16[32,1152]{1,0:T(8,128)(2,1)S(1)} custom-call(s32[13]{0:T(128)S(1)} %stack.55.plan_ref, bf16[32,1152]{1,0:T(8,128)(2,1)S(1)} %collective-permute-done.4.queries_ref.refs_3_, bf16[2048,128]{1,0:T(8,128)(2,1)S(1)} %bitcast.33, bf16[2048,128]{1,0:T(8,128)(2,1)S(1)} %bitcast.37, bf16[64,2048]{1,0:T(8,128)(2,1)S(1)} %sight.1.sight_ref), custom_call_target="tpu_custom_call" | custom-call | flops 536870912 | bytes 1048576 | tf_op jit(solution)/shard_map/attend/pallas_call | solution.py:164
  22.9 1.8 %attend.4.refs_0_ = bf16[32,1152]{1,0:T(8,128)(2,1)S(1)} custom-call(s32[13]{0:T(128)S(1)} %stack.55.plan_ref, bf16[32,1152]{1,0:T(8,128)(2,1)S(1)} %pack.1.queries_ref.refs_0_, bf16[2048,128]{1,0:T(8,128)(2,1)S(1)} %bitcast.34, bf16[2048,128]{1,0:T(8,128)(2,1)S(1)} %bitcast.38, bf16[64,2048]{1,0:T(8,128)(2,1)S(1)} %sight.1.sight_ref), custom_call_target="tpu_custom_call" | custom-call | flops 536870912 | bytes 1048576 | tf_op jit(solution)/shard_map/attend/pallas_call | solution.py:164
  24.7 4.3 %collective-permute-done.5.refs_3_ = bf16[32,1152]{1,0:T(8,128)(2,1)S(1)} collective-permute-done((bf16[32,1152]{1,0:T(8,128)(2,1)S(1)}, bf16[32,1152]{1,0:T(8,128)(2,1)S(1)}, u32[]{:S(2)}, u32[]{:S(2)}) %collective-permute-start.5) | collective-permute-done | bytes 73760 | tf_op jit(solution)/shard_map/ppermute | solution.py:64
  29.0 2.2 %copy-done.1 = bf16[1,1024,2048]{2,1,0:T(8,128)(2,1)S(1)} copy-done((bf16[1,1024,2048]{2,1,0:T(8,128)(2,1)S(1)}, bf16[1,1024,2048]{2,1,0:T(8,128)(2,1)}, u32[]{:S(2)}) %copy-start.1) | copy-done | bytes 4194328
  34.7 1.8 %collective-permute-done.6.refs_1_ = bf16[32,512]{1,0:T(8,128)(2,1)S(1)} collective-permute-done((bf16[32,512]{1,0:T(8,128)(2,1)S(1)}, bf16[32,512]{1,0:T(8,128)(2,1)S(1)}, u32[]{:S(2)}, u32[]{:S(2)}) %collective-permute-start.6) | collective-permute-done | bytes 32800 | tf_op jit(solution)/shard_map/ppermute | solution.py:64
  37.3 4.1 %collective-permute-start.9 = (bf16[32,640]{1,0:T(8,128)(2,1)S(1)}, bf16[32,640]{1,0:T(8,128)(2,1)S(1)}, u32[]{:S(2)}, u32[]{:S(2)}) collective-permute-start(bf16[32,640]{1,0:T(8,128)(2,1)S(1)} %get-tuple-element.24.refs_0_), channel_id=1, source_target_pairs={{0,4},{4,0},{8,12},{12,8},{1,5},{5,1},{9,13},{13,9},{2,6},{6,2},{1... | collective-permute-start | bytes 122888 | tf_op jit(solution)/shard_map/ppermute | solution.py:64
  44.2 8.1 %copy-done = bf16[16,512,1536]{2,1,0:T(8,128)(2,1)S(1)} copy-done((bf16[16,512,1536]{2,1,0:T(8,128)(2,1)S(1)}, bf16[16,512,1536]{2,1,0:T(8,128)(2,1)}, u32[]{:S(2)}) %copy-start) | copy-done | bytes 25165848
  52.3 2.1 %gate_up.2 = bf16[128,1664]{1,0:T(8,128)(2,1)S(1)} custom-call(s32[13]{0:T(128)S(1)} %stack.55.plan_ref, bf16[4,128,640]{2,1,0:T(8,128)(2,1)S(1)} %pick.1.picked_ref, bf16[16,512,1536]{2,1,0:T(8,128)(2,1)S(1)} %copy-done), custom_call_target="tpu_custom_call" | custom-call | flops 201326592 | bytes 6291456 | tf_op jit(solution)/shard_map/gate_up/pallas_call | solution.py:350
  54.4 2.1 %gate_up.3 = bf16[128,1664]{1,0:T(8,128)(2,1)S(1)} custom-call(s32[13]{0:T(128)S(1)} %stack.55.plan_ref, bf16[4,128,640]{2,1,0:T(8,128)(2,1)S(1)} %pick.1.picked_ref, bf16[16,512,1536]{2,1,0:T(8,128)(2,1)S(1)} %copy-done), custom_call_target="tpu_custom_call" | custom-call | flops 201326592 | bytes 6291456 | tf_op jit(solution)/shard_map/gate_up/pallas_call | solution.py:350
  57.0 2.1 %gate_up_sum.2 = bf16[128,1664]{1,0:T(8,128)(2,1)S(1)} custom-call(s32[13]{0:T(128)S(1)} %stack.55.plan_ref, bf16[4,128,640]{2,1,0:T(8,128)(2,1)S(1)} %pick.1.picked_ref, bf16[16,512,1536]{2,1,0:T(8,128)(2,1)S(1)} %copy-done, bf16[128,1664]{1,0:T(8,128)(2,1)S(1)} %collective-permute-done.12.rest_0_), custom_call_target="tpu_custom_call" | custom-call | flops 201326592 | bytes 6291456 | tf_op jit(solution)/shard_map/gate_up_sum/pallas_call | solution.py:350
  60.3 2.1 %gate_up_sum.3.refs_1_ = bf16[128,1664]{1,0:T(8,128)(2,1)S(1)} custom-call(s32[13]{0:T(128)S(1)} %stack.55.plan_ref, bf16[4,128,640]{2,1,0:T(8,128)(2,1)S(1)} %pick.1.picked_ref, bf16[16,512,1536]{2,1,0:T(8,128)(2,1)S(1)} %copy-done, bf16[128,1664]{1,0:T(8,128)(2,1)S(1)} %collective-permute-done.14.rest_0_), custom_call_target="tpu_custom_call" | custom-call | flops 201326592 | bytes 6291456 | tf_op jit(solution)/shard_map/gate_up_sum/pallas_call | solution.py:350
  62.4 8.5 %collective-permute-done.13.refs_0_ = bf16[128,1664]{1,0:T(8,128)(2,1)S(1)} collective-permute-done((bf16[128,1664]{1,0:T(8,128)(2,1)S(1)}, bf16[128,1664]{1,0:T(8,128)(2,1)S(1)}, u32[]{:S(2)}, u32[]{:S(2)}) %collective-permute-start.13) | collective-permute-done | bytes 426016 | tf_op jit(solution)/shard_map/ppermute | solution.py:64
  72.5 4.8 %collective-permute-done.15.hidden_ref = bf16[128,768]{1,0:T(8,128)(2,1)S(1)} collective-permute-done((bf16[128,768]{1,0:T(8,128)(2,1)S(1)}, bf16[128,768]{1,0:T(8,128)(2,1)S(1)}, u32[]{:S(2)}, u32[]{:S(2)}) %collective-permute-start.15) | collective-permute-done | bytes 196640 | tf_op jit(solution)/shard_map/ppermute | solution.py:64
  77.3 1.8 %down.4.refs_0_ = f32[128,512]{1,0:T(8,128)S(1)} custom-call(s32[13]{0:T(128)S(1)} %stack.55.plan_ref, bf16[128,768]{1,0:T(8,128)(2,1)S(1)} %hidden.1.hidden_ref, bf16[16,768,512]{2,1,0:T(8,128)(2,1)S(1)} %bitcast.23, bf16[4,128,128]{2,1,0:T(8,128)(2,1)S(1)} %get-tuple-element.25.high_ref, bf16[4,128,128]{2,1,0:T(8,128)(2,1)S(1)} %get-tuple-element.26.low_ref), custom_call_target="tpu_custom_call" | custom-call | flops 100663296 | bytes 3145728 | tf_op jit(solution)/shard_map/down/pallas_call | solution.py:435
  79.1 1.8 %down.5.refs_0_ = f32[128,512]{1,0:T(8,128)S(1)} custom-call(s32[13]{0:T(128)S(1)} %stack.55.plan_ref, bf16[128,768]{1,0:T(8,128)(2,1)S(1)} %collective-permute-done.17.hidden_ref, bf16[16,768,512]{2,1,0:T(8,128)(2,1)S(1)} %bitcast.23, bf16[4,128,128]{2,1,0:T(8,128)(2,1)S(1)} %get-tuple-element.25.high_ref, ...), custom_call_target="tpu_custom_call" | custom-call | flops 100663296 | bytes 3145728 | tf_op jit(solution)/shard_map/down/pallas_call | solution.py:435
  80.9 1.8 %down.6.refs_0_ = f32[128,512]{1,0:T(8,128)S(1)} custom-call(s32[13]{0:T(128)S(1)} %stack.55.plan_ref, bf16[128,768]{1,0:T(8,128)(2,1)S(1)} %collective-permute-done.15.hidden_ref, bf16[16,768,512]{2,1,0:T(8,128)(2,1)S(1)} %bitcast.23, bf16[4,128,128]{2,1,0:T(8,128)(2,1)S(1)} %get-tuple-element.25.high_ref, ...), custom_call_target="tpu_custom_call" | custom-call | flops 100663296 | bytes 3145728 | tf_op jit(solution)/shard_map/down/pallas_call | solution.py:435
  82.7 1.8 %down.7 = (bf16[32,512]{1,0:T(8,128)(2,1)S(1)}, bf16[32,512]{1,0:T(8,128)(2,1)S(1)}, bf16[32,512]{1,0:T(8,128)(2,1)S(1)}, bf16[32,512]{1,0:T(8,128)(2,1)S(1)}) custom-call(s32[13]{0:T(128)S(1)} %stack.55.plan_ref, bf16[128,768]{1,0:T(8,128)(2,1)S(1)} %collective-permute-done.16.hidden_ref, bf16[16,768,512]{2,1,0:T(8,128)(2,1)S(1)} %bitcast.23, ...), custom_call_target="tpu_custom_call" | custom-call | flops 100663296 | bytes 3145728 | tf_op jit(solution)/shard_map/down/pallas_call | solution.py:435
  84.5 2.0 %collective-permute-start.18 = (bf16[32,512]{1,0:T(8,128)(2,1)S(1)}, bf16[32,512]{1,0:T(8,128)(2,1)S(1)}, u32[]{:S(2)}, u32[]{:S(2)}) collective-permute-start(bf16[32,512]{1,0:T(8,128)(2,1)S(1)} %get-tuple-element.28), channel_id=1, source_target_pairs={{0,12},{4,8},{8,4},{12,0},{1,13},{5,9},{9,5},{13,1},{2,14},{6,10},... | collective-permute-start | bytes 98312 | tf_op jit(solution)/shard_map/ppermute | solution.py:64
  88.9 1.7 %collective-permute-done.18.refs_1_ = bf16[32,512]{1,0:T(8,128)(2,1)S(1)} collective-permute-done((bf16[32,512]{1,0:T(8,128)(2,1)S(1)}, bf16[32,512]{1,0:T(8,128)(2,1)S(1)}, u32[]{:S(2)}, u32[]{:S(2)}) %collective-permute-start.18) | collective-permute-done | bytes 32800 | tf_op jit(solution)/shard_map/ppermute | solution.py:64
  (71 shorter events, 23.1 us)
Async XLA Ops:
  0.0 34.7 %copy-start.11 = (bf16[512]{0:T(512)(128)(2,1)S(1)}, bf16[512]{0:T(512)(128)(2,1)}, u32[]{:S(2)}) copy-start(bf16[512]{0:T(512)(128)(2,1)} %param.21) | copy-start | bytes 3076
  2.9 34.0 %copy-start.3 = (bf16[32,512]{1,0:T(8,128)(2,1)S(1)}, bf16[32,512]{1,0:T(8,128)(2,1)}, u32[]{:S(2)}) copy-start(bf16[32,512]{1,0:T(8,128)(2,1)} %residual_ref.1) | copy-start | bytes 98308
  3.1 7.7 %collective-permute-start = (bf16[32,1152]{1,0:T(8,128)(2,1)S(1)}, bf16[32,1152]{1,0:T(8,128)(2,1)S(1)}, u32[]{:S(2)}, u32[]{:S(2)}) collective-permute-start(bf16[32,1152]{1,0:T(8,128)(2,1)S(1)} %pack.1.queries_ref.refs_0_), channel_id=1, source_target_pairs={{0,4},{4,0},{8,12},{12,8},{1,5},{5,1},{9,13},{13,9},{2,6},{6,2},{1... | collective-permute-start | bytes 221192 | tf_op jit(solution)/shard_map/ppermute | solution.py:64
  6.1 9.5 %collective-permute-start.2 = (bf16[32,1152]{1,0:T(8,128)(2,1)S(1)}, bf16[32,1152]{1,0:T(8,128)(2,1)S(1)}, u32[]{:S(2)}, u32[]{:S(2)}) collective-permute-start(bf16[32,1152]{1,0:T(8,128)(2,1)S(1)} %pack.1.queries_ref.refs_0_), channel_id=1, source_target_pairs={{0,8},{4,12},{8,0},{12,4},{1,9},{5,13},{9,1},{13,5},{2,10},{6,14},... | collective-permute-start | bytes 221192 | tf_op jit(solution)/shard_map/ppermute | solution.py:64
  8.7 12.3 %collective-permute-start.4 = (bf16[32,1152]{1,0:T(8,128)(2,1)S(1)}, bf16[32,1152]{1,0:T(8,128)(2,1)S(1)}, u32[]{:S(2)}, u32[]{:S(2)}) collective-permute-start(bf16[32,1152]{1,0:T(8,128)(2,1)S(1)} %pack.1.queries_ref.refs_0_), channel_id=1, source_target_pairs={{0,12},{4,8},{8,4},{12,0},{1,13},{5,9},{9,5},{13,1},{2,14},{6,10},... | collective-permute-start | bytes 221192 | tf_op jit(solution)/shard_map/ppermute | solution.py:64
  14.7 10.0 %collective-permute-start.1 = (bf16[32,1152]{1,0:T(8,128)(2,1)S(1)}, bf16[32,1152]{1,0:T(8,128)(2,1)S(1)}, u32[]{:S(2)}, u32[]{:S(2)}) collective-permute-start(bf16[32,1152]{1,0:T(8,128)(2,1)S(1)} %attend.5), channel_id=1, source_target_pairs={{0,4},{4,0},{8,12},{12,8},{1,5},{5,1},{9,13},{13,9},{2,6},{6,2},{1... | collective-permute-start | bytes 221192 | tf_op jit(solution)/shard_map/ppermute | solution.py:64
  17.5 7.3 %collective-permute-start.3 = (bf16[32,1152]{1,0:T(8,128)(2,1)S(1)}, bf16[32,1152]{1,0:T(8,128)(2,1)S(1)}, u32[]{:S(2)}, u32[]{:S(2)}) collective-permute-start(bf16[32,1152]{1,0:T(8,128)(2,1)S(1)} %attend.6), channel_id=1, source_target_pairs={{0,8},{4,12},{8,0},{12,4},{1,9},{5,13},{9,1},{13,5},{2,10},{6,14},... | collective-permute-start | bytes 221192 | tf_op jit(solution)/shard_map/ppermute | solution.py:64
  22.8 6.2 %collective-permute-start.5 = (bf16[32,1152]{1,0:T(8,128)(2,1)S(1)}, bf16[32,1152]{1,0:T(8,128)(2,1)S(1)}, u32[]{:S(2)}, u32[]{:S(2)}) collective-permute-start(bf16[32,1152]{1,0:T(8,128)(2,1)S(1)} %attend.7), channel_id=1, source_target_pairs={{0,12},{4,8},{8,4},{12,0},{1,13},{5,9},{9,5},{13,1},{2,14},{6,10},... | collective-permute-start | bytes 221192 | tf_op jit(solution)/shard_map/ppermute | solution.py:64
  32.8 3.7 %collective-permute-start.6 = (bf16[32,512]{1,0:T(8,128)(2,1)S(1)}, bf16[32,512]{1,0:T(8,128)(2,1)S(1)}, u32[]{:S(2)}, u32[]{:S(2)}) collective-permute-start(bf16[32,512]{1,0:T(8,128)(2,1)S(1)} %get-tuple-element.19), channel_id=1, source_target_pairs={{0,3},{1,2},{2,1},{3,0},{4,7},{5,6},{6,5},{7,4},{8,11},{9,10},{10,... | collective-permute-start | bytes 98312 | tf_op jit(solution)/shard_map/ppermute | solution.py:64
  32.8 4.0 %collective-permute-start.7 = (bf16[32,512]{1,0:T(8,128)(2,1)S(1)}, bf16[32,512]{1,0:T(8,128)(2,1)S(1)}, u32[]{:S(2)}, u32[]{:S(2)}) collective-permute-start(bf16[32,512]{1,0:T(8,128)(2,1)S(1)} %get-tuple-element.20), channel_id=1, source_target_pairs={{0,2},{1,3},{2,0},{3,1},{4,6},{5,7},{6,4},{7,5},{8,10},{9,11},{10,... | collective-permute-start | bytes 98312 | tf_op jit(solution)/shard_map/ppermute | solution.py:64
  34.4 2.5 %collective-permute-start.8 = (bf16[32,512]{1,0:T(8,128)(2,1)S(1)}, bf16[32,512]{1,0:T(8,128)(2,1)S(1)}, u32[]{:S(2)}, u32[]{:S(2)}) collective-permute-start(bf16[32,512]{1,0:T(8,128)(2,1)S(1)} %get-tuple-element.21), channel_id=1, source_target_pairs={{0,1},{1,0},{2,3},{3,2},{4,5},{5,4},{6,7},{7,6},{8,9},{9,8},{10,11... | collective-permute-start | bytes 98312 | tf_op jit(solution)/shard_map/ppermute | solution.py:64
  37.0 6.3 %collective-permute-start.11 = (bf16[32,640]{1,0:T(8,128)(2,1)S(1)}, bf16[32,640]{1,0:T(8,128)(2,1)S(1)}, u32[]{:S(2)}, u32[]{:S(2)}) collective-permute-start(bf16[32,640]{1,0:T(8,128)(2,1)S(1)} %get-tuple-element.24.refs_0_), channel_id=1, source_target_pairs={{0,12},{4,8},{8,4},{12,0},{1,13},{5,9},{9,5},{13,1},{2,14},{6,10},... | collective-permute-start | bytes 122888 | tf_op jit(solution)/shard_map/ppermute | solution.py:64
  37.1 6.3 %collective-permute-start.10 = (bf16[32,640]{1,0:T(8,128)(2,1)S(1)}, bf16[32,640]{1,0:T(8,128)(2,1)S(1)}, u32[]{:S(2)}, u32[]{:S(2)}) collective-permute-start(bf16[32,640]{1,0:T(8,128)(2,1)S(1)} %get-tuple-element.24.refs_0_), channel_id=1, source_target_pairs={{0,8},{4,12},{8,0},{12,4},{1,9},{5,13},{9,1},{13,5},{2,10},{6,14},... | collective-permute-start | bytes 122888 | tf_op jit(solution)/shard_map/ppermute | solution.py:64
  37.3 6.5 %collective-permute-start.9 = (bf16[32,640]{1,0:T(8,128)(2,1)S(1)}, bf16[32,640]{1,0:T(8,128)(2,1)S(1)}, u32[]{:S(2)}, u32[]{:S(2)}) collective-permute-start(bf16[32,640]{1,0:T(8,128)(2,1)S(1)} %get-tuple-element.24.refs_0_), channel_id=1, source_target_pairs={{0,4},{4,0},{8,12},{12,8},{1,5},{5,1},{9,13},{13,9},{2,6},{6,2},{1... | collective-permute-start | bytes 122888 | tf_op jit(solution)/shard_map/ppermute | solution.py:64
  54.4 2.6 %collective-permute-start.12 = (bf16[128,1664]{1,0:T(8,128)(2,1)S(1)}, bf16[128,1664]{1,0:T(8,128)(2,1)S(1)}, u32[]{:S(2)}, u32[]{:S(2)}) collective-permute-start(bf16[128,1664]{1,0:T(8,128)(2,1)S(1)} %gate_up.2), channel_id=1, source_target_pairs={{0,1},{1,0},{2,3},{3,2},{4,5},{5,4},{6,7},{7,6},{8,9},{9,8},{10,11... | collective-permute-start | bytes 1277960 | tf_op jit(solution)/shard_map/ppermute | solution.py:64
  56.5 3.8 %collective-permute-start.14 = (bf16[128,1664]{1,0:T(8,128)(2,1)S(1)}, bf16[128,1664]{1,0:T(8,128)(2,1)S(1)}, u32[]{:S(2)}, u32[]{:S(2)}) collective-permute-start(bf16[128,1664]{1,0:T(8,128)(2,1)S(1)} %gate_up.3), channel_id=1, source_target_pairs={{0,1},{1,0},{2,3},{3,2},{4,5},{5,4},{6,7},{7,6},{8,9},{9,8},{10,11... | collective-permute-start | bytes 1277960 | tf_op jit(solution)/shard_map/ppermute | solution.py:64
  57.0 20.3 %slice-start.1 = ((s8[12582912]{0:T(1024)(128)(4,1)}), s8[4194304]{0:T(1024)(128)(4,1)S(1)}, s32[]{:S(2)}) async-start(s8[12582912]{0:T(1024)(128)(4,1)} %bitcast.22), calls=%async_computation.1 | async-start | bytes 8388608
  59.1 11.8 %collective-permute-start.13 = (bf16[128,1664]{1,0:T(8,128)(2,1)S(1)}, bf16[128,1664]{1,0:T(8,128)(2,1)S(1)}, u32[]{:S(2)}, u32[]{:S(2)}) collective-permute-start(bf16[128,1664]{1,0:T(8,128)(2,1)S(1)} %gate_up_sum.2), channel_id=1, source_target_pairs={{0,2},{2,0},{1,3},{3,1},{4,6},{6,4},{5,7},{7,5},{8,10},{10,8},{9,1... | collective-permute-start | bytes 1277960 | tf_op jit(solution)/shard_map/ppermute | solution.py:64
  71.2 6.1 %collective-permute-start.15 = (bf16[128,768]{1,0:T(8,128)(2,1)S(1)}, bf16[128,768]{1,0:T(8,128)(2,1)S(1)}, u32[]{:S(2)}, u32[]{:S(2)}) collective-permute-start(bf16[128,768]{1,0:T(8,128)(2,1)S(1)} %hidden.1.hidden_ref), channel_id=1, source_target_pairs={{0,2},{2,0},{1,3},{3,1},{4,6},{6,4},{5,7},{7,5},{8,10},{10,8},{9,1... | collective-permute-start | bytes 589832 | tf_op jit(solution)/shard_map/ppermute | solution.py:64
  72.5 6.6 %collective-permute-start.17 = (bf16[128,768]{1,0:T(8,128)(2,1)S(1)}, bf16[128,768]{1,0:T(8,128)(2,1)S(1)}, u32[]{:S(2)}, u32[]{:S(2)}) collective-permute-start(bf16[128,768]{1,0:T(8,128)(2,1)S(1)} %hidden.1.hidden_ref), channel_id=1, source_target_pairs={{0,1},{1,0},{2,3},{3,2},{4,5},{5,4},{6,7},{7,6},{8,9},{9,8},{10,11... | collective-permute-start | bytes 589832 | tf_op jit(solution)/shard_map/ppermute | solution.py:64
  77.3 5.4 %collective-permute-start.16 = (bf16[128,768]{1,0:T(8,128)(2,1)S(1)}, bf16[128,768]{1,0:T(8,128)(2,1)S(1)}, u32[]{:S(2)}, u32[]{:S(2)}) collective-permute-start(bf16[128,768]{1,0:T(8,128)(2,1)S(1)} %collective-permute-done.15.hidden_ref), channel_id=1, source_target_pairs={{0,1},{1,0},{2,3},{3,2},{4,5},{5,4},{6,7},{7,6},{8,9},{9,8},{10,11... | collective-permute-start | bytes 589832 | tf_op jit(solution)/shard_map/ppermute | solution.py:64
  84.5 6.1 %collective-permute-start.18 = (bf16[32,512]{1,0:T(8,128)(2,1)S(1)}, bf16[32,512]{1,0:T(8,128)(2,1)S(1)}, u32[]{:S(2)}, u32[]{:S(2)}) collective-permute-start(bf16[32,512]{1,0:T(8,128)(2,1)S(1)} %get-tuple-element.28), channel_id=1, source_target_pairs={{0,12},{4,8},{8,4},{12,0},{1,13},{5,9},{9,5},{13,1},{2,14},{6,10},... | collective-permute-start | bytes 98312 | tf_op jit(solution)/shard_map/ppermute | solution.py:64
  86.5 5.2 %collective-permute-start.19 = (bf16[32,512]{1,0:T(8,128)(2,1)S(1)}, bf16[32,512]{1,0:T(8,128)(2,1)S(1)}, u32[]{:S(2)}, u32[]{:S(2)}) collective-permute-start(bf16[32,512]{1,0:T(8,128)(2,1)S(1)} %get-tuple-element.29), channel_id=1, source_target_pairs={{0,8},{4,12},{8,0},{12,4},{1,9},{5,13},{9,1},{13,5},{2,10},{6,14},... | collective-permute-start | bytes 98312 | tf_op jit(solution)/shard_map/ppermute | solution.py:64
  87.6 4.3 %collective-permute-start.20 = (bf16[32,512]{1,0:T(8,128)(2,1)S(1)}, bf16[32,512]{1,0:T(8,128)(2,1)S(1)}, u32[]{:S(2)}, u32[]{:S(2)}) collective-permute-start(bf16[32,512]{1,0:T(8,128)(2,1)S(1)} %get-tuple-element.30), channel_id=1, source_target_pairs={{0,4},{4,0},{8,12},{12,8},{1,5},{5,1},{9,13},{13,9},{2,6},{6,2},{1... | collective-permute-start | bytes 98312 | tf_op jit(solution)/shard_map/ppermute | solution.py:64
  (12 other events, 55.2 us)

commit v3 on v2

--- a/solution.py
+++ b/solution.py
@@ -37,6 +37,14 @@
     return pl.BlockSpec(memory_space=memory_space)
 
 
+def in_hbm(values):
+    return [pltpu.with_memory_space_constraint(value, pltpu.HBM) for value in values]
+
+
+def in_vmem(value):
+    return pltpu.with_memory_space_constraint(value, pltpu.VMEM)
+
+
 def lane_ids(shape):
     return lax.broadcasted_iota(jnp.int32, shape, len(shape) - 1)
 
@@ -68,60 +76,114 @@
     return list(range(count - 1, 0, -1))
 
 
-def pack_kernel(width, queries_ref, seg_ref, ids_ref, weight_ref, out_ref):
-    rows = out_ref.shape[0]
+def pack_kernel(
+    queries_ref, seg_ref, ids_ref, weight_ref, out_ref, seg_here, ids_here, weight_here, done
+):
+    rows, width = queries_ref.shape
     choices = ids_ref.shape[0]
-    out_ref[:, :width] = queries_ref[...]
+    copies = [
+        pltpu.make_async_copy(source, target, done.at[i])
+        for i, (source, target) in enumerate(
+            [
+                (seg_ref, seg_here),
+                (ids_ref, ids_here),
+                (weight_ref, weight_here),
+                (queries_ref, out_ref.at[:, :width]),
+            ]
+        )
+    ]
+    for copy in copies:
+        copy.start()
     shape = (choices, LANES)
 
     def placed(value, first, last):
         to_lane = (lane_ids(shape) == row_ids(shape) + first) & (row_ids(shape) <= last)
         return dot(value.astype(bf16), as_bf16(to_lane), ((0,), (0,)))
 
-    segs = jnp.broadcast_to(seg_ref[...], (choices, rows)).astype(f32)
-    high, low = in_two(weight_ref[...])
-    info = placed(segs, 0, 0) + placed(ids_ref[...].astype(f32), 1, choices)
+    for copy in copies[:3]:
+        copy.wait()
+    segs = jnp.broadcast_to(seg_here[...], (choices, rows)).astype(f32)
+    high, low = in_two(weight_here[...])
+    info = placed(segs, 0, 0) + placed(ids_here[...].astype(f32), 1, choices)
     info = info + placed(high, 1 + choices, choices) + placed(low, 1 + 2 * choices, choices)
     out_ref[:, width:] = info.astype(bf16)
+    copies[3].wait()
 
 
 def pack(queries, query_seg, expert_ids, route_weight):
     rows, width = queries.shape
-    return pl.pallas_call(
-        functools.partial(pack_kernel, width),
+    small = [query_seg[None, :], expert_ids.T, route_weight.T]
+    return pl.pallas_call(
+        pack_kernel,
+        in_specs=[whole(pltpu.HBM)] * 4,
         out_shape=jax.ShapeDtypeStruct((rows, width + LANES), bf16),
+        scratch_shapes=[pltpu.VMEM(value.shape, value.dtype) for value in small]
+        + [pltpu.SemaphoreType.DMA((4,))],
         compiler_params=params(4),
         name="pack",
-    )(queries, query_seg[None, :], expert_ids.T, route_weight.T)
-
-
-def sight_kernel(parent_ref, key_seg_ref, sight_ref):
+    )(*in_hbm([queries] + small))
+
+
+def sight_kernel(load_count, parent_ref, key_seg_ref, *refs):
+    sources, sight_ref = refs[:load_count], refs[load_count]
+    targets = refs[load_count + 1 : 2 * load_count + 1]
+    parent_here, key_seg_here, done = refs[2 * load_count + 1 :]
+    copies = [
+        pltpu.make_async_copy(source, target, done.at[i])
+        for i, (source, target) in enumerate(
+            zip((parent_ref, key_seg_ref) + sources, (parent_here, key_seg_here) + targets)
+        )
+    ]
+    for copy in copies:
+        copy.start()
+    for copy in copies[:2]:
+        copy.wait()
     seg_count, key_count = sight_ref.shape
     square = (seg_count, seg_count)
     same = row_ids(square) == lane_ids(square)
-    one = as_bf16((parent_ref[...] == row_ids(square)) | same)
+    one = as_bf16((parent_here[...] == row_ids(square)) | same)
     two = as_bf16(dot(one, one) > 0.5)
     four = as_bf16(dot(two, two) > 0.5)
     six = as_bf16(dot(four, two) > 0.5)
-    keys = as_bf16(key_seg_ref[...] == row_ids((seg_count, key_count)))
+    keys = as_bf16(key_seg_here[...] == row_ids((seg_count, key_count)))
     sight_ref[...] = dot(six, keys, ((0,), (0,))).astype(bf16)
-
-
-def sight_of(parent, key_seg):
+    for copy in copies[2:]:
+        copy.wait()
+
+
+def sight_of(parent, key_seg, loaded):
     assert DEPTH == 6
-    return pl.pallas_call(
-        sight_kernel,
-        out_shape=jax.ShapeDtypeStruct((parent.shape[0], key_seg.shape[0]), bf16),
+    small = [parent[None, :], key_seg[None, :]]
+    shapes = [pltpu.VMEM(value.shape, value.dtype) for value in loaded]
+    return pl.pallas_call(
+        functools.partial(sight_kernel, len(loaded)),
+        in_specs=[whole(pltpu.HBM)] * (2 + len(loaded)),
+        out_specs=[whole()] * (1 + len(loaded)),
+        out_shape=[jax.ShapeDtypeStruct((parent.shape[0], key_seg.shape[0]), bf16)] + shapes,
+        scratch_shapes=[pltpu.VMEM(value.shape, value.dtype) for value in small]
+        + [pltpu.SemaphoreType.DMA((2 + len(loaded),))],
         compiler_params=params(4),
-        cost_estimate=cost(2**24, 2**19),
+        cost_estimate=cost(2**24, 2**23),
         name="sight",
-    )(parent[None, :], key_seg[None, :])
+    )(*in_hbm(small + loaded))
 
 
 def attend_kernel(
-    heads, scale, lead_at, plan_ref, queries_ref, keys_ref, values_ref, sight_ref, out_ref,
-    stacked_ref, probs_ref,
+    heads, scale, lead_at, loads, plan_ref, queries_ref, keys_ref, values_ref, sight_ref,
+    weight_ref, out_ref, *refs,
 ):
+    loaded_refs, (stacked_ref, probs_ref, done) = refs[: len(loads)], refs[len(loads) :]
+    copies = []
+    for target, (expert_at, spread) in zip(loaded_refs, loads):
+        for i in range(target.shape[0]):
+            expert = plan_ref[expert_at] // spread + i
+            copies.append(
+                pltpu.make_async_copy(
+                    weight_ref.at[expert], target.at[i], done.at[len(copies)]
+                )
+            )
+    for copy in copies:
+        copy.start()
     rows = queries_ref.shape[0]
     key_count, head_size = keys_ref.shape
     seg_count = sight_ref.shape[0]
@@ -155,24 +217,32 @@
     for head in range(heads):
         columns = slice(head * head_size, (head + 1) * head_size)
         out_ref[:, columns] = sums[head * rows : (head + 1) * rows, :].astype(bf16)
-
-
-def attend(plan, lead_at, queries, keys, values, sight, heads, scale):
+    for copy in copies:
+        copy.wait()
+
+
+def attend(plan, lead_at, queries, keys, values, sight, heads, scale, weight, loads, experts, spread):
     rows, columns = queries.shape
     key_count, head_size = keys.shape
     work = rows * heads * key_count
-    return pl.pallas_call(
-        functools.partial(attend_kernel, heads, scale, lead_at),
-        in_specs=[whole(pltpu.SMEM)] + [whole()] * 4,
-        out_shape=jax.ShapeDtypeStruct((rows, columns), bf16),
+    held = pltpu.VMEM((experts,) + weight.shape[1:], weight.dtype)
+    part, *loaded = pl.pallas_call(
+        functools.partial(
+            attend_kernel, heads, scale, lead_at, [(load, spread) for load in loads]
+        ),
+        in_specs=[whole(pltpu.SMEM)] + [whole()] * 4 + [whole(pltpu.HBM)],
+        out_specs=[whole()] * (1 + len(loads)),
+        out_shape=[jax.ShapeDtypeStruct((rows, columns), bf16)] + [held] * len(loads),
         scratch_shapes=[
             pltpu.VMEM((rows * heads, head_size), bf16),
             pltpu.VMEM((rows * heads, key_count), bf16),
+            pltpu.SemaphoreType.DMA((max(1, len(loads) * experts),)),
         ],
-        compiler_params=params(12),
+        compiler_params=params(8),
         cost_estimate=cost(8 * work * head_size, 2**20, work),
         name="attend",
-    )(plan, queries, keys, values, sight)
+    )(plan, queries, in_vmem(keys), in_vmem(values), sight, *in_hbm([weight]))
+    return part, loaded
 
 
 def project_kernel(heads, scale, order_at, source_count, plan_ref, *refs):
@@ -213,7 +283,7 @@
         compiler_params=params(8),
         cost_estimate=cost(2 * rows * width * model_width, 2 * width * model_width),
         name="project",
-    )(plan, *parts, weight)
+    )(plan, *parts, in_vmem(weight))
 
 
 def mix_kernel(residual_ref, gain_ref, *refs):
@@ -309,57 +379,57 @@
     )(place, *rows)
 
 
-def gate_up_kernel(plan_ref, picked_ref, weight_ref, *rest):
+def squares_joined(squares):
+    high, low = in_two(squares[:, :1] + squares[:, 1:2])
+    lane = lane_ids(squares.shape)
+    return jnp.where(lane == 0, high, jnp.where(lane == 1, low, 0.0))
+
+
+def gate_up_kernel(piece_at, plan_ref, picked_ref, weight_ref, *rest):
     added_refs, out_ref = rest[:-1], rest[-1]
-    _, width, ff_pair = weight_ref.shape
-    picked = picked_ref[0]
-    product = dot(picked[:, :width], weight_ref[0])
-    squares = picked[:, width:].astype(f32)
-    for ref in added_refs:
-        product = product + ref[:, :ff_pair].astype(f32)
-        squares = squares + ref[:, ff_pair:].astype(f32)
-        high, low = in_two(squares[:, :1] + squares[:, 1:2])
-        lane = lane_ids(squares.shape)
-        squares = jnp.where(lane == 0, high, jnp.where(lane == 1, low, 0.0))
+    experts, width, ff_pair = weight_ref.shape
+    rows = out_ref.shape[0] // experts
+    piece = plan_ref[piece_at]
+    for i in range(experts):
+        here = slice(i * rows, (i + 1) * rows)
+        picked = picked_ref[piece, here, :]
+        product = dot(picked[:, :width], weight_ref[i])
+        squares = picked[:, width:].astype(f32)
+        for ref in added_refs:
+            product = product + ref[here, :ff_pair].astype(f32)
+            squares = squares_joined(squares + ref[here, ff_pair:].astype(f32))
+        out_ref[here, :ff_pair] = product.astype(bf16)
+        out_ref[here, ff_pair:] = squares.astype(bf16)
+
+
+def gate_up(plan, piece_at, picked, weight, added=()):
+    slots = picked.shape[1]
+    experts, width, ff_pair = weight.shape
+    return pl.pallas_call(
+        functools.partial(gate_up_kernel, piece_at),
+        in_specs=[whole(pltpu.SMEM)] + [whole()] * (2 + len(added)),
+        out_shape=jax.ShapeDtypeStruct((slots, ff_pair + LANES), bf16),
+        compiler_params=params(8),
+        cost_estimate=cost(slots * width * ff_pair // 8, experts * width * ff_pair // 8),
+        name="gate_up_sum" if added else "gate_up",
+    )(plan, picked, in_vmem(weight), *added)
+
+
+def join_kernel(left_ref, right_ref, out_ref):
+    ff_pair = out_ref.shape[1] - LANES
+    product = left_ref[:, :ff_pair].astype(f32) + right_ref[:, :ff_pair].astype(f32)
     out_ref[:, :ff_pair] = product.astype(bf16)
-    out_ref[:, ff_pair:] = squares.astype(bf16)
-
-
-def gate_up(plan, piece_at, picked, weight, added=None):
-    piece_count, slots, picked_columns = picked.shape
-    local_experts, width, ff_pair = weight.shape
-    capacity = piece_count * slots // local_experts
-    steps = max(1, slots // capacity)
-    per_step = slots // steps
-    columns = ff_pair + LANES
-
-    def weight_block(step, plan_ref):
-        return (plan_ref[piece_at] * slots // capacity + step, 0, 0)
-
-    in_specs = [
-        pl.BlockSpec(
-            (1, per_step, picked_columns),
-            lambda step, plan_ref: (plan_ref[piece_at], step, 0),
-        ),
-        pl.BlockSpec((1, width, ff_pair), weight_block),
-    ]
-    operands = [picked, weight]
-    if added is not None:
-        in_specs.append(pl.BlockSpec((per_step, columns), lambda step, plan_ref: (step, 0)))
-        operands.append(added)
-    return pl.pallas_call(
-        gate_up_kernel,
-        grid_spec=pltpu.PrefetchScalarGridSpec(
-            num_scalar_prefetch=1,
-            grid=(steps,),
-            in_specs=in_specs,
-            out_specs=pl.BlockSpec((per_step, columns), lambda step, plan_ref: (step, 0)),
-        ),
-        out_shape=jax.ShapeDtypeStruct((slots, columns), bf16),
-        compiler_params=params(8, 1),
-        cost_estimate=cost(2 * slots * width * ff_pair, 2 * steps * width * ff_pair),
-        name="gate_up_sum" if added is not None else "gate_up",
-    )(plan, *operands)
+    squares = left_ref[:, ff_pair:].astype(f32) + right_ref[:, ff_pair:].astype(f32)
+    out_ref[:, ff_pair:] = squares_joined(squares).astype(bf16)
+
+
+def join(left, right):
+    return pl.pallas_call(
+        join_kernel,
+        out_shape=jax.ShapeDtypeStruct(left.shape, bf16),
+        compiler_params=params(4),
+        name="join",
+    )(left, right)
 
 
 def hidden_kernel(part_count, model_width, *refs):
@@ -384,68 +454,39 @@
     )(*parts)
 
 
-def down_kernel(source_count, plan_ref, hidden_ref, weight_ref, high_ref, low_ref, *refs):
-    total_ref = refs[0] if source_count else None
-    *out_refs, held_ref = refs[source_count:]
-    step = pl.program_id(0)
-    each = hidden_ref.shape[0]
-    start = pl.multiple_of(step * each, each)
-    held_ref[pl.ds(start, each), :] = dot(hidden_ref[...], weight_ref[0]).astype(bf16)
-
-    @pl.when(step == pl.num_programs(0) - 1)
-    def combine():
-        held = held_ref[...]
-        total = dot(high_ref[0], held) + dot(low_ref[0], held)
-        if total_ref is not None:
-            total = total + total_ref[...]
-        rows = out_refs[0].shape[0]
-        for i, ref in enumerate(out_refs):
-            ref[...] = total[i * rows : (i + 1) * rows, :].astype(ref.dtype)
-
-
-def down(plan, piece_at, hidden, weight, high, low, total=None, out_count=1):
+def down(plan, piece_at, expert_at, spread, hidden, weight, high, low, total=None, out_count=1):
     slots, ff_width = hidden.shape
     piece_count, tokens, _ = high.shape
     local_experts, _, piece_width = weight.shape
-    capacity = piece_count * slots // local_experts
-    steps = max(1, slots // capacity)
-    per_step = slots // steps
+    experts = max(1, local_experts // piece_count)
+    each = slots // experts
     rows = tokens // out_count
-
-    def weight_block(step, plan_ref):
-        return (plan_ref[piece_at] * slots // capacity + step, 0, 0)
-
-    def route_block(step, plan_ref):
-        return (plan_ref[piece_at], 0, 0)
-
-    def fixed(step, plan_ref):
-        return (0, 0)
-
-    in_specs = [
-        pl.BlockSpec((per_step, ff_width), lambda step, plan_ref: (step, 0)),
-        pl.BlockSpec((1, ff_width, piece_width), weight_block),
-        pl.BlockSpec((1, tokens, slots), route_block),
-        pl.BlockSpec((1, tokens, slots), route_block),
-    ]
-    operands = [hidden, weight, high, low]
-    if total is not None:
-        in_specs.append(pl.BlockSpec((tokens, piece_width), fixed))
-        operands.append(total)
     out_type = f32 if out_count == 1 else bf16
-    return pl.pallas_call(
-        functools.partial(down_kernel, 0 if total is None else 1),
-        grid_spec=pltpu.PrefetchScalarGridSpec(
-            num_scalar_prefetch=1,
-            grid=(steps,),
-            in_specs=in_specs,
-            out_specs=[pl.BlockSpec((rows, piece_width), fixed)] * out_count,
-            scratch_shapes=[pltpu.VMEM((slots, piece_width), bf16)],
-        ),
+
+    def kernel(plan_ref, hidden_ref, weight_ref, high_ref, low_ref, *refs):
+        total_refs, out_refs, held_ref = refs[: -1 - out_count], refs[-1 - out_count : -1], refs[-1]
+        piece = plan_ref[piece_at]
+        first = plan_ref[expert_at] // spread
+        for i in range(experts):
+            here = slice(i * each, (i + 1) * each)
+            held_ref[here, :] = dot(hidden_ref[here, :], weight_ref[first + i]).astype(bf16)
+        held = held_ref[...]
+        summed = dot(high_ref[piece], held) + dot(low_ref[piece], held)
+        for ref in total_refs:
+            summed = summed + ref[...]
+        for i, ref in enumerate(out_refs):
+            ref[...] = summed[i * rows : (i + 1) * rows, :].astype(ref.dtype)
+
+    before = [] if total is None else [total]
+    return pl.pallas_call(
+        kernel,
+        in_specs=[whole(pltpu.SMEM)] + [whole()] * (4 + len(before)),
         out_shape=[jax.ShapeDtypeStruct((rows, piece_width), out_type)] * out_count,
-        compiler_params=params(8, 1),
-        cost_estimate=cost(2 * slots * ff_width * piece_width, 2 * steps * ff_width * piece_width),
+        scratch_shapes=[pltpu.VMEM((slots, piece_width), bf16)],
+        compiler_params=params(8),
+        cost_estimate=cost(2 * slots * ff_width * piece_width, 2 * experts * ff_width * piece_width),
         name="down",
-    )(plan, *operands)
+    )(plan, hidden, weight, high, low, *before)
 
 
 def finish_kernel(mixed_ref, *refs):
@@ -502,24 +543,54 @@
     slot_pieces = [
         (own_tp ^ flip) * exp_count + (own_exp ^ k) for flip in (0, 1) for k in range(exp_count)
     ]
+    capacity = ctx_count * MOST
+    experts = max(1, slots // capacity)
+    spread = max(1, capacity // slots)
     scalars = [own_ctx * local_experts] + leads + column_pieces + slot_pieces
+    scalars = scalars + [piece * experts for piece in slot_pieces]
     plan = jnp.stack([jnp.asarray(value, jnp.int32) for value in scalars])
     lead_at = 1
     order_at = lead_at + ctx_count
     mine_at = order_at + piece_count
     away_at = mine_at + exp_count
+    expert_at = piece_count
 
     packed = pack(queries.reshape(query_rows, width), query_seg, expert_ids, route_weight)
     gathered = {0: packed}
     for k in far_first(ctx_count):
         gathered[k] = swapped(packed, "ctx", k)
-    sight = sight_of(parent, key_seg)
-    keys = cached_keys.reshape(key_count, head_size)
-    values = cached_values.reshape(key_count, head_size)
-    parts = []
-    for k in range(ctx_count):
-        part = attend(plan, lead_at + k, gathered[k], keys, values, sight, heads, scale)
-        parts.append(swapped(part, "ctx", k) if k else part)
+    sight, keys, values, out_matrix = sight_of(
+        parent,
+        key_seg,
+        [
+            cached_keys.reshape(key_count, head_size),
+            cached_values.reshape(key_count, head_size),
+            out_weight.reshape(width, model_width),
+        ],
+    )
+    steps = far_first(exp_count) + [0]
+    wanted = [at + k for k in steps for at in (away_at, mine_at)]
+    assert ctx_count >= piece_count
+    parts = {}
+    held = {}
+    for turn, k in enumerate(list(range(1, ctx_count)) + [0]):
+        loads = wanted[turn : turn + 1]
+        part, loaded = attend(
+            plan,
+            lead_at + k,
+            gathered[k],
+            keys,
+            values,
+            sight,
+            heads,
+            scale,
+            gate_up_weight,
+            [at + expert_at for at in loads],
+            experts,
+            spread,
+        )
+        held.update(zip(loads, loaded))
+        parts[k] = swapped(part, "ctx", k) if k else part
     place, combine_high, combine_low = route(
         plan,
         0,
@@ -531,7 +602,13 @@
         slots,
     )
     projected = project(
-        plan, order_at, parts, out_weight.reshape(width, model_width), heads, scale, piece_count
+        plan,
+        order_at,
+        [parts[k] for k in range(ctx_count)],
+        out_matrix,
+        heads,
+        scale,
+        piece_count,
     )
     pieces = [projected[0]] + [
         swapped(projected[k], ("exp", "tp"), k) for k in far_first(piece_count)
@@ -543,21 +620,33 @@
     picked = pick(place, [rows[k] for k in range(ctx_count)])
 
     finals = []
-    for k in far_first(exp_count) + [0]:
-        away = gate_up(plan, away_at + k, picked, gate_up_weight)
-        summed = gate_up(plan, mine_at + k, picked, gate_up_weight, swapped(away, "tp", 1))
-        finals.append(swapped(summed, "exp", k) if k else summed)
+    for k in steps:
+        away = gate_up(plan, away_at + k, picked, held[away_at + k])
+        arrived = swapped(away, "tp", 1)
+        if k:
+            mine = gate_up(plan, mine_at + k, picked, held[mine_at + k])
+            joined = join(mine, arrived)
+            finals.append(swapped(joined, "exp", k))
+            picked, _ = lax.optimization_barrier((picked, joined))
+        else:
+            mine = gate_up(plan, mine_at, picked, held[mine_at])
+            finals, mine = lax.optimization_barrier((finals, mine))
+            finals = [arrived, mine] + finals
     own_hidden = hidden_of(finals, ff_width, model_width)
 
     total = None
     for k in range(exp_count):
-        here = swapped(own_hidden, "exp", k) if k else own_hidden
+        here = own_hidden
+        if k:
+            here, total = lax.optimization_barrier((swapped(own_hidden, "exp", k), total))
         there = swapped(here, "tp", 1)
         for piece_at, hidden in ((mine_at + k, here), (away_at + k, there)):
             ends = piece_at == away_at + exp_count - 1
             totals = down(
                 plan,
                 piece_at,
+                piece_at + expert_at,
+                spread,
                 hidden,
                 down_weight,
                 combine_high,

time: 93.1 us -> 78.2 us (0.84)
  local copies, waits for them, and re-layouts: 16.8 us -> 0.12 us
  Pallas kernels: 27.5 us -> 34.3 us
  waiting for transfers between devices: 24.1 us -> 19 us
    unnamed x30 -> x10, local copies, waits for them, and re-layouts: 16.7 us -> 0.03 us
    pallas_call x14 -> x15, Pallas kernels: 23.4 us -> 30.2 us  [the longest x4 14 us: attend(): pl.pallas_call(functools.partial(attend_kernel, heads, scale, lead_at, [(...]
    ppermute x21, waiting for transfers between devices: 24.1 us -> 19 us  [swapped(): return lax.ppermute(value, axes, pairs)]
  transfers between devices with their start and end apart: 21 -> 21, of which waited for: 11 -> 11; matrix products, arithmetic and copies ran while one was open for 0% -> 0% of each run, Pallas kernels for 22% -> 35%
where the time goes in v3:
time: 78.2 us; the launch traced here: 78 us
  Pallas kernels  34.3 us (44%)
  starting transfers between devices  24.3 us (31%)
  waiting for transfers between devices  19 us (24%)
    ppermute x21, starting transfers between devices, swapped(): return lax.ppermute(value, axes, pairs)  24.3 us
    ppermute x21, waiting for transfers between devices, swapped(): return lax.ppermute(value, axes, pairs)  19 us
    pallas_call x4, Pallas kernels, attend(): pl.pallas_call(functools.partial(attend_kernel, heads, scale, lead_at, [(...  14 us
    pallas_call x4, Pallas kernels, gate_up(): pl.pallas_call(functools.partial(gate_up_kernel, piece_at), in_specs=[who...  6.84 us
    pallas_call x4, Pallas kernels, down(): pl.pallas_call(kernel, in_specs=[whole(pltpu.SMEM)] + [whole()] * (4 + le...  5.54 us
    pallas_call x1, Pallas kernels, sight_of(): pl.pallas_call(functools.partial(sight_kernel, len(loaded)), in_specs=[wh...  2.59 us
  transfers between devices with their start and end apart: 21, of which 11 were waited for; matrix products, arithmetic and copies ran while one was open for 0% of the time, Pallas kernels for 35%

profile of v3, /device:TPU:0, one launch (start us, length us, event | category | flops | bytes accessed | tf_op | source)
XLA Modules:
  0.0 78.0 jit_solution(18394513403058669596)
XLA Ops:
  1.0 4.1 %collective-permute-start.2 = (bf16[32,1152]{1,0:T(8,128)(2,1)S(1)}, bf16[32,1152]{1,0:T(8,128)(2,1)S(1)}, u32[]{:S(2)}, u32[]{:S(2)}) collective-permute-start(bf16[32,1152]{1,0:T(8,128)(2,1)S(1)} %pack.1.queries_ref.refs_0_), channel_id=1, source_target_pairs={{0,8},{4,12},{8,0},{12,4},{1,9},{5,13},{9,1},{13,5},{2,10},{6,14},... | collective-permute-start | bytes 221192 | tf_op jit(solution)/shard_map/ppermute | solution.py:72
  6.7 2.6 %sight.1 = (bf16[64,2048]{1,0:T(8,128)(2,1)S(1)}, bf16[2048,128]{1,0:T(8,128)(2,1)S(1)}, bf16[2048,128]{1,0:T(8,128)(2,1)S(1)}, bf16[1024,2048]{1,0:T(8,128)(2,1)S(1)}) custom-call(s32[1,64]{1,0:T(1,128)} %bitcast.36, s32[1,2048]{1,0:T(1,128)} %bitcast.32, bf16[2048,128]{1,0:T(8,128)(2,1)} %bitcast.29, bf16[2048,128]{1,0:T(8,128)(2,1)} %bitcast.30, ...), custom_call_target="tpu_custom_call" | custom-call | flops 16777216 | bytes 8388608 | tf_op jit(solution)/shard_map/sight/pallas_call | solution.py:158
  9.9 3.5 %attend.6 = (bf16[32,1152]{1,0:T(8,128)(2,1)S(1)}, bf16[4,512,1536]{2,1,0:T(8,128)(2,1)S(1)}) custom-call(s32[17]{0:T(128)S(1)} %stack.71.plan_ref, bf16[32,1152]{1,0:T(8,128)(2,1)S(1)} %collective-permute-done.2.queries_ref.refs_2_, bf16[2048,128]{1,0:T(8,128)(2,1)S(1)} %get-tuple-element.35.keys_ref, bf16[2048,128]{1,0:T(8,128)(2,1)S(1)} %get-tuple-element.36.values_ref, ...), custom_call_target="tpu_custom_call" | custom-call | flops 536870912 | bytes 1048576 | tf_op jit(solution)/shard_map/attend/pallas_call | solution.py:229
  13.4 2.3 %collective-permute-start.3 = (bf16[32,1152]{1,0:T(8,128)(2,1)S(1)}, bf16[32,1152]{1,0:T(8,128)(2,1)S(1)}, u32[]{:S(2)}, u32[]{:S(2)}) collective-permute-start(bf16[32,1152]{1,0:T(8,128)(2,1)S(1)} %get-tuple-element.40), channel_id=1, source_target_pairs={{0,8},{4,12},{8,0},{12,4},{1,9},{5,13},{9,1},{13,5},{2,10},{6,14},... | collective-permute-start | bytes 221192 | tf_op jit(solution)/shard_map/ppermute | solution.py:72
  15.7 3.5 %attend.7 = (bf16[32,1152]{1,0:T(8,128)(2,1)S(1)}, bf16[4,512,1536]{2,1,0:T(8,128)(2,1)S(1)}) custom-call(s32[17]{0:T(128)S(1)} %stack.71.plan_ref, bf16[32,1152]{1,0:T(8,128)(2,1)S(1)} %collective-permute-done.4.queries_ref.refs_3_, bf16[2048,128]{1,0:T(8,128)(2,1)S(1)} %get-tuple-element.35.keys_ref, bf16[2048,128]{1,0:T(8,128)(2,1)S(1)} %get-tuple-element.36.values_ref, ...), custom_call_target="tpu_custom_call" | custom-call | flops 536870912 | bytes 1048576 | tf_op jit(solution)/shard_map/attend/pallas_call | solution.py:229
  19.2 2.3 %collective-permute-start.5 = (bf16[32,1152]{1,0:T(8,128)(2,1)S(1)}, bf16[32,1152]{1,0:T(8,128)(2,1)S(1)}, u32[]{:S(2)}, u32[]{:S(2)}) collective-permute-start(bf16[32,1152]{1,0:T(8,128)(2,1)S(1)} %get-tuple-element.41), channel_id=1, source_target_pairs={{0,12},{4,8},{8,4},{12,0},{1,13},{5,9},{9,5},{13,1},{2,14},{6,10},... | collective-permute-start | bytes 221192 | tf_op jit(solution)/shard_map/ppermute | solution.py:72
  21.5 3.5 %attend.5 = (bf16[32,1152]{1,0:T(8,128)(2,1)S(1)}, bf16[4,512,1536]{2,1,0:T(8,128)(2,1)S(1)}) custom-call(s32[17]{0:T(128)S(1)} %stack.71.plan_ref, bf16[32,1152]{1,0:T(8,128)(2,1)S(1)} %collective-permute-done.queries_ref.refs_1_, bf16[2048,128]{1,0:T(8,128)(2,1)S(1)} %get-tuple-element.35.keys_ref, bf16[2048,128]{1,0:T(8,128)(2,1)S(1)} %get-tuple-element.36.values_ref, ...), custom_call_target="tpu_custom_call" | custom-call | flops 536870912 | bytes 1048576 | tf_op jit(solution)/shard_map/attend/pallas_call | solution.py:229
  25.7 3.5 %attend.4 = (bf16[32,1152]{1,0:T(8,128)(2,1)S(1)}, bf16[4,512,1536]{2,1,0:T(8,128)(2,1)S(1)}) custom-call(s32[17]{0:T(128)S(1)} %stack.71.plan_ref, bf16[32,1152]{1,0:T(8,128)(2,1)S(1)} %pack.1.queries_ref.refs_0_, bf16[2048,128]{1,0:T(8,128)(2,1)S(1)} %get-tuple-element.35.keys_ref, bf16[2048,128]{1,0:T(8,128)(2,1)S(1)} %get-tuple-element.36.values_ref, ...), custom_call_target="tpu_custom_call" | custom-call | flops 536870912 | bytes 1048576 | tf_op jit(solution)/shard_map/attend/pallas_call | solution.py:229
  31.1 1.6 %collective-permute-start.7 = (bf16[32,512]{1,0:T(8,128)(2,1)S(1)}, bf16[32,512]{1,0:T(8,128)(2,1)S(1)}, u32[]{:S(2)}, u32[]{:S(2)}) collective-permute-start(bf16[32,512]{1,0:T(8,128)(2,1)S(1)} %get-tuple-element.45), channel_id=1, source_target_pairs={{0,2},{1,3},{2,0},{3,1},{4,6},{5,7},{6,4},{7,5},{8,10},{9,11},{10,... | collective-permute-start | bytes 98312 | tf_op jit(solution)/shard_map/ppermute | solution.py:72
  33.0 1.8 %collective-permute-done.6.refs_1_ = bf16[32,512]{1,0:T(8,128)(2,1)S(1)} collective-permute-done((bf16[32,512]{1,0:T(8,128)(2,1)S(1)}, bf16[32,512]{1,0:T(8,128)(2,1)S(1)}, u32[]{:S(2)}, u32[]{:S(2)}) %collective-permute-start.6) | collective-permute-done | bytes 32800 | tf_op jit(solution)/shard_map/ppermute | solution.py:72
  35.2 2.1 %collective-permute-start.10 = (bf16[32,640]{1,0:T(8,128)(2,1)S(1)}, bf16[32,640]{1,0:T(8,128)(2,1)S(1)}, u32[]{:S(2)}, u32[]{:S(2)}) collective-permute-start(bf16[32,640]{1,0:T(8,128)(2,1)S(1)} %get-tuple-element.49.refs_0_), channel_id=1, source_target_pairs={{0,8},{4,12},{8,0},{12,4},{1,9},{5,13},{9,1},{13,5},{2,10},{6,14},... | collective-permute-start | bytes 122888 | tf_op jit(solution)/shard_map/ppermute | solution.py:72
  37.3 1.6 %collective-permute-start.11 = (bf16[32,640]{1,0:T(8,128)(2,1)S(1)}, bf16[32,640]{1,0:T(8,128)(2,1)S(1)}, u32[]{:S(2)}, u32[]{:S(2)}) collective-permute-start(bf16[32,640]{1,0:T(8,128)(2,1)S(1)} %get-tuple-element.49.refs_0_), channel_id=1, source_target_pairs={{0,12},{4,8},{8,4},{12,0},{1,13},{5,9},{9,5},{13,1},{2,14},{6,10},... | collective-permute-start | bytes 122888 | tf_op jit(solution)/shard_map/ppermute | solution.py:72
  41.3 1.9 %collective-permute-done.11.refs_3_ = bf16[32,640]{1,0:T(8,128)(2,1)S(1)} collective-permute-done((bf16[32,640]{1,0:T(8,128)(2,1)S(1)}, bf16[32,640]{1,0:T(8,128)(2,1)S(1)}, u32[]{:S(2)}, u32[]{:S(2)}) %collective-permute-start.11) | collective-permute-done | bytes 40992 | tf_op jit(solution)/shard_map/ppermute | solution.py:72
  43.7 1.7 %gate_up.5 = bf16[128,1664]{1,0:T(8,128)(2,1)S(1)} custom-call(s32[17]{0:T(128)S(1)} %stack.71.plan_ref, bf16[4,128,640]{2,1,0:T(8,128)(2,1)S(1)} %pick.1.picked_ref, bf16[4,512,1536]{2,1,0:T(8,128)(2,1)S(1)} %get-tuple-element.51.weight_ref), custom_call_target="tpu_custom_call" | custom-call | flops 12582912 | bytes 393216 | tf_op jit(solution)/shard_map/gate_up/pallas_call | solution.py:408
  45.4 1.7 %gate_up.4.left_ref = bf16[128,1664]{1,0:T(8,128)(2,1)S(1)} custom-call(s32[17]{0:T(128)S(1)} %stack.71.plan_ref, bf16[4,128,640]{2,1,0:T(8,128)(2,1)S(1)} %pick.1.picked_ref, bf16[4,512,1536]{2,1,0:T(8,128)(2,1)S(1)} %get-tuple-element.50.weight_ref), custom_call_target="tpu_custom_call" | custom-call | flops 12582912 | bytes 393216 | tf_op jit(solution)/shard_map/gate_up/pallas_call | solution.py:408
  47.5 1.6 %collective-permute-start.14 = (bf16[128,1664]{1,0:T(8,128)(2,1)S(1)}, bf16[128,1664]{1,0:T(8,128)(2,1)S(1)}, u32[]{:S(2)}, u32[]{:S(2)}) collective-permute-start(bf16[128,1664]{1,0:T(8,128)(2,1)S(1)} %join.1), channel_id=1, source_target_pairs={{0,2},{2,0},{1,3},{3,1},{4,6},{6,4},{5,7},{7,5},{8,10},{10,8},{9,1... | collective-permute-start | bytes 1277960 | tf_op jit(solution)/shard_map/ppermute | solution.py:72
  49.0 1.7 %gate_up.6 = bf16[128,1664]{1,0:T(8,128)(2,1)S(1)} custom-call(s32[17]{0:T(128)S(1)} %stack.71.plan_ref, bf16[4,128,640]{2,1,0:T(8,128)(2,1)S(1)} %pick.1.picked_ref, bf16[4,512,1536]{2,1,0:T(8,128)(2,1)S(1)} %get-tuple-element.53.weight_ref), custom_call_target="tpu_custom_call" | custom-call | flops 12582912 | bytes 393216 | tf_op jit(solution)/shard_map/gate_up/pallas_call | solution.py:408
  51.0 1.7 %gate_up.7.refs_1_ = bf16[128,1664]{1,0:T(8,128)(2,1)S(1)} custom-call(s32[17]{0:T(128)S(1)} %stack.71.plan_ref, bf16[4,128,640]{2,1,0:T(8,128)(2,1)S(1)} %pick.1.picked_ref, bf16[4,512,1536]{2,1,0:T(8,128)(2,1)S(1)} %get-tuple-element.54.weight_ref), custom_call_target="tpu_custom_call" | custom-call | flops 12582912 | bytes 393216 | tf_op jit(solution)/shard_map/gate_up/pallas_call | solution.py:408
  52.7 7.1 %collective-permute-done.14.refs_2_ = bf16[128,1664]{1,0:T(8,128)(2,1)S(1)} collective-permute-done((bf16[128,1664]{1,0:T(8,128)(2,1)S(1)}, bf16[128,1664]{1,0:T(8,128)(2,1)S(1)}, u32[]{:S(2)}, u32[]{:S(2)}) %collective-permute-start.14) | collective-permute-done | bytes 426016 | tf_op jit(solution)/shard_map/ppermute | solution.py:72
  60.2 1.6 %collective-permute-start.15 = (bf16[128,768]{1,0:T(8,128)(2,1)S(1)}, bf16[128,768]{1,0:T(8,128)(2,1)S(1)}, u32[]{:S(2)}, u32[]{:S(2)}) collective-permute-start(bf16[128,768]{1,0:T(8,128)(2,1)S(1)} %hidden.1.hidden_ref), channel_id=1, source_target_pairs={{0,2},{2,0},{1,3},{3,1},{4,6},{6,4},{5,7},{7,5},{8,10},{10,8},{9,1... | collective-permute-start | bytes 589832 | tf_op jit(solution)/shard_map/ppermute | solution.py:72
  64.5 3.0 %collective-permute-done.15.hidden_ref = bf16[128,768]{1,0:T(8,128)(2,1)S(1)} collective-permute-done((bf16[128,768]{1,0:T(8,128)(2,1)S(1)}, bf16[128,768]{1,0:T(8,128)(2,1)S(1)}, u32[]{:S(2)}, u32[]{:S(2)}) %collective-permute-start.15) | collective-permute-done | bytes 196640 | tf_op jit(solution)/shard_map/ppermute | solution.py:72
  70.3 2.1 %collective-permute-start.18 = (bf16[32,512]{1,0:T(8,128)(2,1)S(1)}, bf16[32,512]{1,0:T(8,128)(2,1)S(1)}, u32[]{:S(2)}, u32[]{:S(2)}) collective-permute-start(bf16[32,512]{1,0:T(8,128)(2,1)S(1)} %get-tuple-element.62), channel_id=1, source_target_pairs={{0,12},{4,8},{8,4},{12,0},{1,13},{5,9},{9,5},{13,1},{2,14},{6,10},... | collective-permute-start | bytes 98312 | tf_op jit(solution)/shard_map/ppermute | solution.py:72
  72.4 2.3 %collective-permute-start.20 = (bf16[32,512]{1,0:T(8,128)(2,1)S(1)}, bf16[32,512]{1,0:T(8,128)(2,1)S(1)}, u32[]{:S(2)}, u32[]{:S(2)}) collective-permute-start(bf16[32,512]{1,0:T(8,128)(2,1)S(1)} %get-tuple-element.64), channel_id=1, source_target_pairs={{0,4},{4,0},{8,12},{12,8},{1,5},{5,1},{9,13},{13,9},{2,6},{6,2},{1... | collective-permute-start | bytes 98312 | tf_op jit(solution)/shard_map/ppermute | solution.py:72
  74.8 1.5 %collective-permute-done.18.refs_1_ = bf16[32,512]{1,0:T(8,128)(2,1)S(1)} collective-permute-done((bf16[32,512]{1,0:T(8,128)(2,1)S(1)}, bf16[32,512]{1,0:T(8,128)(2,1)S(1)}, u32[]{:S(2)}, u32[]{:S(2)}) %collective-permute-start.18) | collective-permute-done | bytes 32800 | tf_op jit(solution)/shard_map/ppermute | solution.py:72
  (52 shorter events, 17.6 us)
Async XLA Ops:
  1.0 9.0 %collective-permute-start.2 = (bf16[32,1152]{1,0:T(8,128)(2,1)S(1)}, bf16[32,1152]{1,0:T(8,128)(2,1)S(1)}, u32[]{:S(2)}, u32[]{:S(2)}) collective-permute-start(bf16[32,1152]{1,0:T(8,128)(2,1)S(1)} %pack.1.queries_ref.refs_0_), channel_id=1, source_target_pairs={{0,8},{4,12},{8,0},{12,4},{1,9},{5,13},{9,1},{13,5},{2,10},{6,14},... | collective-permute-start | bytes 221192 | tf_op jit(solution)/shard_map/ppermute | solution.py:72
  5.1 10.7 %collective-permute-start.4 = (bf16[32,1152]{1,0:T(8,128)(2,1)S(1)}, bf16[32,1152]{1,0:T(8,128)(2,1)S(1)}, u32[]{:S(2)}, u32[]{:S(2)}) collective-permute-start(bf16[32,1152]{1,0:T(8,128)(2,1)S(1)} %pack.1.queries_ref.refs_0_), channel_id=1, source_target_pairs={{0,12},{4,8},{8,4},{12,0},{1,13},{5,9},{9,5},{13,1},{2,14},{6,10},... | collective-permute-start | bytes 221192 | tf_op jit(solution)/shard_map/ppermute | solution.py:72
  6.4 15.1 %collective-permute-start = (bf16[32,1152]{1,0:T(8,128)(2,1)S(1)}, bf16[32,1152]{1,0:T(8,128)(2,1)S(1)}, u32[]{:S(2)}, u32[]{:S(2)}) collective-permute-start(bf16[32,1152]{1,0:T(8,128)(2,1)S(1)} %pack.1.queries_ref.refs_0_), channel_id=1, source_target_pairs={{0,4},{4,0},{8,12},{12,8},{1,5},{5,1},{9,13},{13,9},{2,6},{6,2},{1... | collective-permute-start | bytes 221192 | tf_op jit(solution)/shard_map/ppermute | solution.py:72
  13.4 15.8 %collective-permute-start.3 = (bf16[32,1152]{1,0:T(8,128)(2,1)S(1)}, bf16[32,1152]{1,0:T(8,128)(2,1)S(1)}, u32[]{:S(2)}, u32[]{:S(2)}) collective-permute-start(bf16[32,1152]{1,0:T(8,128)(2,1)S(1)} %get-tuple-element.40), channel_id=1, source_target_pairs={{0,8},{4,12},{8,0},{12,4},{1,9},{5,13},{9,1},{13,5},{2,10},{6,14},... | collective-permute-start | bytes 221192 | tf_op jit(solution)/shard_map/ppermute | solution.py:72
  19.2 10.0 %collective-permute-start.5 = (bf16[32,1152]{1,0:T(8,128)(2,1)S(1)}, bf16[32,1152]{1,0:T(8,128)(2,1)S(1)}, u32[]{:S(2)}, u32[]{:S(2)}) collective-permute-start(bf16[32,1152]{1,0:T(8,128)(2,1)S(1)} %get-tuple-element.41), channel_id=1, source_target_pairs={{0,12},{4,8},{8,4},{12,0},{1,13},{5,9},{9,5},{13,1},{2,14},{6,10},... | collective-permute-start | bytes 221192 | tf_op jit(solution)/shard_map/ppermute | solution.py:72
  25.1 4.4 %collective-permute-start.1 = (bf16[32,1152]{1,0:T(8,128)(2,1)S(1)}, bf16[32,1152]{1,0:T(8,128)(2,1)S(1)}, u32[]{:S(2)}, u32[]{:S(2)}) collective-permute-start(bf16[32,1152]{1,0:T(8,128)(2,1)S(1)} %get-tuple-element.39), channel_id=1, source_target_pairs={{0,4},{4,0},{8,12},{12,8},{1,5},{5,1},{9,13},{13,9},{2,6},{6,2},{1... | collective-permute-start | bytes 221192 | tf_op jit(solution)/shard_map/ppermute | solution.py:72
  31.1 3.7 %collective-permute-start.6 = (bf16[32,512]{1,0:T(8,128)(2,1)S(1)}, bf16[32,512]{1,0:T(8,128)(2,1)S(1)}, u32[]{:S(2)}, u32[]{:S(2)}) collective-permute-start(bf16[32,512]{1,0:T(8,128)(2,1)S(1)} %get-tuple-element.44), channel_id=1, source_target_pairs={{0,3},{1,2},{2,1},{3,0},{4,7},{5,6},{6,5},{7,4},{8,11},{9,10},{10,... | collective-permute-start | bytes 98312 | tf_op jit(solution)/shard_map/ppermute | solution.py:72
  31.1 4.0 %collective-permute-start.7 = (bf16[32,512]{1,0:T(8,128)(2,1)S(1)}, bf16[32,512]{1,0:T(8,128)(2,1)S(1)}, u32[]{:S(2)}, u32[]{:S(2)}) collective-permute-start(bf16[32,512]{1,0:T(8,128)(2,1)S(1)} %get-tuple-element.45), channel_id=1, source_target_pairs={{0,2},{1,3},{2,0},{3,1},{4,6},{5,7},{6,4},{7,5},{8,10},{9,11},{10,... | collective-permute-start | bytes 98312 | tf_op jit(solution)/shard_map/ppermute | solution.py:72
  32.7 2.5 %collective-permute-start.8 = (bf16[32,512]{1,0:T(8,128)(2,1)S(1)}, bf16[32,512]{1,0:T(8,128)(2,1)S(1)}, u32[]{:S(2)}, u32[]{:S(2)}) collective-permute-start(bf16[32,512]{1,0:T(8,128)(2,1)S(1)} %get-tuple-element.46), channel_id=1, source_target_pairs={{0,1},{1,0},{2,3},{3,2},{4,5},{5,4},{6,7},{7,6},{8,9},{9,8},{10,11... | collective-permute-start | bytes 98312 | tf_op jit(solution)/shard_map/ppermute | solution.py:72
  35.2 6.1 %collective-permute-start.10 = (bf16[32,640]{1,0:T(8,128)(2,1)S(1)}, bf16[32,640]{1,0:T(8,128)(2,1)S(1)}, u32[]{:S(2)}, u32[]{:S(2)}) collective-permute-start(bf16[32,640]{1,0:T(8,128)(2,1)S(1)} %get-tuple-element.49.refs_0_), channel_id=1, source_target_pairs={{0,8},{4,12},{8,0},{12,4},{1,9},{5,13},{9,1},{13,5},{2,10},{6,14},... | collective-permute-start | bytes 122888 | tf_op jit(solution)/shard_map/ppermute | solution.py:72
  37.3 5.9 %collective-permute-start.11 = (bf16[32,640]{1,0:T(8,128)(2,1)S(1)}, bf16[32,640]{1,0:T(8,128)(2,1)S(1)}, u32[]{:S(2)}, u32[]{:S(2)}) collective-permute-start(bf16[32,640]{1,0:T(8,128)(2,1)S(1)} %get-tuple-element.49.refs_0_), channel_id=1, source_target_pairs={{0,12},{4,8},{8,4},{12,0},{1,13},{5,9},{9,5},{13,1},{2,14},{6,10},... | collective-permute-start | bytes 122888 | tf_op jit(solution)/shard_map/ppermute | solution.py:72
  38.9 4.4 %collective-permute-start.9 = (bf16[32,640]{1,0:T(8,128)(2,1)S(1)}, bf16[32,640]{1,0:T(8,128)(2,1)S(1)}, u32[]{:S(2)}, u32[]{:S(2)}) collective-permute-start(bf16[32,640]{1,0:T(8,128)(2,1)S(1)} %get-tuple-element.49.refs_0_), channel_id=1, source_target_pairs={{0,4},{4,0},{8,12},{12,8},{1,5},{5,1},{9,13},{13,9},{2,6},{6,2},{1... | collective-permute-start | bytes 122888 | tf_op jit(solution)/shard_map/ppermute | solution.py:72
  45.4 1.8 %collective-permute-start.12 = (bf16[128,1664]{1,0:T(8,128)(2,1)S(1)}, bf16[128,1664]{1,0:T(8,128)(2,1)S(1)}, u32[]{:S(2)}, u32[]{:S(2)}) collective-permute-start(bf16[128,1664]{1,0:T(8,128)(2,1)S(1)} %gate_up.5), channel_id=1, source_target_pairs={{0,1},{1,0},{2,3},{3,2},{4,5},{5,4},{6,7},{7,6},{8,9},{9,8},{10,11... | collective-permute-start | bytes 1277960 | tf_op jit(solution)/shard_map/ppermute | solution.py:72
  45.4 16.3 %slice-start = ((s8[12582912]{0:T(1024)(128)(4,1)}), s8[4194304]{0:T(1024)(128)(4,1)S(1)}, s32[]{:S(2)}) async-start(s8[12582912]{0:T(1024)(128)(4,1)} %bitcast.26), calls=%async_computation | async-start | bytes 8388608
  47.2 14.6 %slice-start.1 = ((s8[12582912]{0:T(1024)(128)(4,1)}), s8[4194304]{0:T(1024)(128)(4,1)S(1)}, s32[]{:S(2)}) async-start(s8[12582912]{0:T(1024)(128)(4,1)} %bitcast.26), calls=%async_computation.1 | async-start | bytes 8388608
  47.5 12.3 %collective-permute-start.14 = (bf16[128,1664]{1,0:T(8,128)(2,1)S(1)}, bf16[128,1664]{1,0:T(8,128)(2,1)S(1)}, u32[]{:S(2)}, u32[]{:S(2)}) collective-permute-start(bf16[128,1664]{1,0:T(8,128)(2,1)S(1)} %join.1), channel_id=1, source_target_pairs={{0,2},{2,0},{1,3},{3,1},{4,6},{6,4},{5,7},{7,5},{8,10},{10,8},{9,1... | collective-permute-start | bytes 1277960 | tf_op jit(solution)/shard_map/ppermute | solution.py:72
  50.8 9.0 %collective-permute-start.13 = (bf16[128,1664]{1,0:T(8,128)(2,1)S(1)}, bf16[128,1664]{1,0:T(8,128)(2,1)S(1)}, u32[]{:S(2)}, u32[]{:S(2)}) collective-permute-start(bf16[128,1664]{1,0:T(8,128)(2,1)S(1)} %gate_up.6), channel_id=1, source_target_pairs={{0,1},{1,0},{2,3},{3,2},{4,5},{5,4},{6,7},{7,6},{8,9},{9,8},{10,11... | collective-permute-start | bytes 1277960 | tf_op jit(solution)/shard_map/ppermute | solution.py:72
  51.0 10.8 %slice-start.2 = ((s8[12582912]{0:T(1024)(128)(4,1)}), s8[4194304]{0:T(1024)(128)(4,1)S(1)}, s32[]{:S(2)}) async-start(s8[12582912]{0:T(1024)(128)(4,1)} %bitcast.26), calls=%async_computation.2 | async-start | bytes 8388608
  60.1 3.0 %collective-permute-start.16 = (bf16[128,768]{1,0:T(8,128)(2,1)S(1)}, bf16[128,768]{1,0:T(8,128)(2,1)S(1)}, u32[]{:S(2)}, u32[]{:S(2)}) collective-permute-start(bf16[128,768]{1,0:T(8,128)(2,1)S(1)} %hidden.1.hidden_ref), channel_id=1, source_target_pairs={{0,1},{1,0},{2,3},{3,2},{4,5},{5,4},{6,7},{7,6},{8,9},{9,8},{10,11... | collective-permute-start | bytes 589832 | tf_op jit(solution)/shard_map/ppermute | solution.py:72
  60.2 7.3 %collective-permute-start.15 = (bf16[128,768]{1,0:T(8,128)(2,1)S(1)}, bf16[128,768]{1,0:T(8,128)(2,1)S(1)}, u32[]{:S(2)}, u32[]{:S(2)}) collective-permute-start(bf16[128,768]{1,0:T(8,128)(2,1)S(1)} %hidden.1.hidden_ref), channel_id=1, source_target_pairs={{0,2},{2,0},{1,3},{3,1},{4,6},{6,4},{5,7},{7,5},{8,10},{10,8},{9,1... | collective-permute-start | bytes 589832 | tf_op jit(solution)/shard_map/ppermute | solution.py:72
  67.5 1.4 %collective-permute-start.17 = (bf16[128,768]{1,0:T(8,128)(2,1)S(1)}, bf16[128,768]{1,0:T(8,128)(2,1)S(1)}, u32[]{:S(2)}, u32[]{:S(2)}) collective-permute-start(bf16[128,768]{1,0:T(8,128)(2,1)S(1)} %collective-permute-done.15.hidden_ref), channel_id=1, source_target_pairs={{0,1},{1,0},{2,3},{3,2},{4,5},{5,4},{6,7},{7,6},{8,9},{9,8},{10,11... | collective-permute-start | bytes 589832 | tf_op jit(solution)/shard_map/ppermute | solution.py:72
  70.3 6.0 %collective-permute-start.18 = (bf16[32,512]{1,0:T(8,128)(2,1)S(1)}, bf16[32,512]{1,0:T(8,128)(2,1)S(1)}, u32[]{:S(2)}, u32[]{:S(2)}) collective-permute-start(bf16[32,512]{1,0:T(8,128)(2,1)S(1)} %get-tuple-element.62), channel_id=1, source_target_pairs={{0,12},{4,8},{8,4},{12,0},{1,13},{5,9},{9,5},{13,1},{2,14},{6,10},... | collective-permute-start | bytes 98312 | tf_op jit(solution)/shard_map/ppermute | solution.py:72
  72.4 4.9 %collective-permute-start.19 = (bf16[32,512]{1,0:T(8,128)(2,1)S(1)}, bf16[32,512]{1,0:T(8,128)(2,1)S(1)}, u32[]{:S(2)}, u32[]{:S(2)}) collective-permute-start(bf16[32,512]{1,0:T(8,128)(2,1)S(1)} %get-tuple-element.63), channel_id=1, source_target_pairs={{0,8},{4,12},{8,0},{12,4},{1,9},{5,13},{9,1},{13,5},{2,10},{6,14},... | collective-permute-start | bytes 98312 | tf_op jit(solution)/shard_map/ppermute | solution.py:72
  72.4 4.9 %collective-permute-start.20 = (bf16[32,512]{1,0:T(8,128)(2,1)S(1)}, bf16[32,512]{1,0:T(8,128)(2,1)S(1)}, u32[]{:S(2)}, u32[]{:S(2)}) collective-permute-start(bf16[32,512]{1,0:T(8,128)(2,1)S(1)} %get-tuple-element.64), channel_id=1, source_target_pairs={{0,4},{4,0},{8,12},{12,8},{1,5},{5,1},{9,13},{13,9},{2,6},{6,2},{1... | collective-permute-start | bytes 98312 | tf_op jit(solution)/shard_map/ppermute | solution.py:72
  (2 other events, 18.0 us)

commit v4 on v3

--- a/solution.py
+++ b/solution.py
@@ -41,10 +41,6 @@
     return [pltpu.with_memory_space_constraint(value, pltpu.HBM) for value in values]
 
 
-def in_vmem(value):
-    return pltpu.with_memory_space_constraint(value, pltpu.VMEM)
-
-
 def lane_ids(shape):
     return lax.broadcasted_iota(jnp.int32, shape, len(shape) - 1)
 
@@ -77,7 +73,8 @@
 
 
 def pack_kernel(
-    queries_ref, seg_ref, ids_ref, weight_ref, out_ref, seg_here, ids_here, weight_here, done
+    queries_ref, seg_ref, ids_ref, weight_ref, beside_ref, out_ref,
+    seg_here, ids_here, weight_here, done,
 ):
     rows, width = queries_ref.shape
     choices = ids_ref.shape[0]
@@ -110,33 +107,28 @@
     copies[3].wait()
 
 
-def pack(queries, query_seg, expert_ids, route_weight):
+def pack(queries, query_seg, expert_ids, route_weight, beside):
     rows, width = queries.shape
     small = [query_seg[None, :], expert_ids.T, route_weight.T]
     return pl.pallas_call(
         pack_kernel,
-        in_specs=[whole(pltpu.HBM)] * 4,
+        in_specs=[whole(pltpu.HBM)] * 5,
         out_shape=jax.ShapeDtypeStruct((rows, width + LANES), bf16),
         scratch_shapes=[pltpu.VMEM(value.shape, value.dtype) for value in small]
         + [pltpu.SemaphoreType.DMA((4,))],
         compiler_params=params(4),
         name="pack",
-    )(*in_hbm([queries] + small))
-
-
-def sight_kernel(load_count, parent_ref, key_seg_ref, *refs):
-    sources, sight_ref = refs[:load_count], refs[load_count]
-    targets = refs[load_count + 1 : 2 * load_count + 1]
-    parent_here, key_seg_here, done = refs[2 * load_count + 1 :]
+    )(*in_hbm([queries] + small + [beside]))
+
+
+def sight_kernel(parent_ref, key_seg_ref, beside_ref, sight_ref, parent_here, key_seg_here, done):
     copies = [
-        pltpu.make_async_copy(source, target, done.at[i])
-        for i, (source, target) in enumerate(
-            zip((parent_ref, key_seg_ref) + sources, (parent_here, key_seg_here) + targets)
-        )
+        pltpu.make_async_copy(parent_ref, parent_here, done.at[0]),
+        pltpu.make_async_copy(key_seg_ref, key_seg_here, done.at[1]),
     ]
     for copy in copies:
         copy.start()
-    for copy in copies[:2]:
+    for copy in copies:
         copy.wait()
     seg_count, key_count = sight_ref.shape
     square = (seg_count, seg_count)
@@ -147,43 +139,27 @@
     six = as_bf16(dot(four, two) > 0.5)
     keys = as_bf16(key_seg_here[...] == row_ids((seg_count, key_count)))
     sight_ref[...] = dot(six, keys, ((0,), (0,))).astype(bf16)
-    for copy in copies[2:]:
-        copy.wait()
-
-
-def sight_of(parent, key_seg, loaded):
+
+
+def sight_of(parent, key_seg, beside):
     assert DEPTH == 6
     small = [parent[None, :], key_seg[None, :]]
-    shapes = [pltpu.VMEM(value.shape, value.dtype) for value in loaded]
-    return pl.pallas_call(
-        functools.partial(sight_kernel, len(loaded)),
-        in_specs=[whole(pltpu.HBM)] * (2 + len(loaded)),
-        out_specs=[whole()] * (1 + len(loaded)),
-        out_shape=[jax.ShapeDtypeStruct((parent.shape[0], key_seg.shape[0]), bf16)] + shapes,
+    return pl.pallas_call(
+        sight_kernel,
+        in_specs=[whole(pltpu.HBM)] * 3,
+        out_shape=jax.ShapeDtypeStruct((parent.shape[0], key_seg.shape[0]), bf16),
         scratch_shapes=[pltpu.VMEM(value.shape, value.dtype) for value in small]
-        + [pltpu.SemaphoreType.DMA((2 + len(loaded),))],
+        + [pltpu.SemaphoreType.DMA((2,))],
         compiler_params=params(4),
-        cost_estimate=cost(2**24, 2**23),
+        cost_estimate=cost(2**24, 2**19),
         name="sight",
-    )(*in_hbm(small + loaded))
+    )(*in_hbm(small + [beside]))
 
 
 def attend_kernel(
-    heads, scale, lead_at, loads, plan_ref, queries_ref, keys_ref, values_ref, sight_ref,
-    weight_ref, out_ref, *refs,
+    heads, scale, lead_at, plan_ref, queries_ref, keys_ref, values_ref, sight_ref, beside_ref,
+    out_ref, stacked_ref, probs_ref,
 ):
-    loaded_refs, (stacked_ref, probs_ref, done) = refs[: len(loads)], refs[len(loads) :]
-    copies = []
-    for target, (expert_at, spread) in zip(loaded_refs, loads):
-        for i in range(target.shape[0]):
-            expert = plan_ref[expert_at] // spread + i
-            copies.append(
-                pltpu.make_async_copy(
-                    weight_ref.at[expert], target.at[i], done.at[len(copies)]
-                )
-            )
-    for copy in copies:
-        copy.start()
     rows = queries_ref.shape[0]
     key_count, head_size = keys_ref.shape
     seg_count = sight_ref.shape[0]
@@ -217,32 +193,24 @@
     for head in range(heads):
         columns = slice(head * head_size, (head + 1) * head_size)
         out_ref[:, columns] = sums[head * rows : (head + 1) * rows, :].astype(bf16)
-    for copy in copies:
-        copy.wait()
-
-
-def attend(plan, lead_at, queries, keys, values, sight, heads, scale, weight, loads, experts, spread):
+
+
+def attend(plan, lead_at, queries, keys, values, sight, heads, scale, beside):
     rows, columns = queries.shape
     key_count, head_size = keys.shape
     work = rows * heads * key_count
-    held = pltpu.VMEM((experts,) + weight.shape[1:], weight.dtype)
-    part, *loaded = pl.pallas_call(
-        functools.partial(
-            attend_kernel, heads, scale, lead_at, [(load, spread) for load in loads]
-        ),
+    return pl.pallas_call(
+        functools.partial(attend_kernel, heads, scale, lead_at),
         in_specs=[whole(pltpu.SMEM)] + [whole()] * 4 + [whole(pltpu.HBM)],
-        out_specs=[whole()] * (1 + len(loads)),
-        out_shape=[jax.ShapeDtypeStruct((rows, columns), bf16)] + [held] * len(loads),
+        out_shape=jax.ShapeDtypeStruct((rows, columns), bf16),
         scratch_shapes=[
             pltpu.VMEM((rows * heads, head_size), bf16),
             pltpu.VMEM((rows * heads, key_count), bf16),
-            pltpu.SemaphoreType.DMA((max(1, len(loads) * experts),)),
         ],
         compiler_params=params(8),
         cost_estimate=cost(8 * work * head_size, 2**20, work),
         name="attend",
-    )(plan, queries, in_vmem(keys), in_vmem(values), sight, *in_hbm([weight]))
-    return part, loaded
+    )(plan, queries, keys, values, sight, *in_hbm([beside]))
 
 
 def project_kernel(heads, scale, order_at, source_count, plan_ref, *refs):
@@ -283,7 +251,7 @@
         compiler_params=params(8),
         cost_estimate=cost(2 * rows * width * model_width, 2 * width * model_width),
         name="project",
-    )(plan, *parts, in_vmem(weight))
+    )(plan, *parts, weight)
 
 
 def mix_kernel(residual_ref, gain_ref, *refs):
@@ -357,7 +325,7 @@
     )(plan, *packed)
 
 
-def pick_kernel(place_ref, *refs):
+def pick_kernel(beside_ref, place_ref, *refs):
     rows_refs, (out_ref, rows_ref) = refs[:-2], refs[-2:]
     rows = rows_refs[0].shape[0]
     for i, ref in enumerate(rows_refs):
@@ -366,17 +334,18 @@
         out_ref[piece] = dot(place_ref[piece], rows_ref[...], ((0,), (0,))).astype(bf16)
 
 
-def pick(place, rows):
+def pick(place, rows, beside):
     piece_count, tokens, slots = place.shape
     columns = rows[0].shape[1]
     return pl.pallas_call(
         pick_kernel,
+        in_specs=[whole(pltpu.HBM)] + [whole()] * (1 + len(rows)),
         out_shape=jax.ShapeDtypeStruct((piece_count, slots, columns), bf16),
         scratch_shapes=[pltpu.VMEM((tokens, columns), bf16)],
         compiler_params=params(8),
         cost_estimate=cost(2**26, 2**20),
         name="pick",
-    )(place, *rows)
+    )(*in_hbm([beside]), place, *rows)
 
 
 def squares_joined(squares):
@@ -385,34 +354,29 @@
     return jnp.where(lane == 0, high, jnp.where(lane == 1, low, 0.0))
 
 
-def gate_up_kernel(piece_at, plan_ref, picked_ref, weight_ref, *rest):
-    added_refs, out_ref = rest[:-1], rest[-1]
-    experts, width, ff_pair = weight_ref.shape
-    rows = out_ref.shape[0] // experts
-    piece = plan_ref[piece_at]
-    for i in range(experts):
-        here = slice(i * rows, (i + 1) * rows)
-        picked = picked_ref[piece, here, :]
-        product = dot(picked[:, :width], weight_ref[i])
-        squares = picked[:, width:].astype(f32)
-        for ref in added_refs:
-            product = product + ref[here, :ff_pair].astype(f32)
-            squares = squares_joined(squares + ref[here, ff_pair:].astype(f32))
-        out_ref[here, :ff_pair] = product.astype(bf16)
-        out_ref[here, ff_pair:] = squares.astype(bf16)
-
-
-def gate_up(plan, piece_at, picked, weight, added=()):
-    slots = picked.shape[1]
-    experts, width, ff_pair = weight.shape
-    return pl.pallas_call(
-        functools.partial(gate_up_kernel, piece_at),
-        in_specs=[whole(pltpu.SMEM)] + [whole()] * (2 + len(added)),
+def gate_up(plan, piece_at, expert_at, spread, picked, weight):
+    piece_count, slots, _ = picked.shape
+    local_experts, width, ff_pair = weight.shape
+    experts = max(1, local_experts // piece_count)
+    rows = slots // experts
+
+    def kernel(plan_ref, picked_ref, weight_ref, out_ref):
+        piece = plan_ref[piece_at]
+        first = plan_ref[expert_at] // spread
+        for i in range(experts):
+            here = slice(i * rows, (i + 1) * rows)
+            picked = picked_ref[piece, here, :]
+            out_ref[here, :ff_pair] = dot(picked[:, :width], weight_ref[first + i]).astype(bf16)
+            out_ref[here, ff_pair:] = picked[:, width:]
+
+    return pl.pallas_call(
+        kernel,
+        in_specs=[whole(pltpu.SMEM)] + [whole()] * 2,
         out_shape=jax.ShapeDtypeStruct((slots, ff_pair + LANES), bf16),
         compiler_params=params(8),
-        cost_estimate=cost(slots * width * ff_pair // 8, experts * width * ff_pair // 8),
-        name="gate_up_sum" if added else "gate_up",
-    )(plan, picked, in_vmem(weight), *added)
+        cost_estimate=cost(2 * slots * width * ff_pair, 2 * experts * width * ff_pair),
+        name="gate_up",
+    )(plan, picked, weight)
 
 
 def join_kernel(left_ref, right_ref, out_ref):
@@ -435,6 +399,7 @@
 def hidden_kernel(part_count, model_width, *refs):
     out_ref = refs[-1]
     ff_width = out_ref.shape[1]
+    refs = refs[1:]
     total = refs[0][...].astype(f32)
     for ref in refs[1:part_count]:
         total = total + ref[...].astype(f32)
@@ -445,13 +410,14 @@
     out_ref[...] = (gate / (1.0 + jnp.exp(-gate)) * up).astype(bf16)
 
 
-def hidden_of(parts, ff_width, model_width):
+def hidden_of(parts, ff_width, model_width, beside):
     return pl.pallas_call(
         functools.partial(hidden_kernel, len(parts), model_width),
+        in_specs=[whole(pltpu.HBM)] + [whole()] * len(parts),
         out_shape=jax.ShapeDtypeStruct((parts[0].shape[0], ff_width), bf16),
         compiler_params=params(8),
         name="hidden",
-    )(*parts)
+    )(*in_hbm([beside]), *parts)
 
 
 def down(plan, piece_at, expert_at, spread, hidden, weight, high, low, total=None, out_count=1):
@@ -555,41 +521,21 @@
     away_at = mine_at + exp_count
     expert_at = piece_count
 
-    packed = pack(queries.reshape(query_rows, width), query_seg, expert_ids, route_weight)
+    packed = pack(
+        queries.reshape(query_rows, width), query_seg, expert_ids, route_weight, gate_up_weight
+    )
     gathered = {0: packed}
     for k in far_first(ctx_count):
         gathered[k] = swapped(packed, "ctx", k)
-    sight, keys, values, out_matrix = sight_of(
-        parent,
-        key_seg,
-        [
-            cached_keys.reshape(key_count, head_size),
-            cached_values.reshape(key_count, head_size),
-            out_weight.reshape(width, model_width),
-        ],
-    )
-    steps = far_first(exp_count) + [0]
-    wanted = [at + k for k in steps for at in (away_at, mine_at)]
-    assert ctx_count >= piece_count
+    sight = sight_of(parent, key_seg, gate_up_weight)
+    keys = cached_keys.reshape(key_count, head_size)
+    values = cached_values.reshape(key_count, head_size)
+    out_matrix = out_weight.reshape(width, model_width)
     parts = {}
-    held = {}
-    for turn, k in enumerate(list(range(1, ctx_count)) + [0]):
-        loads = wanted[turn : turn + 1]
-        part, loaded = attend(
-            plan,
-            lead_at + k,
-            gathered[k],
-            keys,
-            values,
-            sight,
-            heads,
-            scale,
-            gate_up_weight,
-            [at + expert_at for at in loads],
-            experts,
-            spread,
+    for k in list(range(1, ctx_count)) + [0]:
+        part = attend(
+            plan, lead_at + k, gathered[k], keys, values, sight, heads, scale, gate_up_weight
         )
-        held.update(zip(loads, loaded))
         parts[k] = swapped(part, "ctx", k) if k else part
     place, combine_high, combine_low = route(
         plan,
@@ -617,22 +563,23 @@
     rows = {0: sent}
     for k in far_first(ctx_count):
         rows[k] = swapped(sent, "ctx", k)
-    picked = pick(place, [rows[k] for k in range(ctx_count)])
+    picked = pick(place, [rows[k] for k in range(ctx_count)], gate_up_weight)
+
+    def first_half(piece_at):
+        return gate_up(plan, piece_at, piece_at + expert_at, spread, picked, gate_up_weight)
 
     finals = []
-    for k in steps:
-        away = gate_up(plan, away_at + k, picked, held[away_at + k])
-        arrived = swapped(away, "tp", 1)
+    for k in far_first(exp_count) + [0]:
+        arrived = swapped(first_half(away_at + k), "tp", 1)
+        mine = first_half(mine_at + k)
         if k:
-            mine = gate_up(plan, mine_at + k, picked, held[mine_at + k])
             joined = join(mine, arrived)
             finals.append(swapped(joined, "exp", k))
             picked, _ = lax.optimization_barrier((picked, joined))
         else:
-            mine = gate_up(plan, mine_at, picked, held[mine_at])
             finals, mine = lax.optimization_barrier((finals, mine))
             finals = [arrived, mine] + finals
-    own_hidden = hidden_of(finals, ff_width, model_width)
+    own_hidden = hidden_of(finals, ff_width, model_width, gate_up_weight)
 
     total = None
     for k in range(exp_count):

time: 78.2 us -> 75.5 us (0.965)
  Pallas kernels: 34.3 us -> 26.5 us
  local copies, waits for them, and re-layouts: 0.12 us -> 3.22 us
  waiting for transfers between devices: 19 us -> 21.9 us
  starting transfers between devices: 24.3 us -> 23.4 us
    pallas_call x11, Pallas kernels: 24.8 us -> 16.9 us  [the longest x4 7.27 us: attend(): pl.pallas_call(functools.partial(attend_kernel, heads, scale, lead_at), i...]
    unnamed x10 -> x28, local copies, waits for them, and re-layouts: 0.03 us -> 3.12 us
    ppermute x21, waiting for transfers between devices: 19 us -> 21.9 us  [swapped(): return lax.ppermute(value, axes, pairs)]
    ppermute x21, starting transfers between devices: 24.3 us -> 23.4 us  [swapped(): return lax.ppermute(value, axes, pairs)]
  transfers between devices with their start and end apart: 21 -> 21, of which waited for: 11 -> 13; matrix products, arithmetic and copies ran while one was open for 0% -> 0% of each run, Pallas kernels for 35% -> 25%
where the time goes in v4:
time: 75.5 us; the launch traced here: 75.3 us
  Pallas kernels  26.5 us (35%)
  starting transfers between devices  23.4 us (31%)
  waiting for transfers between devices  21.9 us (29%)
  local copies, waits for them, and re-layouts  3.22 us (4%)
    ppermute x21, starting transfers between devices, swapped(): return lax.ppermute(value, axes, pairs)  23.4 us
    ppermute x21, waiting for transfers between devices, swapped(): return lax.ppermute(value, axes, pairs)  21.9 us
    pallas_call x4, Pallas kernels, attend(): pl.pallas_call(functools.partial(attend_kernel, heads, scale, lead_at), i...  7.27 us
    pallas_call x4, Pallas kernels, gate_up(): pl.pallas_call(kernel, in_specs=[whole(pltpu.SMEM)] + [whole()] * 2, out_...  6.85 us
    pallas_call x4, Pallas kernels, down(): pl.pallas_call(kernel, in_specs=[whole(pltpu.SMEM)] + [whole()] * (4 + le...  5.54 us
    unnamed x28, local copies, waits for them, and re-layouts  3.12 us
    pallas_call x1, Pallas kernels, project(): pl.pallas_call(functools.partial(project_kernel, heads, scale, order_at,...  1.55 us
  transfers between devices with their start and end apart: 21, of which 13 were waited for; matrix products, arithmetic and copies ran while one was open for 0% of the time, Pallas kernels for 25%

profile of v4, /device:TPU:0, one launch (start us, length us, event | category | flops | bytes accessed | tf_op | source)
XLA Modules:
  0.0 75.3 jit_solution(2675487331395851972)
XLA Ops:
  1.0 3.1 %collective-permute-start = (bf16[32,1152]{1,0:T(8,128)(2,1)S(1)}, bf16[32,1152]{1,0:T(8,128)(2,1)S(1)}, u32[]{:S(2)}, u32[]{:S(2)}) collective-permute-start(bf16[32,1152]{1,0:T(8,128)(2,1)S(1)} %pack.1.queries_ref.refs_0_), channel_id=1, source_target_pairs={{0,4},{4,0},{8,12},{12,8},{1,5},{5,1},{9,13},{13,9},{2,6},{6,2},{1... | collective-permute-start | bytes 221192 | tf_op jit(solution)/shard_map/ppermute | solution.py:68
  4.0 2.6 %collective-permute-start.2 = (bf16[32,1152]{1,0:T(8,128)(2,1)S(1)}, bf16[32,1152]{1,0:T(8,128)(2,1)S(1)}, u32[]{:S(2)}, u32[]{:S(2)}) collective-permute-start(bf16[32,1152]{1,0:T(8,128)(2,1)S(1)} %pack.1.queries_ref.refs_0_), channel_id=1, source_target_pairs={{0,8},{4,12},{8,0},{12,4},{1,9},{5,13},{9,1},{13,5},{2,10},{6,14},... | collective-permute-start | bytes 221192 | tf_op jit(solution)/shard_map/ppermute | solution.py:68
  6.8 1.4 %sight.1.sight_ref = bf16[64,2048]{1,0:T(8,128)(2,1)S(1)} custom-call(s32[1,64]{1,0:T(1,128)} %bitcast.44, s32[1,2048]{1,0:T(1,128)} %bitcast.40, bf16[16,512,1536]{2,1,0:T(8,128)(2,1)} %refs_0_.1), custom_call_target="tpu_custom_call" | custom-call | flops 16777216 | bytes 524288 | tf_op jit(solution)/shard_map/sight/pallas_call | solution.py:147
  8.2 1.8 %attend.5 = bf16[32,1152]{1,0:T(8,128)(2,1)S(1)} custom-call(s32[17]{0:T(128)S(1)} %stack.71.plan_ref, bf16[32,1152]{1,0:T(8,128)(2,1)S(1)} %collective-permute-done.queries_ref.refs_1_, bf16[2048,128]{1,0:T(8,128)(2,1)S(1)} %bitcast.30, bf16[2048,128]{1,0:T(8,128)(2,1)S(1)} %bitcast.34, bf16[64,2048]{1,0:T(8,128)(2,1)S(1)} %sight.1.sight_ref, ...), custom_call_target="tpu_custom_call" | custom-call | flops 536870912 | bytes 1048576 | tf_op jit(solution)/shard_map/attend/pallas_call | solution.py:202
  11.8 1.8 %attend.6 = bf16[32,1152]{1,0:T(8,128)(2,1)S(1)} custom-call(s32[17]{0:T(128)S(1)} %stack.71.plan_ref, bf16[32,1152]{1,0:T(8,128)(2,1)S(1)} %collective-permute-done.2.queries_ref.refs_2_, bf16[2048,128]{1,0:T(8,128)(2,1)S(1)} %bitcast.31, bf16[2048,128]{1,0:T(8,128)(2,1)S(1)} %bitcast.35, bf16[64,2048]{1,0:T(8,128)(2,1)S(1)} %sight.1.sight_ref, ...), custom_call_target="tpu_custom_call" | custom-call | flops 536870912 | bytes 1048576 | tf_op jit(solution)/shard_map/attend/pallas_call | solution.py:202
  13.6 2.8 %collective-permute-start.3 = (bf16[32,1152]{1,0:T(8,128)(2,1)S(1)}, bf16[32,1152]{1,0:T(8,128)(2,1)S(1)}, u32[]{:S(2)}, u32[]{:S(2)}) collective-permute-start(bf16[32,1152]{1,0:T(8,128)(2,1)S(1)} %attend.6), channel_id=1, source_target_pairs={{0,8},{4,12},{8,0},{12,4},{1,9},{5,13},{9,1},{13,5},{2,10},{6,14},... | collective-permute-start | bytes 221192 | tf_op jit(solution)/shard_map/ppermute | solution.py:68
  16.4 1.8 %attend.7 = bf16[32,1152]{1,0:T(8,128)(2,1)S(1)} custom-call(s32[17]{0:T(128)S(1)} %stack.71.plan_ref, bf16[32,1152]{1,0:T(8,128)(2,1)S(1)} %collective-permute-done.4.queries_ref.refs_3_, bf16[2048,128]{1,0:T(8,128)(2,1)S(1)} %bitcast.32, bf16[2048,128]{1,0:T(8,128)(2,1)S(1)} %bitcast.36, bf16[64,2048]{1,0:T(8,128)(2,1)S(1)} %sight.1.sight_ref, ...), custom_call_target="tpu_custom_call" | custom-call | flops 536870912 | bytes 1048576 | tf_op jit(solution)/shard_map/attend/pallas_call | solution.py:202
  18.9 1.8 %attend.4.refs_0_ = bf16[32,1152]{1,0:T(8,128)(2,1)S(1)} custom-call(s32[17]{0:T(128)S(1)} %stack.71.plan_ref, bf16[32,1152]{1,0:T(8,128)(2,1)S(1)} %pack.1.queries_ref.refs_0_, bf16[2048,128]{1,0:T(8,128)(2,1)S(1)} %bitcast.33, bf16[2048,128]{1,0:T(8,128)(2,1)S(1)} %bitcast.37, bf16[64,2048]{1,0:T(8,128)(2,1)S(1)} %sight.1.sight_ref, ...), custom_call_target="tpu_custom_call" | custom-call | flops 536870912 | bytes 1048576 | tf_op jit(solution)/shard_map/attend/pallas_call | solution.py:202
  20.8 3.7 %collective-permute-done.5.refs_3_ = bf16[32,1152]{1,0:T(8,128)(2,1)S(1)} collective-permute-done((bf16[32,1152]{1,0:T(8,128)(2,1)S(1)}, bf16[32,1152]{1,0:T(8,128)(2,1)S(1)}, u32[]{:S(2)}, u32[]{:S(2)}) %collective-permute-start.5) | collective-permute-done | bytes 73760 | tf_op jit(solution)/shard_map/ppermute | solution.py:68
  24.5 1.5 %project.1 = (bf16[32,512]{1,0:T(8,128)(2,1)S(1)}, bf16[32,512]{1,0:T(8,128)(2,1)S(1)}, bf16[32,512]{1,0:T(8,128)(2,1)S(1)}, bf16[32,512]{1,0:T(8,128)(2,1)S(1)}) custom-call(s32[17]{0:T(128)S(1)} %stack.71.plan_ref, bf16[32,1152]{1,0:T(8,128)(2,1)S(1)} %attend.4.refs_0_, bf16[32,1152]{1,0:T(8,128)(2,1)S(1)} %collective-permute-done.1.refs_1_, ...), custom_call_target="tpu_custom_call" | custom-call | flops 134217728 | bytes 4194304 | tf_op jit(solution)/shard_map/project/pallas_call | solution.py:246
  26.1 1.5 %collective-permute-start.7 = (bf16[32,512]{1,0:T(8,128)(2,1)S(1)}, bf16[32,512]{1,0:T(8,128)(2,1)S(1)}, u32[]{:S(2)}, u32[]{:S(2)}) collective-permute-start(bf16[32,512]{1,0:T(8,128)(2,1)S(1)} %get-tuple-element.25), channel_id=1, source_target_pairs={{0,2},{1,3},{2,0},{3,1},{4,6},{5,7},{6,4},{7,5},{8,10},{9,11},{10,... | collective-permute-start | bytes 98312 | tf_op jit(solution)/shard_map/ppermute | solution.py:68
  28.0 1.8 %collective-permute-done.6.refs_1_ = bf16[32,512]{1,0:T(8,128)(2,1)S(1)} collective-permute-done((bf16[32,512]{1,0:T(8,128)(2,1)S(1)}, bf16[32,512]{1,0:T(8,128)(2,1)S(1)}, u32[]{:S(2)}, u32[]{:S(2)}) %collective-permute-start.6) | collective-permute-done | bytes 32800 | tf_op jit(solution)/shard_map/ppermute | solution.py:68
  31.1 3.6 %collective-permute-start.9 = (bf16[32,640]{1,0:T(8,128)(2,1)S(1)}, bf16[32,640]{1,0:T(8,128)(2,1)S(1)}, u32[]{:S(2)}, u32[]{:S(2)}) collective-permute-start(bf16[32,640]{1,0:T(8,128)(2,1)S(1)} %get-tuple-element.29.refs_0_), channel_id=1, source_target_pairs={{0,4},{4,0},{8,12},{12,8},{1,5},{5,1},{9,13},{13,9},{2,6},{6,2},{1... | collective-permute-start | bytes 122888 | tf_op jit(solution)/shard_map/ppermute | solution.py:68
  37.6 1.8 %slice-done.4 = s8[4194304]{0:T(1024)(128)(4,1)S(1)} async-done(((s8[25165824]{0:T(1024)(128)(4,1)}), s8[4194304]{0:T(1024)(128)(4,1)S(1)}, s32[]{:S(2)}) %slice-start.4) | async-done | bytes 4194328
  40.7 1.7 %gate_up.5 = bf16[128,1664]{1,0:T(8,128)(2,1)S(1)} custom-call(s32[17]{0:T(128)S(1)} %stack.71.plan_ref, bf16[4,128,640]{2,1,0:T(8,128)(2,1)S(1)} %pick.1.picked_ref, bf16[16,512,1536]{2,1,0:T(8,128)(2,1)S(1)} %bitcast.27), custom_call_target="tpu_custom_call" | custom-call | flops 201326592 | bytes 6291456 | tf_op jit(solution)/shard_map/gate_up/pallas_call | solution.py:372
  42.4 1.7 %gate_up.4.left_ref = bf16[128,1664]{1,0:T(8,128)(2,1)S(1)} custom-call(s32[17]{0:T(128)S(1)} %stack.71.plan_ref, bf16[4,128,640]{2,1,0:T(8,128)(2,1)S(1)} %pick.1.picked_ref, bf16[16,512,1536]{2,1,0:T(8,128)(2,1)S(1)} %bitcast.27), custom_call_target="tpu_custom_call" | custom-call | flops 201326592 | bytes 6291456 | tf_op jit(solution)/shard_map/gate_up/pallas_call | solution.py:372
  45.6 1.7 %gate_up.6 = bf16[128,1664]{1,0:T(8,128)(2,1)S(1)} custom-call(s32[17]{0:T(128)S(1)} %stack.71.plan_ref, bf16[4,128,640]{2,1,0:T(8,128)(2,1)S(1)} %pick.1.picked_ref, bf16[16,512,1536]{2,1,0:T(8,128)(2,1)S(1)} %bitcast.27), custom_call_target="tpu_custom_call" | custom-call | flops 201326592 | bytes 6291456 | tf_op jit(solution)/shard_map/gate_up/pallas_call | solution.py:372
  47.5 1.7 %gate_up.7.refs_2_ = bf16[128,1664]{1,0:T(8,128)(2,1)S(1)} custom-call(s32[17]{0:T(128)S(1)} %stack.71.plan_ref, bf16[4,128,640]{2,1,0:T(8,128)(2,1)S(1)} %pick.1.picked_ref, bf16[16,512,1536]{2,1,0:T(8,128)(2,1)S(1)} %bitcast.27), custom_call_target="tpu_custom_call" | custom-call | flops 201326592 | bytes 6291456 | tf_op jit(solution)/shard_map/gate_up/pallas_call | solution.py:372
  49.2 7.5 %collective-permute-done.14.refs_3_ = bf16[128,1664]{1,0:T(8,128)(2,1)S(1)} collective-permute-done((bf16[128,1664]{1,0:T(8,128)(2,1)S(1)}, bf16[128,1664]{1,0:T(8,128)(2,1)S(1)}, u32[]{:S(2)}, u32[]{:S(2)}) %collective-permute-start.14) | collective-permute-done | bytes 426016 | tf_op jit(solution)/shard_map/ppermute | solution.py:68
  61.1 3.4 %collective-permute-done.15.hidden_ref = bf16[128,768]{1,0:T(8,128)(2,1)S(1)} collective-permute-done((bf16[128,768]{1,0:T(8,128)(2,1)S(1)}, bf16[128,768]{1,0:T(8,128)(2,1)S(1)}, u32[]{:S(2)}, u32[]{:S(2)}) %collective-permute-start.15) | collective-permute-done | bytes 196640 | tf_op jit(solution)/shard_map/ppermute | solution.py:68
  64.5 1.4 %down.6.refs_0_ = f32[128,512]{1,0:T(8,128)S(1)} custom-call(s32[17]{0:T(128)S(1)} %stack.71.plan_ref, bf16[128,768]{1,0:T(8,128)(2,1)S(1)} %collective-permute-done.15.hidden_ref, bf16[16,768,512]{2,1,0:T(8,128)(2,1)S(1)} %bitcast.29, bf16[4,128,128]{2,1,0:T(8,128)(2,1)S(1)} %get-tuple-element.33.high_ref, ...), custom_call_target="tpu_custom_call" | custom-call | flops 100663296 | bytes 3145728 | tf_op jit(solution)/shard_map/down/pallas_call | solution.py:447
  67.3 1.9 %collective-permute-start.18 = (bf16[32,512]{1,0:T(8,128)(2,1)S(1)}, bf16[32,512]{1,0:T(8,128)(2,1)S(1)}, u32[]{:S(2)}, u32[]{:S(2)}) collective-permute-start(bf16[32,512]{1,0:T(8,128)(2,1)S(1)} %get-tuple-element.38), channel_id=1, source_target_pairs={{0,12},{4,8},{8,4},{12,0},{1,13},{5,9},{9,5},{13,1},{2,14},{6,10},... | collective-permute-start | bytes 98312 | tf_op jit(solution)/shard_map/ppermute | solution.py:68
  70.3 1.4 %collective-permute-start.20 = (bf16[32,512]{1,0:T(8,128)(2,1)S(1)}, bf16[32,512]{1,0:T(8,128)(2,1)S(1)}, u32[]{:S(2)}, u32[]{:S(2)}) collective-permute-start(bf16[32,512]{1,0:T(8,128)(2,1)S(1)} %get-tuple-element.40), channel_id=1, source_target_pairs={{0,4},{4,0},{8,12},{12,8},{1,5},{5,1},{9,13},{13,9},{2,6},{6,2},{1... | collective-permute-start | bytes 98312 | tf_op jit(solution)/shard_map/ppermute | solution.py:68
  71.8 1.6 %collective-permute-done.18.refs_1_ = bf16[32,512]{1,0:T(8,128)(2,1)S(1)} collective-permute-done((bf16[32,512]{1,0:T(8,128)(2,1)S(1)}, bf16[32,512]{1,0:T(8,128)(2,1)S(1)}, u32[]{:S(2)}, u32[]{:S(2)}) %collective-permute-start.18) | collective-permute-done | bytes 32800 | tf_op jit(solution)/shard_map/ppermute | solution.py:68
  (71 shorter events, 19.9 us)
Async XLA Ops:
  1.0 7.3 %collective-permute-start = (bf16[32,1152]{1,0:T(8,128)(2,1)S(1)}, bf16[32,1152]{1,0:T(8,128)(2,1)S(1)}, u32[]{:S(2)}, u32[]{:S(2)}) collective-permute-start(bf16[32,1152]{1,0:T(8,128)(2,1)S(1)} %pack.1.queries_ref.refs_0_), channel_id=1, source_target_pairs={{0,4},{4,0},{8,12},{12,8},{1,5},{5,1},{9,13},{13,9},{2,6},{6,2},{1... | collective-permute-start | bytes 221192 | tf_op jit(solution)/shard_map/ppermute | solution.py:68
  4.0 7.8 %collective-permute-start.2 = (bf16[32,1152]{1,0:T(8,128)(2,1)S(1)}, bf16[32,1152]{1,0:T(8,128)(2,1)S(1)}, u32[]{:S(2)}, u32[]{:S(2)}) collective-permute-start(bf16[32,1152]{1,0:T(8,128)(2,1)S(1)} %pack.1.queries_ref.refs_0_), channel_id=1, source_target_pairs={{0,8},{4,12},{8,0},{12,4},{1,9},{5,13},{9,1},{13,5},{2,10},{6,14},... | collective-permute-start | bytes 221192 | tf_op jit(solution)/shard_map/ppermute | solution.py:68
  6.6 9.8 %collective-permute-start.4 = (bf16[32,1152]{1,0:T(8,128)(2,1)S(1)}, bf16[32,1152]{1,0:T(8,128)(2,1)S(1)}, u32[]{:S(2)}, u32[]{:S(2)}) collective-permute-start(bf16[32,1152]{1,0:T(8,128)(2,1)S(1)} %pack.1.queries_ref.refs_0_), channel_id=1, source_target_pairs={{0,12},{4,8},{8,4},{12,0},{1,13},{5,9},{9,5},{13,1},{2,14},{6,10},... | collective-permute-start | bytes 221192 | tf_op jit(solution)/shard_map/ppermute | solution.py:68
  10.1 10.7 %collective-permute-start.1 = (bf16[32,1152]{1,0:T(8,128)(2,1)S(1)}, bf16[32,1152]{1,0:T(8,128)(2,1)S(1)}, u32[]{:S(2)}, u32[]{:S(2)}) collective-permute-start(bf16[32,1152]{1,0:T(8,128)(2,1)S(1)} %attend.5), channel_id=1, source_target_pairs={{0,4},{4,0},{8,12},{12,8},{1,5},{5,1},{9,13},{13,9},{2,6},{6,2},{1... | collective-permute-start | bytes 221192 | tf_op jit(solution)/shard_map/ppermute | solution.py:68
  13.6 7.1 %collective-permute-start.3 = (bf16[32,1152]{1,0:T(8,128)(2,1)S(1)}, bf16[32,1152]{1,0:T(8,128)(2,1)S(1)}, u32[]{:S(2)}, u32[]{:S(2)}) collective-permute-start(bf16[32,1152]{1,0:T(8,128)(2,1)S(1)} %attend.6), channel_id=1, source_target_pairs={{0,8},{4,12},{8,0},{12,4},{1,9},{5,13},{9,1},{13,5},{2,10},{6,14},... | collective-permute-start | bytes 221192 | tf_op jit(solution)/shard_map/ppermute | solution.py:68
  18.3 6.2 %collective-permute-start.5 = (bf16[32,1152]{1,0:T(8,128)(2,1)S(1)}, bf16[32,1152]{1,0:T(8,128)(2,1)S(1)}, u32[]{:S(2)}, u32[]{:S(2)}) collective-permute-start(bf16[32,1152]{1,0:T(8,128)(2,1)S(1)} %attend.7), channel_id=1, source_target_pairs={{0,12},{4,8},{8,4},{12,0},{1,13},{5,9},{9,5},{13,1},{2,14},{6,10},... | collective-permute-start | bytes 221192 | tf_op jit(solution)/shard_map/ppermute | solution.py:68
  18.9 18.6 %slice-start = ((s8[25165824]{0:T(1024)(128)(4,1)}), s8[4194304]{0:T(1024)(128)(4,1)S(1)}, s32[]{:S(2)}) async-start(s8[25165824]{0:T(1024)(128)(4,1)} %bitcast.26), calls=%async_computation | async-start | bytes 8388608
  18.9 18.6 %slice-start.1 = ((s8[25165824]{0:T(1024)(128)(4,1)}), s8[4194304]{0:T(1024)(128)(4,1)S(1)}, s32[]{:S(2)}) async-start(s8[25165824]{0:T(1024)(128)(4,1)} %bitcast.26), calls=%async_computation.1 | async-start | bytes 8388608
  18.9 18.6 %slice-start.2 = ((s8[25165824]{0:T(1024)(128)(4,1)}), s8[4194304]{0:T(1024)(128)(4,1)S(1)}, s32[]{:S(2)}) async-start(s8[25165824]{0:T(1024)(128)(4,1)} %bitcast.26), calls=%async_computation.2 | async-start | bytes 8388608
  26.0 3.7 %collective-permute-start.6 = (bf16[32,512]{1,0:T(8,128)(2,1)S(1)}, bf16[32,512]{1,0:T(8,128)(2,1)S(1)}, u32[]{:S(2)}, u32[]{:S(2)}) collective-permute-start(bf16[32,512]{1,0:T(8,128)(2,1)S(1)} %get-tuple-element.24), channel_id=1, source_target_pairs={{0,3},{1,2},{2,1},{3,0},{4,7},{5,6},{6,5},{7,4},{8,11},{9,10},{10,... | collective-permute-start | bytes 98312 | tf_op jit(solution)/shard_map/ppermute | solution.py:68
  26.1 4.0 %collective-permute-start.7 = (bf16[32,512]{1,0:T(8,128)(2,1)S(1)}, bf16[32,512]{1,0:T(8,128)(2,1)S(1)}, u32[]{:S(2)}, u32[]{:S(2)}) collective-permute-start(bf16[32,512]{1,0:T(8,128)(2,1)S(1)} %get-tuple-element.25), channel_id=1, source_target_pairs={{0,2},{1,3},{2,0},{3,1},{4,6},{5,7},{6,4},{7,5},{8,10},{9,11},{10,... | collective-permute-start | bytes 98312 | tf_op jit(solution)/shard_map/ppermute | solution.py:68
  27.6 2.5 %collective-permute-start.8 = (bf16[32,512]{1,0:T(8,128)(2,1)S(1)}, bf16[32,512]{1,0:T(8,128)(2,1)S(1)}, u32[]{:S(2)}, u32[]{:S(2)}) collective-permute-start(bf16[32,512]{1,0:T(8,128)(2,1)S(1)} %get-tuple-element.26), channel_id=1, source_target_pairs={{0,1},{1,0},{2,3},{3,2},{4,5},{5,4},{6,7},{7,6},{8,9},{9,8},{10,11... | collective-permute-start | bytes 98312 | tf_op jit(solution)/shard_map/ppermute | solution.py:68
  30.2 6.3 %collective-permute-start.11 = (bf16[32,640]{1,0:T(8,128)(2,1)S(1)}, bf16[32,640]{1,0:T(8,128)(2,1)S(1)}, u32[]{:S(2)}, u32[]{:S(2)}) collective-permute-start(bf16[32,640]{1,0:T(8,128)(2,1)S(1)} %get-tuple-element.29.refs_0_), channel_id=1, source_target_pairs={{0,12},{4,8},{8,4},{12,0},{1,13},{5,9},{9,5},{13,1},{2,14},{6,10},... | collective-permute-start | bytes 122888 | tf_op jit(solution)/shard_map/ppermute | solution.py:68
  31.0 6.0 %collective-permute-start.10 = (bf16[32,640]{1,0:T(8,128)(2,1)S(1)}, bf16[32,640]{1,0:T(8,128)(2,1)S(1)}, u32[]{:S(2)}, u32[]{:S(2)}) collective-permute-start(bf16[32,640]{1,0:T(8,128)(2,1)S(1)} %get-tuple-element.29.refs_0_), channel_id=1, source_target_pairs={{0,8},{4,12},{8,0},{12,4},{1,9},{5,13},{9,1},{13,5},{2,10},{6,14},... | collective-permute-start | bytes 122888 | tf_op jit(solution)/shard_map/ppermute | solution.py:68
  31.1 6.1 %collective-permute-start.9 = (bf16[32,640]{1,0:T(8,128)(2,1)S(1)}, bf16[32,640]{1,0:T(8,128)(2,1)S(1)}, u32[]{:S(2)}, u32[]{:S(2)}) collective-permute-start(bf16[32,640]{1,0:T(8,128)(2,1)S(1)} %get-tuple-element.29.refs_0_), channel_id=1, source_target_pairs={{0,4},{4,0},{8,12},{12,8},{1,5},{5,1},{9,13},{13,9},{2,6},{6,2},{1... | collective-permute-start | bytes 122888 | tf_op jit(solution)/shard_map/ppermute | solution.py:68
  42.4 1.8 %collective-permute-start.12 = (bf16[128,1664]{1,0:T(8,128)(2,1)S(1)}, bf16[128,1664]{1,0:T(8,128)(2,1)S(1)}, u32[]{:S(2)}, u32[]{:S(2)}) collective-permute-start(bf16[128,1664]{1,0:T(8,128)(2,1)S(1)} %gate_up.5), channel_id=1, source_target_pairs={{0,1},{1,0},{2,3},{3,2},{4,5},{5,4},{6,7},{7,6},{8,9},{9,8},{10,11... | collective-permute-start | bytes 1277960 | tf_op jit(solution)/shard_map/ppermute | solution.py:68
  44.5 12.3 %collective-permute-start.14 = (bf16[128,1664]{1,0:T(8,128)(2,1)S(1)}, bf16[128,1664]{1,0:T(8,128)(2,1)S(1)}, u32[]{:S(2)}, u32[]{:S(2)}) collective-permute-start(bf16[128,1664]{1,0:T(8,128)(2,1)S(1)} %join.1), channel_id=1, source_target_pairs={{0,2},{2,0},{1,3},{3,1},{4,6},{6,4},{5,7},{7,5},{8,10},{10,8},{9,1... | collective-permute-start | bytes 1277960 | tf_op jit(solution)/shard_map/ppermute | solution.py:68
  47.3 9.4 %collective-permute-start.13 = (bf16[128,1664]{1,0:T(8,128)(2,1)S(1)}, bf16[128,1664]{1,0:T(8,128)(2,1)S(1)}, u32[]{:S(2)}, u32[]{:S(2)}) collective-permute-start(bf16[128,1664]{1,0:T(8,128)(2,1)S(1)} %gate_up.6), channel_id=1, source_target_pairs={{0,1},{1,0},{2,3},{3,2},{4,5},{5,4},{6,7},{7,6},{8,9},{9,8},{10,11... | collective-permute-start | bytes 1277960 | tf_op jit(solution)/shard_map/ppermute | solution.py:68
  57.1 2.6 %collective-permute-start.16 = (bf16[128,768]{1,0:T(8,128)(2,1)S(1)}, bf16[128,768]{1,0:T(8,128)(2,1)S(1)}, u32[]{:S(2)}, u32[]{:S(2)}) collective-permute-start(bf16[128,768]{1,0:T(8,128)(2,1)S(1)} %hidden.1.hidden_ref), channel_id=1, source_target_pairs={{0,1},{1,0},{2,3},{3,2},{4,5},{5,4},{6,7},{7,6},{8,9},{9,8},{10,11... | collective-permute-start | bytes 589832 | tf_op jit(solution)/shard_map/ppermute | solution.py:68
  57.2 7.3 %collective-permute-start.15 = (bf16[128,768]{1,0:T(8,128)(2,1)S(1)}, bf16[128,768]{1,0:T(8,128)(2,1)S(1)}, u32[]{:S(2)}, u32[]{:S(2)}) collective-permute-start(bf16[128,768]{1,0:T(8,128)(2,1)S(1)} %hidden.1.hidden_ref), channel_id=1, source_target_pairs={{0,2},{2,0},{1,3},{3,1},{4,6},{6,4},{5,7},{7,5},{8,10},{10,8},{9,1... | collective-permute-start | bytes 589832 | tf_op jit(solution)/shard_map/ppermute | solution.py:68
  64.5 1.4 %collective-permute-start.17 = (bf16[128,768]{1,0:T(8,128)(2,1)S(1)}, bf16[128,768]{1,0:T(8,128)(2,1)S(1)}, u32[]{:S(2)}, u32[]{:S(2)}) collective-permute-start(bf16[128,768]{1,0:T(8,128)(2,1)S(1)} %collective-permute-done.15.hidden_ref), channel_id=1, source_target_pairs={{0,1},{1,0},{2,3},{3,2},{4,5},{5,4},{6,7},{7,6},{8,9},{9,8},{10,11... | collective-permute-start | bytes 589832 | tf_op jit(solution)/shard_map/ppermute | solution.py:68
  67.3 6.0 %collective-permute-start.18 = (bf16[32,512]{1,0:T(8,128)(2,1)S(1)}, bf16[32,512]{1,0:T(8,128)(2,1)S(1)}, u32[]{:S(2)}, u32[]{:S(2)}) collective-permute-start(bf16[32,512]{1,0:T(8,128)(2,1)S(1)} %get-tuple-element.38), channel_id=1, source_target_pairs={{0,12},{4,8},{8,4},{12,0},{1,13},{5,9},{9,5},{13,1},{2,14},{6,10},... | collective-permute-start | bytes 98312 | tf_op jit(solution)/shard_map/ppermute | solution.py:68
  69.2 5.2 %collective-permute-start.19 = (bf16[32,512]{1,0:T(8,128)(2,1)S(1)}, bf16[32,512]{1,0:T(8,128)(2,1)S(1)}, u32[]{:S(2)}, u32[]{:S(2)}) collective-permute-start(bf16[32,512]{1,0:T(8,128)(2,1)S(1)} %get-tuple-element.39), channel_id=1, source_target_pairs={{0,8},{4,12},{8,0},{12,4},{1,9},{5,13},{9,1},{13,5},{2,10},{6,14},... | collective-permute-start | bytes 98312 | tf_op jit(solution)/shard_map/ppermute | solution.py:68
  70.3 4.4 %collective-permute-start.20 = (bf16[32,512]{1,0:T(8,128)(2,1)S(1)}, bf16[32,512]{1,0:T(8,128)(2,1)S(1)}, u32[]{:S(2)}, u32[]{:S(2)}) collective-permute-start(bf16[32,512]{1,0:T(8,128)(2,1)S(1)} %get-tuple-element.40), channel_id=1, source_target_pairs={{0,4},{4,0},{8,12},{12,8},{1,5},{5,1},{9,13},{13,9},{2,6},{6,2},{1... | collective-permute-start | bytes 98312 | tf_op jit(solution)/shard_map/ppermute | solution.py:68
  (11 other events, 80.2 us)

commit v5 on v4

--- a/solution.py
+++ b/solution.py
@@ -325,7 +325,7 @@
     )(plan, *packed)
 
 
-def pick_kernel(beside_ref, place_ref, *refs):
+def pick_kernel(place_ref, *refs):
     rows_refs, (out_ref, rows_ref) = refs[:-2], refs[-2:]
     rows = rows_refs[0].shape[0]
     for i, ref in enumerate(rows_refs):
@@ -334,18 +334,17 @@
         out_ref[piece] = dot(place_ref[piece], rows_ref[...], ((0,), (0,))).astype(bf16)
 
 
-def pick(place, rows, beside):
+def pick(place, rows):
     piece_count, tokens, slots = place.shape
     columns = rows[0].shape[1]
     return pl.pallas_call(
         pick_kernel,
-        in_specs=[whole(pltpu.HBM)] + [whole()] * (1 + len(rows)),
         out_shape=jax.ShapeDtypeStruct((piece_count, slots, columns), bf16),
         scratch_shapes=[pltpu.VMEM((tokens, columns), bf16)],
         compiler_params=params(8),
         cost_estimate=cost(2**26, 2**20),
         name="pick",
-    )(*in_hbm([beside]), place, *rows)
+    )(place, *rows)
 
 
 def squares_joined(squares):
@@ -563,7 +562,7 @@
     rows = {0: sent}
     for k in far_first(ctx_count):
         rows[k] = swapped(sent, "ctx", k)
-    picked = pick(place, [rows[k] for k in range(ctx_count)], gate_up_weight)
+    picked = pick(place, [rows[k] for k in range(ctx_count)])
 
     def first_half(piece_at):
         return gate_up(plan, piece_at, piece_at + expert_at, spread, picked, gate_up_weight)

time: 75.5 us -> 72.6 us (0.962)
  local copies, waits for them, and re-layouts: 3.22 us -> 0.17 us
    unnamed x28, local copies, waits for them, and re-layouts: 3.12 us -> 0.07 us
  transfers between devices with their start and end apart: 21 -> 21, of which waited for: 13 -> 13; matrix products, arithmetic and copies ran while one was open for 0% -> 0% of each run, Pallas kernels for 25% -> 26%
where the time goes in v5:
time: 72.6 us; the launch traced here: 72.4 us
  Pallas kernels  26.5 us (37%)
  starting transfers between devices  23.5 us (32%)
  waiting for transfers between devices  21.9 us (30%)
    ppermute x21, starting transfers between devices, swapped(): return lax.ppermute(value, axes, pairs)  23.5 us
    ppermute x21, waiting for transfers between devices, swapped(): return lax.ppermute(value, axes, pairs)  21.9 us
    pallas_call x4, Pallas kernels, attend(): pl.pallas_call(functools.partial(attend_kernel, heads, scale, lead_at), i...  7.27 us
    pallas_call x4, Pallas kernels, gate_up(): pl.pallas_call(kernel, in_specs=[whole(pltpu.SMEM)] + [whole()] * 2, out_...  6.86 us
    pallas_call x4, Pallas kernels, down(): pl.pallas_call(kernel, in_specs=[whole(pltpu.SMEM)] + [whole()] * (4 + le...  5.53 us
    pallas_call x1, Pallas kernels, project(): pl.pallas_call(functools.partial(project_kernel, heads, scale, order_at,...  1.55 us
  transfers between devices with their start and end apart: 21, of which 13 were waited for; matrix products, arithmetic and copies ran while one was open for 0% of the time, Pallas kernels for 26%

profile of v5, /device:TPU:0, one launch (start us, length us, event | category | flops | bytes accessed | tf_op | source)
XLA Modules:
  0.0 72.4 jit_solution(9947072926242432597)
XLA Ops:
  1.0 3.1 %collective-permute-start = (bf16[32,1152]{1,0:T(8,128)(2,1)S(1)}, bf16[32,1152]{1,0:T(8,128)(2,1)S(1)}, u32[]{:S(2)}, u32[]{:S(2)}) collective-permute-start(bf16[32,1152]{1,0:T(8,128)(2,1)S(1)} %pack.1.queries_ref.refs_0_), channel_id=1, source_target_pairs={{0,4},{4,0},{8,12},{12,8},{1,5},{5,1},{9,13},{13,9},{2,6},{6,2},{1... | collective-permute-start | bytes 221192 | tf_op jit(solution)/shard_map/ppermute | solution.py:68
  4.0 2.6 %collective-permute-start.2 = (bf16[32,1152]{1,0:T(8,128)(2,1)S(1)}, bf16[32,1152]{1,0:T(8,128)(2,1)S(1)}, u32[]{:S(2)}, u32[]{:S(2)}) collective-permute-start(bf16[32,1152]{1,0:T(8,128)(2,1)S(1)} %pack.1.queries_ref.refs_0_), channel_id=1, source_target_pairs={{0,8},{4,12},{8,0},{12,4},{1,9},{5,13},{9,1},{13,5},{2,10},{6,14},... | collective-permute-start | bytes 221192 | tf_op jit(solution)/shard_map/ppermute | solution.py:68
  6.8 1.4 %sight.1.sight_ref = bf16[64,2048]{1,0:T(8,128)(2,1)S(1)} custom-call(s32[1,64]{1,0:T(1,128)} %bitcast.44, s32[1,2048]{1,0:T(1,128)} %bitcast.40, bf16[16,512,1536]{2,1,0:T(8,128)(2,1)} %refs_0_.1), custom_call_target="tpu_custom_call" | custom-call | flops 16777216 | bytes 524288 | tf_op jit(solution)/shard_map/sight/pallas_call | solution.py:147
  8.2 1.8 %attend.5 = bf16[32,1152]{1,0:T(8,128)(2,1)S(1)} custom-call(s32[17]{0:T(128)S(1)} %stack.71.plan_ref, bf16[32,1152]{1,0:T(8,128)(2,1)S(1)} %collective-permute-done.queries_ref.refs_1_, bf16[2048,128]{1,0:T(8,128)(2,1)S(1)} %bitcast.30, bf16[2048,128]{1,0:T(8,128)(2,1)S(1)} %bitcast.34, bf16[64,2048]{1,0:T(8,128)(2,1)S(1)} %sight.1.sight_ref, ...), custom_call_target="tpu_custom_call" | custom-call | flops 536870912 | bytes 1048576 | tf_op jit(solution)/shard_map/attend/pallas_call | solution.py:202
  11.8 1.8 %attend.6 = bf16[32,1152]{1,0:T(8,128)(2,1)S(1)} custom-call(s32[17]{0:T(128)S(1)} %stack.71.plan_ref, bf16[32,1152]{1,0:T(8,128)(2,1)S(1)} %collective-permute-done.2.queries_ref.refs_2_, bf16[2048,128]{1,0:T(8,128)(2,1)S(1)} %bitcast.31, bf16[2048,128]{1,0:T(8,128)(2,1)S(1)} %bitcast.35, bf16[64,2048]{1,0:T(8,128)(2,1)S(1)} %sight.1.sight_ref, ...), custom_call_target="tpu_custom_call" | custom-call | flops 536870912 | bytes 1048576 | tf_op jit(solution)/shard_map/attend/pallas_call | solution.py:202
  13.6 2.8 %collective-permute-start.3 = (bf16[32,1152]{1,0:T(8,128)(2,1)S(1)}, bf16[32,1152]{1,0:T(8,128)(2,1)S(1)}, u32[]{:S(2)}, u32[]{:S(2)}) collective-permute-start(bf16[32,1152]{1,0:T(8,128)(2,1)S(1)} %attend.6), channel_id=1, source_target_pairs={{0,8},{4,12},{8,0},{12,4},{1,9},{5,13},{9,1},{13,5},{2,10},{6,14},... | collective-permute-start | bytes 221192 | tf_op jit(solution)/shard_map/ppermute | solution.py:68
  16.4 1.8 %attend.7 = bf16[32,1152]{1,0:T(8,128)(2,1)S(1)} custom-call(s32[17]{0:T(128)S(1)} %stack.71.plan_ref, bf16[32,1152]{1,0:T(8,128)(2,1)S(1)} %collective-permute-done.4.queries_ref.refs_3_, bf16[2048,128]{1,0:T(8,128)(2,1)S(1)} %bitcast.32, bf16[2048,128]{1,0:T(8,128)(2,1)S(1)} %bitcast.36, bf16[64,2048]{1,0:T(8,128)(2,1)S(1)} %sight.1.sight_ref, ...), custom_call_target="tpu_custom_call" | custom-call | flops 536870912 | bytes 1048576 | tf_op jit(solution)/shard_map/attend/pallas_call | solution.py:202
  19.0 1.8 %attend.4.refs_0_ = bf16[32,1152]{1,0:T(8,128)(2,1)S(1)} custom-call(s32[17]{0:T(128)S(1)} %stack.71.plan_ref, bf16[32,1152]{1,0:T(8,128)(2,1)S(1)} %pack.1.queries_ref.refs_0_, bf16[2048,128]{1,0:T(8,128)(2,1)S(1)} %bitcast.33, bf16[2048,128]{1,0:T(8,128)(2,1)S(1)} %bitcast.37, bf16[64,2048]{1,0:T(8,128)(2,1)S(1)} %sight.1.sight_ref, ...), custom_call_target="tpu_custom_call" | custom-call | flops 536870912 | bytes 1048576 | tf_op jit(solution)/shard_map/attend/pallas_call | solution.py:202
  20.9 3.7 %collective-permute-done.5.refs_3_ = bf16[32,1152]{1,0:T(8,128)(2,1)S(1)} collective-permute-done((bf16[32,1152]{1,0:T(8,128)(2,1)S(1)}, bf16[32,1152]{1,0:T(8,128)(2,1)S(1)}, u32[]{:S(2)}, u32[]{:S(2)}) %collective-permute-start.5) | collective-permute-done | bytes 73760 | tf_op jit(solution)/shard_map/ppermute | solution.py:68
  24.5 1.5 %project.1 = (bf16[32,512]{1,0:T(8,128)(2,1)S(1)}, bf16[32,512]{1,0:T(8,128)(2,1)S(1)}, bf16[32,512]{1,0:T(8,128)(2,1)S(1)}, bf16[32,512]{1,0:T(8,128)(2,1)S(1)}) custom-call(s32[17]{0:T(128)S(1)} %stack.71.plan_ref, bf16[32,1152]{1,0:T(8,128)(2,1)S(1)} %attend.4.refs_0_, bf16[32,1152]{1,0:T(8,128)(2,1)S(1)} %collective-permute-done.1.refs_1_, ...), custom_call_target="tpu_custom_call" | custom-call | flops 134217728 | bytes 4194304 | tf_op jit(solution)/shard_map/project/pallas_call | solution.py:246
  26.1 1.6 %collective-permute-start.7 = (bf16[32,512]{1,0:T(8,128)(2,1)S(1)}, bf16[32,512]{1,0:T(8,128)(2,1)S(1)}, u32[]{:S(2)}, u32[]{:S(2)}) collective-permute-start(bf16[32,512]{1,0:T(8,128)(2,1)S(1)} %get-tuple-element.25), channel_id=1, source_target_pairs={{0,2},{1,3},{2,0},{3,1},{4,6},{5,7},{6,4},{7,5},{8,10},{9,11},{10,... | collective-permute-start | bytes 98312 | tf_op jit(solution)/shard_map/ppermute | solution.py:68
  28.0 1.8 %collective-permute-done.6.refs_1_ = bf16[32,512]{1,0:T(8,128)(2,1)S(1)} collective-permute-done((bf16[32,512]{1,0:T(8,128)(2,1)S(1)}, bf16[32,512]{1,0:T(8,128)(2,1)S(1)}, u32[]{:S(2)}, u32[]{:S(2)}) %collective-permute-start.6) | collective-permute-done | bytes 32800 | tf_op jit(solution)/shard_map/ppermute | solution.py:68
  31.1 3.6 %collective-permute-start.9 = (bf16[32,640]{1,0:T(8,128)(2,1)S(1)}, bf16[32,640]{1,0:T(8,128)(2,1)S(1)}, u32[]{:S(2)}, u32[]{:S(2)}) collective-permute-start(bf16[32,640]{1,0:T(8,128)(2,1)S(1)} %get-tuple-element.29.refs_0_), channel_id=1, source_target_pairs={{0,4},{4,0},{8,12},{12,8},{1,5},{5,1},{9,13},{13,9},{2,6},{6,2},{1... | collective-permute-start | bytes 122888 | tf_op jit(solution)/shard_map/ppermute | solution.py:68
  37.7 1.7 %gate_up.5 = bf16[128,1664]{1,0:T(8,128)(2,1)S(1)} custom-call(s32[17]{0:T(128)S(1)} %stack.71.plan_ref, bf16[4,128,640]{2,1,0:T(8,128)(2,1)S(1)} %pick.1.picked_ref, bf16[16,512,1536]{2,1,0:T(8,128)(2,1)S(1)} %bitcast.27), custom_call_target="tpu_custom_call" | custom-call | flops 201326592 | bytes 6291456 | tf_op jit(solution)/shard_map/gate_up/pallas_call | solution.py:371
  39.4 1.7 %gate_up.4.left_ref = bf16[128,1664]{1,0:T(8,128)(2,1)S(1)} custom-call(s32[17]{0:T(128)S(1)} %stack.71.plan_ref, bf16[4,128,640]{2,1,0:T(8,128)(2,1)S(1)} %pick.1.picked_ref, bf16[16,512,1536]{2,1,0:T(8,128)(2,1)S(1)} %bitcast.27), custom_call_target="tpu_custom_call" | custom-call | flops 201326592 | bytes 6291456 | tf_op jit(solution)/shard_map/gate_up/pallas_call | solution.py:371
  42.6 1.7 %gate_up.6 = bf16[128,1664]{1,0:T(8,128)(2,1)S(1)} custom-call(s32[17]{0:T(128)S(1)} %stack.71.plan_ref, bf16[4,128,640]{2,1,0:T(8,128)(2,1)S(1)} %pick.1.picked_ref, bf16[16,512,1536]{2,1,0:T(8,128)(2,1)S(1)} %bitcast.27), custom_call_target="tpu_custom_call" | custom-call | flops 201326592 | bytes 6291456 | tf_op jit(solution)/shard_map/gate_up/pallas_call | solution.py:371
  44.6 1.7 %gate_up.7.refs_2_ = bf16[128,1664]{1,0:T(8,128)(2,1)S(1)} custom-call(s32[17]{0:T(128)S(1)} %stack.71.plan_ref, bf16[4,128,640]{2,1,0:T(8,128)(2,1)S(1)} %pick.1.picked_ref, bf16[16,512,1536]{2,1,0:T(8,128)(2,1)S(1)} %bitcast.27), custom_call_target="tpu_custom_call" | custom-call | flops 201326592 | bytes 6291456 | tf_op jit(solution)/shard_map/gate_up/pallas_call | solution.py:371
  46.3 7.5 %collective-permute-done.14.refs_3_ = bf16[128,1664]{1,0:T(8,128)(2,1)S(1)} collective-permute-done((bf16[128,1664]{1,0:T(8,128)(2,1)S(1)}, bf16[128,1664]{1,0:T(8,128)(2,1)S(1)}, u32[]{:S(2)}, u32[]{:S(2)}) %collective-permute-start.14) | collective-permute-done | bytes 426016 | tf_op jit(solution)/shard_map/ppermute | solution.py:68
  58.1 3.4 %collective-permute-done.15.hidden_ref = bf16[128,768]{1,0:T(8,128)(2,1)S(1)} collective-permute-done((bf16[128,768]{1,0:T(8,128)(2,1)S(1)}, bf16[128,768]{1,0:T(8,128)(2,1)S(1)}, u32[]{:S(2)}, u32[]{:S(2)}) %collective-permute-start.15) | collective-permute-done | bytes 196640 | tf_op jit(solution)/shard_map/ppermute | solution.py:68
  61.5 1.4 %down.6.refs_0_ = f32[128,512]{1,0:T(8,128)S(1)} custom-call(s32[17]{0:T(128)S(1)} %stack.71.plan_ref, bf16[128,768]{1,0:T(8,128)(2,1)S(1)} %collective-permute-done.15.hidden_ref, bf16[16,768,512]{2,1,0:T(8,128)(2,1)S(1)} %bitcast.29, bf16[4,128,128]{2,1,0:T(8,128)(2,1)S(1)} %get-tuple-element.33.high_ref, ...), custom_call_target="tpu_custom_call" | custom-call | flops 100663296 | bytes 3145728 | tf_op jit(solution)/shard_map/down/pallas_call | solution.py:446
  62.9 1.4 %down.7 = (bf16[32,512]{1,0:T(8,128)(2,1)S(1)}, bf16[32,512]{1,0:T(8,128)(2,1)S(1)}, bf16[32,512]{1,0:T(8,128)(2,1)S(1)}, bf16[32,512]{1,0:T(8,128)(2,1)S(1)}) custom-call(s32[17]{0:T(128)S(1)} %stack.71.plan_ref, bf16[128,768]{1,0:T(8,128)(2,1)S(1)} %collective-permute-done.17.hidden_ref, bf16[16,768,512]{2,1,0:T(8,128)(2,1)S(1)} %bitcast.29, ...), custom_call_target="tpu_custom_call" | custom-call | flops 100663296 | bytes 3145728 | tf_op jit(solution)/shard_map/down/pallas_call | solution.py:446
  64.3 1.9 %collective-permute-start.18 = (bf16[32,512]{1,0:T(8,128)(2,1)S(1)}, bf16[32,512]{1,0:T(8,128)(2,1)S(1)}, u32[]{:S(2)}, u32[]{:S(2)}) collective-permute-start(bf16[32,512]{1,0:T(8,128)(2,1)S(1)} %get-tuple-element.38), channel_id=1, source_target_pairs={{0,12},{4,8},{8,4},{12,0},{1,13},{5,9},{9,5},{13,1},{2,14},{6,10},... | collective-permute-start | bytes 98312 | tf_op jit(solution)/shard_map/ppermute | solution.py:68
  67.3 1.4 %collective-permute-start.20 = (bf16[32,512]{1,0:T(8,128)(2,1)S(1)}, bf16[32,512]{1,0:T(8,128)(2,1)S(1)}, u32[]{:S(2)}, u32[]{:S(2)}) collective-permute-start(bf16[32,512]{1,0:T(8,128)(2,1)S(1)} %get-tuple-element.40), channel_id=1, source_target_pairs={{0,4},{4,0},{8,12},{12,8},{1,5},{5,1},{9,13},{13,9},{2,6},{6,2},{1... | collective-permute-start | bytes 98312 | tf_op jit(solution)/shard_map/ppermute | solution.py:68
  68.8 1.6 %collective-permute-done.18.refs_1_ = bf16[32,512]{1,0:T(8,128)(2,1)S(1)} collective-permute-done((bf16[32,512]{1,0:T(8,128)(2,1)S(1)}, bf16[32,512]{1,0:T(8,128)(2,1)S(1)}, u32[]{:S(2)}, u32[]{:S(2)}) %collective-permute-start.18) | collective-permute-done | bytes 32800 | tf_op jit(solution)/shard_map/ppermute | solution.py:68
  (71 shorter events, 17.4 us)
Async XLA Ops:
  1.0 7.3 %collective-permute-start = (bf16[32,1152]{1,0:T(8,128)(2,1)S(1)}, bf16[32,1152]{1,0:T(8,128)(2,1)S(1)}, u32[]{:S(2)}, u32[]{:S(2)}) collective-permute-start(bf16[32,1152]{1,0:T(8,128)(2,1)S(1)} %pack.1.queries_ref.refs_0_), channel_id=1, source_target_pairs={{0,4},{4,0},{8,12},{12,8},{1,5},{5,1},{9,13},{13,9},{2,6},{6,2},{1... | collective-permute-start | bytes 221192 | tf_op jit(solution)/shard_map/ppermute | solution.py:68
  4.0 7.8 %collective-permute-start.2 = (bf16[32,1152]{1,0:T(8,128)(2,1)S(1)}, bf16[32,1152]{1,0:T(8,128)(2,1)S(1)}, u32[]{:S(2)}, u32[]{:S(2)}) collective-permute-start(bf16[32,1152]{1,0:T(8,128)(2,1)S(1)} %pack.1.queries_ref.refs_0_), channel_id=1, source_target_pairs={{0,8},{4,12},{8,0},{12,4},{1,9},{5,13},{9,1},{13,5},{2,10},{6,14},... | collective-permute-start | bytes 221192 | tf_op jit(solution)/shard_map/ppermute | solution.py:68
  6.6 9.8 %collective-permute-start.4 = (bf16[32,1152]{1,0:T(8,128)(2,1)S(1)}, bf16[32,1152]{1,0:T(8,128)(2,1)S(1)}, u32[]{:S(2)}, u32[]{:S(2)}) collective-permute-start(bf16[32,1152]{1,0:T(8,128)(2,1)S(1)} %pack.1.queries_ref.refs_0_), channel_id=1, source_target_pairs={{0,12},{4,8},{8,4},{12,0},{1,13},{5,9},{9,5},{13,1},{2,14},{6,10},... | collective-permute-start | bytes 221192 | tf_op jit(solution)/shard_map/ppermute | solution.py:68
  10.1 10.8 %collective-permute-start.1 = (bf16[32,1152]{1,0:T(8,128)(2,1)S(1)}, bf16[32,1152]{1,0:T(8,128)(2,1)S(1)}, u32[]{:S(2)}, u32[]{:S(2)}) collective-permute-start(bf16[32,1152]{1,0:T(8,128)(2,1)S(1)} %attend.5), channel_id=1, source_target_pairs={{0,4},{4,0},{8,12},{12,8},{1,5},{5,1},{9,13},{13,9},{2,6},{6,2},{1... | collective-permute-start | bytes 221192 | tf_op jit(solution)/shard_map/ppermute | solution.py:68
  13.6 7.2 %collective-permute-start.3 = (bf16[32,1152]{1,0:T(8,128)(2,1)S(1)}, bf16[32,1152]{1,0:T(8,128)(2,1)S(1)}, u32[]{:S(2)}, u32[]{:S(2)}) collective-permute-start(bf16[32,1152]{1,0:T(8,128)(2,1)S(1)} %attend.6), channel_id=1, source_target_pairs={{0,8},{4,12},{8,0},{12,4},{1,9},{5,13},{9,1},{13,5},{2,10},{6,14},... | collective-permute-start | bytes 221192 | tf_op jit(solution)/shard_map/ppermute | solution.py:68
  16.4 21.2 %slice-start = ((s8[25165824]{0:T(1024)(128)(4,1)}), s8[4194304]{0:T(1024)(128)(4,1)S(1)}, s32[]{:S(2)}) async-start(s8[25165824]{0:T(1024)(128)(4,1)} %bitcast.26), calls=%async_computation | async-start | bytes 8388608
  16.4 21.2 %slice-start.1 = ((s8[25165824]{0:T(1024)(128)(4,1)}), s8[4194304]{0:T(1024)(128)(4,1)S(1)}, s32[]{:S(2)}) async-start(s8[25165824]{0:T(1024)(128)(4,1)} %bitcast.26), calls=%async_computation.1 | async-start | bytes 8388608
  16.4 21.2 %slice-start.2 = ((s8[25165824]{0:T(1024)(128)(4,1)}), s8[4194304]{0:T(1024)(128)(4,1)S(1)}, s32[]{:S(2)}) async-start(s8[25165824]{0:T(1024)(128)(4,1)} %bitcast.26), calls=%async_computation.2 | async-start | bytes 8388608
  18.3 6.2 %collective-permute-start.5 = (bf16[32,1152]{1,0:T(8,128)(2,1)S(1)}, bf16[32,1152]{1,0:T(8,128)(2,1)S(1)}, u32[]{:S(2)}, u32[]{:S(2)}) collective-permute-start(bf16[32,1152]{1,0:T(8,128)(2,1)S(1)} %attend.7), channel_id=1, source_target_pairs={{0,12},{4,8},{8,4},{12,0},{1,13},{5,9},{9,5},{13,1},{2,14},{6,10},... | collective-permute-start | bytes 221192 | tf_op jit(solution)/shard_map/ppermute | solution.py:68
  26.1 3.7 %collective-permute-start.6 = (bf16[32,512]{1,0:T(8,128)(2,1)S(1)}, bf16[32,512]{1,0:T(8,128)(2,1)S(1)}, u32[]{:S(2)}, u32[]{:S(2)}) collective-permute-start(bf16[32,512]{1,0:T(8,128)(2,1)S(1)} %get-tuple-element.24), channel_id=1, source_target_pairs={{0,3},{1,2},{2,1},{3,0},{4,7},{5,6},{6,5},{7,4},{8,11},{9,10},{10,... | collective-permute-start | bytes 98312 | tf_op jit(solution)/shard_map/ppermute | solution.py:68
  26.1 4.0 %collective-permute-start.7 = (bf16[32,512]{1,0:T(8,128)(2,1)S(1)}, bf16[32,512]{1,0:T(8,128)(2,1)S(1)}, u32[]{:S(2)}, u32[]{:S(2)}) collective-permute-start(bf16[32,512]{1,0:T(8,128)(2,1)S(1)} %get-tuple-element.25), channel_id=1, source_target_pairs={{0,2},{1,3},{2,0},{3,1},{4,6},{5,7},{6,4},{7,5},{8,10},{9,11},{10,... | collective-permute-start | bytes 98312 | tf_op jit(solution)/shard_map/ppermute | solution.py:68
  27.7 2.5 %collective-permute-start.8 = (bf16[32,512]{1,0:T(8,128)(2,1)S(1)}, bf16[32,512]{1,0:T(8,128)(2,1)S(1)}, u32[]{:S(2)}, u32[]{:S(2)}) collective-permute-start(bf16[32,512]{1,0:T(8,128)(2,1)S(1)} %get-tuple-element.26), channel_id=1, source_target_pairs={{0,1},{1,0},{2,3},{3,2},{4,5},{5,4},{6,7},{7,6},{8,9},{9,8},{10,11... | collective-permute-start | bytes 98312 | tf_op jit(solution)/shard_map/ppermute | solution.py:68
  30.3 6.3 %collective-permute-start.11 = (bf16[32,640]{1,0:T(8,128)(2,1)S(1)}, bf16[32,640]{1,0:T(8,128)(2,1)S(1)}, u32[]{:S(2)}, u32[]{:S(2)}) collective-permute-start(bf16[32,640]{1,0:T(8,128)(2,1)S(1)} %get-tuple-element.29.refs_0_), channel_id=1, source_target_pairs={{0,12},{4,8},{8,4},{12,0},{1,13},{5,9},{9,5},{13,1},{2,14},{6,10},... | collective-permute-start | bytes 122888 | tf_op jit(solution)/shard_map/ppermute | solution.py:68
  31.1 6.0 %collective-permute-start.10 = (bf16[32,640]{1,0:T(8,128)(2,1)S(1)}, bf16[32,640]{1,0:T(8,128)(2,1)S(1)}, u32[]{:S(2)}, u32[]{:S(2)}) collective-permute-start(bf16[32,640]{1,0:T(8,128)(2,1)S(1)} %get-tuple-element.29.refs_0_), channel_id=1, source_target_pairs={{0,8},{4,12},{8,0},{12,4},{1,9},{5,13},{9,1},{13,5},{2,10},{6,14},... | collective-permute-start | bytes 122888 | tf_op jit(solution)/shard_map/ppermute | solution.py:68
  31.1 6.1 %collective-permute-start.9 = (bf16[32,640]{1,0:T(8,128)(2,1)S(1)}, bf16[32,640]{1,0:T(8,128)(2,1)S(1)}, u32[]{:S(2)}, u32[]{:S(2)}) collective-permute-start(bf16[32,640]{1,0:T(8,128)(2,1)S(1)} %get-tuple-element.29.refs_0_), channel_id=1, source_target_pairs={{0,4},{4,0},{8,12},{12,8},{1,5},{5,1},{9,13},{13,9},{2,6},{6,2},{1... | collective-permute-start | bytes 122888 | tf_op jit(solution)/shard_map/ppermute | solution.py:68
  39.4 1.8 %collective-permute-start.12 = (bf16[128,1664]{1,0:T(8,128)(2,1)S(1)}, bf16[128,1664]{1,0:T(8,128)(2,1)S(1)}, u32[]{:S(2)}, u32[]{:S(2)}) collective-permute-start(bf16[128,1664]{1,0:T(8,128)(2,1)S(1)} %gate_up.5), channel_id=1, source_target_pairs={{0,1},{1,0},{2,3},{3,2},{4,5},{5,4},{6,7},{7,6},{8,9},{9,8},{10,11... | collective-permute-start | bytes 1277960 | tf_op jit(solution)/shard_map/ppermute | solution.py:68
  41.5 12.3 %collective-permute-start.14 = (bf16[128,1664]{1,0:T(8,128)(2,1)S(1)}, bf16[128,1664]{1,0:T(8,128)(2,1)S(1)}, u32[]{:S(2)}, u32[]{:S(2)}) collective-permute-start(bf16[128,1664]{1,0:T(8,128)(2,1)S(1)} %join.1), channel_id=1, source_target_pairs={{0,2},{2,0},{1,3},{3,1},{4,6},{6,4},{5,7},{7,5},{8,10},{10,8},{9,1... | collective-permute-start | bytes 1277960 | tf_op jit(solution)/shard_map/ppermute | solution.py:68
  44.3 9.4 %collective-permute-start.13 = (bf16[128,1664]{1,0:T(8,128)(2,1)S(1)}, bf16[128,1664]{1,0:T(8,128)(2,1)S(1)}, u32[]{:S(2)}, u32[]{:S(2)}) collective-permute-start(bf16[128,1664]{1,0:T(8,128)(2,1)S(1)} %gate_up.6), channel_id=1, source_target_pairs={{0,1},{1,0},{2,3},{3,2},{4,5},{5,4},{6,7},{7,6},{8,9},{9,8},{10,11... | collective-permute-start | bytes 1277960 | tf_op jit(solution)/shard_map/ppermute | solution.py:68
  54.1 2.6 %collective-permute-start.16 = (bf16[128,768]{1,0:T(8,128)(2,1)S(1)}, bf16[128,768]{1,0:T(8,128)(2,1)S(1)}, u32[]{:S(2)}, u32[]{:S(2)}) collective-permute-start(bf16[128,768]{1,0:T(8,128)(2,1)S(1)} %hidden.1.hidden_ref), channel_id=1, source_target_pairs={{0,1},{1,0},{2,3},{3,2},{4,5},{5,4},{6,7},{7,6},{8,9},{9,8},{10,11... | collective-permute-start | bytes 589832 | tf_op jit(solution)/shard_map/ppermute | solution.py:68
  54.2 7.3 %collective-permute-start.15 = (bf16[128,768]{1,0:T(8,128)(2,1)S(1)}, bf16[128,768]{1,0:T(8,128)(2,1)S(1)}, u32[]{:S(2)}, u32[]{:S(2)}) collective-permute-start(bf16[128,768]{1,0:T(8,128)(2,1)S(1)} %hidden.1.hidden_ref), channel_id=1, source_target_pairs={{0,2},{2,0},{1,3},{3,1},{4,6},{6,4},{5,7},{7,5},{8,10},{10,8},{9,1... | collective-permute-start | bytes 589832 | tf_op jit(solution)/shard_map/ppermute | solution.py:68
  61.5 1.4 %collective-permute-start.17 = (bf16[128,768]{1,0:T(8,128)(2,1)S(1)}, bf16[128,768]{1,0:T(8,128)(2,1)S(1)}, u32[]{:S(2)}, u32[]{:S(2)}) collective-permute-start(bf16[128,768]{1,0:T(8,128)(2,1)S(1)} %collective-permute-done.15.hidden_ref), channel_id=1, source_target_pairs={{0,1},{1,0},{2,3},{3,2},{4,5},{5,4},{6,7},{7,6},{8,9},{9,8},{10,11... | collective-permute-start | bytes 589832 | tf_op jit(solution)/shard_map/ppermute | solution.py:68
  64.3 6.0 %collective-permute-start.18 = (bf16[32,512]{1,0:T(8,128)(2,1)S(1)}, bf16[32,512]{1,0:T(8,128)(2,1)S(1)}, u32[]{:S(2)}, u32[]{:S(2)}) collective-permute-start(bf16[32,512]{1,0:T(8,128)(2,1)S(1)} %get-tuple-element.38), channel_id=1, source_target_pairs={{0,12},{4,8},{8,4},{12,0},{1,13},{5,9},{9,5},{13,1},{2,14},{6,10},... | collective-permute-start | bytes 98312 | tf_op jit(solution)/shard_map/ppermute | solution.py:68
  66.2 5.2 %collective-permute-start.19 = (bf16[32,512]{1,0:T(8,128)(2,1)S(1)}, bf16[32,512]{1,0:T(8,128)(2,1)S(1)}, u32[]{:S(2)}, u32[]{:S(2)}) collective-permute-start(bf16[32,512]{1,0:T(8,128)(2,1)S(1)} %get-tuple-element.39), channel_id=1, source_target_pairs={{0,8},{4,12},{8,0},{12,4},{1,9},{5,13},{9,1},{13,5},{2,10},{6,14},... | collective-permute-start | bytes 98312 | tf_op jit(solution)/shard_map/ppermute | solution.py:68
  67.3 4.4 %collective-permute-start.20 = (bf16[32,512]{1,0:T(8,128)(2,1)S(1)}, bf16[32,512]{1,0:T(8,128)(2,1)S(1)}, u32[]{:S(2)}, u32[]{:S(2)}) collective-permute-start(bf16[32,512]{1,0:T(8,128)(2,1)S(1)} %get-tuple-element.40), channel_id=1, source_target_pairs={{0,4},{4,0},{8,12},{12,8},{1,5},{5,1},{9,13},{13,9},{2,6},{6,2},{1... | collective-permute-start | bytes 98312 | tf_op jit(solution)/shard_map/ppermute | solution.py:68
  (11 other events, 119.6 us)

commit v6 on v5

--- a/solution.py
+++ b/solution.py
@@ -213,45 +213,80 @@
     )(plan, queries, keys, values, sight, *in_hbm([beside]))
 
 
-def project_kernel(heads, scale, order_at, source_count, plan_ref, *refs):
-    parts_refs, weight_ref = refs[:source_count], refs[source_count]
-    out_refs, attention_ref = refs[source_count + 1 : -1], refs[-1]
+def merged(parts, heads, scale, width):
+    head_size = width // heads
+    tops = [part[2] for part in parts]
+    top = functools.reduce(jnp.maximum, tops)
+    factors = [jnp.exp2(jnp.minimum((each - top) * scale, 0.0)) for each in tops]
+    total = sum(part[1] * factor for part, factor in zip(parts, factors))
+    columns = []
+    for head in range(heads):
+        here = slice(head * head_size, (head + 1) * head_size)
+        columns.append(
+            sum(part[0](here) * factor[:, head : head + 1] for part, factor in zip(parts, factors))
+        )
+    return columns, total, top
+
+
+def as_part(ref, heads, width):
+    stats = ref[:, width:].astype(f32)
+    total = pltpu.roll(stats, LANES - heads, 1) + pltpu.roll(stats, LANES - 2 * heads, 1)
+    return (lambda here: ref[:, here].astype(f32), total, stats)
+
+
+def merge_kernel(heads, scale, beside_ref, *refs):
+    parts_refs, (sums_ref, total_ref, top_ref) = refs[:-3], refs[-3:]
+    width = sums_ref.shape[1]
+    head_size = width // heads
+    parts = [as_part(ref, heads, width) for ref in parts_refs]
+    columns, total_ref[...], top_ref[...] = merged(parts, heads, scale, width)
+    for head, column in enumerate(columns):
+        sums_ref[:, head * head_size : (head + 1) * head_size] = column
+
+
+def merge(parts, heads, scale, width, beside):
+    rows = parts[0].shape[0]
+    narrow = jax.ShapeDtypeStruct((rows, LANES), f32)
+    return pl.pallas_call(
+        functools.partial(merge_kernel, heads, scale),
+        in_specs=[whole(pltpu.HBM)] + [whole()] * len(parts),
+        out_shape=(jax.ShapeDtypeStruct((rows, width), f32), narrow, narrow),
+        compiler_params=params(8),
+        name="merge",
+    )(*in_hbm([beside]), *parts)
+
+
+def project_kernel(
+    heads, scale, order_at, plan_ref, sums_ref, total_ref, top_ref, part_ref, weight_ref, *refs
+):
+    out_refs, attention_ref = refs[:-1], refs[-1]
     width = attention_ref.shape[1]
     head_size = width // heads
-    stats = [ref[:, width:].astype(f32) for ref in parts_refs]
-    top = functools.reduce(jnp.maximum, stats)
-    factors = [jnp.exp2(jnp.minimum((stat - top) * scale, 0.0)) for stat in stats]
-    total = 0.0
-    for stat, factor in zip(stats, factors):
-        high = pltpu.roll(stat, LANES - heads, 1)
-        low = pltpu.roll(stat, LANES - 2 * heads, 1)
-        total = total + factor * (high + low)
-    shares = [factor / total for factor in factors]
-    for head in range(heads):
-        columns = slice(head * head_size, (head + 1) * head_size)
-        merged = 0.0
-        for ref, share in zip(parts_refs, shares):
-            merged = merged + ref[:, columns].astype(f32) * share[:, head : head + 1]
-        attention_ref[:, columns] = merged.astype(bf16)
+    before = (lambda here: sums_ref[:, here], total_ref[...], top_ref[...])
+    columns, total, _ = merged([before, as_part(part_ref, heads, width)], heads, scale, width)
+    share = 1.0 / total
+    for head, column in enumerate(columns):
+        here = slice(head * head_size, (head + 1) * head_size)
+        attention_ref[:, here] = (column * share[:, head : head + 1]).astype(bf16)
     for i, out_ref in enumerate(out_refs):
         piece_width = out_ref.shape[1]
         start = pl.multiple_of(plan_ref[order_at + i] * piece_width, piece_width)
         out_ref[...] = dot(attention_ref[...], weight_ref[:, pl.ds(start, piece_width)]).astype(bf16)
 
 
-def project(plan, order_at, parts, weight, heads, scale, piece_count):
-    rows = parts[0].shape[0]
+def project(plan, order_at, before, part, weight, heads, scale, piece_count):
+    rows = part.shape[0]
     width, model_width = weight.shape
     piece_width = model_width // piece_count
     return pl.pallas_call(
-        functools.partial(project_kernel, heads, scale, order_at, len(parts)),
-        in_specs=[whole(pltpu.SMEM)] + [whole()] * (len(parts) + 1),
+        functools.partial(project_kernel, heads, scale, order_at),
+        in_specs=[whole(pltpu.SMEM)] + [whole()] * 5,
         out_shape=[jax.ShapeDtypeStruct((rows, piece_width), bf16)] * piece_count,
         scratch_shapes=[pltpu.VMEM((rows, width), bf16)],
         compiler_params=params(8),
         cost_estimate=cost(2 * rows * width * model_width, 2 * width * model_width),
         name="project",
-    )(plan, *parts, weight)
+    )(plan, *before, part, weight)
 
 
 def mix_kernel(residual_ref, gain_ref, *refs):
@@ -523,19 +558,20 @@
     packed = pack(
         queries.reshape(query_rows, width), query_seg, expert_ids, route_weight, gate_up_weight
     )
+    sight = sight_of(parent, key_seg, gate_up_weight)
     gathered = {0: packed}
     for k in far_first(ctx_count):
         gathered[k] = swapped(packed, "ctx", k)
-    sight = sight_of(parent, key_seg, gate_up_weight)
     keys = cached_keys.reshape(key_count, head_size)
     values = cached_values.reshape(key_count, head_size)
     out_matrix = out_weight.reshape(width, model_width)
     parts = {}
-    for k in list(range(1, ctx_count)) + [0]:
+    for k in range(ctx_count):
         part = attend(
             plan, lead_at + k, gathered[k], keys, values, sight, heads, scale, gate_up_weight
         )
         parts[k] = swapped(part, "ctx", k) if k else part
+        sight, _ = lax.optimization_barrier((sight, part))
     place, combine_high, combine_low = route(
         plan,
         0,
@@ -546,14 +582,10 @@
         piece_count,
         slots,
     )
+    last_part = parts.pop(ctx_count - 1)
+    before = merge(list(parts.values()), heads, scale, width, gate_up_weight)
     projected = project(
-        plan,
-        order_at,
-        [parts[k] for k in range(ctx_count)],
-        out_matrix,
-        heads,
-        scale,
-        piece_count,
+        plan, order_at, before, last_part, out_matrix, heads, scale, piece_count
     )
     pieces = [projected[0]] + [
         swapped(projected[k], ("exp", "tp"), k) for k in far_first(piece_count)

time: 72.6 us -> 74.7 us (1.029)
  waiting for transfers between devices: 21.9 us -> 23.9 us
    ppermute x21, waiting for transfers between devices: 21.9 us -> 23.9 us  [swapped(): return lax.ppermute(value, axes, pairs)]
    pallas_call x1 -> x2, Pallas kernels: 1.55 us -> 1.69 us  [the longest x1 1.49 us: project(): pl.pallas_call(functools.partial(project_kernel, heads, scale, order_at),...]
  transfers between devices with their start and end apart: 21 -> 21, of which waited for: 13 -> 10; matrix products, arithmetic and copies ran while one was open for 0% -> 0% of each run, Pallas kernels for 26% -> 26%
where the time goes in v6:
time: 74.7 us; the launch traced here: 74.5 us
  Pallas kernels  26.6 us (36%)
  waiting for transfers between devices  23.9 us (32%)
  starting transfers between devices  23.5 us (31%)
    ppermute x21, waiting for transfers between devices, swapped(): return lax.ppermute(value, axes, pairs)  23.9 us
    ppermute x21, starting transfers between devices, swapped(): return lax.ppermute(value, axes, pairs)  23.5 us
    pallas_call x4, Pallas kernels, attend(): pl.pallas_call(functools.partial(attend_kernel, heads, scale, lead_at), i...  7.28 us
    pallas_call x4, Pallas kernels, gate_up(): pl.pallas_call(kernel, in_specs=[whole(pltpu.SMEM)] + [whole()] * 2, out_...  6.85 us
    pallas_call x4, Pallas kernels, down(): pl.pallas_call(kernel, in_specs=[whole(pltpu.SMEM)] + [whole()] * (4 + le...  5.53 us
  transfers between devices with their start and end apart: 21, of which 10 were waited for; matrix products, arithmetic and copies ran while one was open for 0% of the time, Pallas kernels for 26%

profile of v6, /device:TPU:0, one launch (start us, length us, event | category | flops | bytes accessed | tf_op | source)
XLA Modules:
  0.0 74.5 jit_solution(5791779242417591870)
XLA Ops:
  1.0 3.1 %collective-permute-start = (bf16[32,1152]{1,0:T(8,128)(2,1)S(1)}, bf16[32,1152]{1,0:T(8,128)(2,1)S(1)}, u32[]{:S(2)}, u32[]{:S(2)}) collective-permute-start(bf16[32,1152]{1,0:T(8,128)(2,1)S(1)} %pack.1.queries_ref.refs_0_), channel_id=1, source_target_pairs={{0,4},{4,0},{8,12},{12,8},{1,5},{5,1},{9,13},{13,9},{2,6},{6,2},{1... | collective-permute-start | bytes 221192 | tf_op jit(solution)/shard_map/ppermute | solution.py:68
  4.0 2.5 %collective-permute-start.4 = (bf16[32,1152]{1,0:T(8,128)(2,1)S(1)}, bf16[32,1152]{1,0:T(8,128)(2,1)S(1)}, u32[]{:S(2)}, u32[]{:S(2)}) collective-permute-start(bf16[32,1152]{1,0:T(8,128)(2,1)S(1)} %pack.1.queries_ref.refs_0_), channel_id=1, source_target_pairs={{0,12},{4,8},{8,4},{12,0},{1,13},{5,9},{9,5},{13,1},{2,14},{6,10},... | collective-permute-start | bytes 221192 | tf_op jit(solution)/shard_map/ppermute | solution.py:68
  8.2 1.8 %attend.4.refs_0_ = bf16[32,1152]{1,0:T(8,128)(2,1)S(1)} custom-call(s32[17]{0:T(128)S(1)} %stack.71.plan_ref, bf16[32,1152]{1,0:T(8,128)(2,1)S(1)} %pack.1.queries_ref.refs_0_, bf16[2048,128]{1,0:T(8,128)(2,1)S(1)} %bitcast.30, bf16[2048,128]{1,0:T(8,128)(2,1)S(1)} %bitcast.34, bf16[64,2048]{1,0:T(8,128)(2,1)S(1)} %sight.1.sight_ref, ...), custom_call_target="tpu_custom_call" | custom-call | flops 536870912 | bytes 1048576 | tf_op jit(solution)/shard_map/attend/pallas_call | solution.py:202
  10.1 1.8 %attend.5 = bf16[32,1152]{1,0:T(8,128)(2,1)S(1)} custom-call(s32[17]{0:T(128)S(1)} %stack.71.plan_ref, bf16[32,1152]{1,0:T(8,128)(2,1)S(1)} %collective-permute-done.queries_ref.refs_1_, bf16[2048,128]{1,0:T(8,128)(2,1)S(1)} %bitcast.31, bf16[2048,128]{1,0:T(8,128)(2,1)S(1)} %bitcast.35, bf16[64,2048]{1,0:T(8,128)(2,1)S(1)} %sight.1.sight_ref, ...), custom_call_target="tpu_custom_call" | custom-call | flops 536870912 | bytes 1048576 | tf_op jit(solution)/shard_map/attend/pallas_call | solution.py:202
  11.9 1.7 %collective-permute-done.2.queries_ref.refs_2_ = bf16[32,1152]{1,0:T(8,128)(2,1)S(1)} collective-permute-done((bf16[32,1152]{1,0:T(8,128)(2,1)S(1)}, bf16[32,1152]{1,0:T(8,128)(2,1)S(1)}, u32[]{:S(2)}, u32[]{:S(2)}) %collective-permute-start.2) | collective-permute-done | bytes 73760 | tf_op jit(solution)/shard_map/ppermute | solution.py:68
  13.6 1.8 %attend.6 = bf16[32,1152]{1,0:T(8,128)(2,1)S(1)} custom-call(s32[17]{0:T(128)S(1)} %stack.71.plan_ref, bf16[32,1152]{1,0:T(8,128)(2,1)S(1)} %collective-permute-done.2.queries_ref.refs_2_, bf16[2048,128]{1,0:T(8,128)(2,1)S(1)} %bitcast.32, bf16[2048,128]{1,0:T(8,128)(2,1)S(1)} %bitcast.36, bf16[64,2048]{1,0:T(8,128)(2,1)S(1)} %sight.1.sight_ref, ...), custom_call_target="tpu_custom_call" | custom-call | flops 536870912 | bytes 1048576 | tf_op jit(solution)/shard_map/attend/pallas_call | solution.py:202
  16.6 1.8 %collective-permute-start.1 = (bf16[32,1152]{1,0:T(8,128)(2,1)S(1)}, bf16[32,1152]{1,0:T(8,128)(2,1)S(1)}, u32[]{:S(2)}, u32[]{:S(2)}) collective-permute-start(bf16[32,1152]{1,0:T(8,128)(2,1)S(1)} %attend.5), channel_id=1, source_target_pairs={{0,4},{4,0},{8,12},{12,8},{1,5},{5,1},{9,13},{13,9},{2,6},{6,2},{1... | collective-permute-start | bytes 221192 | tf_op jit(solution)/shard_map/ppermute | solution.py:68
  18.5 1.8 %attend.7 = bf16[32,1152]{1,0:T(8,128)(2,1)S(1)} custom-call(s32[17]{0:T(128)S(1)} %stack.71.plan_ref, bf16[32,1152]{1,0:T(8,128)(2,1)S(1)} %collective-permute-done.4.queries_ref.refs_3_, bf16[2048,128]{1,0:T(8,128)(2,1)S(1)} %bitcast.33, bf16[2048,128]{1,0:T(8,128)(2,1)S(1)} %bitcast.37, bf16[64,2048]{1,0:T(8,128)(2,1)S(1)} %sight.1.sight_ref, ...), custom_call_target="tpu_custom_call" | custom-call | flops 536870912 | bytes 1048576 | tf_op jit(solution)/shard_map/attend/pallas_call | solution.py:202
  20.4 1.5 %collective-permute-start.5 = (bf16[32,1152]{1,0:T(8,128)(2,1)S(1)}, bf16[32,1152]{1,0:T(8,128)(2,1)S(1)}, u32[]{:S(2)}, u32[]{:S(2)}) collective-permute-start(bf16[32,1152]{1,0:T(8,128)(2,1)S(1)} %attend.7), channel_id=1, source_target_pairs={{0,12},{4,8},{8,4},{12,0},{1,13},{5,9},{9,5},{13,1},{2,14},{6,10},... | collective-permute-start | bytes 221192 | tf_op jit(solution)/shard_map/ppermute | solution.py:68
  22.0 4.6 %collective-permute-done.5.part_ref = bf16[32,1152]{1,0:T(8,128)(2,1)S(1)} collective-permute-done((bf16[32,1152]{1,0:T(8,128)(2,1)S(1)}, bf16[32,1152]{1,0:T(8,128)(2,1)S(1)}, u32[]{:S(2)}, u32[]{:S(2)}) %collective-permute-start.5) | collective-permute-done | bytes 73760 | tf_op jit(solution)/shard_map/ppermute | solution.py:68
  26.6 1.5 %project.1 = (bf16[32,512]{1,0:T(8,128)(2,1)S(1)}, bf16[32,512]{1,0:T(8,128)(2,1)S(1)}, bf16[32,512]{1,0:T(8,128)(2,1)S(1)}, bf16[32,512]{1,0:T(8,128)(2,1)S(1)}) custom-call(s32[17]{0:T(128)S(1)} %stack.71.plan_ref, f32[32,1024]{1,0:T(8,128)S(1)} %get-tuple-element.31.sums_ref, f32[32,128]{1,0:T(8,128)S(1)} %get-tuple-element.32.total_ref, ...), custom_call_target="tpu_custom_call" | custom-call | flops 134217728 | bytes 4194304 | tf_op jit(solution)/shard_map/project/pallas_call | solution.py:281
  28.1 1.6 %collective-permute-start.7 = (bf16[32,512]{1,0:T(8,128)(2,1)S(1)}, bf16[32,512]{1,0:T(8,128)(2,1)S(1)}, u32[]{:S(2)}, u32[]{:S(2)}) collective-permute-start(bf16[32,512]{1,0:T(8,128)(2,1)S(1)} %get-tuple-element.37), channel_id=1, source_target_pairs={{0,2},{1,3},{2,0},{3,1},{4,6},{5,7},{6,4},{7,5},{8,10},{9,11},{10,... | collective-permute-start | bytes 98312 | tf_op jit(solution)/shard_map/ppermute | solution.py:68
  30.0 1.8 %collective-permute-done.6.refs_1_ = bf16[32,512]{1,0:T(8,128)(2,1)S(1)} collective-permute-done((bf16[32,512]{1,0:T(8,128)(2,1)S(1)}, bf16[32,512]{1,0:T(8,128)(2,1)S(1)}, u32[]{:S(2)}, u32[]{:S(2)}) %collective-permute-start.6) | collective-permute-done | bytes 32800 | tf_op jit(solution)/shard_map/ppermute | solution.py:68
  32.3 1.5 %collective-permute-start.11 = (bf16[32,640]{1,0:T(8,128)(2,1)S(1)}, bf16[32,640]{1,0:T(8,128)(2,1)S(1)}, u32[]{:S(2)}, u32[]{:S(2)}) collective-permute-start(bf16[32,640]{1,0:T(8,128)(2,1)S(1)} %get-tuple-element.41.refs_0_), channel_id=1, source_target_pairs={{0,12},{4,8},{8,4},{12,0},{1,13},{5,9},{9,5},{13,1},{2,14},{6,10},... | collective-permute-start | bytes 122888 | tf_op jit(solution)/shard_map/ppermute | solution.py:68
  33.7 3.0 %collective-permute-start.9 = (bf16[32,640]{1,0:T(8,128)(2,1)S(1)}, bf16[32,640]{1,0:T(8,128)(2,1)S(1)}, u32[]{:S(2)}, u32[]{:S(2)}) collective-permute-start(bf16[32,640]{1,0:T(8,128)(2,1)S(1)} %get-tuple-element.41.refs_0_), channel_id=1, source_target_pairs={{0,4},{4,0},{8,12},{12,8},{1,5},{5,1},{9,13},{13,9},{2,6},{6,2},{1... | collective-permute-start | bytes 122888 | tf_op jit(solution)/shard_map/ppermute | solution.py:68
  40.1 1.7 %gate_up.5 = bf16[128,1664]{1,0:T(8,128)(2,1)S(1)} custom-call(s32[17]{0:T(128)S(1)} %stack.71.plan_ref, bf16[4,128,640]{2,1,0:T(8,128)(2,1)S(1)} %pick.1.picked_ref, bf16[16,512,1536]{2,1,0:T(8,128)(2,1)S(1)} %bitcast.27), custom_call_target="tpu_custom_call" | custom-call | flops 201326592 | bytes 6291456 | tf_op jit(solution)/shard_map/gate_up/pallas_call | solution.py:406
  41.9 1.7 %gate_up.4.left_ref = bf16[128,1664]{1,0:T(8,128)(2,1)S(1)} custom-call(s32[17]{0:T(128)S(1)} %stack.71.plan_ref, bf16[4,128,640]{2,1,0:T(8,128)(2,1)S(1)} %pick.1.picked_ref, bf16[16,512,1536]{2,1,0:T(8,128)(2,1)S(1)} %bitcast.27), custom_call_target="tpu_custom_call" | custom-call | flops 201326592 | bytes 6291456 | tf_op jit(solution)/shard_map/gate_up/pallas_call | solution.py:406
  45.0 1.7 %gate_up.6 = bf16[128,1664]{1,0:T(8,128)(2,1)S(1)} custom-call(s32[17]{0:T(128)S(1)} %stack.71.plan_ref, bf16[4,128,640]{2,1,0:T(8,128)(2,1)S(1)} %pick.1.picked_ref, bf16[16,512,1536]{2,1,0:T(8,128)(2,1)S(1)} %bitcast.27), custom_call_target="tpu_custom_call" | custom-call | flops 201326592 | bytes 6291456 | tf_op jit(solution)/shard_map/gate_up/pallas_call | solution.py:406
  46.9 1.7 %gate_up.7.refs_2_ = bf16[128,1664]{1,0:T(8,128)(2,1)S(1)} custom-call(s32[17]{0:T(128)S(1)} %stack.71.plan_ref, bf16[4,128,640]{2,1,0:T(8,128)(2,1)S(1)} %pick.1.picked_ref, bf16[16,512,1536]{2,1,0:T(8,128)(2,1)S(1)} %bitcast.27), custom_call_target="tpu_custom_call" | custom-call | flops 201326592 | bytes 6291456 | tf_op jit(solution)/shard_map/gate_up/pallas_call | solution.py:406
  48.7 7.5 %collective-permute-done.14.refs_3_ = bf16[128,1664]{1,0:T(8,128)(2,1)S(1)} collective-permute-done((bf16[128,1664]{1,0:T(8,128)(2,1)S(1)}, bf16[128,1664]{1,0:T(8,128)(2,1)S(1)}, u32[]{:S(2)}, u32[]{:S(2)}) %collective-permute-start.14) | collective-permute-done | bytes 426016 | tf_op jit(solution)/shard_map/ppermute | solution.py:68
  60.5 3.4 %collective-permute-done.15.hidden_ref = bf16[128,768]{1,0:T(8,128)(2,1)S(1)} collective-permute-done((bf16[128,768]{1,0:T(8,128)(2,1)S(1)}, bf16[128,768]{1,0:T(8,128)(2,1)S(1)}, u32[]{:S(2)}, u32[]{:S(2)}) %collective-permute-start.15) | collective-permute-done | bytes 196640 | tf_op jit(solution)/shard_map/ppermute | solution.py:68
  66.8 1.4 %collective-permute-start.18 = (bf16[32,512]{1,0:T(8,128)(2,1)S(1)}, bf16[32,512]{1,0:T(8,128)(2,1)S(1)}, u32[]{:S(2)}, u32[]{:S(2)}) collective-permute-start(bf16[32,512]{1,0:T(8,128)(2,1)S(1)} %get-tuple-element.50), channel_id=1, source_target_pairs={{0,12},{4,8},{8,4},{12,0},{1,13},{5,9},{9,5},{13,1},{2,14},{6,10},... | collective-permute-start | bytes 98312 | tf_op jit(solution)/shard_map/ppermute | solution.py:68
  69.3 1.9 %collective-permute-start.20 = (bf16[32,512]{1,0:T(8,128)(2,1)S(1)}, bf16[32,512]{1,0:T(8,128)(2,1)S(1)}, u32[]{:S(2)}, u32[]{:S(2)}) collective-permute-start(bf16[32,512]{1,0:T(8,128)(2,1)S(1)} %get-tuple-element.52), channel_id=1, source_target_pairs={{0,4},{4,0},{8,12},{12,8},{1,5},{5,1},{9,13},{13,9},{2,6},{6,2},{1... | collective-permute-start | bytes 98312 | tf_op jit(solution)/shard_map/ppermute | solution.py:68
  71.2 1.6 %collective-permute-done.18.refs_1_ = bf16[32,512]{1,0:T(8,128)(2,1)S(1)} collective-permute-done((bf16[32,512]{1,0:T(8,128)(2,1)S(1)}, bf16[32,512]{1,0:T(8,128)(2,1)S(1)}, u32[]{:S(2)}, u32[]{:S(2)}) %collective-permute-start.18) | collective-permute-done | bytes 32800 | tf_op jit(solution)/shard_map/ppermute | solution.py:68
  (72 shorter events, 19.7 us)
Async XLA Ops:
  1.0 9.1 %collective-permute-start = (bf16[32,1152]{1,0:T(8,128)(2,1)S(1)}, bf16[32,1152]{1,0:T(8,128)(2,1)S(1)}, u32[]{:S(2)}, u32[]{:S(2)}) collective-permute-start(bf16[32,1152]{1,0:T(8,128)(2,1)S(1)} %pack.1.queries_ref.refs_0_), channel_id=1, source_target_pairs={{0,4},{4,0},{8,12},{12,8},{1,5},{5,1},{9,13},{13,9},{2,6},{6,2},{1... | collective-permute-start | bytes 221192 | tf_op jit(solution)/shard_map/ppermute | solution.py:68
  4.0 14.4 %collective-permute-start.4 = (bf16[32,1152]{1,0:T(8,128)(2,1)S(1)}, bf16[32,1152]{1,0:T(8,128)(2,1)S(1)}, u32[]{:S(2)}, u32[]{:S(2)}) collective-permute-start(bf16[32,1152]{1,0:T(8,128)(2,1)S(1)} %pack.1.queries_ref.refs_0_), channel_id=1, source_target_pairs={{0,12},{4,8},{8,4},{12,0},{1,13},{5,9},{9,5},{13,1},{2,14},{6,10},... | collective-permute-start | bytes 221192 | tf_op jit(solution)/shard_map/ppermute | solution.py:68
  6.5 7.1 %collective-permute-start.2 = (bf16[32,1152]{1,0:T(8,128)(2,1)S(1)}, bf16[32,1152]{1,0:T(8,128)(2,1)S(1)}, u32[]{:S(2)}, u32[]{:S(2)}) collective-permute-start(bf16[32,1152]{1,0:T(8,128)(2,1)S(1)} %pack.1.queries_ref.refs_0_), channel_id=1, source_target_pairs={{0,8},{4,12},{8,0},{12,4},{1,9},{5,13},{9,1},{13,5},{2,10},{6,14},... | collective-permute-start | bytes 221192 | tf_op jit(solution)/shard_map/ppermute | solution.py:68
  15.4 6.4 %collective-permute-start.3 = (bf16[32,1152]{1,0:T(8,128)(2,1)S(1)}, bf16[32,1152]{1,0:T(8,128)(2,1)S(1)}, u32[]{:S(2)}, u32[]{:S(2)}) collective-permute-start(bf16[32,1152]{1,0:T(8,128)(2,1)S(1)} %attend.6), channel_id=1, source_target_pairs={{0,8},{4,12},{8,0},{12,4},{1,9},{5,13},{9,1},{13,5},{2,10},{6,14},... | collective-permute-start | bytes 221192 | tf_op jit(solution)/shard_map/ppermute | solution.py:68
  16.6 5.2 %collective-permute-start.1 = (bf16[32,1152]{1,0:T(8,128)(2,1)S(1)}, bf16[32,1152]{1,0:T(8,128)(2,1)S(1)}, u32[]{:S(2)}, u32[]{:S(2)}) collective-permute-start(bf16[32,1152]{1,0:T(8,128)(2,1)S(1)} %attend.5), channel_id=1, source_target_pairs={{0,4},{4,0},{8,12},{12,8},{1,5},{5,1},{9,13},{13,9},{2,6},{6,2},{1... | collective-permute-start | bytes 221192 | tf_op jit(solution)/shard_map/ppermute | solution.py:68
  18.4 21.6 %slice-start = ((s8[25165824]{0:T(1024)(128)(4,1)}), s8[4194304]{0:T(1024)(128)(4,1)S(1)}, s32[]{:S(2)}) async-start(s8[25165824]{0:T(1024)(128)(4,1)} %bitcast.26), calls=%async_computation | async-start | bytes 8388608
  18.4 21.6 %slice-start.1 = ((s8[25165824]{0:T(1024)(128)(4,1)}), s8[4194304]{0:T(1024)(128)(4,1)S(1)}, s32[]{:S(2)}) async-start(s8[25165824]{0:T(1024)(128)(4,1)} %bitcast.26), calls=%async_computation.1 | async-start | bytes 8388608
  18.4 21.6 %slice-start.2 = ((s8[25165824]{0:T(1024)(128)(4,1)}), s8[4194304]{0:T(1024)(128)(4,1)S(1)}, s32[]{:S(2)}) async-start(s8[25165824]{0:T(1024)(128)(4,1)} %bitcast.26), calls=%async_computation.2 | async-start | bytes 8388608
  20.4 6.2 %collective-permute-start.5 = (bf16[32,1152]{1,0:T(8,128)(2,1)S(1)}, bf16[32,1152]{1,0:T(8,128)(2,1)S(1)}, u32[]{:S(2)}, u32[]{:S(2)}) collective-permute-start(bf16[32,1152]{1,0:T(8,128)(2,1)S(1)} %attend.7), channel_id=1, source_target_pairs={{0,12},{4,8},{8,4},{12,0},{1,13},{5,9},{9,5},{13,1},{2,14},{6,10},... | collective-permute-start | bytes 221192 | tf_op jit(solution)/shard_map/ppermute | solution.py:68
  28.1 3.7 %collective-permute-start.6 = (bf16[32,512]{1,0:T(8,128)(2,1)S(1)}, bf16[32,512]{1,0:T(8,128)(2,1)S(1)}, u32[]{:S(2)}, u32[]{:S(2)}) collective-permute-start(bf16[32,512]{1,0:T(8,128)(2,1)S(1)} %get-tuple-element.36), channel_id=1, source_target_pairs={{0,3},{1,2},{2,1},{3,0},{4,7},{5,6},{6,5},{7,4},{8,11},{9,10},{10,... | collective-permute-start | bytes 98312 | tf_op jit(solution)/shard_map/ppermute | solution.py:68
  28.1 4.0 %collective-permute-start.7 = (bf16[32,512]{1,0:T(8,128)(2,1)S(1)}, bf16[32,512]{1,0:T(8,128)(2,1)S(1)}, u32[]{:S(2)}, u32[]{:S(2)}) collective-permute-start(bf16[32,512]{1,0:T(8,128)(2,1)S(1)} %get-tuple-element.37), channel_id=1, source_target_pairs={{0,2},{1,3},{2,0},{3,1},{4,6},{5,7},{6,4},{7,5},{8,10},{9,11},{10,... | collective-permute-start | bytes 98312 | tf_op jit(solution)/shard_map/ppermute | solution.py:68
  29.7 2.5 %collective-permute-start.8 = (bf16[32,512]{1,0:T(8,128)(2,1)S(1)}, bf16[32,512]{1,0:T(8,128)(2,1)S(1)}, u32[]{:S(2)}, u32[]{:S(2)}) collective-permute-start(bf16[32,512]{1,0:T(8,128)(2,1)S(1)} %get-tuple-element.38), channel_id=1, source_target_pairs={{0,1},{1,0},{2,3},{3,2},{4,5},{5,4},{6,7},{7,6},{8,9},{9,8},{10,11... | collective-permute-start | bytes 98312 | tf_op jit(solution)/shard_map/ppermute | solution.py:68
  32.3 6.2 %collective-permute-start.11 = (bf16[32,640]{1,0:T(8,128)(2,1)S(1)}, bf16[32,640]{1,0:T(8,128)(2,1)S(1)}, u32[]{:S(2)}, u32[]{:S(2)}) collective-permute-start(bf16[32,640]{1,0:T(8,128)(2,1)S(1)} %get-tuple-element.41.refs_0_), channel_id=1, source_target_pairs={{0,12},{4,8},{8,4},{12,0},{1,13},{5,9},{9,5},{13,1},{2,14},{6,10},... | collective-permute-start | bytes 122888 | tf_op jit(solution)/shard_map/ppermute | solution.py:68
  33.7 6.0 %collective-permute-start.10 = (bf16[32,640]{1,0:T(8,128)(2,1)S(1)}, bf16[32,640]{1,0:T(8,128)(2,1)S(1)}, u32[]{:S(2)}, u32[]{:S(2)}) collective-permute-start(bf16[32,640]{1,0:T(8,128)(2,1)S(1)} %get-tuple-element.41.refs_0_), channel_id=1, source_target_pairs={{0,8},{4,12},{8,0},{12,4},{1,9},{5,13},{9,1},{13,5},{2,10},{6,14},... | collective-permute-start | bytes 122888 | tf_op jit(solution)/shard_map/ppermute | solution.py:68
  33.7 6.0 %collective-permute-start.9 = (bf16[32,640]{1,0:T(8,128)(2,1)S(1)}, bf16[32,640]{1,0:T(8,128)(2,1)S(1)}, u32[]{:S(2)}, u32[]{:S(2)}) collective-permute-start(bf16[32,640]{1,0:T(8,128)(2,1)S(1)} %get-tuple-element.41.refs_0_), channel_id=1, source_target_pairs={{0,4},{4,0},{8,12},{12,8},{1,5},{5,1},{9,13},{13,9},{2,6},{6,2},{1... | collective-permute-start | bytes 122888 | tf_op jit(solution)/shard_map/ppermute | solution.py:68
  41.8 1.8 %collective-permute-start.12 = (bf16[128,1664]{1,0:T(8,128)(2,1)S(1)}, bf16[128,1664]{1,0:T(8,128)(2,1)S(1)}, u32[]{:S(2)}, u32[]{:S(2)}) collective-permute-start(bf16[128,1664]{1,0:T(8,128)(2,1)S(1)} %gate_up.5), channel_id=1, source_target_pairs={{0,1},{1,0},{2,3},{3,2},{4,5},{5,4},{6,7},{7,6},{8,9},{9,8},{10,11... | collective-permute-start | bytes 1277960 | tf_op jit(solution)/shard_map/ppermute | solution.py:68
  43.9 12.3 %collective-permute-start.14 = (bf16[128,1664]{1,0:T(8,128)(2,1)S(1)}, bf16[128,1664]{1,0:T(8,128)(2,1)S(1)}, u32[]{:S(2)}, u32[]{:S(2)}) collective-permute-start(bf16[128,1664]{1,0:T(8,128)(2,1)S(1)} %join.1), channel_id=1, source_target_pairs={{0,2},{2,0},{1,3},{3,1},{4,6},{6,4},{5,7},{7,5},{8,10},{10,8},{9,1... | collective-permute-start | bytes 1277960 | tf_op jit(solution)/shard_map/ppermute | solution.py:68
  46.7 9.5 %collective-permute-start.13 = (bf16[128,1664]{1,0:T(8,128)(2,1)S(1)}, bf16[128,1664]{1,0:T(8,128)(2,1)S(1)}, u32[]{:S(2)}, u32[]{:S(2)}) collective-permute-start(bf16[128,1664]{1,0:T(8,128)(2,1)S(1)} %gate_up.6), channel_id=1, source_target_pairs={{0,1},{1,0},{2,3},{3,2},{4,5},{5,4},{6,7},{7,6},{8,9},{9,8},{10,11... | collective-permute-start | bytes 1277960 | tf_op jit(solution)/shard_map/ppermute | solution.py:68
  56.5 2.6 %collective-permute-start.16 = (bf16[128,768]{1,0:T(8,128)(2,1)S(1)}, bf16[128,768]{1,0:T(8,128)(2,1)S(1)}, u32[]{:S(2)}, u32[]{:S(2)}) collective-permute-start(bf16[128,768]{1,0:T(8,128)(2,1)S(1)} %hidden.1.hidden_ref), channel_id=1, source_target_pairs={{0,1},{1,0},{2,3},{3,2},{4,5},{5,4},{6,7},{7,6},{8,9},{9,8},{10,11... | collective-permute-start | bytes 589832 | tf_op jit(solution)/shard_map/ppermute | solution.py:68
  56.6 7.3 %collective-permute-start.15 = (bf16[128,768]{1,0:T(8,128)(2,1)S(1)}, bf16[128,768]{1,0:T(8,128)(2,1)S(1)}, u32[]{:S(2)}, u32[]{:S(2)}) collective-permute-start(bf16[128,768]{1,0:T(8,128)(2,1)S(1)} %hidden.1.hidden_ref), channel_id=1, source_target_pairs={{0,2},{2,0},{1,3},{3,1},{4,6},{6,4},{5,7},{7,5},{8,10},{10,8},{9,1... | collective-permute-start | bytes 589832 | tf_op jit(solution)/shard_map/ppermute | solution.py:68
  63.9 1.4 %collective-permute-start.17 = (bf16[128,768]{1,0:T(8,128)(2,1)S(1)}, bf16[128,768]{1,0:T(8,128)(2,1)S(1)}, u32[]{:S(2)}, u32[]{:S(2)}) collective-permute-start(bf16[128,768]{1,0:T(8,128)(2,1)S(1)} %collective-permute-done.15.hidden_ref), channel_id=1, source_target_pairs={{0,1},{1,0},{2,3},{3,2},{4,5},{5,4},{6,7},{7,6},{8,9},{9,8},{10,11... | collective-permute-start | bytes 589832 | tf_op jit(solution)/shard_map/ppermute | solution.py:68
  66.8 6.1 %collective-permute-start.18 = (bf16[32,512]{1,0:T(8,128)(2,1)S(1)}, bf16[32,512]{1,0:T(8,128)(2,1)S(1)}, u32[]{:S(2)}, u32[]{:S(2)}) collective-permute-start(bf16[32,512]{1,0:T(8,128)(2,1)S(1)} %get-tuple-element.50), channel_id=1, source_target_pairs={{0,12},{4,8},{8,4},{12,0},{1,13},{5,9},{9,5},{13,1},{2,14},{6,10},... | collective-permute-start | bytes 98312 | tf_op jit(solution)/shard_map/ppermute | solution.py:68
  68.2 5.6 %collective-permute-start.19 = (bf16[32,512]{1,0:T(8,128)(2,1)S(1)}, bf16[32,512]{1,0:T(8,128)(2,1)S(1)}, u32[]{:S(2)}, u32[]{:S(2)}) collective-permute-start(bf16[32,512]{1,0:T(8,128)(2,1)S(1)} %get-tuple-element.51), channel_id=1, source_target_pairs={{0,8},{4,12},{8,0},{12,4},{1,9},{5,13},{9,1},{13,5},{2,10},{6,14},... | collective-permute-start | bytes 98312 | tf_op jit(solution)/shard_map/ppermute | solution.py:68
  69.3 4.5 %collective-permute-start.20 = (bf16[32,512]{1,0:T(8,128)(2,1)S(1)}, bf16[32,512]{1,0:T(8,128)(2,1)S(1)}, u32[]{:S(2)}, u32[]{:S(2)}) collective-permute-start(bf16[32,512]{1,0:T(8,128)(2,1)S(1)} %get-tuple-element.52), channel_id=1, source_target_pairs={{0,4},{4,0},{8,12},{12,8},{1,5},{5,1},{9,13},{13,9},{2,6},{6,2},{1... | collective-permute-start | bytes 98312 | tf_op jit(solution)/shard_map/ppermute | solution.py:68
  (11 other events, 120.6 us)

commit v7 on v5

--- a/solution.py
+++ b/solution.py
@@ -11,6 +11,7 @@
 MOST = 8
 DEPTH = 6
 LANES = 128
+CELLS = 2
 
 epsilon = 1e-06
 masked_score = -1e30
@@ -353,27 +354,43 @@
     return jnp.where(lane == 0, high, jnp.where(lane == 1, low, 0.0))
 
 
-def gate_up(plan, piece_at, expert_at, spread, picked, weight):
-    piece_count, slots, _ = picked.shape
-    local_experts, width, ff_pair = weight.shape
-    experts = max(1, local_experts // piece_count)
-    rows = slots // experts
+class Layout:
+    def __init__(self, local_experts, piece_count, capacity):
+        slots = local_experts * capacity // piece_count
+        self.rows = slots // CELLS
+        self.experts = max(1, slots // capacity)
+        self.spread = max(1, capacity // slots)
+        self.each = max(1, self.experts // CELLS)
+        self.cell_count = piece_count * CELLS
+
+    def first_expert(self, piece, cell):
+        within = cell * self.each if self.experts > 1 else 0
+        return (piece * self.experts + within) // self.spread
+
+
+def gate_up(plan, piece_at, cells, layout, picked, weight):
+    _, width, ff_pair = weight.shape
+    rows = layout.rows // layout.each
 
     def kernel(plan_ref, picked_ref, weight_ref, out_ref):
         piece = plan_ref[piece_at]
-        first = plan_ref[expert_at] // spread
-        for i in range(experts):
-            here = slice(i * rows, (i + 1) * rows)
-            picked = picked_ref[piece, here, :]
-            out_ref[here, :ff_pair] = dot(picked[:, :width], weight_ref[first + i]).astype(bf16)
-            out_ref[here, ff_pair:] = picked[:, width:]
-
+        for place, cell in enumerate(cells):
+            first = layout.first_expert(piece, cell)
+            for i in range(layout.each):
+                picked = picked_ref[piece * CELLS + cell, i * rows : (i + 1) * rows, :]
+                start = place * layout.rows + i * rows
+                here = slice(start, start + rows)
+                product = dot(picked[:, :width], weight_ref[first + i])
+                out_ref[here, :ff_pair] = product.astype(bf16)
+                out_ref[here, ff_pair:] = picked[:, width:]
+
+    total = len(cells) * layout.rows
     return pl.pallas_call(
         kernel,
         in_specs=[whole(pltpu.SMEM)] + [whole()] * 2,
-        out_shape=jax.ShapeDtypeStruct((slots, ff_pair + LANES), bf16),
+        out_shape=jax.ShapeDtypeStruct((total, ff_pair + LANES), bf16),
         compiler_params=params(8),
-        cost_estimate=cost(2 * slots * width * ff_pair, 2 * experts * width * ff_pair),
+        cost_estimate=cost(2 * total * width * ff_pair, 2 * total * ff_pair),
         name="gate_up",
     )(plan, picked, weight)
 
@@ -395,48 +412,49 @@
     )(left, right)
 
 
-def hidden_kernel(part_count, model_width, *refs):
-    out_ref = refs[-1]
-    ff_width = out_ref.shape[1]
-    refs = refs[1:]
-    total = refs[0][...].astype(f32)
-    for ref in refs[1:part_count]:
-        total = total + ref[...].astype(f32)
-    squares = total[:, 2 * ff_width : 2 * ff_width + 1] + total[:, 2 * ff_width + 1 : 2 * ff_width + 2]
-    norm = lax.rsqrt(squares / model_width + epsilon)
-    gate = total[:, :ff_width] * norm
-    up = total[:, ff_width : 2 * ff_width] * norm
-    out_ref[...] = (gate / (1.0 + jnp.exp(-gate)) * up).astype(bf16)
-
-
-def hidden_of(parts, ff_width, model_width, beside):
-    return pl.pallas_call(
-        functools.partial(hidden_kernel, len(parts), model_width),
+def hidden_of(parts, starts, layout, ff_width, model_width, beside):
+    def kernel(beside_ref, *refs):
+        out_ref = refs[-1]
+        total = 0.0
+        for ref, start in zip(refs, starts):
+            total = total + ref[start : start + layout.rows, :].astype(f32)
+        high = total[:, 2 * ff_width : 2 * ff_width + 1]
+        low = total[:, 2 * ff_width + 1 : 2 * ff_width + 2]
+        norm = lax.rsqrt((high + low) / model_width + epsilon)
+        gate = total[:, :ff_width] * norm
+        up = total[:, ff_width : 2 * ff_width] * norm
+        out_ref[...] = (gate / (1.0 + jnp.exp(-gate)) * up).astype(bf16)
+
+    return pl.pallas_call(
+        kernel,
         in_specs=[whole(pltpu.HBM)] + [whole()] * len(parts),
-        out_shape=jax.ShapeDtypeStruct((parts[0].shape[0], ff_width), bf16),
+        out_shape=jax.ShapeDtypeStruct((layout.rows, ff_width), bf16),
         compiler_params=params(8),
         name="hidden",
     )(*in_hbm([beside]), *parts)
 
 
-def down(plan, piece_at, expert_at, spread, hidden, weight, high, low, total=None, out_count=1):
-    slots, ff_width = hidden.shape
-    piece_count, tokens, _ = high.shape
-    local_experts, _, piece_width = weight.shape
-    experts = max(1, local_experts // piece_count)
-    each = slots // experts
+def down(plan, cells, layout, hidden, weight, high, low, total=None, out_count=1):
+    ff_width = hidden[0].shape[1]
+    tokens = high.shape[1]
+    piece_width = weight.shape[2]
+    each = layout.rows // layout.each
     rows = tokens // out_count
     out_type = f32 if out_count == 1 else bf16
 
-    def kernel(plan_ref, hidden_ref, weight_ref, high_ref, low_ref, *refs):
+    def kernel(plan_ref, weight_ref, high_ref, low_ref, *refs):
+        hidden_refs, refs = refs[: len(cells)], refs[len(cells) :]
         total_refs, out_refs, held_ref = refs[: -1 - out_count], refs[-1 - out_count : -1], refs[-1]
-        piece = plan_ref[piece_at]
-        first = plan_ref[expert_at] // spread
-        for i in range(experts):
-            here = slice(i * each, (i + 1) * each)
-            held_ref[here, :] = dot(hidden_ref[here, :], weight_ref[first + i]).astype(bf16)
-        held = held_ref[...]
-        summed = dot(high_ref[piece], held) + dot(low_ref[piece], held)
+        summed = 0.0
+        for ref, (piece_at, cell) in zip(hidden_refs, cells):
+            piece = plan_ref[piece_at]
+            first = layout.first_expert(piece, cell)
+            for i in range(layout.each):
+                here = slice(i * each, (i + 1) * each)
+                held_ref[here, :] = dot(ref[here, :], weight_ref[first + i]).astype(bf16)
+            held = held_ref[...]
+            at = piece * CELLS + cell
+            summed = summed + dot(high_ref[at], held) + dot(low_ref[at], held)
         for ref in total_refs:
             summed = summed + ref[...]
         for i, ref in enumerate(out_refs):
@@ -445,13 +463,13 @@
     before = [] if total is None else [total]
     return pl.pallas_call(
         kernel,
-        in_specs=[whole(pltpu.SMEM)] + [whole()] * (4 + len(before)),
+        in_specs=[whole(pltpu.SMEM)] + [whole()] * (3 + len(cells) + len(before)),
         out_shape=[jax.ShapeDtypeStruct((rows, piece_width), out_type)] * out_count,
-        scratch_shapes=[pltpu.VMEM((slots, piece_width), bf16)],
+        scratch_shapes=[pltpu.VMEM((layout.rows, piece_width), bf16)],
         compiler_params=params(8),
-        cost_estimate=cost(2 * slots * ff_width * piece_width, 2 * experts * ff_width * piece_width),
+        cost_estimate=cost(2 * layout.rows * ff_width * piece_width, 2**20),
         name="down",
-    )(plan, hidden, weight, high, low, *before)
+    )(plan, weight, high, low, *hidden, *before)
 
 
 def finish_kernel(mixed_ref, *refs):
@@ -498,7 +516,6 @@
     local_experts, piece_width, _ = gate_up_weight.shape
     ff_width = down_weight.shape[1]
     choices = expert_ids.shape[1]
-    slots = local_experts * ctx_count * MOST // piece_count
     scale = math.log2(math.e) / math.sqrt(head_size)
 
     last = ctx_count * (key_count - query_rows) - own_ctx * key_count
@@ -508,17 +525,13 @@
     slot_pieces = [
         (own_tp ^ flip) * exp_count + (own_exp ^ k) for flip in (0, 1) for k in range(exp_count)
     ]
-    capacity = ctx_count * MOST
-    experts = max(1, slots // capacity)
-    spread = max(1, capacity // slots)
+    layout = Layout(local_experts, piece_count, ctx_count * MOST)
     scalars = [own_ctx * local_experts] + leads + column_pieces + slot_pieces
-    scalars = scalars + [piece * experts for piece in slot_pieces]
     plan = jnp.stack([jnp.asarray(value, jnp.int32) for value in scalars])
     lead_at = 1
     order_at = lead_at + ctx_count
     mine_at = order_at + piece_count
     away_at = mine_at + exp_count
-    expert_at = piece_count
 
     packed = pack(
         queries.reshape(query_rows, width), query_seg, expert_ids, route_weight, gate_up_weight
@@ -543,8 +556,8 @@
         width,
         local_experts,
         choices,
-        piece_count,
-        slots,
+        layout.cell_count,
+        layout.rows,
     )
     projected = project(
         plan,
@@ -564,43 +577,63 @@
         rows[k] = swapped(sent, "ctx", k)
     picked = pick(place, [rows[k] for k in range(ctx_count)])
 
-    def first_half(piece_at):
-        return gate_up(plan, piece_at, piece_at + expert_at, spread, picked, gate_up_weight)
-
-    finals = []
-    for k in far_first(exp_count) + [0]:
-        arrived = swapped(first_half(away_at + k), "tp", 1)
-        mine = first_half(mine_at + k)
-        if k:
-            joined = join(mine, arrived)
-            finals.append(swapped(joined, "exp", k))
-            picked, _ = lax.optimization_barrier((picked, joined))
-        else:
-            finals, mine = lax.optimization_barrier((finals, mine))
-            finals = [arrived, mine] + finals
-    own_hidden = hidden_of(finals, ff_width, model_width, gate_up_weight)
+    def after(value, *others):
+        return lax.optimization_barrier((value,) + others)[0]
+
+    def first_half(piece_at, cells):
+        return gate_up(plan, piece_at, cells, layout, picked, gate_up_weight)
+
+    crossed = [[] for _ in range(CELLS)]
+    arrived = [None] * CELLS
+    for k in far_first(exp_count):
+        near = [swapped(first_half(away_at + k, (0,)), "tp", 1)]
+        mine = first_half(mine_at + k, (0,))
+        picked = after(picked, mine)
+        near.append(swapped(first_half(away_at + k, (1,)), "tp", 1))
+        for cell in range(CELLS):
+            if cell:
+                mine = first_half(mine_at + k, (cell,))
+            joined = join(mine, near[cell])
+            picked = after(picked, joined)
+            crossed[cell].append(swapped(joined, "exp", k))
+            if k == 1:
+                arrived[cell] = swapped(first_half(away_at, (cell,)), "tp", 1)
+    kept = first_half(mine_at, tuple(range(CELLS)))
+
+    def add(cells, hidden, total, out_count=1):
+        return down(
+            plan, cells, layout, hidden, down_weight, combine_high, combine_low, total, out_count
+        )
 
     total = None
-    for k in range(exp_count):
-        here = own_hidden
-        if k:
-            here, total = lax.optimization_barrier((swapped(own_hidden, "exp", k), total))
-        there = swapped(here, "tp", 1)
-        for piece_at, hidden in ((mine_at + k, here), (away_at + k, there)):
-            ends = piece_at == away_at + exp_count - 1
-            totals = down(
-                plan,
-                piece_at,
-                piece_at + expert_at,
-                spread,
-                hidden,
-                down_weight,
-                combine_high,
-                combine_low,
-                total,
-                ctx_count if ends else 1,
-            )
-            total = totals[0]
+    own_hidden = []
+    for cell in range(CELLS):
+        if total is not None:
+            kept = after(kept, total)
+        crossed[cell], kept = lax.optimization_barrier((crossed[cell], kept))
+        parts = [kept, arrived[cell]] + crossed[cell]
+        starts = [cell * layout.rows] + [0] * (len(parts) - 1)
+        hidden = hidden_of(parts, starts, layout, ff_width, model_width, gate_up_weight)
+        own_hidden.append(hidden)
+        if cell == 0:
+            cells = [(mine_at, 0), (away_at, 0)]
+            total = add(cells, [hidden, swapped(hidden, "tp", 1)], total)[0]
+    far = {
+        (k, cell): swapped(own_hidden[cell], "exp", k)
+        for cell in range(CELLS)
+        for k in range(1, exp_count)
+    }
+    cells = [(mine_at, 1), (away_at, 1)]
+    total = add(cells, [own_hidden[1], swapped(own_hidden[1], "tp", 1)], total)[0]
+    last = {}
+    for (k, cell), hidden in far.items():
+        if last:
+            hidden = after(hidden, total)
+        last[k, cell] = swapped(hidden, "tp", 1)
+        total = add([(mine_at + k, cell)], [hidden], total)[0]
+    totals = add(
+        [(away_at + k, cell) for k, cell in last], list(last.values()), total, ctx_count
+    )
     returned = [totals[0]] + [swapped(totals[k], "ctx", k) for k in far_first(ctx_count)]
     return finish(mixed, returned)
 

time: 72.6 us -> 71.2 us (0.981)
  waiting for transfers between devices: 21.9 us -> 12.2 us
  Pallas kernels: 26.5 us -> 30.1 us
  starting transfers between devices: 23.5 us -> 26.7 us
  local copies, waits for them, and re-layouts: 0.17 us -> 1.6 us
    ppermute x21 -> x27, waiting for transfers between devices: 21.9 us -> 12.2 us  [swapped(): return lax.ppermute(value, axes, pairs)]
    ppermute x21 -> x27, starting transfers between devices: 23.5 us -> 26.7 us  [swapped(): return lax.ppermute(value, axes, pairs)]
    pallas_call x4 -> x7, Pallas kernels: 6.86 us -> 8.78 us  [gate_up(): pl.pallas_call(kernel, in_specs=[whole(pltpu.SMEM)] + [whole()] * 2, out_...]
    unnamed x28, local copies, waits for them, and re-layouts: 0.07 us -> 1.51 us
    pallas_call x5 -> x7, Pallas kernels: 5.87 us -> 7.26 us  [the longest x5 6.82 us: down(): pl.pallas_call(kernel, in_specs=[whole(pltpu.SMEM)] + [whole()] * (3 + le...]
  transfers between devices with their start and end apart: 21 -> 27, of which waited for: 13 -> 12; matrix products, arithmetic and copies ran while one was open for 0% -> 0% of each run, Pallas kernels for 26% -> 33%
where the time goes in v7:
time: 71.2 us; the launch traced here: 71 us
  Pallas kernels  30.1 us (42%)
  starting transfers between devices  26.7 us (38%)
  waiting for transfers between devices  12.2 us (17%)
  local copies, waits for them, and re-layouts  1.6 us (2%)
    ppermute x27, starting transfers between devices, swapped(): return lax.ppermute(value, axes, pairs)  26.7 us
    ppermute x27, waiting for transfers between devices, swapped(): return lax.ppermute(value, axes, pairs)  12.2 us
    pallas_call x7, Pallas kernels, gate_up(): pl.pallas_call(kernel, in_specs=[whole(pltpu.SMEM)] + [whole()] * 2, out_...  8.78 us
    pallas_call x4, Pallas kernels, attend(): pl.pallas_call(functools.partial(attend_kernel, heads, scale, lead_at), i...  7.28 us
    pallas_call x5, Pallas kernels, down(): pl.pallas_call(kernel, in_specs=[whole(pltpu.SMEM)] + [whole()] * (3 + le...  6.82 us
    pallas_call x1, Pallas kernels, project(): pl.pallas_call(functools.partial(project_kernel, heads, scale, order_at,...  1.55 us
    unnamed x28, local copies, waits for them, and re-layouts  1.51 us
    pallas_call x1, Pallas kernels, sight_of(): pl.pallas_call(sight_kernel, in_specs=[whole(pltpu.HBM)] * 3, out_shape=j...  1.45 us
  transfers between devices with their start and end apart: 27, of which 12 were waited for; matrix products, arithmetic and copies ran while one was open for 0% of the time, Pallas kernels for 33%

profile of v7, /device:TPU:0, one launch (start us, length us, event | category | flops | bytes accessed | tf_op | source)
XLA Modules:
  0.0 71.0 jit_solution(713859692051652446)
XLA Ops:
  1.0 3.1 %collective-permute-start = (bf16[32,1152]{1,0:T(8,128)(2,1)S(1)}, bf16[32,1152]{1,0:T(8,128)(2,1)S(1)}, u32[]{:S(2)}, u32[]{:S(2)}) collective-permute-start(bf16[32,1152]{1,0:T(8,128)(2,1)S(1)} %pack.1.queries_ref.refs_0_), channel_id=1, source_target_pairs={{0,4},{4,0},{8,12},{12,8},{1,5},{5,1},{9,13},{13,9},{2,6},{6,2},{1... | collective-permute-start | bytes 221192 | tf_op jit(solution)/shard_map/ppermute | solution.py:69
  4.0 2.6 %collective-permute-start.2 = (bf16[32,1152]{1,0:T(8,128)(2,1)S(1)}, bf16[32,1152]{1,0:T(8,128)(2,1)S(1)}, u32[]{:S(2)}, u32[]{:S(2)}) collective-permute-start(bf16[32,1152]{1,0:T(8,128)(2,1)S(1)} %pack.1.queries_ref.refs_0_), channel_id=1, source_target_pairs={{0,8},{4,12},{8,0},{12,4},{1,9},{5,13},{9,1},{13,5},{2,10},{6,14},... | collective-permute-start | bytes 221192 | tf_op jit(solution)/shard_map/ppermute | solution.py:69
  6.7 1.4 %sight.1.sight_ref = bf16[64,2048]{1,0:T(8,128)(2,1)S(1)} custom-call(s32[1,64]{1,0:T(1,128)} %bitcast.40, s32[1,2048]{1,0:T(1,128)} %bitcast.36, bf16[16,512,1536]{2,1,0:T(8,128)(2,1)} %beside_ref.15), custom_call_target="tpu_custom_call" | custom-call | flops 16777216 | bytes 524288 | tf_op jit(solution)/shard_map/sight/pallas_call | solution.py:148
  8.2 1.8 %attend.5 = bf16[32,1152]{1,0:T(8,128)(2,1)S(1)} custom-call(s32[13]{0:T(128)S(1)} %stack.55.plan_ref, bf16[32,1152]{1,0:T(8,128)(2,1)S(1)} %collective-permute-done.queries_ref.refs_1_, bf16[2048,128]{1,0:T(8,128)(2,1)S(1)} %bitcast.26, bf16[2048,128]{1,0:T(8,128)(2,1)S(1)} %bitcast.30, bf16[64,2048]{1,0:T(8,128)(2,1)S(1)} %sight.1.sight_ref, ...), custom_call_target="tpu_custom_call" | custom-call | flops 536870912 | bytes 1048576 | tf_op jit(solution)/shard_map/attend/pallas_call | solution.py:203
  11.8 1.8 %attend.6 = bf16[32,1152]{1,0:T(8,128)(2,1)S(1)} custom-call(s32[13]{0:T(128)S(1)} %stack.55.plan_ref, bf16[32,1152]{1,0:T(8,128)(2,1)S(1)} %collective-permute-done.2.queries_ref.refs_2_, bf16[2048,128]{1,0:T(8,128)(2,1)S(1)} %bitcast.27, bf16[2048,128]{1,0:T(8,128)(2,1)S(1)} %bitcast.31, bf16[64,2048]{1,0:T(8,128)(2,1)S(1)} %sight.1.sight_ref, ...), custom_call_target="tpu_custom_call" | custom-call | flops 536870912 | bytes 1048576 | tf_op jit(solution)/shard_map/attend/pallas_call | solution.py:203
  13.6 2.8 %collective-permute-start.3 = (bf16[32,1152]{1,0:T(8,128)(2,1)S(1)}, bf16[32,1152]{1,0:T(8,128)(2,1)S(1)}, u32[]{:S(2)}, u32[]{:S(2)}) collective-permute-start(bf16[32,1152]{1,0:T(8,128)(2,1)S(1)} %attend.6), channel_id=1, source_target_pairs={{0,8},{4,12},{8,0},{12,4},{1,9},{5,13},{9,1},{13,5},{2,10},{6,14},... | collective-permute-start | bytes 221192 | tf_op jit(solution)/shard_map/ppermute | solution.py:69
  16.4 1.8 %attend.7 = bf16[32,1152]{1,0:T(8,128)(2,1)S(1)} custom-call(s32[13]{0:T(128)S(1)} %stack.55.plan_ref, bf16[32,1152]{1,0:T(8,128)(2,1)S(1)} %collective-permute-done.4.queries_ref.refs_3_, bf16[2048,128]{1,0:T(8,128)(2,1)S(1)} %bitcast.28, bf16[2048,128]{1,0:T(8,128)(2,1)S(1)} %bitcast.32, bf16[64,2048]{1,0:T(8,128)(2,1)S(1)} %sight.1.sight_ref, ...), custom_call_target="tpu_custom_call" | custom-call | flops 536870912 | bytes 1048576 | tf_op jit(solution)/shard_map/attend/pallas_call | solution.py:203
  19.0 1.8 %attend.4.refs_0_ = bf16[32,1152]{1,0:T(8,128)(2,1)S(1)} custom-call(s32[13]{0:T(128)S(1)} %stack.55.plan_ref, bf16[32,1152]{1,0:T(8,128)(2,1)S(1)} %pack.1.queries_ref.refs_0_, bf16[2048,128]{1,0:T(8,128)(2,1)S(1)} %bitcast.29, bf16[2048,128]{1,0:T(8,128)(2,1)S(1)} %bitcast.33, bf16[64,2048]{1,0:T(8,128)(2,1)S(1)} %sight.1.sight_ref, ...), custom_call_target="tpu_custom_call" | custom-call | flops 536870912 | bytes 1048576 | tf_op jit(solution)/shard_map/attend/pallas_call | solution.py:203
  20.9 3.7 %collective-permute-done.5.refs_3_ = bf16[32,1152]{1,0:T(8,128)(2,1)S(1)} collective-permute-done((bf16[32,1152]{1,0:T(8,128)(2,1)S(1)}, bf16[32,1152]{1,0:T(8,128)(2,1)S(1)}, u32[]{:S(2)}, u32[]{:S(2)}) %collective-permute-start.5) | collective-permute-done | bytes 73760 | tf_op jit(solution)/shard_map/ppermute | solution.py:69
  24.5 1.5 %project.1 = (bf16[32,512]{1,0:T(8,128)(2,1)S(1)}, bf16[32,512]{1,0:T(8,128)(2,1)S(1)}, bf16[32,512]{1,0:T(8,128)(2,1)S(1)}, bf16[32,512]{1,0:T(8,128)(2,1)S(1)}) custom-call(s32[13]{0:T(128)S(1)} %stack.55.plan_ref, bf16[32,1152]{1,0:T(8,128)(2,1)S(1)} %attend.4.refs_0_, bf16[32,1152]{1,0:T(8,128)(2,1)S(1)} %collective-permute-done.1.refs_1_, ...), custom_call_target="tpu_custom_call" | custom-call | flops 134217728 | bytes 4194304 | tf_op jit(solution)/shard_map/project/pallas_call | solution.py:247
  26.1 1.6 %collective-permute-start.7 = (bf16[32,512]{1,0:T(8,128)(2,1)S(1)}, bf16[32,512]{1,0:T(8,128)(2,1)S(1)}, u32[]{:S(2)}, u32[]{:S(2)}) collective-permute-start(bf16[32,512]{1,0:T(8,128)(2,1)S(1)} %get-tuple-element.29), channel_id=1, source_target_pairs={{0,2},{1,3},{2,0},{3,1},{4,6},{5,7},{6,4},{7,5},{8,10},{9,11},{10,... | collective-permute-start | bytes 98312 | tf_op jit(solution)/shard_map/ppermute | solution.py:69
  28.0 1.8 %collective-permute-done.6.refs_1_ = bf16[32,512]{1,0:T(8,128)(2,1)S(1)} collective-permute-done((bf16[32,512]{1,0:T(8,128)(2,1)S(1)}, bf16[32,512]{1,0:T(8,128)(2,1)S(1)}, u32[]{:S(2)}, u32[]{:S(2)}) %collective-permute-start.6) | collective-permute-done | bytes 32800 | tf_op jit(solution)/shard_map/ppermute | solution.py:69
  31.1 3.6 %collective-permute-start.9 = (bf16[32,640]{1,0:T(8,128)(2,1)S(1)}, bf16[32,640]{1,0:T(8,128)(2,1)S(1)}, u32[]{:S(2)}, u32[]{:S(2)}) collective-permute-start(bf16[32,640]{1,0:T(8,128)(2,1)S(1)} %get-tuple-element.35.refs_0_), channel_id=1, source_target_pairs={{0,4},{4,0},{8,12},{12,8},{1,5},{5,1},{9,13},{13,9},{2,6},{6,2},{1... | collective-permute-start | bytes 122888 | tf_op jit(solution)/shard_map/ppermute | solution.py:69
  34.7 1.2 %route.1 = (bf16[8,128,64]{2,1,0:T(8,128)(2,1)S(1)}, bf16[8,128,64]{2,1,0:T(8,128)(2,1)S(1)}, bf16[8,128,64]{2,1,0:T(8,128)(2,1)S(1)}) custom-call(s32[13]{0:T(128)S(1)} %stack.55.plan_ref, bf16[32,1152]{1,0:T(8,128)(2,1)S(1)} %pack.1.queries_ref.refs_0_, bf16[32,1152]{1,0:T(8,128)(2,1)S(1)} %collective-permute-done.queries_ref.refs_1_, ...), custom_call_target="tpu_custom_call" | custom-call | flops 33554432 | bytes 1048576 | tf_op jit(solution)/shard_map/route/pallas_call | solution.py:319
  38.9 1.2 %gate_up.7.left_ref = bf16[64,1664]{1,0:T(8,128)(2,1)S(1)} custom-call(s32[13]{0:T(128)S(1)} %stack.55.plan_ref, bf16[8,64,640]{2,1,0:T(8,128)(2,1)S(1)} %pick.1.picked_ref, bf16[16,512,1536]{2,1,0:T(8,128)(2,1)S(1)} %bitcast.23), custom_call_target="tpu_custom_call" | custom-call | flops 100663296 | bytes 196608 | tf_op jit(solution)/shard_map/gate_up/pallas_call | solution.py:388
  40.1 1.2 %gate_up.10 = bf16[64,1664]{1,0:T(8,128)(2,1)S(1)} custom-call(s32[13]{0:T(128)S(1)} %stack.55.plan_ref, bf16[8,64,640]{2,1,0:T(8,128)(2,1)S(1)} %pick.1.picked_ref, bf16[16,512,1536]{2,1,0:T(8,128)(2,1)S(1)} %bitcast.23), custom_call_target="tpu_custom_call" | custom-call | flops 100663296 | bytes 196608 | tf_op jit(solution)/shard_map/gate_up/pallas_call | solution.py:388
  48.2 1.7 %gate_up.11.refs_0_ = bf16[128,1664]{1,0:T(8,128)(2,1)S(1)} custom-call(s32[13]{0:T(128)S(1)} %stack.55.plan_ref, bf16[8,64,640]{2,1,0:T(8,128)(2,1)S(1)} %pick.1.picked_ref, bf16[16,512,1536]{2,1,0:T(8,128)(2,1)S(1)} %bitcast.23), custom_call_target="tpu_custom_call" | custom-call | flops 201326592 | bytes 393216 | tf_op jit(solution)/shard_map/gate_up/pallas_call | solution.py:388
  51.7 1.4 %slice-done.8 = s8[4194304]{0:T(1024)(128)(4,1)S(1)} async-done(((s8[12582912]{0:T(1024)(128)(4,1)}), s8[4194304]{0:T(1024)(128)(4,1)S(1)}, s32[]{:S(2)}) %slice-start.8) | async-done | bytes 4194328
  53.1 1.5 %down.5.refs_2_ = f32[128,512]{1,0:T(8,128)S(1)} custom-call(s32[13]{0:T(128)S(1)} %stack.55.plan_ref, bf16[16,768,512]{2,1,0:T(8,128)(2,1)S(1)} %bitcast.25, bf16[8,128,64]{2,1,0:T(8,128)(2,1)S(1)} %get-tuple-element.32.high_ref, bf16[8,128,64]{2,1,0:T(8,128)(2,1)S(1)} %get-tuple-element.33.low_ref, bf16[64,768]{1,0:T(8,128)(2,1)S(1)} %hidden.2.refs_0_, ...), custom_call_target="tpu_custom_call" | custom-call | flops 50331648 | bytes 1048576 | tf_op jit(solution)/shard_map/down/pallas_call | solution.py:464
  56.3 1.5 %down.6.refs_1_ = f32[128,512]{1,0:T(8,128)S(1)} custom-call(s32[13]{0:T(128)S(1)} %stack.55.plan_ref, bf16[16,768,512]{2,1,0:T(8,128)(2,1)S(1)} %bitcast.25, bf16[8,128,64]{2,1,0:T(8,128)(2,1)S(1)} %get-tuple-element.32.high_ref, bf16[8,128,64]{2,1,0:T(8,128)(2,1)S(1)} %get-tuple-element.33.low_ref, bf16[64,768]{1,0:T(8,128)(2,1)S(1)} %hidden.3.refs_0_, ...), custom_call_target="tpu_custom_call" | custom-call | flops 50331648 | bytes 1048576 | tf_op jit(solution)/shard_map/down/pallas_call | solution.py:464
  61.5 1.5 %down.9 = (bf16[32,512]{1,0:T(8,128)(2,1)S(1)}, bf16[32,512]{1,0:T(8,128)(2,1)S(1)}, bf16[32,512]{1,0:T(8,128)(2,1)S(1)}, bf16[32,512]{1,0:T(8,128)(2,1)S(1)}) custom-call(s32[13]{0:T(128)S(1)} %stack.55.plan_ref, bf16[16,768,512]{2,1,0:T(8,128)(2,1)S(1)} %bitcast.25, bf16[8,128,64]{2,1,0:T(8,128)(2,1)S(1)} %get-tuple-element.32.high_ref, ...), custom_call_target="tpu_custom_call" | custom-call | flops 50331648 | bytes 1048576 | tf_op jit(solution)/shard_map/down/pallas_call | solution.py:464
  63.0 1.9 %collective-permute-start.24 = (bf16[32,512]{1,0:T(8,128)(2,1)S(1)}, bf16[32,512]{1,0:T(8,128)(2,1)S(1)}, u32[]{:S(2)}, u32[]{:S(2)}) collective-permute-start(bf16[32,512]{1,0:T(8,128)(2,1)S(1)} %get-tuple-element.46), channel_id=1, source_target_pairs={{0,12},{4,8},{8,4},{12,0},{1,13},{5,9},{9,5},{13,1},{2,14},{6,10},... | collective-permute-start | bytes 98312 | tf_op jit(solution)/shard_map/ppermute | solution.py:69
  66.0 1.4 %collective-permute-start.26 = (bf16[32,512]{1,0:T(8,128)(2,1)S(1)}, bf16[32,512]{1,0:T(8,128)(2,1)S(1)}, u32[]{:S(2)}, u32[]{:S(2)}) collective-permute-start(bf16[32,512]{1,0:T(8,128)(2,1)S(1)} %get-tuple-element.48), channel_id=1, source_target_pairs={{0,4},{4,0},{8,12},{12,8},{1,5},{5,1},{9,13},{13,9},{2,6},{6,2},{1... | collective-permute-start | bytes 98312 | tf_op jit(solution)/shard_map/ppermute | solution.py:69
  67.5 1.6 %collective-permute-done.24.refs_1_ = bf16[32,512]{1,0:T(8,128)(2,1)S(1)} collective-permute-done((bf16[32,512]{1,0:T(8,128)(2,1)S(1)}, bf16[32,512]{1,0:T(8,128)(2,1)S(1)}, u32[]{:S(2)}, u32[]{:S(2)}) %collective-permute-start.24) | collective-permute-done | bytes 32800 | tf_op jit(solution)/shard_map/ppermute | solution.py:69
  (89 shorter events, 25.2 us)
Async XLA Ops:
  1.0 7.3 %collective-permute-start = (bf16[32,1152]{1,0:T(8,128)(2,1)S(1)}, bf16[32,1152]{1,0:T(8,128)(2,1)S(1)}, u32[]{:S(2)}, u32[]{:S(2)}) collective-permute-start(bf16[32,1152]{1,0:T(8,128)(2,1)S(1)} %pack.1.queries_ref.refs_0_), channel_id=1, source_target_pairs={{0,4},{4,0},{8,12},{12,8},{1,5},{5,1},{9,13},{13,9},{2,6},{6,2},{1... | collective-permute-start | bytes 221192 | tf_op jit(solution)/shard_map/ppermute | solution.py:69
  4.0 7.8 %collective-permute-start.2 = (bf16[32,1152]{1,0:T(8,128)(2,1)S(1)}, bf16[32,1152]{1,0:T(8,128)(2,1)S(1)}, u32[]{:S(2)}, u32[]{:S(2)}) collective-permute-start(bf16[32,1152]{1,0:T(8,128)(2,1)S(1)} %pack.1.queries_ref.refs_0_), channel_id=1, source_target_pairs={{0,8},{4,12},{8,0},{12,4},{1,9},{5,13},{9,1},{13,5},{2,10},{6,14},... | collective-permute-start | bytes 221192 | tf_op jit(solution)/shard_map/ppermute | solution.py:69
  6.6 9.8 %collective-permute-start.4 = (bf16[32,1152]{1,0:T(8,128)(2,1)S(1)}, bf16[32,1152]{1,0:T(8,128)(2,1)S(1)}, u32[]{:S(2)}, u32[]{:S(2)}) collective-permute-start(bf16[32,1152]{1,0:T(8,128)(2,1)S(1)} %pack.1.queries_ref.refs_0_), channel_id=1, source_target_pairs={{0,12},{4,8},{8,4},{12,0},{1,13},{5,9},{9,5},{13,1},{2,14},{6,10},... | collective-permute-start | bytes 221192 | tf_op jit(solution)/shard_map/ppermute | solution.py:69
  10.1 10.8 %collective-permute-start.1 = (bf16[32,1152]{1,0:T(8,128)(2,1)S(1)}, bf16[32,1152]{1,0:T(8,128)(2,1)S(1)}, u32[]{:S(2)}, u32[]{:S(2)}) collective-permute-start(bf16[32,1152]{1,0:T(8,128)(2,1)S(1)} %attend.5), channel_id=1, source_target_pairs={{0,4},{4,0},{8,12},{12,8},{1,5},{5,1},{9,13},{13,9},{2,6},{6,2},{1... | collective-permute-start | bytes 221192 | tf_op jit(solution)/shard_map/ppermute | solution.py:69
  13.6 7.2 %collective-permute-start.3 = (bf16[32,1152]{1,0:T(8,128)(2,1)S(1)}, bf16[32,1152]{1,0:T(8,128)(2,1)S(1)}, u32[]{:S(2)}, u32[]{:S(2)}) collective-permute-start(bf16[32,1152]{1,0:T(8,128)(2,1)S(1)} %attend.6), channel_id=1, source_target_pairs={{0,8},{4,12},{8,0},{12,4},{1,9},{5,13},{9,1},{13,5},{2,10},{6,14},... | collective-permute-start | bytes 221192 | tf_op jit(solution)/shard_map/ppermute | solution.py:69
  18.3 6.2 %collective-permute-start.5 = (bf16[32,1152]{1,0:T(8,128)(2,1)S(1)}, bf16[32,1152]{1,0:T(8,128)(2,1)S(1)}, u32[]{:S(2)}, u32[]{:S(2)}) collective-permute-start(bf16[32,1152]{1,0:T(8,128)(2,1)S(1)} %attend.7), channel_id=1, source_target_pairs={{0,12},{4,8},{8,4},{12,0},{1,13},{5,9},{9,5},{13,1},{2,14},{6,10},... | collective-permute-start | bytes 221192 | tf_op jit(solution)/shard_map/ppermute | solution.py:69
  26.1 3.7 %collective-permute-start.6 = (bf16[32,512]{1,0:T(8,128)(2,1)S(1)}, bf16[32,512]{1,0:T(8,128)(2,1)S(1)}, u32[]{:S(2)}, u32[]{:S(2)}) collective-permute-start(bf16[32,512]{1,0:T(8,128)(2,1)S(1)} %get-tuple-element.28), channel_id=1, source_target_pairs={{0,3},{1,2},{2,1},{3,0},{4,7},{5,6},{6,5},{7,4},{8,11},{9,10},{10,... | collective-permute-start | bytes 98312 | tf_op jit(solution)/shard_map/ppermute | solution.py:69
  26.1 4.0 %collective-permute-start.7 = (bf16[32,512]{1,0:T(8,128)(2,1)S(1)}, bf16[32,512]{1,0:T(8,128)(2,1)S(1)}, u32[]{:S(2)}, u32[]{:S(2)}) collective-permute-start(bf16[32,512]{1,0:T(8,128)(2,1)S(1)} %get-tuple-element.29), channel_id=1, source_target_pairs={{0,2},{1,3},{2,0},{3,1},{4,6},{5,7},{6,4},{7,5},{8,10},{9,11},{10,... | collective-permute-start | bytes 98312 | tf_op jit(solution)/shard_map/ppermute | solution.py:69
  27.7 2.5 %collective-permute-start.8 = (bf16[32,512]{1,0:T(8,128)(2,1)S(1)}, bf16[32,512]{1,0:T(8,128)(2,1)S(1)}, u32[]{:S(2)}, u32[]{:S(2)}) collective-permute-start(bf16[32,512]{1,0:T(8,128)(2,1)S(1)} %get-tuple-element.30), channel_id=1, source_target_pairs={{0,1},{1,0},{2,3},{3,2},{4,5},{5,4},{6,7},{7,6},{8,9},{9,8},{10,11... | collective-permute-start | bytes 98312 | tf_op jit(solution)/shard_map/ppermute | solution.py:69
  30.3 6.3 %collective-permute-start.11 = (bf16[32,640]{1,0:T(8,128)(2,1)S(1)}, bf16[32,640]{1,0:T(8,128)(2,1)S(1)}, u32[]{:S(2)}, u32[]{:S(2)}) collective-permute-start(bf16[32,640]{1,0:T(8,128)(2,1)S(1)} %get-tuple-element.35.refs_0_), channel_id=1, source_target_pairs={{0,12},{4,8},{8,4},{12,0},{1,13},{5,9},{9,5},{13,1},{2,14},{6,10},... | collective-permute-start | bytes 122888 | tf_op jit(solution)/shard_map/ppermute | solution.py:69
  31.1 6.0 %collective-permute-start.10 = (bf16[32,640]{1,0:T(8,128)(2,1)S(1)}, bf16[32,640]{1,0:T(8,128)(2,1)S(1)}, u32[]{:S(2)}, u32[]{:S(2)}) collective-permute-start(bf16[32,640]{1,0:T(8,128)(2,1)S(1)} %get-tuple-element.35.refs_0_), channel_id=1, source_target_pairs={{0,8},{4,12},{8,0},{12,4},{1,9},{5,13},{9,1},{13,5},{2,10},{6,14},... | collective-permute-start | bytes 122888 | tf_op jit(solution)/shard_map/ppermute | solution.py:69
  31.1 6.1 %collective-permute-start.9 = (bf16[32,640]{1,0:T(8,128)(2,1)S(1)}, bf16[32,640]{1,0:T(8,128)(2,1)S(1)}, u32[]{:S(2)}, u32[]{:S(2)}) collective-permute-start(bf16[32,640]{1,0:T(8,128)(2,1)S(1)} %get-tuple-element.35.refs_0_), channel_id=1, source_target_pairs={{0,4},{4,0},{8,12},{12,8},{1,5},{5,1},{9,13},{13,9},{2,6},{6,2},{1... | collective-permute-start | bytes 122888 | tf_op jit(solution)/shard_map/ppermute | solution.py:69
  38.9 2.9 %collective-permute-start.12 = (bf16[64,1664]{1,0:T(8,128)(2,1)S(1)}, bf16[64,1664]{1,0:T(8,128)(2,1)S(1)}, u32[]{:S(2)}, u32[]{:S(2)}) collective-permute-start(bf16[64,1664]{1,0:T(8,128)(2,1)S(1)} %gate_up.8), channel_id=1, source_target_pairs={{0,1},{1,0},{2,3},{3,2},{4,5},{5,4},{6,7},{7,6},{8,9},{9,8},{10,11... | collective-permute-start | bytes 638984 | tf_op jit(solution)/shard_map/ppermute | solution.py:69
  41.3 4.3 %collective-permute-start.14 = (bf16[64,1664]{1,0:T(8,128)(2,1)S(1)}, bf16[64,1664]{1,0:T(8,128)(2,1)S(1)}, u32[]{:S(2)}, u32[]{:S(2)}) collective-permute-start(bf16[64,1664]{1,0:T(8,128)(2,1)S(1)} %gate_up.10), channel_id=1, source_target_pairs={{0,1},{1,0},{2,3},{3,2},{4,5},{5,4},{6,7},{7,6},{8,9},{9,8},{10,11... | collective-permute-start | bytes 638984 | tf_op jit(solution)/shard_map/ppermute | solution.py:69
  42.0 7.9 %collective-permute-start.13 = (bf16[64,1664]{1,0:T(8,128)(2,1)S(1)}, bf16[64,1664]{1,0:T(8,128)(2,1)S(1)}, u32[]{:S(2)}, u32[]{:S(2)}) collective-permute-start(bf16[64,1664]{1,0:T(8,128)(2,1)S(1)} %join.2), channel_id=1, source_target_pairs={{0,2},{2,0},{1,3},{3,1},{4,6},{6,4},{5,7},{7,5},{8,10},{10,8},{9,1... | collective-permute-start | bytes 638984 | tf_op jit(solution)/shard_map/ppermute | solution.py:69
  44.4 5.6 %collective-permute-start.15 = (bf16[64,1664]{1,0:T(8,128)(2,1)S(1)}, bf16[64,1664]{1,0:T(8,128)(2,1)S(1)}, u32[]{:S(2)}, u32[]{:S(2)}) collective-permute-start(bf16[64,1664]{1,0:T(8,128)(2,1)S(1)} %gate_up.12), channel_id=1, source_target_pairs={{0,1},{1,0},{2,3},{3,2},{4,5},{5,4},{6,7},{7,6},{8,9},{9,8},{10,11... | collective-permute-start | bytes 638984 | tf_op jit(solution)/shard_map/ppermute | solution.py:69
  45.8 8.8 %collective-permute-start.18 = (bf16[64,1664]{1,0:T(8,128)(2,1)S(1)}, bf16[64,1664]{1,0:T(8,128)(2,1)S(1)}, u32[]{:S(2)}, u32[]{:S(2)}) collective-permute-start(bf16[64,1664]{1,0:T(8,128)(2,1)S(1)} %join.3), channel_id=1, source_target_pairs={{0,2},{2,0},{1,3},{3,1},{4,6},{6,4},{5,7},{7,5},{8,10},{10,8},{9,1... | collective-permute-start | bytes 638984 | tf_op jit(solution)/shard_map/ppermute | solution.py:69
  48.0 6.7 %collective-permute-start.20 = (bf16[64,1664]{1,0:T(8,128)(2,1)S(1)}, bf16[64,1664]{1,0:T(8,128)(2,1)S(1)}, u32[]{:S(2)}, u32[]{:S(2)}) collective-permute-start(bf16[64,1664]{1,0:T(8,128)(2,1)S(1)} %gate_up.13), channel_id=1, source_target_pairs={{0,1},{1,0},{2,3},{3,2},{4,5},{5,4},{6,7},{7,6},{8,9},{9,8},{10,11... | collective-permute-start | bytes 638984 | tf_op jit(solution)/shard_map/ppermute | solution.py:69
  50.6 5.8 %collective-permute-start.16 = (bf16[64,768]{1,0:T(8,128)(2,1)S(1)}, bf16[64,768]{1,0:T(8,128)(2,1)S(1)}, u32[]{:S(2)}, u32[]{:S(2)}) collective-permute-start(bf16[64,768]{1,0:T(8,128)(2,1)S(1)} %hidden.2.refs_0_), channel_id=1, source_target_pairs={{0,2},{2,0},{1,3},{3,1},{4,6},{6,4},{5,7},{7,5},{8,10},{10,8},{9,1... | collective-permute-start | bytes 294920 | tf_op jit(solution)/shard_map/ppermute | solution.py:69
  55.2 4.9 %collective-permute-start.21 = (bf16[64,768]{1,0:T(8,128)(2,1)S(1)}, bf16[64,768]{1,0:T(8,128)(2,1)S(1)}, u32[]{:S(2)}, u32[]{:S(2)}) collective-permute-start(bf16[64,768]{1,0:T(8,128)(2,1)S(1)} %hidden.3.refs_0_), channel_id=1, source_target_pairs={{0,2},{2,0},{1,3},{3,1},{4,6},{6,4},{5,7},{7,5},{8,10},{10,8},{9,1... | collective-permute-start | bytes 294920 | tf_op jit(solution)/shard_map/ppermute | solution.py:69
  56.3 5.0 %collective-permute-start.17 = (bf16[64,768]{1,0:T(8,128)(2,1)S(1)}, bf16[64,768]{1,0:T(8,128)(2,1)S(1)}, u32[]{:S(2)}, u32[]{:S(2)}) collective-permute-start(bf16[64,768]{1,0:T(8,128)(2,1)S(1)} %collective-permute-done.16.refs_0_), channel_id=1, source_target_pairs={{0,1},{1,0},{2,3},{3,2},{4,5},{5,4},{6,7},{7,6},{8,9},{9,8},{10,11... | collective-permute-start | bytes 294920 | tf_op jit(solution)/shard_map/ppermute | solution.py:69
  63.0 6.0 %collective-permute-start.24 = (bf16[32,512]{1,0:T(8,128)(2,1)S(1)}, bf16[32,512]{1,0:T(8,128)(2,1)S(1)}, u32[]{:S(2)}, u32[]{:S(2)}) collective-permute-start(bf16[32,512]{1,0:T(8,128)(2,1)S(1)} %get-tuple-element.46), channel_id=1, source_target_pairs={{0,12},{4,8},{8,4},{12,0},{1,13},{5,9},{9,5},{13,1},{2,14},{6,10},... | collective-permute-start | bytes 98312 | tf_op jit(solution)/shard_map/ppermute | solution.py:69
  64.9 5.2 %collective-permute-start.25 = (bf16[32,512]{1,0:T(8,128)(2,1)S(1)}, bf16[32,512]{1,0:T(8,128)(2,1)S(1)}, u32[]{:S(2)}, u32[]{:S(2)}) collective-permute-start(bf16[32,512]{1,0:T(8,128)(2,1)S(1)} %get-tuple-element.47), channel_id=1, source_target_pairs={{0,8},{4,12},{8,0},{12,4},{1,9},{5,13},{9,1},{13,5},{2,10},{6,14},... | collective-permute-start | bytes 98312 | tf_op jit(solution)/shard_map/ppermute | solution.py:69
  66.0 4.3 %collective-permute-start.26 = (bf16[32,512]{1,0:T(8,128)(2,1)S(1)}, bf16[32,512]{1,0:T(8,128)(2,1)S(1)}, u32[]{:S(2)}, u32[]{:S(2)}) collective-permute-start(bf16[32,512]{1,0:T(8,128)(2,1)S(1)} %get-tuple-element.48), channel_id=1, source_target_pairs={{0,4},{4,0},{8,12},{12,8},{1,5},{5,1},{9,13},{13,9},{2,6},{6,2},{1... | collective-permute-start | bytes 98312 | tf_op jit(solution)/shard_map/ppermute | solution.py:69
  (17 other events, 167.1 us)

commit v8 on v7

--- a/solution.py
+++ b/solution.py
@@ -40,6 +40,38 @@
 
 def in_hbm(values):
     return [pltpu.with_memory_space_constraint(value, pltpu.HBM) for value in values]
+
+
+class Layout:
+    def __init__(self, local_experts, key_count, query_rows):
+        self.ctx, self.exp, self.tp = (lax.axis_size(axis) for axis in ("ctx", "exp", "tp"))
+        self.key_count, self.query_rows = key_count, query_rows
+        self.local_experts = local_experts
+        self.piece_count = self.exp * self.tp
+        capacity = self.ctx * MOST
+        slots = local_experts * capacity // self.piece_count
+        self.rows = slots // CELLS
+        self.experts = max(1, slots // capacity)
+        self.spread = max(1, capacity // slots)
+        self.each = max(1, self.experts // CELLS)
+        self.cell_count = self.piece_count * CELLS
+
+    def lead(self, k):
+        own = lax.axis_index("ctx")
+        start = self.ctx * (self.key_count - self.query_rows)
+        return start + (own ^ k) * self.query_rows - own * self.key_count
+
+    def column_piece(self, k):
+        return (lax.axis_index("exp") * self.tp + lax.axis_index("tp")) ^ k
+
+    def first_local_expert(self):
+        return lax.axis_index("ctx") * self.local_experts
+
+    def cell(self, name):
+        flip, k, cell = name
+        piece = (lax.axis_index("tp") ^ flip) * self.exp + (lax.axis_index("exp") ^ k)
+        within = cell * self.each if self.experts > 1 else 0
+        return piece * CELLS + cell, lax.div(piece * self.experts + within, self.spread)
 
 
 def lane_ids(shape):
@@ -122,43 +154,31 @@
     )(*in_hbm([queries] + small + [beside]))
 
 
-def sight_kernel(parent_ref, key_seg_ref, beside_ref, sight_ref, parent_here, key_seg_here, done):
-    copies = [
-        pltpu.make_async_copy(parent_ref, parent_here, done.at[0]),
-        pltpu.make_async_copy(key_seg_ref, key_seg_here, done.at[1]),
-    ]
-    for copy in copies:
-        copy.start()
-    for copy in copies:
-        copy.wait()
+def sight_kernel(parent_ref, key_seg_ref, sight_ref):
     seg_count, key_count = sight_ref.shape
     square = (seg_count, seg_count)
     same = row_ids(square) == lane_ids(square)
-    one = as_bf16((parent_here[...] == row_ids(square)) | same)
+    one = as_bf16((parent_ref[...] == row_ids(square)) | same)
     two = as_bf16(dot(one, one) > 0.5)
     four = as_bf16(dot(two, two) > 0.5)
     six = as_bf16(dot(four, two) > 0.5)
-    keys = as_bf16(key_seg_here[...] == row_ids((seg_count, key_count)))
+    keys = as_bf16(key_seg_ref[...] == row_ids((seg_count, key_count)))
     sight_ref[...] = dot(six, keys, ((0,), (0,))).astype(bf16)
 
 
-def sight_of(parent, key_seg, beside):
+def sight_of(parent, key_seg):
     assert DEPTH == 6
-    small = [parent[None, :], key_seg[None, :]]
     return pl.pallas_call(
         sight_kernel,
-        in_specs=[whole(pltpu.HBM)] * 3,
         out_shape=jax.ShapeDtypeStruct((parent.shape[0], key_seg.shape[0]), bf16),
-        scratch_shapes=[pltpu.VMEM(value.shape, value.dtype) for value in small]
-        + [pltpu.SemaphoreType.DMA((2,))],
         compiler_params=params(4),
         cost_estimate=cost(2**24, 2**19),
         name="sight",
-    )(*in_hbm(small + [beside]))
+    )(parent[None, :], key_seg[None, :])
 
 
 def attend_kernel(
-    heads, scale, lead_at, plan_ref, queries_ref, keys_ref, values_ref, sight_ref, beside_ref,
+    heads, scale, layout, k, queries_ref, keys_ref, values_ref, sight_ref, beside_ref,
     out_ref, stacked_ref, probs_ref,
 ):
     rows = queries_ref.shape[0]
@@ -170,7 +190,7 @@
     onehot = as_bf16(own_seg == lane_ids((rows, seg_count)))
     seen = dot(onehot, sight_ref[...]) > 0.5
     place = (rows, key_count)
-    causal = lane_ids(place) - row_ids(place) <= plan_ref[lead_at]
+    causal = lane_ids(place) - row_ids(place) <= layout.lead(k)
     bias = jnp.where(seen & causal, 0.0, masked_score)
     for head in range(heads):
         columns = slice(head * head_size, (head + 1) * head_size)
@@ -196,13 +216,13 @@
         out_ref[:, columns] = sums[head * rows : (head + 1) * rows, :].astype(bf16)
 
 
-def attend(plan, lead_at, queries, keys, values, sight, heads, scale, beside):
+def attend(layout, k, queries, keys, values, sight, heads, scale, beside):
     rows, columns = queries.shape
     key_count, head_size = keys.shape
     work = rows * heads * key_count
     return pl.pallas_call(
-        functools.partial(attend_kernel, heads, scale, lead_at),
-        in_specs=[whole(pltpu.SMEM)] + [whole()] * 4 + [whole(pltpu.HBM)],
+        functools.partial(attend_kernel, heads, scale, layout, k),
+        in_specs=[whole()] * 4 + [whole(pltpu.HBM)],
         out_shape=jax.ShapeDtypeStruct((rows, columns), bf16),
         scratch_shapes=[
             pltpu.VMEM((rows * heads, head_size), bf16),
@@ -211,10 +231,10 @@
         compiler_params=params(8),
         cost_estimate=cost(8 * work * head_size, 2**20, work),
         name="attend",
-    )(plan, queries, keys, values, sight, *in_hbm([beside]))
-
-
-def project_kernel(heads, scale, order_at, source_count, plan_ref, *refs):
+    )(queries, keys, values, sight, *in_hbm([beside]))
+
+
+def project_kernel(heads, scale, layout, source_count, *refs):
     parts_refs, weight_ref = refs[:source_count], refs[source_count]
     out_refs, attention_ref = refs[source_count + 1 : -1], refs[-1]
     width = attention_ref.shape[1]
@@ -236,23 +256,22 @@
         attention_ref[:, columns] = merged.astype(bf16)
     for i, out_ref in enumerate(out_refs):
         piece_width = out_ref.shape[1]
-        start = pl.multiple_of(plan_ref[order_at + i] * piece_width, piece_width)
+        start = pl.multiple_of(layout.column_piece(i) * piece_width, piece_width)
         out_ref[...] = dot(attention_ref[...], weight_ref[:, pl.ds(start, piece_width)]).astype(bf16)
 
 
-def project(plan, order_at, parts, weight, heads, scale, piece_count):
+def project(layout, parts, weight, heads, scale):
     rows = parts[0].shape[0]
     width, model_width = weight.shape
-    piece_width = model_width // piece_count
-    return pl.pallas_call(
-        functools.partial(project_kernel, heads, scale, order_at, len(parts)),
-        in_specs=[whole(pltpu.SMEM)] + [whole()] * (len(parts) + 1),
-        out_shape=[jax.ShapeDtypeStruct((rows, piece_width), bf16)] * piece_count,
+    piece_width = model_width // layout.piece_count
+    return pl.pallas_call(
+        functools.partial(project_kernel, heads, scale, layout, len(parts)),
+        out_shape=[jax.ShapeDtypeStruct((rows, piece_width), bf16)] * layout.piece_count,
         scratch_shapes=[pltpu.VMEM((rows, width), bf16)],
         compiler_params=params(8),
         cost_estimate=cost(2 * rows * width * model_width, 2 * width * model_width),
         name="project",
-    )(plan, *parts, weight)
+    )(*parts, weight)
 
 
 def mix_kernel(residual_ref, gain_ref, *refs):
@@ -282,11 +301,12 @@
     )(residual, gain[None, :], *parts)
 
 
-def route_kernel(local_experts, choices, width, first_at, plan_ref, *refs):
+def route_kernel(layout, choices, width, *refs):
     info_refs, (place_ref, high_ref, low_ref) = refs[:-3], refs[-3:]
-    piece_count, tokens, slots = place_ref.shape
+    cell_count, tokens, slots = place_ref.shape
+    local_experts = layout.local_experts
     info = jnp.concatenate([ref[:, width:] for ref in info_refs], axis=0).astype(f32)
-    expert = (lane_ids((tokens, local_experts)) + plan_ref[first_at]).astype(f32)
+    expert = (lane_ids((tokens, local_experts)) + layout.first_local_expert()).astype(f32)
     member = jnp.zeros((tokens, local_experts), f32)
     weight_high = jnp.zeros((tokens, local_experts), f32)
     weight_low = jnp.zeros((tokens, local_experts), f32)
@@ -302,8 +322,8 @@
     rank = jnp.where(member > 0.5, dot(earlier, member.astype(bf16)), -1.0).astype(bf16)
     weight_high = weight_high.astype(bf16)
     weight_low = weight_low.astype(bf16)
-    capacity = piece_count * slots // local_experts
-    for piece in range(piece_count):
+    capacity = cell_count * slots // local_experts
+    for piece in range(cell_count):
         slot = lane_ids((local_experts, slots)) + piece * slots
         spread = as_bf16(slot // capacity == row_ids((local_experts, slots)))
         wanted = (lane_ids((tokens, slots)) + piece * slots) % capacity
@@ -313,17 +333,16 @@
         low_ref[piece] = jnp.where(placed, dot(weight_low, spread), 0.0).astype(bf16)
 
 
-def route(plan, first_at, packed, width, local_experts, choices, piece_count, slots):
+def route(layout, packed, width, choices):
     tokens = sum(value.shape[0] for value in packed)
-    shape = jax.ShapeDtypeStruct((piece_count, tokens, slots), bf16)
-    return pl.pallas_call(
-        functools.partial(route_kernel, local_experts, choices, width, first_at),
-        in_specs=[whole(pltpu.SMEM)] + [whole()] * len(packed),
+    shape = jax.ShapeDtypeStruct((layout.cell_count, tokens, layout.rows), bf16)
+    return pl.pallas_call(
+        functools.partial(route_kernel, layout, choices, width),
         out_shape=(shape, shape, shape),
         compiler_params=params(16),
         cost_estimate=cost(2**25, 2**20),
         name="route",
-    )(plan, *packed)
+    )(*packed)
 
 
 def pick_kernel(place_ref, *refs):
@@ -354,45 +373,29 @@
     return jnp.where(lane == 0, high, jnp.where(lane == 1, low, 0.0))
 
 
-class Layout:
-    def __init__(self, local_experts, piece_count, capacity):
-        slots = local_experts * capacity // piece_count
-        self.rows = slots // CELLS
-        self.experts = max(1, slots // capacity)
-        self.spread = max(1, capacity // slots)
-        self.each = max(1, self.experts // CELLS)
-        self.cell_count = piece_count * CELLS
-
-    def first_expert(self, piece, cell):
-        within = cell * self.each if self.experts > 1 else 0
-        return (piece * self.experts + within) // self.spread
-
-
-def gate_up(plan, piece_at, cells, layout, picked, weight):
+def gate_up(names, layout, picked, weight):
     _, width, ff_pair = weight.shape
     rows = layout.rows // layout.each
 
-    def kernel(plan_ref, picked_ref, weight_ref, out_ref):
-        piece = plan_ref[piece_at]
-        for place, cell in enumerate(cells):
-            first = layout.first_expert(piece, cell)
+    def kernel(picked_ref, weight_ref, out_ref):
+        for place, name in enumerate(names):
+            at, first = layout.cell(name)
             for i in range(layout.each):
-                picked = picked_ref[piece * CELLS + cell, i * rows : (i + 1) * rows, :]
+                picked = picked_ref[at, i * rows : (i + 1) * rows, :]
                 start = place * layout.rows + i * rows
                 here = slice(start, start + rows)
                 product = dot(picked[:, :width], weight_ref[first + i])
                 out_ref[here, :ff_pair] = product.astype(bf16)
                 out_ref[here, ff_pair:] = picked[:, width:]
 
-    total = len(cells) * layout.rows
+    total = len(names) * layout.rows
     return pl.pallas_call(
         kernel,
-        in_specs=[whole(pltpu.SMEM)] + [whole()] * 2,
         out_shape=jax.ShapeDtypeStruct((total, ff_pair + LANES), bf16),
         compiler_params=params(8),
         cost_estimate=cost(2 * total * width * ff_pair, 2 * total * ff_pair),
         name="gate_up",
-    )(plan, picked, weight)
+    )(picked, weight)
 
 
 def join_kernel(left_ref, right_ref, out_ref):
@@ -434,7 +437,7 @@
     )(*in_hbm([beside]), *parts)
 
 
-def down(plan, cells, layout, hidden, weight, high, low, total=None, out_count=1):
+def down(names, layout, hidden, weight, high, low, total=None, out_count=1):
     ff_width = hidden[0].shape[1]
     tokens = high.shape[1]
     piece_width = weight.shape[2]
@@ -442,18 +445,16 @@
     rows = tokens // out_count
     out_type = f32 if out_count == 1 else bf16
 
-    def kernel(plan_ref, weight_ref, high_ref, low_ref, *refs):
-        hidden_refs, refs = refs[: len(cells)], refs[len(cells) :]
+    def kernel(weight_ref, high_ref, low_ref, *refs):
+        hidden_refs, refs = refs[: len(names)], refs[len(names) :]
         total_refs, out_refs, held_ref = refs[: -1 - out_count], refs[-1 - out_count : -1], refs[-1]
         summed = 0.0
-        for ref, (piece_at, cell) in zip(hidden_refs, cells):
-            piece = plan_ref[piece_at]
-            first = layout.first_expert(piece, cell)
+        for ref, name in zip(hidden_refs, names):
+            at, first = layout.cell(name)
             for i in range(layout.each):
                 here = slice(i * each, (i + 1) * each)
                 held_ref[here, :] = dot(ref[here, :], weight_ref[first + i]).astype(bf16)
             held = held_ref[...]
-            at = piece * CELLS + cell
             summed = summed + dot(high_ref[at], held) + dot(low_ref[at], held)
         for ref in total_refs:
             summed = summed + ref[...]
@@ -463,13 +464,12 @@
     before = [] if total is None else [total]
     return pl.pallas_call(
         kernel,
-        in_specs=[whole(pltpu.SMEM)] + [whole()] * (3 + len(cells) + len(before)),
         out_shape=[jax.ShapeDtypeStruct((rows, piece_width), out_type)] * out_count,
         scratch_shapes=[pltpu.VMEM((layout.rows, piece_width), bf16)],
         compiler_params=params(8),
         cost_estimate=cost(2 * layout.rows * ff_width * piece_width, 2**20),
         name="down",
-    )(plan, weight, high, low, *hidden, *before)
+    )(weight, high, low, *hidden, *before)
 
 
 def finish_kernel(mixed_ref, *refs):
@@ -504,7 +504,6 @@
     route_weight,
 ):
     ctx_count, exp_count, tp_count = (lax.axis_size(axis) for axis in ("ctx", "exp", "tp"))
-    own_ctx, own_exp, own_tp = (lax.axis_index(axis) for axis in ("ctx", "exp", "tp"))
     assert tp_count == 2 and cached_keys.shape[1] == 1
     assert ctx_count & (ctx_count - 1) == 0 and exp_count & (exp_count - 1) == 0
     piece_count = exp_count * tp_count
@@ -518,20 +517,7 @@
     choices = expert_ids.shape[1]
     scale = math.log2(math.e) / math.sqrt(head_size)
 
-    last = ctx_count * (key_count - query_rows) - own_ctx * key_count
-    leads = [last + (own_ctx ^ k) * query_rows for k in range(ctx_count)]
-    own_piece = own_exp * tp_count + own_tp
-    column_pieces = [own_piece ^ k for k in range(piece_count)]
-    slot_pieces = [
-        (own_tp ^ flip) * exp_count + (own_exp ^ k) for flip in (0, 1) for k in range(exp_count)
-    ]
-    layout = Layout(local_experts, piece_count, ctx_count * MOST)
-    scalars = [own_ctx * local_experts] + leads + column_pieces + slot_pieces
-    plan = jnp.stack([jnp.asarray(value, jnp.int32) for value in scalars])
-    lead_at = 1
-    order_at = lead_at + ctx_count
-    mine_at = order_at + piece_count
-    away_at = mine_at + exp_count
+    layout = Layout(local_experts, key_count, query_rows)
 
     packed = pack(
         queries.reshape(query_rows, width), query_seg, expert_ids, route_weight, gate_up_weight
@@ -539,34 +525,21 @@
     gathered = {0: packed}
     for k in far_first(ctx_count):
         gathered[k] = swapped(packed, "ctx", k)
-    sight = sight_of(parent, key_seg, gate_up_weight)
+    sight = sight_of(parent, key_seg)
     keys = cached_keys.reshape(key_count, head_size)
     values = cached_values.reshape(key_count, head_size)
     out_matrix = out_weight.reshape(width, model_width)
     parts = {}
     for k in list(range(1, ctx_count)) + [0]:
         part = attend(
-            plan, lead_at + k, gathered[k], keys, values, sight, heads, scale, gate_up_weight
+            layout, k, gathered[k], keys, values, sight, heads, scale, gate_up_weight
         )
         parts[k] = swapped(part, "ctx", k) if k else part
     place, combine_high, combine_low = route(
-        plan,
-        0,
-        [gathered[k] for k in range(ctx_count)],
-        width,
-        local_experts,
-        choices,
-        layout.cell_count,
-        layout.rows,
+        layout, [gathered[k] for k in range(ctx_count)], width, choices
     )
     projected = project(
-        plan,
-        order_at,
-        [parts[k] for k in range(ctx_count)],
-        out_matrix,
-        heads,
-        scale,
-        piece_count,
+        layout, [parts[k] for k in range(ctx_count)], out_matrix, heads, scale
     )
     pieces = [projected[0]] + [
         swapped(projected[k], ("exp", "tp"), k) for k in far_first(piece_count)
@@ -580,60 +553,69 @@
     def after(value, *others):
         return lax.optimization_barrier((value,) + others)[0]
 
-    def first_half(piece_at, cells):
-        return gate_up(plan, piece_at, cells, layout, picked, gate_up_weight)
+    def first_half(*names):
+        return gate_up(names, layout, picked, gate_up_weight)
 
     crossed = [[] for _ in range(CELLS)]
     arrived = [None] * CELLS
     for k in far_first(exp_count):
-        near = [swapped(first_half(away_at + k, (0,)), "tp", 1)]
-        mine = first_half(mine_at + k, (0,))
+        near = [swapped(first_half((1, k, 0)), "tp", 1)]
+        mine = first_half((0, k, 0))
         picked = after(picked, mine)
-        near.append(swapped(first_half(away_at + k, (1,)), "tp", 1))
+        near.append(swapped(first_half((1, k, 1)), "tp", 1))
         for cell in range(CELLS):
             if cell:
-                mine = first_half(mine_at + k, (cell,))
+                mine = first_half((0, k, cell))
             joined = join(mine, near[cell])
             picked = after(picked, joined)
             crossed[cell].append(swapped(joined, "exp", k))
             if k == 1:
-                arrived[cell] = swapped(first_half(away_at, (cell,)), "tp", 1)
-    kept = first_half(mine_at, tuple(range(CELLS)))
-
-    def add(cells, hidden, total, out_count=1):
-        return down(
-            plan, cells, layout, hidden, down_weight, combine_high, combine_low, total, out_count
-        )
-
-    total = None
+                arrived[cell] = swapped(first_half((1, 0, cell)), "tp", 1)
+    kept = first_half((0, 0, 0), (0, 0, 1))
+
     own_hidden = []
     for cell in range(CELLS):
-        if total is not None:
-            kept = after(kept, total)
         crossed[cell], kept = lax.optimization_barrier((crossed[cell], kept))
         parts = [kept, arrived[cell]] + crossed[cell]
         starts = [cell * layout.rows] + [0] * (len(parts) - 1)
         hidden = hidden_of(parts, starts, layout, ff_width, model_width, gate_up_weight)
+        kept = after(kept, hidden)
         own_hidden.append(hidden)
-        if cell == 0:
-            cells = [(mine_at, 0), (away_at, 0)]
-            total = add(cells, [hidden, swapped(hidden, "tp", 1)], total)[0]
+
+    def add(hidden, total, out_count=1):
+        return down(
+            list(hidden),
+            layout,
+            list(hidden.values()),
+            down_weight,
+            combine_high,
+            combine_low,
+            total,
+            out_count,
+        )
+
+    near = {
+        (flip, 0, cell): swapped(hidden, "tp", 1) if flip else hidden
+        for cell, hidden in enumerate(own_hidden)
+        for flip in (0, 1)
+    }
     far = {
-        (k, cell): swapped(own_hidden[cell], "exp", k)
+        (0, k, cell): swapped(own_hidden[cell], "exp", k)
         for cell in range(CELLS)
         for k in range(1, exp_count)
     }
-    cells = [(mine_at, 1), (away_at, 1)]
-    total = add(cells, [own_hidden[1], swapped(own_hidden[1], "tp", 1)], total)[0]
+    total = add({name: near[name] for name in list(near)[:2]}, None)[0]
+    names = list(near)[2:]
+    near[names[0]] = after(near[names[0]], total)
+    first = next(iter(far))
+    total = add({**{name: near[name] for name in names}, first: far[first]}, total)[0]
     last = {}
-    for (k, cell), hidden in far.items():
-        if last:
+    for turn, ((_, k, cell), hidden) in enumerate(far.items()):
+        if turn:
             hidden = after(hidden, total)
-        last[k, cell] = swapped(hidden, "tp", 1)
-        total = add([(mine_at + k, cell)], [hidden], total)[0]
-    totals = add(
-        [(away_at + k, cell) for k, cell in last], list(last.values()), total, ctx_count
-    )
+            total = add({(0, k, cell): hidden}, total)[0]
+        last[1, k, cell] = swapped(hidden, "tp", 1)
+    totals = add(last, total, ctx_count)
     returned = [totals[0]] + [swapped(totals[k], "ctx", k) for k in far_first(ctx_count)]
     return finish(mixed, returned)
 

time: 71.2 us -> 65.7 us (0.923)
  Pallas kernels: 30.1 us -> 19.4 us
  waiting for transfers between devices: 12.2 us -> 17.7 us
  local copies, waits for them, and re-layouts: 1.6 us -> 0.08 us
  starting transfers between devices: 26.7 us -> 28 us
    pallas_call x19 -> x18, Pallas kernels: 27.1 us -> 16.4 us  [the longest x4 5.04 us: attend(): pl.pallas_call(functools.partial(attend_kernel, heads, scale, layout, k),...]
    ppermute x27, waiting for transfers between devices: 12.2 us -> 17.7 us  [swapped(): return lax.ppermute(value, axes, pairs)]
    unnamed x28 -> x32, local copies, waits for them, and re-layouts: 1.51 us -> 0.08 us
    ppermute x27, starting transfers between devices: 26.7 us -> 28 us  [swapped(): return lax.ppermute(value, axes, pairs)]
  transfers between devices with their start and end apart: 27 -> 27, of which waited for: 12 -> 15; matrix products, arithmetic and copies ran while one was open for 0% -> 0% of each run, Pallas kernels for 33% -> 22%
where the time goes in v8:
time: 65.7 us; the launch traced here: 65.6 us
  starting transfers between devices  28 us (43%)
  Pallas kernels  19.4 us (30%)
  waiting for transfers between devices  17.7 us (27%)
    ppermute x27, starting transfers between devices, swapped(): return lax.ppermute(value, axes, pairs)  28 us
    ppermute x27, waiting for transfers between devices, swapped(): return lax.ppermute(value, axes, pairs)  17.7 us
    pallas_call x4, Pallas kernels, attend(): pl.pallas_call(functools.partial(attend_kernel, heads, scale, layout, k),...  5.04 us
    pallas_call x7, Pallas kernels, gate_up(): pl.pallas_call(kernel, out_shape=jax.ShapeDtypeStruct((total, ff_pair + L...  5.02 us
    pallas_call x4, Pallas kernels, down(): pl.pallas_call(kernel, out_shape=[jax.ShapeDtypeStruct((rows, piece_width...  3.98 us
  transfers between devices with their start and end apart: 27, of which 15 were waited for; matrix products, arithmetic and copies ran while one was open for 0% of the time, Pallas kernels for 22%

profile of v8, /device:TPU:0, one launch (start us, length us, event | category | flops | bytes accessed | tf_op | source)
XLA Modules:
  0.0 65.6 jit_solution(15385449826692743070)
XLA Ops:
  1.0 3.1 %collective-permute-start = (bf16[32,1152]{1,0:T(8,128)(2,1)S(1)}, bf16[32,1152]{1,0:T(8,128)(2,1)S(1)}, u32[]{:S(2)}, u32[]{:S(2)}) collective-permute-start(bf16[32,1152]{1,0:T(8,128)(2,1)S(1)} %pack.1.queries_ref.refs_0_), channel_id=1, source_target_pairs={{0,4},{4,0},{8,12},{12,8},{1,5},{5,1},{9,13},{13,9},{2,6},{6,2},{1... | collective-permute-start | bytes 221192 | tf_op jit(solution)/shard_map/ppermute | solution.py:101
  4.2 2.6 %collective-permute-start.2 = (bf16[32,1152]{1,0:T(8,128)(2,1)S(1)}, bf16[32,1152]{1,0:T(8,128)(2,1)S(1)}, u32[]{:S(2)}, u32[]{:S(2)}) collective-permute-start(bf16[32,1152]{1,0:T(8,128)(2,1)S(1)} %pack.1.queries_ref.refs_0_), channel_id=1, source_target_pairs={{0,8},{4,12},{8,0},{12,4},{1,9},{5,13},{9,1},{13,5},{2,10},{6,14},... | collective-permute-start | bytes 221192 | tf_op jit(solution)/shard_map/ppermute | solution.py:101
  7.4 1.3 %attend.5 = bf16[32,1152]{1,0:T(8,128)(2,1)S(1)} custom-call(bf16[32,1152]{1,0:T(8,128)(2,1)S(1)} %collective-permute-done.queries_ref.refs_1_, bf16[2048,128]{1,0:T(8,128)(2,1)S(1)} %bitcast.13, bf16[2048,128]{1,0:T(8,128)(2,1)S(1)} %bitcast.17, bf16[64,2048]{1,0:T(8,128)(2,1)S(1)} %sight.1.sight_ref, bf16[16,512,1536]{2,1,0:T(8,128)(2,1)} %beside_ref.13), custom_call_target="tpu_custom_call" | custom-call | flops 536870912 | bytes 1048576 | tf_op jit(solution)/shard_map/attend/pallas_call | solution.py:223
  9.8 2.1 %collective-permute-done.2.queries_ref.refs_2_ = bf16[32,1152]{1,0:T(8,128)(2,1)S(1)} collective-permute-done((bf16[32,1152]{1,0:T(8,128)(2,1)S(1)}, bf16[32,1152]{1,0:T(8,128)(2,1)S(1)}, u32[]{:S(2)}, u32[]{:S(2)}) %collective-permute-start.2) | collective-permute-done | bytes 73760 | tf_op jit(solution)/shard_map/ppermute | solution.py:101
  11.9 1.3 %attend.6 = bf16[32,1152]{1,0:T(8,128)(2,1)S(1)} custom-call(bf16[32,1152]{1,0:T(8,128)(2,1)S(1)} %collective-permute-done.2.queries_ref.refs_2_, bf16[2048,128]{1,0:T(8,128)(2,1)S(1)} %bitcast.14, bf16[2048,128]{1,0:T(8,128)(2,1)S(1)} %bitcast.18, bf16[64,2048]{1,0:T(8,128)(2,1)S(1)} %sight.1.sight_ref, bf16[16,512,1536]{2,1,0:T(8,128)(2,1)} %beside_ref.13), custom_call_target="tpu_custom_call" | custom-call | flops 536870912 | bytes 1048576 | tf_op jit(solution)/shard_map/attend/pallas_call | solution.py:223
  13.2 1.3 %collective-permute-start.3 = (bf16[32,1152]{1,0:T(8,128)(2,1)S(1)}, bf16[32,1152]{1,0:T(8,128)(2,1)S(1)}, u32[]{:S(2)}, u32[]{:S(2)}) collective-permute-start(bf16[32,1152]{1,0:T(8,128)(2,1)S(1)} %attend.6), channel_id=1, source_target_pairs={{0,8},{4,12},{8,0},{12,4},{1,9},{5,13},{9,1},{13,5},{2,10},{6,14},... | collective-permute-start | bytes 221192 | tf_op jit(solution)/shard_map/ppermute | solution.py:101
  14.5 1.3 %attend.7 = bf16[32,1152]{1,0:T(8,128)(2,1)S(1)} custom-call(bf16[32,1152]{1,0:T(8,128)(2,1)S(1)} %collective-permute-done.4.queries_ref.refs_3_, bf16[2048,128]{1,0:T(8,128)(2,1)S(1)} %bitcast.15, bf16[2048,128]{1,0:T(8,128)(2,1)S(1)} %bitcast.19, bf16[64,2048]{1,0:T(8,128)(2,1)S(1)} %sight.1.sight_ref, bf16[16,512,1536]{2,1,0:T(8,128)(2,1)} %beside_ref.13), custom_call_target="tpu_custom_call" | custom-call | flops 536870912 | bytes 1048576 | tf_op jit(solution)/shard_map/attend/pallas_call | solution.py:223
  15.8 2.2 %collective-permute-start.5 = (bf16[32,1152]{1,0:T(8,128)(2,1)S(1)}, bf16[32,1152]{1,0:T(8,128)(2,1)S(1)}, u32[]{:S(2)}, u32[]{:S(2)}) collective-permute-start(bf16[32,1152]{1,0:T(8,128)(2,1)S(1)} %attend.7), channel_id=1, source_target_pairs={{0,12},{4,8},{8,4},{12,0},{1,13},{5,9},{9,5},{13,1},{2,14},{6,10},... | collective-permute-start | bytes 221192 | tf_op jit(solution)/shard_map/ppermute | solution.py:101
  18.0 1.3 %attend.4.refs_0_ = bf16[32,1152]{1,0:T(8,128)(2,1)S(1)} custom-call(bf16[32,1152]{1,0:T(8,128)(2,1)S(1)} %pack.1.queries_ref.refs_0_, bf16[2048,128]{1,0:T(8,128)(2,1)S(1)} %bitcast.16, bf16[2048,128]{1,0:T(8,128)(2,1)S(1)} %bitcast.20, bf16[64,2048]{1,0:T(8,128)(2,1)S(1)} %sight.1.sight_ref, bf16[16,512,1536]{2,1,0:T(8,128)(2,1)} %beside_ref.13), custom_call_target="tpu_custom_call" | custom-call | flops 536870912 | bytes 1048576 | tf_op jit(solution)/shard_map/attend/pallas_call | solution.py:223
  20.1 2.0 %collective-permute-done.5.refs_3_ = bf16[32,1152]{1,0:T(8,128)(2,1)S(1)} collective-permute-done((bf16[32,1152]{1,0:T(8,128)(2,1)S(1)}, bf16[32,1152]{1,0:T(8,128)(2,1)S(1)}, u32[]{:S(2)}, u32[]{:S(2)}) %collective-permute-start.5) | collective-permute-done | bytes 73760 | tf_op jit(solution)/shard_map/ppermute | solution.py:101
  23.1 1.6 %collective-permute-start.7 = (bf16[32,512]{1,0:T(8,128)(2,1)S(1)}, bf16[32,512]{1,0:T(8,128)(2,1)S(1)}, u32[]{:S(2)}, u32[]{:S(2)}) collective-permute-start(bf16[32,512]{1,0:T(8,128)(2,1)S(1)} %get-tuple-element.30), channel_id=1, source_target_pairs={{0,2},{1,3},{2,0},{3,1},{4,6},{5,7},{6,4},{7,5},{8,10},{9,11},{10,... | collective-permute-start | bytes 98312 | tf_op jit(solution)/shard_map/ppermute | solution.py:101
  25.0 1.8 %collective-permute-done.6.refs_1_ = bf16[32,512]{1,0:T(8,128)(2,1)S(1)} collective-permute-done((bf16[32,512]{1,0:T(8,128)(2,1)S(1)}, bf16[32,512]{1,0:T(8,128)(2,1)S(1)}, u32[]{:S(2)}, u32[]{:S(2)}) %collective-permute-start.6) | collective-permute-done | bytes 32800 | tf_op jit(solution)/shard_map/ppermute | solution.py:101
  27.3 2.2 %collective-permute-start.11 = (bf16[32,640]{1,0:T(8,128)(2,1)S(1)}, bf16[32,640]{1,0:T(8,128)(2,1)S(1)}, u32[]{:S(2)}, u32[]{:S(2)}) collective-permute-start(bf16[32,640]{1,0:T(8,128)(2,1)S(1)} %get-tuple-element.36.refs_0_), channel_id=1, source_target_pairs={{0,12},{4,8},{8,4},{12,0},{1,13},{5,9},{9,5},{13,1},{2,14},{6,10},... | collective-permute-start | bytes 122888 | tf_op jit(solution)/shard_map/ppermute | solution.py:101
  30.1 1.6 %collective-permute-start.9 = (bf16[32,640]{1,0:T(8,128)(2,1)S(1)}, bf16[32,640]{1,0:T(8,128)(2,1)S(1)}, u32[]{:S(2)}, u32[]{:S(2)}) collective-permute-start(bf16[32,640]{1,0:T(8,128)(2,1)S(1)} %get-tuple-element.36.refs_0_), channel_id=1, source_target_pairs={{0,4},{4,0},{8,12},{12,8},{1,5},{5,1},{9,13},{13,9},{2,6},{6,2},{1... | collective-permute-start | bytes 122888 | tf_op jit(solution)/shard_map/ppermute | solution.py:101
  33.4 1.3 %collective-permute-done.10.refs_2_ = bf16[32,640]{1,0:T(8,128)(2,1)S(1)} collective-permute-done((bf16[32,640]{1,0:T(8,128)(2,1)S(1)}, bf16[32,640]{1,0:T(8,128)(2,1)S(1)}, u32[]{:S(2)}, u32[]{:S(2)}) %collective-permute-start.10) | collective-permute-done | bytes 40992 | tf_op jit(solution)/shard_map/ppermute | solution.py:101
  38.1 1.5 %collective-permute-start.13 = (bf16[64,1664]{1,0:T(8,128)(2,1)S(1)}, bf16[64,1664]{1,0:T(8,128)(2,1)S(1)}, u32[]{:S(2)}, u32[]{:S(2)}) collective-permute-start(bf16[64,1664]{1,0:T(8,128)(2,1)S(1)} %join.2), channel_id=1, source_target_pairs={{0,2},{2,0},{1,3},{3,1},{4,6},{6,4},{5,7},{7,5},{8,10},{10,8},{9,1... | collective-permute-start | bytes 638984 | tf_op jit(solution)/shard_map/ppermute | solution.py:101
  44.1 2.2 %collective-permute-done.13.refs_2_ = bf16[64,1664]{1,0:T(8,128)(2,1)S(1)} collective-permute-done((bf16[64,1664]{1,0:T(8,128)(2,1)S(1)}, bf16[64,1664]{1,0:T(8,128)(2,1)S(1)}, u32[]{:S(2)}, u32[]{:S(2)}) %collective-permute-start.13) | collective-permute-done | bytes 213024 | tf_op jit(solution)/shard_map/ppermute | solution.py:101
  46.6 1.5 %collective-permute-start.16 = (bf16[64,768]{1,0:T(8,128)(2,1)S(1)}, bf16[64,768]{1,0:T(8,128)(2,1)S(1)}, u32[]{:S(2)}, u32[]{:S(2)}) collective-permute-start(bf16[64,768]{1,0:T(8,128)(2,1)S(1)} %hidden.2.refs_0_), channel_id=1, source_target_pairs={{0,2},{2,0},{1,3},{3,1},{4,6},{6,4},{5,7},{7,5},{8,10},{10,8},{9,1... | collective-permute-start | bytes 294920 | tf_op jit(solution)/shard_map/ppermute | solution.py:101
  48.1 1.9 %collective-permute-done.18.refs_2_ = bf16[64,1664]{1,0:T(8,128)(2,1)S(1)} collective-permute-done((bf16[64,1664]{1,0:T(8,128)(2,1)S(1)}, bf16[64,1664]{1,0:T(8,128)(2,1)S(1)}, u32[]{:S(2)}, u32[]{:S(2)}) %collective-permute-start.18) | collective-permute-done | bytes 213024 | tf_op jit(solution)/shard_map/ppermute | solution.py:101
  50.3 1.5 %collective-permute-start.20 = (bf16[64,768]{1,0:T(8,128)(2,1)S(1)}, bf16[64,768]{1,0:T(8,128)(2,1)S(1)}, u32[]{:S(2)}, u32[]{:S(2)}) collective-permute-start(bf16[64,768]{1,0:T(8,128)(2,1)S(1)} %hidden.3.refs_0_), channel_id=1, source_target_pairs={{0,2},{2,0},{1,3},{3,1},{4,6},{6,4},{5,7},{7,5},{8,10},{10,8},{9,1... | collective-permute-start | bytes 294920 | tf_op jit(solution)/shard_map/ppermute | solution.py:101
  52.9 1.4 %down.5.refs_1_ = f32[128,512]{1,0:T(8,128)S(1)} custom-call(bf16[16,768,512]{2,1,0:T(8,128)(2,1)S(1)} %bitcast.12, bf16[8,128,64]{2,1,0:T(8,128)(2,1)S(1)} %get-tuple-element.33.high_ref, bf16[8,128,64]{2,1,0:T(8,128)(2,1)S(1)} %get-tuple-element.34.low_ref, bf16[64,768]{1,0:T(8,128)(2,1)S(1)} %hidden.3.refs_0_, ...), custom_call_target="tpu_custom_call" | custom-call | flops 50331648 | bytes 1048576 | tf_op jit(solution)/shard_map/down/pallas_call | solution.py:465
  58.0 2.0 %collective-permute-start.24 = (bf16[32,512]{1,0:T(8,128)(2,1)S(1)}, bf16[32,512]{1,0:T(8,128)(2,1)S(1)}, u32[]{:S(2)}, u32[]{:S(2)}) collective-permute-start(bf16[32,512]{1,0:T(8,128)(2,1)S(1)} %get-tuple-element.48), channel_id=1, source_target_pairs={{0,12},{4,8},{8,4},{12,0},{1,13},{5,9},{9,5},{13,1},{2,14},{6,10},... | collective-permute-start | bytes 98312 | tf_op jit(solution)/shard_map/ppermute | solution.py:101
  60.3 2.1 %collective-permute-start.26 = (bf16[32,512]{1,0:T(8,128)(2,1)S(1)}, bf16[32,512]{1,0:T(8,128)(2,1)S(1)}, u32[]{:S(2)}, u32[]{:S(2)}) collective-permute-start(bf16[32,512]{1,0:T(8,128)(2,1)S(1)} %get-tuple-element.50), channel_id=1, source_target_pairs={{0,4},{4,0},{8,12},{12,8},{1,5},{5,1},{9,13},{13,9},{2,6},{6,2},{1... | collective-permute-start | bytes 98312 | tf_op jit(solution)/shard_map/ppermute | solution.py:101
  62.5 1.4 %collective-permute-done.24.refs_1_ = bf16[32,512]{1,0:T(8,128)(2,1)S(1)} collective-permute-done((bf16[32,512]{1,0:T(8,128)(2,1)S(1)}, bf16[32,512]{1,0:T(8,128)(2,1)S(1)}, u32[]{:S(2)}, u32[]{:S(2)}) %collective-permute-start.24) | collective-permute-done | bytes 32800 | tf_op jit(solution)/shard_map/ppermute | solution.py:101
  (91 shorter events, 22.9 us)
Async XLA Ops:
  1.0 6.3 %collective-permute-start = (bf16[32,1152]{1,0:T(8,128)(2,1)S(1)}, bf16[32,1152]{1,0:T(8,128)(2,1)S(1)}, u32[]{:S(2)}, u32[]{:S(2)}) collective-permute-start(bf16[32,1152]{1,0:T(8,128)(2,1)S(1)} %pack.1.queries_ref.refs_0_), channel_id=1, source_target_pairs={{0,4},{4,0},{8,12},{12,8},{1,5},{5,1},{9,13},{13,9},{2,6},{6,2},{1... | collective-permute-start | bytes 221192 | tf_op jit(solution)/shard_map/ppermute | solution.py:101
  4.2 7.8 %collective-permute-start.2 = (bf16[32,1152]{1,0:T(8,128)(2,1)S(1)}, bf16[32,1152]{1,0:T(8,128)(2,1)S(1)}, u32[]{:S(2)}, u32[]{:S(2)}) collective-permute-start(bf16[32,1152]{1,0:T(8,128)(2,1)S(1)} %pack.1.queries_ref.refs_0_), channel_id=1, source_target_pairs={{0,8},{4,12},{8,0},{12,4},{1,9},{5,13},{9,1},{13,5},{2,10},{6,14},... | collective-permute-start | bytes 221192 | tf_op jit(solution)/shard_map/ppermute | solution.py:101
  6.7 7.8 %collective-permute-start.4 = (bf16[32,1152]{1,0:T(8,128)(2,1)S(1)}, bf16[32,1152]{1,0:T(8,128)(2,1)S(1)}, u32[]{:S(2)}, u32[]{:S(2)}) collective-permute-start(bf16[32,1152]{1,0:T(8,128)(2,1)S(1)} %pack.1.queries_ref.refs_0_), channel_id=1, source_target_pairs={{0,12},{4,8},{8,4},{12,0},{1,13},{5,9},{9,5},{13,1},{2,14},{6,10},... | collective-permute-start | bytes 221192 | tf_op jit(solution)/shard_map/ppermute | solution.py:101
  8.7 10.6 %collective-permute-start.1 = (bf16[32,1152]{1,0:T(8,128)(2,1)S(1)}, bf16[32,1152]{1,0:T(8,128)(2,1)S(1)}, u32[]{:S(2)}, u32[]{:S(2)}) collective-permute-start(bf16[32,1152]{1,0:T(8,128)(2,1)S(1)} %attend.5), channel_id=1, source_target_pairs={{0,4},{4,0},{8,12},{12,8},{1,5},{5,1},{9,13},{13,9},{2,6},{6,2},{1... | collective-permute-start | bytes 221192 | tf_op jit(solution)/shard_map/ppermute | solution.py:101
  13.2 6.9 %collective-permute-start.3 = (bf16[32,1152]{1,0:T(8,128)(2,1)S(1)}, bf16[32,1152]{1,0:T(8,128)(2,1)S(1)}, u32[]{:S(2)}, u32[]{:S(2)}) collective-permute-start(bf16[32,1152]{1,0:T(8,128)(2,1)S(1)} %attend.6), channel_id=1, source_target_pairs={{0,8},{4,12},{8,0},{12,4},{1,9},{5,13},{9,1},{13,5},{2,10},{6,14},... | collective-permute-start | bytes 221192 | tf_op jit(solution)/shard_map/ppermute | solution.py:101
  15.8 6.3 %collective-permute-start.5 = (bf16[32,1152]{1,0:T(8,128)(2,1)S(1)}, bf16[32,1152]{1,0:T(8,128)(2,1)S(1)}, u32[]{:S(2)}, u32[]{:S(2)}) collective-permute-start(bf16[32,1152]{1,0:T(8,128)(2,1)S(1)} %attend.7), channel_id=1, source_target_pairs={{0,12},{4,8},{8,4},{12,0},{1,13},{5,9},{9,5},{13,1},{2,14},{6,10},... | collective-permute-start | bytes 221192 | tf_op jit(solution)/shard_map/ppermute | solution.py:101
  23.1 3.7 %collective-permute-start.6 = (bf16[32,512]{1,0:T(8,128)(2,1)S(1)}, bf16[32,512]{1,0:T(8,128)(2,1)S(1)}, u32[]{:S(2)}, u32[]{:S(2)}) collective-permute-start(bf16[32,512]{1,0:T(8,128)(2,1)S(1)} %get-tuple-element.29), channel_id=1, source_target_pairs={{0,3},{1,2},{2,1},{3,0},{4,7},{5,6},{6,5},{7,4},{8,11},{9,10},{10,... | collective-permute-start | bytes 98312 | tf_op jit(solution)/shard_map/ppermute | solution.py:101
  23.1 4.0 %collective-permute-start.7 = (bf16[32,512]{1,0:T(8,128)(2,1)S(1)}, bf16[32,512]{1,0:T(8,128)(2,1)S(1)}, u32[]{:S(2)}, u32[]{:S(2)}) collective-permute-start(bf16[32,512]{1,0:T(8,128)(2,1)S(1)} %get-tuple-element.30), channel_id=1, source_target_pairs={{0,2},{1,3},{2,0},{3,1},{4,6},{5,7},{6,4},{7,5},{8,10},{9,11},{10,... | collective-permute-start | bytes 98312 | tf_op jit(solution)/shard_map/ppermute | solution.py:101
  24.7 2.5 %collective-permute-start.8 = (bf16[32,512]{1,0:T(8,128)(2,1)S(1)}, bf16[32,512]{1,0:T(8,128)(2,1)S(1)}, u32[]{:S(2)}, u32[]{:S(2)}) collective-permute-start(bf16[32,512]{1,0:T(8,128)(2,1)S(1)} %get-tuple-element.31), channel_id=1, source_target_pairs={{0,1},{1,0},{2,3},{3,2},{4,5},{5,4},{6,7},{7,6},{8,9},{9,8},{10,11... | collective-permute-start | bytes 98312 | tf_op jit(solution)/shard_map/ppermute | solution.py:101
  27.3 6.2 %collective-permute-start.11 = (bf16[32,640]{1,0:T(8,128)(2,1)S(1)}, bf16[32,640]{1,0:T(8,128)(2,1)S(1)}, u32[]{:S(2)}, u32[]{:S(2)}) collective-permute-start(bf16[32,640]{1,0:T(8,128)(2,1)S(1)} %get-tuple-element.36.refs_0_), channel_id=1, source_target_pairs={{0,12},{4,8},{8,4},{12,0},{1,13},{5,9},{9,5},{13,1},{2,14},{6,10},... | collective-permute-start | bytes 122888 | tf_op jit(solution)/shard_map/ppermute | solution.py:101
  29.4 5.3 %collective-permute-start.10 = (bf16[32,640]{1,0:T(8,128)(2,1)S(1)}, bf16[32,640]{1,0:T(8,128)(2,1)S(1)}, u32[]{:S(2)}, u32[]{:S(2)}) collective-permute-start(bf16[32,640]{1,0:T(8,128)(2,1)S(1)} %get-tuple-element.36.refs_0_), channel_id=1, source_target_pairs={{0,8},{4,12},{8,0},{12,4},{1,9},{5,13},{9,1},{13,5},{2,10},{6,14},... | collective-permute-start | bytes 122888 | tf_op jit(solution)/shard_map/ppermute | solution.py:101
  30.1 4.8 %collective-permute-start.9 = (bf16[32,640]{1,0:T(8,128)(2,1)S(1)}, bf16[32,640]{1,0:T(8,128)(2,1)S(1)}, u32[]{:S(2)}, u32[]{:S(2)}) collective-permute-start(bf16[32,640]{1,0:T(8,128)(2,1)S(1)} %get-tuple-element.36.refs_0_), channel_id=1, source_target_pairs={{0,4},{4,0},{8,12},{12,8},{1,5},{5,1},{9,13},{13,9},{2,6},{6,2},{1... | collective-permute-start | bytes 122888 | tf_op jit(solution)/shard_map/ppermute | solution.py:101
  37.3 3.5 %collective-permute-start.14 = (bf16[64,1664]{1,0:T(8,128)(2,1)S(1)}, bf16[64,1664]{1,0:T(8,128)(2,1)S(1)}, u32[]{:S(2)}, u32[]{:S(2)}) collective-permute-start(bf16[64,1664]{1,0:T(8,128)(2,1)S(1)} %gate_up.10), channel_id=1, source_target_pairs={{0,1},{1,0},{2,3},{3,2},{4,5},{5,4},{6,7},{7,6},{8,9},{9,8},{10,11... | collective-permute-start | bytes 638984 | tf_op jit(solution)/shard_map/ppermute | solution.py:101
  38.1 8.2 %collective-permute-start.13 = (bf16[64,1664]{1,0:T(8,128)(2,1)S(1)}, bf16[64,1664]{1,0:T(8,128)(2,1)S(1)}, u32[]{:S(2)}, u32[]{:S(2)}) collective-permute-start(bf16[64,1664]{1,0:T(8,128)(2,1)S(1)} %join.2), channel_id=1, source_target_pairs={{0,2},{2,0},{1,3},{3,1},{4,6},{6,4},{5,7},{7,5},{8,10},{10,8},{9,1... | collective-permute-start | bytes 638984 | tf_op jit(solution)/shard_map/ppermute | solution.py:101
  41.1 8.9 %collective-permute-start.18 = (bf16[64,1664]{1,0:T(8,128)(2,1)S(1)}, bf16[64,1664]{1,0:T(8,128)(2,1)S(1)}, u32[]{:S(2)}, u32[]{:S(2)}) collective-permute-start(bf16[64,1664]{1,0:T(8,128)(2,1)S(1)} %join.3), channel_id=1, source_target_pairs={{0,2},{2,0},{1,3},{3,1},{4,6},{6,4},{5,7},{7,5},{8,10},{10,8},{9,1... | collective-permute-start | bytes 638984 | tf_op jit(solution)/shard_map/ppermute | solution.py:101
  41.8 4.5 %collective-permute-start.15 = (bf16[64,1664]{1,0:T(8,128)(2,1)S(1)}, bf16[64,1664]{1,0:T(8,128)(2,1)S(1)}, u32[]{:S(2)}, u32[]{:S(2)}) collective-permute-start(bf16[64,1664]{1,0:T(8,128)(2,1)S(1)} %gate_up.12), channel_id=1, source_target_pairs={{0,1},{1,0},{2,3},{3,2},{4,5},{5,4},{6,7},{7,6},{8,9},{9,8},{10,11... | collective-permute-start | bytes 638984 | tf_op jit(solution)/shard_map/ppermute | solution.py:101
  42.4 7.6 %collective-permute-start.19 = (bf16[64,1664]{1,0:T(8,128)(2,1)S(1)}, bf16[64,1664]{1,0:T(8,128)(2,1)S(1)}, u32[]{:S(2)}, u32[]{:S(2)}) collective-permute-start(bf16[64,1664]{1,0:T(8,128)(2,1)S(1)} %gate_up.13), channel_id=1, source_target_pairs={{0,1},{1,0},{2,3},{3,2},{4,5},{5,4},{6,7},{7,6},{8,9},{9,8},{10,11... | collective-permute-start | bytes 638984 | tf_op jit(solution)/shard_map/ppermute | solution.py:101
  46.5 5.3 %collective-permute-start.21 = (bf16[64,768]{1,0:T(8,128)(2,1)S(1)}, bf16[64,768]{1,0:T(8,128)(2,1)S(1)}, u32[]{:S(2)}, u32[]{:S(2)}) collective-permute-start(bf16[64,768]{1,0:T(8,128)(2,1)S(1)} %hidden.2.refs_0_), channel_id=1, source_target_pairs={{0,1},{1,0},{2,3},{3,2},{4,5},{5,4},{6,7},{7,6},{8,9},{9,8},{10,11... | collective-permute-start | bytes 294920 | tf_op jit(solution)/shard_map/ppermute | solution.py:101
  46.6 6.3 %collective-permute-start.16 = (bf16[64,768]{1,0:T(8,128)(2,1)S(1)}, bf16[64,768]{1,0:T(8,128)(2,1)S(1)}, u32[]{:S(2)}, u32[]{:S(2)}) collective-permute-start(bf16[64,768]{1,0:T(8,128)(2,1)S(1)} %hidden.2.refs_0_), channel_id=1, source_target_pairs={{0,2},{2,0},{1,3},{3,1},{4,6},{6,4},{5,7},{7,5},{8,10},{10,8},{9,1... | collective-permute-start | bytes 294920 | tf_op jit(solution)/shard_map/ppermute | solution.py:101
  50.2 2.6 %collective-permute-start.22 = (bf16[64,768]{1,0:T(8,128)(2,1)S(1)}, bf16[64,768]{1,0:T(8,128)(2,1)S(1)}, u32[]{:S(2)}, u32[]{:S(2)}) collective-permute-start(bf16[64,768]{1,0:T(8,128)(2,1)S(1)} %hidden.3.refs_0_), channel_id=1, source_target_pairs={{0,1},{1,0},{2,3},{3,2},{4,5},{5,4},{6,7},{7,6},{8,9},{9,8},{10,11... | collective-permute-start | bytes 294920 | tf_op jit(solution)/shard_map/ppermute | solution.py:101
  50.3 5.2 %collective-permute-start.20 = (bf16[64,768]{1,0:T(8,128)(2,1)S(1)}, bf16[64,768]{1,0:T(8,128)(2,1)S(1)}, u32[]{:S(2)}, u32[]{:S(2)}) collective-permute-start(bf16[64,768]{1,0:T(8,128)(2,1)S(1)} %hidden.3.refs_0_), channel_id=1, source_target_pairs={{0,2},{2,0},{1,3},{3,1},{4,6},{6,4},{5,7},{7,5},{8,10},{10,8},{9,1... | collective-permute-start | bytes 294920 | tf_op jit(solution)/shard_map/ppermute | solution.py:101
  58.0 5.9 %collective-permute-start.24 = (bf16[32,512]{1,0:T(8,128)(2,1)S(1)}, bf16[32,512]{1,0:T(8,128)(2,1)S(1)}, u32[]{:S(2)}, u32[]{:S(2)}) collective-permute-start(bf16[32,512]{1,0:T(8,128)(2,1)S(1)} %get-tuple-element.48), channel_id=1, source_target_pairs={{0,12},{4,8},{8,4},{12,0},{1,13},{5,9},{9,5},{13,1},{2,14},{6,10},... | collective-permute-start | bytes 98312 | tf_op jit(solution)/shard_map/ppermute | solution.py:101
  60.0 5.0 %collective-permute-start.25 = (bf16[32,512]{1,0:T(8,128)(2,1)S(1)}, bf16[32,512]{1,0:T(8,128)(2,1)S(1)}, u32[]{:S(2)}, u32[]{:S(2)}) collective-permute-start(bf16[32,512]{1,0:T(8,128)(2,1)S(1)} %get-tuple-element.49), channel_id=1, source_target_pairs={{0,8},{4,12},{8,0},{12,4},{1,9},{5,13},{9,1},{13,5},{2,10},{6,14},... | collective-permute-start | bytes 98312 | tf_op jit(solution)/shard_map/ppermute | solution.py:101
  60.3 4.6 %collective-permute-start.26 = (bf16[32,512]{1,0:T(8,128)(2,1)S(1)}, bf16[32,512]{1,0:T(8,128)(2,1)S(1)}, u32[]{:S(2)}, u32[]{:S(2)}) collective-permute-start(bf16[32,512]{1,0:T(8,128)(2,1)S(1)} %get-tuple-element.50), channel_id=1, source_target_pairs={{0,4},{4,0},{8,12},{12,8},{1,5},{5,1},{9,13},{13,9},{2,6},{6,2},{1... | collective-permute-start | bytes 98312 | tf_op jit(solution)/shard_map/ppermute | solution.py:101
  (19 other events, 197.4 us)

commit v9 on v8

--- a/solution.py
+++ b/solution.py
@@ -48,12 +48,10 @@
         self.key_count, self.query_rows = key_count, query_rows
         self.local_experts = local_experts
         self.piece_count = self.exp * self.tp
-        capacity = self.ctx * MOST
-        slots = local_experts * capacity // self.piece_count
-        self.rows = slots // CELLS
-        self.experts = max(1, slots // capacity)
-        self.spread = max(1, capacity // slots)
-        self.each = max(1, self.experts // CELLS)
+        self.capacity = self.ctx * MOST // CELLS
+        self.rows = local_experts * self.capacity // self.piece_count
+        self.experts = max(1, self.rows // self.capacity)
+        self.spread = max(1, self.capacity // self.rows)
         self.cell_count = self.piece_count * CELLS
 
     def lead(self, k):
@@ -67,11 +65,9 @@
     def first_local_expert(self):
         return lax.axis_index("ctx") * self.local_experts
 
-    def cell(self, name):
-        flip, k, cell = name
+    def cell(self, flip, k, cell):
         piece = (lax.axis_index("tp") ^ flip) * self.exp + (lax.axis_index("exp") ^ k)
-        within = cell * self.each if self.experts > 1 else 0
-        return piece * CELLS + cell, lax.div(piece * self.experts + within, self.spread)
+        return piece * CELLS + cell, lax.div(piece * self.experts, self.spread)
 
 
 def lane_ids(shape):
@@ -304,37 +300,40 @@
 def route_kernel(layout, choices, width, *refs):
     info_refs, (place_ref, high_ref, low_ref) = refs[:-3], refs[-3:]
     cell_count, tokens, slots = place_ref.shape
-    local_experts = layout.local_experts
-    info = jnp.concatenate([ref[:, width:] for ref in info_refs], axis=0).astype(f32)
+    local_experts, capacity = layout.local_experts, layout.capacity
     expert = (lane_ids((tokens, local_experts)) + layout.first_local_expert()).astype(f32)
-    member = jnp.zeros((tokens, local_experts), f32)
-    weight_high = jnp.zeros((tokens, local_experts), f32)
-    weight_low = jnp.zeros((tokens, local_experts), f32)
-    for k in range(choices):
-        chosen = info[:, 1 + k : 2 + k] == expert
-        high = info[:, 1 + choices + k : 2 + choices + k]
-        low = info[:, 1 + 2 * choices + k : 2 + 2 * choices + k]
-        member = jnp.where(chosen, 1.0, member)
-        weight_high = jnp.where(chosen, high, weight_high)
-        weight_low = jnp.where(chosen, low, weight_low)
     square = (tokens, tokens)
     earlier = as_bf16(lane_ids(square) < row_ids(square))
-    rank = jnp.where(member > 0.5, dot(earlier, member.astype(bf16)), -1.0).astype(bf16)
-    weight_high = weight_high.astype(bf16)
-    weight_low = weight_low.astype(bf16)
-    capacity = cell_count * slots // local_experts
-    for piece in range(cell_count):
-        slot = lane_ids((local_experts, slots)) + piece * slots
-        spread = as_bf16(slot // capacity == row_ids((local_experts, slots)))
-        wanted = (lane_ids((tokens, slots)) + piece * slots) % capacity
-        placed = dot(rank, spread) == wanted.astype(f32)
-        place_ref[piece] = jnp.where(placed, 1.0, 0.0).astype(bf16)
-        high_ref[piece] = jnp.where(placed, dot(weight_high, spread), 0.0).astype(bf16)
-        low_ref[piece] = jnp.where(placed, dot(weight_low, spread), 0.0).astype(bf16)
+    count = len(info_refs) // CELLS
+    for cell in range(CELLS):
+        sources = info_refs[cell * count : (cell + 1) * count]
+        info = jnp.concatenate([ref[:, width:] for ref in sources], axis=0).astype(f32)
+        member = jnp.zeros((tokens, local_experts), f32)
+        weight_high = jnp.zeros((tokens, local_experts), f32)
+        weight_low = jnp.zeros((tokens, local_experts), f32)
+        for k in range(choices):
+            chosen = info[:, 1 + k : 2 + k] == expert
+            high = info[:, 1 + choices + k : 2 + choices + k]
+            low = info[:, 1 + 2 * choices + k : 2 + 2 * choices + k]
+            member = jnp.where(chosen, 1.0, member)
+            weight_high = jnp.where(chosen, high, weight_high)
+            weight_low = jnp.where(chosen, low, weight_low)
+        rank = jnp.where(member > 0.5, dot(earlier, member.astype(bf16)), -1.0).astype(bf16)
+        weight_high = weight_high.astype(bf16)
+        weight_low = weight_low.astype(bf16)
+        for piece in range(layout.piece_count):
+            slot = lane_ids((local_experts, slots)) + piece * slots
+            spread = as_bf16(slot // capacity == row_ids((local_experts, slots)))
+            wanted = (lane_ids((tokens, slots)) + piece * slots) % capacity
+            placed = dot(rank, spread) == wanted.astype(f32)
+            at = piece * CELLS + cell
+            place_ref[at] = jnp.where(placed, 1.0, 0.0).astype(bf16)
+            high_ref[at] = jnp.where(placed, dot(weight_high, spread), 0.0).astype(bf16)
+            low_ref[at] = jnp.where(placed, dot(weight_low, spread), 0.0).astype(bf16)
 
 
 def route(layout, packed, width, choices):
-    tokens = sum(value.shape[0] for value in packed)
+    tokens = sum(value.shape[0] for value in packed) // CELLS
     shape = jax.ShapeDtypeStruct((layout.cell_count, tokens, layout.rows), bf16)
     return pl.pallas_call(
         functools.partial(route_kernel, layout, choices, width),
@@ -345,57 +344,40 @@
     )(*packed)
 
 
-def pick_kernel(place_ref, *refs):
-    rows_refs, (out_ref, rows_ref) = refs[:-2], refs[-2:]
-    rows = rows_refs[0].shape[0]
-    for i, ref in enumerate(rows_refs):
-        rows_ref[i * rows : (i + 1) * rows, :] = ref[...]
-    for piece in range(out_ref.shape[0]):
-        out_ref[piece] = dot(place_ref[piece], rows_ref[...], ((0,), (0,))).astype(bf16)
-
-
-def pick(place, rows):
-    piece_count, tokens, slots = place.shape
-    columns = rows[0].shape[1]
-    return pl.pallas_call(
-        pick_kernel,
-        out_shape=jax.ShapeDtypeStruct((piece_count, slots, columns), bf16),
-        scratch_shapes=[pltpu.VMEM((tokens, columns), bf16)],
-        compiler_params=params(8),
-        cost_estimate=cost(2**26, 2**20),
-        name="pick",
-    )(place, *rows)
-
-
 def squares_joined(squares):
     high, low = in_two(squares[:, :1] + squares[:, 1:2])
     lane = lane_ids(squares.shape)
     return jnp.where(lane == 0, high, jnp.where(lane == 1, low, 0.0))
 
 
-def gate_up(names, layout, picked, weight):
+def gate_up(names, layout, place, rows, weight):
     _, width, ff_pair = weight.shape
-    rows = layout.rows // layout.each
-
-    def kernel(picked_ref, weight_ref, out_ref):
-        for place, name in enumerate(names):
-            at, first = layout.cell(name)
-            for i in range(layout.each):
-                picked = picked_ref[at, i * rows : (i + 1) * rows, :]
-                start = place * layout.rows + i * rows
-                here = slice(start, start + rows)
-                product = dot(picked[:, :width], weight_ref[first + i])
+    each = layout.rows // layout.experts
+    row_count = len(rows)
+
+    def kernel(place_ref, weight_ref, *refs):
+        for name, out_ref in zip(names, refs[row_count:]):
+            at, first = layout.cell(*name)
+            picked = 0.0
+            for i, ref in enumerate(refs[:row_count]):
+                count = ref.shape[0]
+                here = place_ref[at, i * count : (i + 1) * count, :]
+                picked = picked + dot(here, ref[...], ((0,), (0,)))
+            picked = picked.astype(bf16)
+            for i in range(layout.experts):
+                here = slice(i * each, (i + 1) * each)
+                product = dot(picked[here, :width], weight_ref[first + i])
                 out_ref[here, :ff_pair] = product.astype(bf16)
-                out_ref[here, ff_pair:] = picked[:, width:]
-
-    total = len(names) * layout.rows
+            out_ref[:, ff_pair:] = picked[:, width:]
+
+    out = jax.ShapeDtypeStruct((layout.rows, ff_pair + LANES), bf16)
     return pl.pallas_call(
         kernel,
-        out_shape=jax.ShapeDtypeStruct((total, ff_pair + LANES), bf16),
+        out_shape=[out] * len(names),
         compiler_params=params(8),
-        cost_estimate=cost(2 * total * width * ff_pair, 2 * total * ff_pair),
+        cost_estimate=cost(2 * layout.rows * width * ff_pair, 2 * layout.rows * ff_pair),
         name="gate_up",
-    )(picked, weight)
+    )(place, weight, *rows)
 
 
 def join_kernel(left_ref, right_ref, out_ref):
@@ -415,12 +397,12 @@
     )(left, right)
 
 
-def hidden_of(parts, starts, layout, ff_width, model_width, beside):
-    def kernel(beside_ref, *refs):
-        out_ref = refs[-1]
+def hidden_of(parts, ff_width, model_width, beside):
+    def kernel(*refs):
+        refs, out_ref = refs[len(beside) : -1], refs[-1]
         total = 0.0
-        for ref, start in zip(refs, starts):
-            total = total + ref[start : start + layout.rows, :].astype(f32)
+        for ref in refs:
+            total = total + ref[...].astype(f32)
         high = total[:, 2 * ff_width : 2 * ff_width + 1]
         low = total[:, 2 * ff_width + 1 : 2 * ff_width + 2]
         norm = lax.rsqrt((high + low) / model_width + epsilon)
@@ -430,44 +412,53 @@
 
     return pl.pallas_call(
         kernel,
-        in_specs=[whole(pltpu.HBM)] + [whole()] * len(parts),
-        out_shape=jax.ShapeDtypeStruct((layout.rows, ff_width), bf16),
+        in_specs=[whole(pltpu.HBM)] * len(beside) + [whole()] * len(parts),
+        out_shape=jax.ShapeDtypeStruct((parts[0].shape[0], ff_width), bf16),
         compiler_params=params(8),
         name="hidden",
-    )(*in_hbm([beside]), *parts)
-
-
-def down(names, layout, hidden, weight, high, low, total=None, out_count=1):
-    ff_width = hidden[0].shape[1]
+    )(*in_hbm(beside), *parts)
+
+
+def down(pieces, layout, weight, high, low, total=None, out_count=1):
+    first_cells = next(iter(pieces.values()))
+    ff_width = first_cells[0].shape[1]
     tokens = high.shape[1]
     piece_width = weight.shape[2]
-    each = layout.rows // layout.each
-    rows = tokens // out_count
+    each = layout.rows // layout.experts
+    rows = tokens * CELLS // out_count
     out_type = f32 if out_count == 1 else bf16
 
     def kernel(weight_ref, high_ref, low_ref, *refs):
-        hidden_refs, refs = refs[: len(names)], refs[len(names) :]
+        hidden_refs, refs = refs[: len(pieces) * CELLS], refs[len(pieces) * CELLS :]
         total_refs, out_refs, held_ref = refs[: -1 - out_count], refs[-1 - out_count : -1], refs[-1]
-        summed = 0.0
-        for ref, name in zip(hidden_refs, names):
-            at, first = layout.cell(name)
-            for i in range(layout.each):
+        summed = [0.0] * CELLS
+        for turn, name in enumerate(pieces):
+            cells = hidden_refs[turn * CELLS : (turn + 1) * CELLS]
+            _, first = layout.cell(*name, 0)
+            for i in range(layout.experts):
                 here = slice(i * each, (i + 1) * each)
-                held_ref[here, :] = dot(ref[here, :], weight_ref[first + i]).astype(bf16)
-            held = held_ref[...]
-            summed = summed + dot(high_ref[at], held) + dot(low_ref[at], held)
+                rows_in = jnp.concatenate([ref[here, :] for ref in cells], axis=0)
+                product = dot(rows_in, weight_ref[first + i]).astype(bf16)
+                for cell in range(CELLS):
+                    held_ref[cell, here, :] = product[cell * each : (cell + 1) * each, :]
+            for cell in range(CELLS):
+                at, _ = layout.cell(*name, cell)
+                held = held_ref[cell]
+                summed[cell] = summed[cell] + dot(high_ref[at], held) + dot(low_ref[at], held)
+        whole_sum = jnp.concatenate(summed, axis=0)
         for ref in total_refs:
-            summed = summed + ref[...]
+            whole_sum = whole_sum + ref[...]
         for i, ref in enumerate(out_refs):
-            ref[...] = summed[i * rows : (i + 1) * rows, :].astype(ref.dtype)
+            ref[...] = whole_sum[i * rows : (i + 1) * rows, :].astype(ref.dtype)
 
     before = [] if total is None else [total]
+    hidden = [value for cells in pieces.values() for value in cells]
     return pl.pallas_call(
         kernel,
         out_shape=[jax.ShapeDtypeStruct((rows, piece_width), out_type)] * out_count,
-        scratch_shapes=[pltpu.VMEM((layout.rows, piece_width), bf16)],
+        scratch_shapes=[pltpu.VMEM((CELLS, layout.rows, piece_width), bf16)],
         compiler_params=params(8),
-        cost_estimate=cost(2 * layout.rows * ff_width * piece_width, 2**20),
+        cost_estimate=cost(4 * layout.rows * ff_width * piece_width, 2**20),
         name="down",
     )(weight, high, low, *hidden, *before)
 
@@ -538,8 +529,15 @@
     place, combine_high, combine_low = route(
         layout, [gathered[k] for k in range(ctx_count)], width, choices
     )
+    def after(value, *others):
+        return lax.optimization_barrier((value,) + others)[0]
+
     projected = project(
-        layout, [parts[k] for k in range(ctx_count)], out_matrix, heads, scale
+        layout,
+        [parts[k] for k in range(ctx_count)],
+        after(out_matrix, place),
+        heads,
+        scale,
     )
     pieces = [projected[0]] + [
         swapped(projected[k], ("exp", "tp"), k) for k in far_first(piece_count)
@@ -548,73 +546,50 @@
     rows = {0: sent}
     for k in far_first(ctx_count):
         rows[k] = swapped(sent, "ctx", k)
-    picked = pick(place, [rows[k] for k in range(ctx_count)])
-
-    def after(value, *others):
-        return lax.optimization_barrier((value,) + others)[0]
-
-    def first_half(*names):
-        return gate_up(names, layout, picked, gate_up_weight)
+    half = ctx_count // CELLS
+    sources = [[rows[k] for k in range(half * i, half * (i + 1))] for i in range(CELLS)]
+
+    def first_half(k, cell, flips):
+        names = [(flip, k, cell) for flip in flips]
+        return gate_up(names, layout, place, sources[cell], gate_up_weight)
 
     crossed = [[] for _ in range(CELLS)]
-    arrived = [None] * CELLS
     for k in far_first(exp_count):
-        near = [swapped(first_half((1, k, 0)), "tp", 1)]
-        mine = first_half((0, k, 0))
-        picked = after(picked, mine)
-        near.append(swapped(first_half((1, k, 1)), "tp", 1))
+        away, mine = first_half(k, 0, (1, 0))
+        here = [swapped(away, "tp", 1)]
+        sources[1] = list(lax.optimization_barrier(tuple(sources[1]) + (mine,)))[:-1]
+        here.append(swapped(first_half(k, 1, (1,))[0], "tp", 1))
         for cell in range(CELLS):
             if cell:
-                mine = first_half((0, k, cell))
-            joined = join(mine, near[cell])
-            picked = after(picked, joined)
+                mine = first_half(k, cell, (0,))[0]
+            joined = join(mine, here[cell])
+            place = after(place, joined)
             crossed[cell].append(swapped(joined, "exp", k))
-            if k == 1:
-                arrived[cell] = swapped(first_half((1, 0, cell)), "tp", 1)
-    kept = first_half((0, 0, 0), (0, 0, 1))
-
     own_hidden = []
     for cell in range(CELLS):
+        arrived = swapped(first_half(0, cell, (1,))[0], "tp", 1)
+        kept = first_half(0, cell, (0,))[0]
         crossed[cell], kept = lax.optimization_barrier((crossed[cell], kept))
-        parts = [kept, arrived[cell]] + crossed[cell]
-        starts = [cell * layout.rows] + [0] * (len(parts) - 1)
-        hidden = hidden_of(parts, starts, layout, ff_width, model_width, gate_up_weight)
-        kept = after(kept, hidden)
+        beside = [gate_up_weight] if cell == CELLS - 1 else []
+        hidden = hidden_of([kept, arrived] + crossed[cell], ff_width, model_width, beside)
+        place = after(place, hidden)
         own_hidden.append(hidden)
 
-    def add(hidden, total, out_count=1):
-        return down(
-            list(hidden),
-            layout,
-            list(hidden.values()),
-            down_weight,
-            combine_high,
-            combine_low,
-            total,
-            out_count,
-        )
-
-    near = {
-        (flip, 0, cell): swapped(hidden, "tp", 1) if flip else hidden
-        for cell, hidden in enumerate(own_hidden)
-        for flip in (0, 1)
+    near = [swapped(hidden, "tp", 1) for hidden in own_hidden]
+    far = {
+        k: [swapped(hidden, "exp", k) for hidden in own_hidden] for k in range(1, exp_count)
     }
-    far = {
-        (0, k, cell): swapped(own_hidden[cell], "exp", k)
-        for cell in range(CELLS)
-        for k in range(1, exp_count)
-    }
-    total = add({name: near[name] for name in list(near)[:2]}, None)[0]
-    names = list(near)[2:]
-    near[names[0]] = after(near[names[0]], total)
-    first = next(iter(far))
-    total = add({**{name: near[name] for name in names}, first: far[first]}, total)[0]
+    own_hidden[-1] = after(own_hidden[-1], far[1][0])
+
+    def add(pieces, total, out_count=1):
+        return down(pieces, layout, down_weight, combine_high, combine_low, total, out_count)
+
+    total = add({(0, 0): own_hidden, (1, 0): near}, None)[0]
     last = {}
-    for turn, ((_, k, cell), hidden) in enumerate(far.items()):
-        if turn:
-            hidden = after(hidden, total)
-            total = add({(0, k, cell): hidden}, total)[0]
-        last[1, k, cell] = swapped(hidden, "tp", 1)
+    for k in far:
+        far[k][-1] = after(far[k][-1], total)
+        last[1, k] = [swapped(hidden, "tp", 1) for hidden in far[k]]
+        total = add({(0, k): far[k]}, total)[0]
     totals = add(last, total, ctx_count)
     returned = [totals[0]] + [swapped(totals[k], "ctx", k) for k in far_first(ctx_count)]
     return finish(mixed, returned)

time: 65.7 us -> 64.7 us (0.985)
  Pallas kernels: 19.4 us -> 22.1 us
  waiting for transfers between devices: 17.7 us -> 15.1 us
  starting transfers between devices: 28 us -> 25.6 us
  local copies, waits for them, and re-layouts: 0.08 us -> 1.42 us
    pallas_call x10 -> x9, Pallas kernels: 5.84 us -> 9.29 us  [the longest x7 8.86 us: gate_up(): pl.pallas_call(kernel, out_shape=[out] * len(names), compiler_params=para...]
    ppermute x27, waiting for transfers between devices: 17.7 us -> 15.1 us  [swapped(): return lax.ppermute(value, axes, pairs)]
    ppermute x27, starting transfers between devices: 28 us -> 25.6 us  [swapped(): return lax.ppermute(value, axes, pairs)]
    unnamed x32, local copies, waits for them, and re-layouts: 0.08 us -> 1.42 us
    pallas_call x4 -> x3, Pallas kernels: 3.98 us -> 3.23 us  [down(): pl.pallas_call(kernel, out_shape=[jax.ShapeDtypeStruct((rows, piece_width...]
  transfers between devices with their start and end apart: 27 -> 27, of which waited for: 15 -> 14; matrix products, arithmetic and copies ran while one was open for 0% -> 0% of each run, Pallas kernels for 22% -> 29%
where the time goes in v9:
time: 64.7 us; the launch traced here: 64.5 us
  starting transfers between devices  25.6 us (40%)
  Pallas kernels  22.1 us (34%)
  waiting for transfers between devices  15.1 us (23%)
  local copies, waits for them, and re-layouts  1.42 us (2%)
    ppermute x27, starting transfers between devices, swapped(): return lax.ppermute(value, axes, pairs)  25.6 us
    ppermute x27, waiting for transfers between devices, swapped(): return lax.ppermute(value, axes, pairs)  15.1 us
    pallas_call x7, Pallas kernels, gate_up(): pl.pallas_call(kernel, out_shape=[out] * len(names), compiler_params=para...  8.86 us
    pallas_call x4, Pallas kernels, attend(): pl.pallas_call(functools.partial(attend_kernel, heads, scale, layout, k),...  5.04 us
    pallas_call x3, Pallas kernels, down(): pl.pallas_call(kernel, out_shape=[jax.ShapeDtypeStruct((rows, piece_width...  3.23 us
    unnamed x32, local copies, waits for them, and re-layouts  1.42 us
  transfers between devices with their start and end apart: 27, of which 14 were waited for; matrix products, arithmetic and copies ran while one was open for 0% of the time, Pallas kernels for 29%

profile of v9, /device:TPU:0, one launch (start us, length us, event | category | flops | bytes accessed | tf_op | source)
XLA Modules:
  0.0 64.5 jit_solution(4426423728759050739)
XLA Ops:
  1.0 3.1 %collective-permute-start = (bf16[32,1152]{1,0:T(8,128)(2,1)S(1)}, bf16[32,1152]{1,0:T(8,128)(2,1)S(1)}, u32[]{:S(2)}, u32[]{:S(2)}) collective-permute-start(bf16[32,1152]{1,0:T(8,128)(2,1)S(1)} %pack.1.queries_ref.refs_0_), channel_id=1, source_target_pairs={{0,4},{4,0},{8,12},{12,8},{1,5},{5,1},{9,13},{13,9},{2,6},{6,2},{1... | collective-permute-start | bytes 221192 | tf_op jit(solution)/shard_map/ppermute | solution.py:97
  4.2 2.6 %collective-permute-start.2 = (bf16[32,1152]{1,0:T(8,128)(2,1)S(1)}, bf16[32,1152]{1,0:T(8,128)(2,1)S(1)}, u32[]{:S(2)}, u32[]{:S(2)}) collective-permute-start(bf16[32,1152]{1,0:T(8,128)(2,1)S(1)} %pack.1.queries_ref.refs_0_), channel_id=1, source_target_pairs={{0,8},{4,12},{8,0},{12,4},{1,9},{5,13},{9,1},{13,5},{2,10},{6,14},... | collective-permute-start | bytes 221192 | tf_op jit(solution)/shard_map/ppermute | solution.py:97
  7.4 1.3 %attend.5 = bf16[32,1152]{1,0:T(8,128)(2,1)S(1)} custom-call(bf16[32,1152]{1,0:T(8,128)(2,1)S(1)} %collective-permute-done.queries_ref.refs_1_, bf16[2048,128]{1,0:T(8,128)(2,1)S(1)} %bitcast.13, bf16[2048,128]{1,0:T(8,128)(2,1)S(1)} %bitcast.17, bf16[64,2048]{1,0:T(8,128)(2,1)S(1)} %sight.1.sight_ref, bf16[16,512,1536]{2,1,0:T(8,128)(2,1)} %refs_0_.1), custom_call_target="tpu_custom_call" | custom-call | flops 536870912 | bytes 1048576 | tf_op jit(solution)/shard_map/attend/pallas_call | solution.py:219
  9.8 2.1 %collective-permute-done.2.queries_ref.refs_2_ = bf16[32,1152]{1,0:T(8,128)(2,1)S(1)} collective-permute-done((bf16[32,1152]{1,0:T(8,128)(2,1)S(1)}, bf16[32,1152]{1,0:T(8,128)(2,1)S(1)}, u32[]{:S(2)}, u32[]{:S(2)}) %collective-permute-start.2) | collective-permute-done | bytes 73760 | tf_op jit(solution)/shard_map/ppermute | solution.py:97
  11.9 1.3 %attend.6 = bf16[32,1152]{1,0:T(8,128)(2,1)S(1)} custom-call(bf16[32,1152]{1,0:T(8,128)(2,1)S(1)} %collective-permute-done.2.queries_ref.refs_2_, bf16[2048,128]{1,0:T(8,128)(2,1)S(1)} %bitcast.14, bf16[2048,128]{1,0:T(8,128)(2,1)S(1)} %bitcast.18, bf16[64,2048]{1,0:T(8,128)(2,1)S(1)} %sight.1.sight_ref, bf16[16,512,1536]{2,1,0:T(8,128)(2,1)} %refs_0_.1), custom_call_target="tpu_custom_call" | custom-call | flops 536870912 | bytes 1048576 | tf_op jit(solution)/shard_map/attend/pallas_call | solution.py:219
  13.2 1.3 %collective-permute-start.3 = (bf16[32,1152]{1,0:T(8,128)(2,1)S(1)}, bf16[32,1152]{1,0:T(8,128)(2,1)S(1)}, u32[]{:S(2)}, u32[]{:S(2)}) collective-permute-start(bf16[32,1152]{1,0:T(8,128)(2,1)S(1)} %attend.6), channel_id=1, source_target_pairs={{0,8},{4,12},{8,0},{12,4},{1,9},{5,13},{9,1},{13,5},{2,10},{6,14},... | collective-permute-start | bytes 221192 | tf_op jit(solution)/shard_map/ppermute | solution.py:97
  14.5 1.3 %attend.7 = bf16[32,1152]{1,0:T(8,128)(2,1)S(1)} custom-call(bf16[32,1152]{1,0:T(8,128)(2,1)S(1)} %collective-permute-done.4.queries_ref.refs_3_, bf16[2048,128]{1,0:T(8,128)(2,1)S(1)} %bitcast.15, bf16[2048,128]{1,0:T(8,128)(2,1)S(1)} %bitcast.19, bf16[64,2048]{1,0:T(8,128)(2,1)S(1)} %sight.1.sight_ref, bf16[16,512,1536]{2,1,0:T(8,128)(2,1)} %refs_0_.1), custom_call_target="tpu_custom_call" | custom-call | flops 536870912 | bytes 1048576 | tf_op jit(solution)/shard_map/attend/pallas_call | solution.py:219
  15.8 2.2 %collective-permute-start.5 = (bf16[32,1152]{1,0:T(8,128)(2,1)S(1)}, bf16[32,1152]{1,0:T(8,128)(2,1)S(1)}, u32[]{:S(2)}, u32[]{:S(2)}) collective-permute-start(bf16[32,1152]{1,0:T(8,128)(2,1)S(1)} %attend.7), channel_id=1, source_target_pairs={{0,12},{4,8},{8,4},{12,0},{1,13},{5,9},{9,5},{13,1},{2,14},{6,10},... | collective-permute-start | bytes 221192 | tf_op jit(solution)/shard_map/ppermute | solution.py:97
  18.0 1.3 %attend.4.refs_0_ = bf16[32,1152]{1,0:T(8,128)(2,1)S(1)} custom-call(bf16[32,1152]{1,0:T(8,128)(2,1)S(1)} %pack.1.queries_ref.refs_0_, bf16[2048,128]{1,0:T(8,128)(2,1)S(1)} %bitcast.16, bf16[2048,128]{1,0:T(8,128)(2,1)S(1)} %bitcast.20, bf16[64,2048]{1,0:T(8,128)(2,1)S(1)} %sight.1.sight_ref, bf16[16,512,1536]{2,1,0:T(8,128)(2,1)} %refs_0_.1), custom_call_target="tpu_custom_call" | custom-call | flops 536870912 | bytes 1048576 | tf_op jit(solution)/shard_map/attend/pallas_call | solution.py:219
  20.1 2.0 %collective-permute-done.5.refs_3_ = bf16[32,1152]{1,0:T(8,128)(2,1)S(1)} collective-permute-done((bf16[32,1152]{1,0:T(8,128)(2,1)S(1)}, bf16[32,1152]{1,0:T(8,128)(2,1)S(1)}, u32[]{:S(2)}, u32[]{:S(2)}) %collective-permute-start.5) | collective-permute-done | bytes 73760 | tf_op jit(solution)/shard_map/ppermute | solution.py:97
  23.2 1.5 %collective-permute-start.7 = (bf16[32,512]{1,0:T(8,128)(2,1)S(1)}, bf16[32,512]{1,0:T(8,128)(2,1)S(1)}, u32[]{:S(2)}, u32[]{:S(2)}) collective-permute-start(bf16[32,512]{1,0:T(8,128)(2,1)S(1)} %get-tuple-element.36), channel_id=1, source_target_pairs={{0,2},{1,3},{2,0},{3,1},{4,6},{5,7},{6,4},{7,5},{8,10},{9,11},{10,... | collective-permute-start | bytes 98312 | tf_op jit(solution)/shard_map/ppermute | solution.py:97
  25.0 1.8 %collective-permute-done.6.refs_1_ = bf16[32,512]{1,0:T(8,128)(2,1)S(1)} collective-permute-done((bf16[32,512]{1,0:T(8,128)(2,1)S(1)}, bf16[32,512]{1,0:T(8,128)(2,1)S(1)}, u32[]{:S(2)}, u32[]{:S(2)}) %collective-permute-start.6) | collective-permute-done | bytes 32800 | tf_op jit(solution)/shard_map/ppermute | solution.py:97
  27.3 1.4 %collective-permute-start.9 = (bf16[32,640]{1,0:T(8,128)(2,1)S(1)}, bf16[32,640]{1,0:T(8,128)(2,1)S(1)}, u32[]{:S(2)}, u32[]{:S(2)}) collective-permute-start(bf16[32,640]{1,0:T(8,128)(2,1)S(1)} %get-tuple-element.41.refs_0_), channel_id=1, source_target_pairs={{0,4},{4,0},{8,12},{12,8},{1,5},{5,1},{9,13},{13,9},{2,6},{6,2},{1... | collective-permute-start | bytes 122888 | tf_op jit(solution)/shard_map/ppermute | solution.py:97
  29.5 1.3 %collective-permute-start.12 = (bf16[32,640]{1,0:T(8,128)(2,1)S(1)}, bf16[32,640]{1,0:T(8,128)(2,1)S(1)}, u32[]{:S(2)}, u32[]{:S(2)}) collective-permute-start(bf16[32,640]{1,0:T(8,128)(2,1)S(1)} %get-tuple-element.41.refs_0_), channel_id=1, source_target_pairs={{0,8},{4,12},{8,0},{12,4},{1,9},{5,13},{9,1},{13,5},{2,10},{6,14},... | collective-permute-start | bytes 122888 | tf_op jit(solution)/shard_map/ppermute | solution.py:97
  31.4 2.1 %gate_up.7 = (bf16[64,1664]{1,0:T(8,128)(2,1)S(1)}, bf16[64,1664]{1,0:T(8,128)(2,1)S(1)}) custom-call(bf16[8,64,64]{2,1,0:T(8,128)(2,1)S(1)} %get-tuple-element.50.place_ref, bf16[16,512,1536]{2,1,0:T(8,128)(2,1)S(1)} %bitcast.10, bf16[32,640]{1,0:T(8,128)(2,1)S(1)} %get-tuple-element.41.refs_0_, bf16[32,640]{1,0:T(8,128)(2,1)S(1)} %collective-permute-done.9.refs_1_), custom_call_target="tpu_custom_call" | custom-call | flops 100663296 | bytes 196608 | tf_op jit(solution)/shard_map/gate_up/pallas_call | solution.py:374
  37.0 1.3 %collective-permute-start.11 = (bf16[64,1664]{1,0:T(8,128)(2,1)S(1)}, bf16[64,1664]{1,0:T(8,128)(2,1)S(1)}, u32[]{:S(2)}, u32[]{:S(2)}) collective-permute-start(bf16[64,1664]{1,0:T(8,128)(2,1)S(1)} %join.2), channel_id=1, source_target_pairs={{0,2},{2,0},{1,3},{3,1},{4,6},{6,4},{5,7},{7,5},{8,10},{10,8},{9,1... | collective-permute-start | bytes 638984 | tf_op jit(solution)/shard_map/ppermute | solution.py:97
  41.8 1.3 %gate_up.10.refs_0_ = bf16[64,1664]{1,0:T(8,128)(2,1)S(1)} custom-call(bf16[8,64,64]{2,1,0:T(8,128)(2,1)S(1)} %get-tuple-element.50.place_ref, bf16[16,512,1536]{2,1,0:T(8,128)(2,1)S(1)} %bitcast.10, bf16[32,640]{1,0:T(8,128)(2,1)S(1)} %get-tuple-element.41.refs_0_, bf16[32,640]{1,0:T(8,128)(2,1)S(1)} %collective-permute-done.9.refs_1_), custom_call_target="tpu_custom_call" | custom-call | flops 100663296 | bytes 196608 | tf_op jit(solution)/shard_map/gate_up/pallas_call | solution.py:374
  43.1 2.1 %collective-permute-done.11.refs_2_ = bf16[64,1664]{1,0:T(8,128)(2,1)S(1)} collective-permute-done((bf16[64,1664]{1,0:T(8,128)(2,1)S(1)}, bf16[64,1664]{1,0:T(8,128)(2,1)S(1)}, u32[]{:S(2)}, u32[]{:S(2)}) %collective-permute-start.11) | collective-permute-done | bytes 213024 | tf_op jit(solution)/shard_map/ppermute | solution.py:97
  49.7 1.3 %collective-permute-start.20 = (bf16[64,768]{1,0:T(8,128)(2,1)S(1)}, bf16[64,768]{1,0:T(8,128)(2,1)S(1)}, u32[]{:S(2)}, u32[]{:S(2)}) collective-permute-start(bf16[64,768]{1,0:T(8,128)(2,1)S(1)} %hidden.3.refs_1_), channel_id=1, source_target_pairs={{0,2},{2,0},{1,3},{3,1},{4,6},{6,4},{5,7},{7,5},{8,10},{10,8},{9,1... | collective-permute-start | bytes 294920 | tf_op jit(solution)/shard_map/ppermute | solution.py:97
  51.8 1.3 %slice-done.8 = s8[4194304]{0:T(1024)(128)(4,1)S(1)} async-done(((s8[12582912]{0:T(1024)(128)(4,1)}), s8[4194304]{0:T(1024)(128)(4,1)S(1)}, s32[]{:S(2)}) %slice-start.8) | async-done | bytes 4194328
  53.1 1.5 %down.3.refs_2_ = f32[128,512]{1,0:T(8,128)S(1)} custom-call(bf16[16,768,512]{2,1,0:T(8,128)(2,1)S(1)} %bitcast.12, bf16[8,64,64]{2,1,0:T(8,128)(2,1)S(1)} %get-tuple-element.39.high_ref, bf16[8,64,64]{2,1,0:T(8,128)(2,1)S(1)} %get-tuple-element.40.low_ref, bf16[64,768]{1,0:T(8,128)(2,1)S(1)} %hidden.2.refs_0_, bf16[64,768]{1,0:T(8,128)(2,1)S(1)} %hidden.3.refs_1_, ...), custom_call_target="tpu_custom_call" | custom-call | flops 100663296 | bytes 1048576 | tf_op jit(solution)/shard_map/down/pallas_call | solution.py:456
  57.0 2.0 %collective-permute-start.24 = (bf16[32,512]{1,0:T(8,128)(2,1)S(1)}, bf16[32,512]{1,0:T(8,128)(2,1)S(1)}, u32[]{:S(2)}, u32[]{:S(2)}) collective-permute-start(bf16[32,512]{1,0:T(8,128)(2,1)S(1)} %get-tuple-element.56), channel_id=1, source_target_pairs={{0,12},{4,8},{8,4},{12,0},{1,13},{5,9},{9,5},{13,1},{2,14},{6,10},... | collective-permute-start | bytes 98312 | tf_op jit(solution)/shard_map/ppermute | solution.py:97
  59.0 2.5 %collective-permute-start.26 = (bf16[32,512]{1,0:T(8,128)(2,1)S(1)}, bf16[32,512]{1,0:T(8,128)(2,1)S(1)}, u32[]{:S(2)}, u32[]{:S(2)}) collective-permute-start(bf16[32,512]{1,0:T(8,128)(2,1)S(1)} %get-tuple-element.58), channel_id=1, source_target_pairs={{0,4},{4,0},{8,12},{12,8},{1,5},{5,1},{9,13},{13,9},{2,6},{6,2},{1... | collective-permute-start | bytes 98312 | tf_op jit(solution)/shard_map/ppermute | solution.py:97
  61.5 1.4 %collective-permute-done.24.refs_1_ = bf16[32,512]{1,0:T(8,128)(2,1)S(1)} collective-permute-done((bf16[32,512]{1,0:T(8,128)(2,1)S(1)}, bf16[32,512]{1,0:T(8,128)(2,1)S(1)}, u32[]{:S(2)}, u32[]{:S(2)}) %collective-permute-start.24) | collective-permute-done | bytes 32800 | tf_op jit(solution)/shard_map/ppermute | solution.py:97
  (89 shorter events, 23.2 us)
Async XLA Ops:
  1.0 6.3 %collective-permute-start = (bf16[32,1152]{1,0:T(8,128)(2,1)S(1)}, bf16[32,1152]{1,0:T(8,128)(2,1)S(1)}, u32[]{:S(2)}, u32[]{:S(2)}) collective-permute-start(bf16[32,1152]{1,0:T(8,128)(2,1)S(1)} %pack.1.queries_ref.refs_0_), channel_id=1, source_target_pairs={{0,4},{4,0},{8,12},{12,8},{1,5},{5,1},{9,13},{13,9},{2,6},{6,2},{1... | collective-permute-start | bytes 221192 | tf_op jit(solution)/shard_map/ppermute | solution.py:97
  4.2 7.8 %collective-permute-start.2 = (bf16[32,1152]{1,0:T(8,128)(2,1)S(1)}, bf16[32,1152]{1,0:T(8,128)(2,1)S(1)}, u32[]{:S(2)}, u32[]{:S(2)}) collective-permute-start(bf16[32,1152]{1,0:T(8,128)(2,1)S(1)} %pack.1.queries_ref.refs_0_), channel_id=1, source_target_pairs={{0,8},{4,12},{8,0},{12,4},{1,9},{5,13},{9,1},{13,5},{2,10},{6,14},... | collective-permute-start | bytes 221192 | tf_op jit(solution)/shard_map/ppermute | solution.py:97
  6.7 7.8 %collective-permute-start.4 = (bf16[32,1152]{1,0:T(8,128)(2,1)S(1)}, bf16[32,1152]{1,0:T(8,128)(2,1)S(1)}, u32[]{:S(2)}, u32[]{:S(2)}) collective-permute-start(bf16[32,1152]{1,0:T(8,128)(2,1)S(1)} %pack.1.queries_ref.refs_0_), channel_id=1, source_target_pairs={{0,12},{4,8},{8,4},{12,0},{1,13},{5,9},{9,5},{13,1},{2,14},{6,10},... | collective-permute-start | bytes 221192 | tf_op jit(solution)/shard_map/ppermute | solution.py:97
  8.7 11.3 %collective-permute-start.1 = (bf16[32,1152]{1,0:T(8,128)(2,1)S(1)}, bf16[32,1152]{1,0:T(8,128)(2,1)S(1)}, u32[]{:S(2)}, u32[]{:S(2)}) collective-permute-start(bf16[32,1152]{1,0:T(8,128)(2,1)S(1)} %attend.5), channel_id=1, source_target_pairs={{0,4},{4,0},{8,12},{12,8},{1,5},{5,1},{9,13},{13,9},{2,6},{6,2},{1... | collective-permute-start | bytes 221192 | tf_op jit(solution)/shard_map/ppermute | solution.py:97
  13.2 6.9 %collective-permute-start.3 = (bf16[32,1152]{1,0:T(8,128)(2,1)S(1)}, bf16[32,1152]{1,0:T(8,128)(2,1)S(1)}, u32[]{:S(2)}, u32[]{:S(2)}) collective-permute-start(bf16[32,1152]{1,0:T(8,128)(2,1)S(1)} %attend.6), channel_id=1, source_target_pairs={{0,8},{4,12},{8,0},{12,4},{1,9},{5,13},{9,1},{13,5},{2,10},{6,14},... | collective-permute-start | bytes 221192 | tf_op jit(solution)/shard_map/ppermute | solution.py:97
  15.8 6.3 %collective-permute-start.5 = (bf16[32,1152]{1,0:T(8,128)(2,1)S(1)}, bf16[32,1152]{1,0:T(8,128)(2,1)S(1)}, u32[]{:S(2)}, u32[]{:S(2)}) collective-permute-start(bf16[32,1152]{1,0:T(8,128)(2,1)S(1)} %attend.7), channel_id=1, source_target_pairs={{0,12},{4,8},{8,4},{12,0},{1,13},{5,9},{9,5},{13,1},{2,14},{6,10},... | collective-permute-start | bytes 221192 | tf_op jit(solution)/shard_map/ppermute | solution.py:97
  23.1 3.7 %collective-permute-start.6 = (bf16[32,512]{1,0:T(8,128)(2,1)S(1)}, bf16[32,512]{1,0:T(8,128)(2,1)S(1)}, u32[]{:S(2)}, u32[]{:S(2)}) collective-permute-start(bf16[32,512]{1,0:T(8,128)(2,1)S(1)} %get-tuple-element.35), channel_id=1, source_target_pairs={{0,3},{1,2},{2,1},{3,0},{4,7},{5,6},{6,5},{7,4},{8,11},{9,10},{10,... | collective-permute-start | bytes 98312 | tf_op jit(solution)/shard_map/ppermute | solution.py:97
  23.2 4.0 %collective-permute-start.7 = (bf16[32,512]{1,0:T(8,128)(2,1)S(1)}, bf16[32,512]{1,0:T(8,128)(2,1)S(1)}, u32[]{:S(2)}, u32[]{:S(2)}) collective-permute-start(bf16[32,512]{1,0:T(8,128)(2,1)S(1)} %get-tuple-element.36), channel_id=1, source_target_pairs={{0,2},{1,3},{2,0},{3,1},{4,6},{5,7},{6,4},{7,5},{8,10},{9,11},{10,... | collective-permute-start | bytes 98312 | tf_op jit(solution)/shard_map/ppermute | solution.py:97
  27.3 4.1 %collective-permute-start.9 = (bf16[32,640]{1,0:T(8,128)(2,1)S(1)}, bf16[32,640]{1,0:T(8,128)(2,1)S(1)}, u32[]{:S(2)}, u32[]{:S(2)}) collective-permute-start(bf16[32,640]{1,0:T(8,128)(2,1)S(1)} %get-tuple-element.41.refs_0_), channel_id=1, source_target_pairs={{0,4},{4,0},{8,12},{12,8},{1,5},{5,1},{9,13},{13,9},{2,6},{6,2},{1... | collective-permute-start | bytes 122888 | tf_op jit(solution)/shard_map/ppermute | solution.py:97
  28.7 5.8 %collective-permute-start.13 = (bf16[32,640]{1,0:T(8,128)(2,1)S(1)}, bf16[32,640]{1,0:T(8,128)(2,1)S(1)}, u32[]{:S(2)}, u32[]{:S(2)}) collective-permute-start(bf16[32,640]{1,0:T(8,128)(2,1)S(1)} %get-tuple-element.41.refs_0_), channel_id=1, source_target_pairs={{0,12},{4,8},{8,4},{12,0},{1,13},{5,9},{9,5},{13,1},{2,14},{6,10},... | collective-permute-start | bytes 122888 | tf_op jit(solution)/shard_map/ppermute | solution.py:97
  29.5 6.2 %collective-permute-start.12 = (bf16[32,640]{1,0:T(8,128)(2,1)S(1)}, bf16[32,640]{1,0:T(8,128)(2,1)S(1)}, u32[]{:S(2)}, u32[]{:S(2)}) collective-permute-start(bf16[32,640]{1,0:T(8,128)(2,1)S(1)} %get-tuple-element.41.refs_0_), channel_id=1, source_target_pairs={{0,8},{4,12},{8,0},{12,4},{1,9},{5,13},{9,1},{13,5},{2,10},{6,14},... | collective-permute-start | bytes 122888 | tf_op jit(solution)/shard_map/ppermute | solution.py:97
  33.5 3.3 %collective-permute-start.10 = (bf16[64,1664]{1,0:T(8,128)(2,1)S(1)}, bf16[64,1664]{1,0:T(8,128)(2,1)S(1)}, u32[]{:S(2)}, u32[]{:S(2)}) collective-permute-start(bf16[64,1664]{1,0:T(8,128)(2,1)S(1)} %get-tuple-element.43), channel_id=1, source_target_pairs={{0,1},{1,0},{2,3},{3,2},{4,5},{5,4},{6,7},{7,6},{8,9},{9,8},{10,11... | collective-permute-start | bytes 638984 | tf_op jit(solution)/shard_map/ppermute | solution.py:97
  36.8 2.7 %collective-permute-start.14 = (bf16[64,1664]{1,0:T(8,128)(2,1)S(1)}, bf16[64,1664]{1,0:T(8,128)(2,1)S(1)}, u32[]{:S(2)}, u32[]{:S(2)}) collective-permute-start(bf16[64,1664]{1,0:T(8,128)(2,1)S(1)} %gate_up.9), channel_id=1, source_target_pairs={{0,1},{1,0},{2,3},{3,2},{4,5},{5,4},{6,7},{7,6},{8,9},{9,8},{10,11... | collective-permute-start | bytes 638984 | tf_op jit(solution)/shard_map/ppermute | solution.py:97
  37.0 8.1 %collective-permute-start.11 = (bf16[64,1664]{1,0:T(8,128)(2,1)S(1)}, bf16[64,1664]{1,0:T(8,128)(2,1)S(1)}, u32[]{:S(2)}, u32[]{:S(2)}) collective-permute-start(bf16[64,1664]{1,0:T(8,128)(2,1)S(1)} %join.2), channel_id=1, source_target_pairs={{0,2},{2,0},{1,3},{3,1},{4,6},{6,4},{5,7},{7,5},{8,10},{10,8},{9,1... | collective-permute-start | bytes 638984 | tf_op jit(solution)/shard_map/ppermute | solution.py:97
  40.8 4.4 %collective-permute-start.15 = (bf16[64,1664]{1,0:T(8,128)(2,1)S(1)}, bf16[64,1664]{1,0:T(8,128)(2,1)S(1)}, u32[]{:S(2)}, u32[]{:S(2)}) collective-permute-start(bf16[64,1664]{1,0:T(8,128)(2,1)S(1)} %gate_up.11), channel_id=1, source_target_pairs={{0,1},{1,0},{2,3},{3,2},{4,5},{5,4},{6,7},{7,6},{8,9},{9,8},{10,11... | collective-permute-start | bytes 638984 | tf_op jit(solution)/shard_map/ppermute | solution.py:97
  41.0 8.3 %collective-permute-start.18 = (bf16[64,1664]{1,0:T(8,128)(2,1)S(1)}, bf16[64,1664]{1,0:T(8,128)(2,1)S(1)}, u32[]{:S(2)}, u32[]{:S(2)}) collective-permute-start(bf16[64,1664]{1,0:T(8,128)(2,1)S(1)} %join.3), channel_id=1, source_target_pairs={{0,2},{2,0},{1,3},{3,1},{4,6},{6,4},{5,7},{7,5},{8,10},{10,8},{9,1... | collective-permute-start | bytes 638984 | tf_op jit(solution)/shard_map/ppermute | solution.py:97
  46.5 2.9 %collective-permute-start.19 = (bf16[64,1664]{1,0:T(8,128)(2,1)S(1)}, bf16[64,1664]{1,0:T(8,128)(2,1)S(1)}, u32[]{:S(2)}, u32[]{:S(2)}) collective-permute-start(bf16[64,1664]{1,0:T(8,128)(2,1)S(1)} %gate_up.13), channel_id=1, source_target_pairs={{0,1},{1,0},{2,3},{3,2},{4,5},{5,4},{6,7},{7,6},{8,9},{9,8},{10,11... | collective-permute-start | bytes 638984 | tf_op jit(solution)/shard_map/ppermute | solution.py:97
  46.5 5.3 %collective-permute-start.21 = (bf16[64,768]{1,0:T(8,128)(2,1)S(1)}, bf16[64,768]{1,0:T(8,128)(2,1)S(1)}, u32[]{:S(2)}, u32[]{:S(2)}) collective-permute-start(bf16[64,768]{1,0:T(8,128)(2,1)S(1)} %hidden.2.refs_0_), channel_id=1, source_target_pairs={{0,1},{1,0},{2,3},{3,2},{4,5},{5,4},{6,7},{7,6},{8,9},{9,8},{10,11... | collective-permute-start | bytes 294920 | tf_op jit(solution)/shard_map/ppermute | solution.py:97
  47.0 4.8 %collective-permute-start.16 = (bf16[64,768]{1,0:T(8,128)(2,1)S(1)}, bf16[64,768]{1,0:T(8,128)(2,1)S(1)}, u32[]{:S(2)}, u32[]{:S(2)}) collective-permute-start(bf16[64,768]{1,0:T(8,128)(2,1)S(1)} %hidden.2.refs_0_), channel_id=1, source_target_pairs={{0,2},{2,0},{1,3},{3,1},{4,6},{6,4},{5,7},{7,5},{8,10},{10,8},{9,1... | collective-permute-start | bytes 294920 | tf_op jit(solution)/shard_map/ppermute | solution.py:97
  49.7 5.2 %collective-permute-start.20 = (bf16[64,768]{1,0:T(8,128)(2,1)S(1)}, bf16[64,768]{1,0:T(8,128)(2,1)S(1)}, u32[]{:S(2)}, u32[]{:S(2)}) collective-permute-start(bf16[64,768]{1,0:T(8,128)(2,1)S(1)} %hidden.3.refs_1_), channel_id=1, source_target_pairs={{0,2},{2,0},{1,3},{3,1},{4,6},{6,4},{5,7},{7,5},{8,10},{10,8},{9,1... | collective-permute-start | bytes 294920 | tf_op jit(solution)/shard_map/ppermute | solution.py:97
  51.7 4.0 %collective-permute-start.17 = (bf16[64,768]{1,0:T(8,128)(2,1)S(1)}, bf16[64,768]{1,0:T(8,128)(2,1)S(1)}, u32[]{:S(2)}, u32[]{:S(2)}) collective-permute-start(bf16[64,768]{1,0:T(8,128)(2,1)S(1)} %collective-permute-done.16.refs_0_), channel_id=1, source_target_pairs={{0,1},{1,0},{2,3},{3,2},{4,5},{5,4},{6,7},{7,6},{8,9},{9,8},{10,11... | collective-permute-start | bytes 294920 | tf_op jit(solution)/shard_map/ppermute | solution.py:97
  57.0 5.9 %collective-permute-start.24 = (bf16[32,512]{1,0:T(8,128)(2,1)S(1)}, bf16[32,512]{1,0:T(8,128)(2,1)S(1)}, u32[]{:S(2)}, u32[]{:S(2)}) collective-permute-start(bf16[32,512]{1,0:T(8,128)(2,1)S(1)} %get-tuple-element.56), channel_id=1, source_target_pairs={{0,12},{4,8},{8,4},{12,0},{1,13},{5,9},{9,5},{13,1},{2,14},{6,10},... | collective-permute-start | bytes 98312 | tf_op jit(solution)/shard_map/ppermute | solution.py:97
  59.0 4.9 %collective-permute-start.25 = (bf16[32,512]{1,0:T(8,128)(2,1)S(1)}, bf16[32,512]{1,0:T(8,128)(2,1)S(1)}, u32[]{:S(2)}, u32[]{:S(2)}) collective-permute-start(bf16[32,512]{1,0:T(8,128)(2,1)S(1)} %get-tuple-element.57), channel_id=1, source_target_pairs={{0,8},{4,12},{8,0},{12,4},{1,9},{5,13},{9,1},{13,5},{2,10},{6,14},... | collective-permute-start | bytes 98312 | tf_op jit(solution)/shard_map/ppermute | solution.py:97
  59.0 4.9 %collective-permute-start.26 = (bf16[32,512]{1,0:T(8,128)(2,1)S(1)}, bf16[32,512]{1,0:T(8,128)(2,1)S(1)}, u32[]{:S(2)}, u32[]{:S(2)}) collective-permute-start(bf16[32,512]{1,0:T(8,128)(2,1)S(1)} %get-tuple-element.58), channel_id=1, source_target_pairs={{0,4},{4,0},{8,12},{12,8},{1,5},{5,1},{9,13},{13,9},{2,6},{6,2},{1... | collective-permute-start | bytes 98312 | tf_op jit(solution)/shard_map/ppermute | solution.py:97
  (19 other events, 169.3 us)

commit v10 on v9

--- a/solution.py
+++ b/solution.py
@@ -549,30 +549,40 @@
     half = ctx_count // CELLS
     sources = [[rows[k] for k in range(half * i, half * (i + 1))] for i in range(CELLS)]
 
-    def first_half(k, cell, flips):
-        names = [(flip, k, cell) for flip in flips]
+    def first_half(names):
+        cell = names[0][2]
         return gate_up(names, layout, place, sources[cell], gate_up_weight)
 
     crossed = [[] for _ in range(CELLS)]
+    arrived, kept = [None] * CELLS, [None] * CELLS
     for k in far_first(exp_count):
-        away, mine = first_half(k, 0, (1, 0))
+        names = [(1, k, 0), (0, k, 0)] + ([(1, 0, 0)] if k == 1 else [])
+        away, mine, *staying = first_half(names)
         here = [swapped(away, "tp", 1)]
+        if staying:
+            arrived[0] = swapped(staying[0], "tp", 1)
         sources[1] = list(lax.optimization_barrier(tuple(sources[1]) + (mine,)))[:-1]
-        here.append(swapped(first_half(k, 1, (1,))[0], "tp", 1))
+        here.append(swapped(first_half([(1, k, 1)])[0], "tp", 1))
         for cell in range(CELLS):
             if cell:
-                mine = first_half(k, cell, (0,))[0]
+                mine = first_half([(0, k, cell)])[0]
             joined = join(mine, here[cell])
             place = after(place, joined)
             crossed[cell].append(swapped(joined, "exp", k))
+    away, kept[1] = first_half([(1, 0, 1), (0, 0, 1)])
+    arrived[1] = swapped(away, "tp", 1)
+    place = after(place, kept[1])
+    kept[0] = first_half([(0, 0, 0)])[0]
     own_hidden = []
     for cell in range(CELLS):
-        arrived = swapped(first_half(0, cell, (1,))[0], "tp", 1)
-        kept = first_half(0, cell, (0,))[0]
-        crossed[cell], kept = lax.optimization_barrier((crossed[cell], kept))
-        beside = [gate_up_weight] if cell == CELLS - 1 else []
-        hidden = hidden_of([kept, arrived] + crossed[cell], ff_width, model_width, beside)
-        place = after(place, hidden)
+        if cell:
+            arrived[cell] = after(arrived[cell], kept[cell], *own_hidden)
+        else:
+            crossed[cell], kept[cell] = lax.optimization_barrier((crossed[cell], kept[cell]))
+        beside = [] if cell else [gate_up_weight]
+        hidden = hidden_of(
+            [kept[cell], arrived[cell]] + crossed[cell], ff_width, model_width, beside
+        )
         own_hidden.append(hidden)
 
     near = [swapped(hidden, "tp", 1) for hidden in own_hidden]

time: 64.7 us -> 66.1 us (1.022)
  waiting for transfers between devices: 15.1 us -> 18.2 us
  local copies, waits for them, and re-layouts: 1.42 us -> 0.08 us
    ppermute x27, waiting for transfers between devices: 15.1 us -> 18.2 us  [swapped(): return lax.ppermute(value, axes, pairs)]
    unnamed x32, local copies, waits for them, and re-layouts: 1.42 us -> 0.07 us
    pallas_call x7 -> x5, Pallas kernels: 8.86 us -> 8.5 us  [gate_up(): pl.pallas_call(kernel, out_shape=[out] * len(names), compiler_params=para...]
  transfers between devices with their start and end apart: 27 -> 27, of which waited for: 14 -> 15; matrix products, arithmetic and copies ran while one was open for 0% -> 0% of each run, Pallas kernels for 29% -> 27%
where the time goes in v10:
time: 66.1 us; the launch traced here: 66 us
  starting transfers between devices  25.7 us (39%)
  Pallas kernels  21.7 us (33%)
  waiting for transfers between devices  18.2 us (28%)
    ppermute x27, starting transfers between devices, swapped(): return lax.ppermute(value, axes, pairs)  25.7 us
    ppermute x27, waiting for transfers between devices, swapped(): return lax.ppermute(value, axes, pairs)  18.2 us
    pallas_call x5, Pallas kernels, gate_up(): pl.pallas_call(kernel, out_shape=[out] * len(names), compiler_params=para...  8.5 us
    pallas_call x4, Pallas kernels, attend(): pl.pallas_call(functools.partial(attend_kernel, heads, scale, layout, k),...  5.04 us
    pallas_call x3, Pallas kernels, down(): pl.pallas_call(kernel, out_shape=[jax.ShapeDtypeStruct((rows, piece_width...  3.22 us
  transfers between devices with their start and end apart: 27, of which 15 were waited for; matrix products, arithmetic and copies ran while one was open for 0% of the time, Pallas kernels for 27%

profile of v10, /device:TPU:0, one launch (start us, length us, event | category | flops | bytes accessed | tf_op | source)
XLA Modules:
  0.0 66.0 jit_solution(2941853929718155082)
XLA Ops:
  1.0 3.1 %collective-permute-start = (bf16[32,1152]{1,0:T(8,128)(2,1)S(1)}, bf16[32,1152]{1,0:T(8,128)(2,1)S(1)}, u32[]{:S(2)}, u32[]{:S(2)}) collective-permute-start(bf16[32,1152]{1,0:T(8,128)(2,1)S(1)} %pack.1.queries_ref.refs_0_), channel_id=1, source_target_pairs={{0,4},{4,0},{8,12},{12,8},{1,5},{5,1},{9,13},{13,9},{2,6},{6,2},{1... | collective-permute-start | bytes 221192 | tf_op jit(solution)/shard_map/ppermute | solution.py:97
  4.2 2.6 %collective-permute-start.2 = (bf16[32,1152]{1,0:T(8,128)(2,1)S(1)}, bf16[32,1152]{1,0:T(8,128)(2,1)S(1)}, u32[]{:S(2)}, u32[]{:S(2)}) collective-permute-start(bf16[32,1152]{1,0:T(8,128)(2,1)S(1)} %pack.1.queries_ref.refs_0_), channel_id=1, source_target_pairs={{0,8},{4,12},{8,0},{12,4},{1,9},{5,13},{9,1},{13,5},{2,10},{6,14},... | collective-permute-start | bytes 221192 | tf_op jit(solution)/shard_map/ppermute | solution.py:97
  7.4 1.3 %attend.5 = bf16[32,1152]{1,0:T(8,128)(2,1)S(1)} custom-call(bf16[32,1152]{1,0:T(8,128)(2,1)S(1)} %collective-permute-done.queries_ref.refs_1_, bf16[2048,128]{1,0:T(8,128)(2,1)S(1)} %bitcast.13, bf16[2048,128]{1,0:T(8,128)(2,1)S(1)} %bitcast.17, bf16[64,2048]{1,0:T(8,128)(2,1)S(1)} %sight.1.sight_ref, bf16[16,512,1536]{2,1,0:T(8,128)(2,1)} %refs_0_.1), custom_call_target="tpu_custom_call" | custom-call | flops 536870912 | bytes 1048576 | tf_op jit(solution)/shard_map/attend/pallas_call | solution.py:219
  9.8 2.1 %collective-permute-done.2.queries_ref.refs_2_ = bf16[32,1152]{1,0:T(8,128)(2,1)S(1)} collective-permute-done((bf16[32,1152]{1,0:T(8,128)(2,1)S(1)}, bf16[32,1152]{1,0:T(8,128)(2,1)S(1)}, u32[]{:S(2)}, u32[]{:S(2)}) %collective-permute-start.2) | collective-permute-done | bytes 73760 | tf_op jit(solution)/shard_map/ppermute | solution.py:97
  11.9 1.3 %attend.6 = bf16[32,1152]{1,0:T(8,128)(2,1)S(1)} custom-call(bf16[32,1152]{1,0:T(8,128)(2,1)S(1)} %collective-permute-done.2.queries_ref.refs_2_, bf16[2048,128]{1,0:T(8,128)(2,1)S(1)} %bitcast.14, bf16[2048,128]{1,0:T(8,128)(2,1)S(1)} %bitcast.18, bf16[64,2048]{1,0:T(8,128)(2,1)S(1)} %sight.1.sight_ref, bf16[16,512,1536]{2,1,0:T(8,128)(2,1)} %refs_0_.1), custom_call_target="tpu_custom_call" | custom-call | flops 536870912 | bytes 1048576 | tf_op jit(solution)/shard_map/attend/pallas_call | solution.py:219
  13.2 1.3 %collective-permute-start.3 = (bf16[32,1152]{1,0:T(8,128)(2,1)S(1)}, bf16[32,1152]{1,0:T(8,128)(2,1)S(1)}, u32[]{:S(2)}, u32[]{:S(2)}) collective-permute-start(bf16[32,1152]{1,0:T(8,128)(2,1)S(1)} %attend.6), channel_id=1, source_target_pairs={{0,8},{4,12},{8,0},{12,4},{1,9},{5,13},{9,1},{13,5},{2,10},{6,14},... | collective-permute-start | bytes 221192 | tf_op jit(solution)/shard_map/ppermute | solution.py:97
  14.5 1.3 %attend.7 = bf16[32,1152]{1,0:T(8,128)(2,1)S(1)} custom-call(bf16[32,1152]{1,0:T(8,128)(2,1)S(1)} %collective-permute-done.4.queries_ref.refs_3_, bf16[2048,128]{1,0:T(8,128)(2,1)S(1)} %bitcast.15, bf16[2048,128]{1,0:T(8,128)(2,1)S(1)} %bitcast.19, bf16[64,2048]{1,0:T(8,128)(2,1)S(1)} %sight.1.sight_ref, bf16[16,512,1536]{2,1,0:T(8,128)(2,1)} %refs_0_.1), custom_call_target="tpu_custom_call" | custom-call | flops 536870912 | bytes 1048576 | tf_op jit(solution)/shard_map/attend/pallas_call | solution.py:219
  15.8 2.2 %collective-permute-start.5 = (bf16[32,1152]{1,0:T(8,128)(2,1)S(1)}, bf16[32,1152]{1,0:T(8,128)(2,1)S(1)}, u32[]{:S(2)}, u32[]{:S(2)}) collective-permute-start(bf16[32,1152]{1,0:T(8,128)(2,1)S(1)} %attend.7), channel_id=1, source_target_pairs={{0,12},{4,8},{8,4},{12,0},{1,13},{5,9},{9,5},{13,1},{2,14},{6,10},... | collective-permute-start | bytes 221192 | tf_op jit(solution)/shard_map/ppermute | solution.py:97
  18.0 1.3 %attend.4.refs_0_ = bf16[32,1152]{1,0:T(8,128)(2,1)S(1)} custom-call(bf16[32,1152]{1,0:T(8,128)(2,1)S(1)} %pack.1.queries_ref.refs_0_, bf16[2048,128]{1,0:T(8,128)(2,1)S(1)} %bitcast.16, bf16[2048,128]{1,0:T(8,128)(2,1)S(1)} %bitcast.20, bf16[64,2048]{1,0:T(8,128)(2,1)S(1)} %sight.1.sight_ref, bf16[16,512,1536]{2,1,0:T(8,128)(2,1)} %refs_0_.1), custom_call_target="tpu_custom_call" | custom-call | flops 536870912 | bytes 1048576 | tf_op jit(solution)/shard_map/attend/pallas_call | solution.py:219
  20.1 2.0 %collective-permute-done.5.refs_3_ = bf16[32,1152]{1,0:T(8,128)(2,1)S(1)} collective-permute-done((bf16[32,1152]{1,0:T(8,128)(2,1)S(1)}, bf16[32,1152]{1,0:T(8,128)(2,1)S(1)}, u32[]{:S(2)}, u32[]{:S(2)}) %collective-permute-start.5) | collective-permute-done | bytes 73760 | tf_op jit(solution)/shard_map/ppermute | solution.py:97
  23.2 1.5 %collective-permute-start.7 = (bf16[32,512]{1,0:T(8,128)(2,1)S(1)}, bf16[32,512]{1,0:T(8,128)(2,1)S(1)}, u32[]{:S(2)}, u32[]{:S(2)}) collective-permute-start(bf16[32,512]{1,0:T(8,128)(2,1)S(1)} %get-tuple-element.38), channel_id=1, source_target_pairs={{0,2},{1,3},{2,0},{3,1},{4,6},{5,7},{6,4},{7,5},{8,10},{9,11},{10,... | collective-permute-start | bytes 98312 | tf_op jit(solution)/shard_map/ppermute | solution.py:97
  25.0 1.8 %collective-permute-done.6.refs_1_ = bf16[32,512]{1,0:T(8,128)(2,1)S(1)} collective-permute-done((bf16[32,512]{1,0:T(8,128)(2,1)S(1)}, bf16[32,512]{1,0:T(8,128)(2,1)S(1)}, u32[]{:S(2)}, u32[]{:S(2)}) %collective-permute-start.6) | collective-permute-done | bytes 32800 | tf_op jit(solution)/shard_map/ppermute | solution.py:97
  27.3 1.4 %collective-permute-start.9 = (bf16[32,640]{1,0:T(8,128)(2,1)S(1)}, bf16[32,640]{1,0:T(8,128)(2,1)S(1)}, u32[]{:S(2)}, u32[]{:S(2)}) collective-permute-start(bf16[32,640]{1,0:T(8,128)(2,1)S(1)} %get-tuple-element.43.refs_0_), channel_id=1, source_target_pairs={{0,4},{4,0},{8,12},{12,8},{1,5},{5,1},{9,13},{13,9},{2,6},{6,2},{1... | collective-permute-start | bytes 122888 | tf_op jit(solution)/shard_map/ppermute | solution.py:97
  29.5 1.3 %collective-permute-start.12 = (bf16[32,640]{1,0:T(8,128)(2,1)S(1)}, bf16[32,640]{1,0:T(8,128)(2,1)S(1)}, u32[]{:S(2)}, u32[]{:S(2)}) collective-permute-start(bf16[32,640]{1,0:T(8,128)(2,1)S(1)} %get-tuple-element.43.refs_0_), channel_id=1, source_target_pairs={{0,8},{4,12},{8,0},{12,4},{1,9},{5,13},{9,1},{13,5},{2,10},{6,14},... | collective-permute-start | bytes 122888 | tf_op jit(solution)/shard_map/ppermute | solution.py:97
  31.4 3.0 %gate_up.5 = (bf16[64,1664]{1,0:T(8,128)(2,1)S(1)}, bf16[64,1664]{1,0:T(8,128)(2,1)S(1)}, bf16[64,1664]{1,0:T(8,128)(2,1)S(1)}) custom-call(bf16[8,64,64]{2,1,0:T(8,128)(2,1)S(1)} %get-tuple-element.51.place_ref, bf16[16,512,1536]{2,1,0:T(8,128)(2,1)S(1)} %bitcast.10, bf16[32,640]{1,0:T(8,128)(2,1)S(1)} %get-tuple-element.43.refs_0_, ...), custom_call_target="tpu_custom_call" | custom-call | flops 100663296 | bytes 196608 | tf_op jit(solution)/shard_map/gate_up/pallas_call | solution.py:374
  37.5 1.3 %collective-permute-start.11 = (bf16[64,1664]{1,0:T(8,128)(2,1)S(1)}, bf16[64,1664]{1,0:T(8,128)(2,1)S(1)}, u32[]{:S(2)}, u32[]{:S(2)}) collective-permute-start(bf16[64,1664]{1,0:T(8,128)(2,1)S(1)} %join.2), channel_id=1, source_target_pairs={{0,2},{2,0},{1,3},{3,1},{4,6},{6,4},{5,7},{7,5},{8,10},{10,8},{9,1... | collective-permute-start | bytes 638984 | tf_op jit(solution)/shard_map/ppermute | solution.py:97
  40.2 2.2 %gate_up.8 = (bf16[64,1664]{1,0:T(8,128)(2,1)S(1)}, bf16[64,1664]{1,0:T(8,128)(2,1)S(1)}) custom-call(bf16[8,64,64]{2,1,0:T(8,128)(2,1)S(1)} %get-tuple-element.51.place_ref, bf16[16,512,1536]{2,1,0:T(8,128)(2,1)S(1)} %bitcast.10, bf16[32,640]{1,0:T(8,128)(2,1)S(1)} %collective-permute-done.12.refs_0_, bf16[32,640]{1,0:T(8,128)(2,1)S(1)} %collective-permute-done.13.refs_1_), custom_call_target="tpu_custom_call" | custom-call | flops 100663296 | bytes 196608 | tf_op jit(solution)/shard_map/gate_up/pallas_call | solution.py:374
  45.1 1.3 %collective-permute-start.16 = (bf16[64,768]{1,0:T(8,128)(2,1)S(1)}, bf16[64,768]{1,0:T(8,128)(2,1)S(1)}, u32[]{:S(2)}, u32[]{:S(2)}) collective-permute-start(bf16[64,768]{1,0:T(8,128)(2,1)S(1)} %hidden.2.refs_0_), channel_id=1, source_target_pairs={{0,2},{2,0},{1,3},{3,1},{4,6},{6,4},{5,7},{7,5},{8,10},{10,8},{9,1... | collective-permute-start | bytes 294920 | tf_op jit(solution)/shard_map/ppermute | solution.py:97
  46.4 4.1 %collective-permute-done.19.refs_2_ = bf16[64,1664]{1,0:T(8,128)(2,1)S(1)} collective-permute-done((bf16[64,1664]{1,0:T(8,128)(2,1)S(1)}, bf16[64,1664]{1,0:T(8,128)(2,1)S(1)}, u32[]{:S(2)}, u32[]{:S(2)}) %collective-permute-start.19) | collective-permute-done | bytes 213024 | tf_op jit(solution)/shard_map/ppermute | solution.py:97
  52.2 1.6 %down.3.refs_2_ = f32[128,512]{1,0:T(8,128)S(1)} custom-call(bf16[16,768,512]{2,1,0:T(8,128)(2,1)S(1)} %bitcast.12, bf16[8,64,64]{2,1,0:T(8,128)(2,1)S(1)} %get-tuple-element.41.high_ref, bf16[8,64,64]{2,1,0:T(8,128)(2,1)S(1)} %get-tuple-element.42.low_ref, bf16[64,768]{1,0:T(8,128)(2,1)S(1)} %hidden.2.refs_0_, bf16[64,768]{1,0:T(8,128)(2,1)S(1)} %hidden.3.refs_1_, ...), custom_call_target="tpu_custom_call" | custom-call | flops 100663296 | bytes 1048576 | tf_op jit(solution)/shard_map/down/pallas_call | solution.py:456
  53.8 2.3 %collective-permute-done.20.refs_1_ = bf16[64,768]{1,0:T(8,128)(2,1)S(1)} collective-permute-done((bf16[64,768]{1,0:T(8,128)(2,1)S(1)}, bf16[64,768]{1,0:T(8,128)(2,1)S(1)}, u32[]{:S(2)}, u32[]{:S(2)}) %collective-permute-start.20) | collective-permute-done | bytes 98336 | tf_op jit(solution)/shard_map/ppermute | solution.py:97
  58.3 2.0 %collective-permute-start.24 = (bf16[32,512]{1,0:T(8,128)(2,1)S(1)}, bf16[32,512]{1,0:T(8,128)(2,1)S(1)}, u32[]{:S(2)}, u32[]{:S(2)}) collective-permute-start(bf16[32,512]{1,0:T(8,128)(2,1)S(1)} %get-tuple-element.60), channel_id=1, source_target_pairs={{0,12},{4,8},{8,4},{12,0},{1,13},{5,9},{9,5},{13,1},{2,14},{6,10},... | collective-permute-start | bytes 98312 | tf_op jit(solution)/shard_map/ppermute | solution.py:97
  60.7 2.1 %collective-permute-start.26 = (bf16[32,512]{1,0:T(8,128)(2,1)S(1)}, bf16[32,512]{1,0:T(8,128)(2,1)S(1)}, u32[]{:S(2)}, u32[]{:S(2)}) collective-permute-start(bf16[32,512]{1,0:T(8,128)(2,1)S(1)} %get-tuple-element.62), channel_id=1, source_target_pairs={{0,4},{4,0},{8,12},{12,8},{1,5},{5,1},{9,13},{13,9},{2,6},{6,2},{1... | collective-permute-start | bytes 98312 | tf_op jit(solution)/shard_map/ppermute | solution.py:97
  62.8 1.4 %collective-permute-done.24.refs_1_ = bf16[32,512]{1,0:T(8,128)(2,1)S(1)} collective-permute-done((bf16[32,512]{1,0:T(8,128)(2,1)S(1)}, bf16[32,512]{1,0:T(8,128)(2,1)S(1)}, u32[]{:S(2)}, u32[]{:S(2)}) %collective-permute-start.24) | collective-permute-done | bytes 32800 | tf_op jit(solution)/shard_map/ppermute | solution.py:97
  (87 shorter events, 20.1 us)
Async XLA Ops:
  1.0 6.3 %collective-permute-start = (bf16[32,1152]{1,0:T(8,128)(2,1)S(1)}, bf16[32,1152]{1,0:T(8,128)(2,1)S(1)}, u32[]{:S(2)}, u32[]{:S(2)}) collective-permute-start(bf16[32,1152]{1,0:T(8,128)(2,1)S(1)} %pack.1.queries_ref.refs_0_), channel_id=1, source_target_pairs={{0,4},{4,0},{8,12},{12,8},{1,5},{5,1},{9,13},{13,9},{2,6},{6,2},{1... | collective-permute-start | bytes 221192 | tf_op jit(solution)/shard_map/ppermute | solution.py:97
  4.2 7.8 %collective-permute-start.2 = (bf16[32,1152]{1,0:T(8,128)(2,1)S(1)}, bf16[32,1152]{1,0:T(8,128)(2,1)S(1)}, u32[]{:S(2)}, u32[]{:S(2)}) collective-permute-start(bf16[32,1152]{1,0:T(8,128)(2,1)S(1)} %pack.1.queries_ref.refs_0_), channel_id=1, source_target_pairs={{0,8},{4,12},{8,0},{12,4},{1,9},{5,13},{9,1},{13,5},{2,10},{6,14},... | collective-permute-start | bytes 221192 | tf_op jit(solution)/shard_map/ppermute | solution.py:97
  6.7 7.8 %collective-permute-start.4 = (bf16[32,1152]{1,0:T(8,128)(2,1)S(1)}, bf16[32,1152]{1,0:T(8,128)(2,1)S(1)}, u32[]{:S(2)}, u32[]{:S(2)}) collective-permute-start(bf16[32,1152]{1,0:T(8,128)(2,1)S(1)} %pack.1.queries_ref.refs_0_), channel_id=1, source_target_pairs={{0,12},{4,8},{8,4},{12,0},{1,13},{5,9},{9,5},{13,1},{2,14},{6,10},... | collective-permute-start | bytes 221192 | tf_op jit(solution)/shard_map/ppermute | solution.py:97
  8.7 11.3 %collective-permute-start.1 = (bf16[32,1152]{1,0:T(8,128)(2,1)S(1)}, bf16[32,1152]{1,0:T(8,128)(2,1)S(1)}, u32[]{:S(2)}, u32[]{:S(2)}) collective-permute-start(bf16[32,1152]{1,0:T(8,128)(2,1)S(1)} %attend.5), channel_id=1, source_target_pairs={{0,4},{4,0},{8,12},{12,8},{1,5},{5,1},{9,13},{13,9},{2,6},{6,2},{1... | collective-permute-start | bytes 221192 | tf_op jit(solution)/shard_map/ppermute | solution.py:97
  13.2 6.9 %collective-permute-start.3 = (bf16[32,1152]{1,0:T(8,128)(2,1)S(1)}, bf16[32,1152]{1,0:T(8,128)(2,1)S(1)}, u32[]{:S(2)}, u32[]{:S(2)}) collective-permute-start(bf16[32,1152]{1,0:T(8,128)(2,1)S(1)} %attend.6), channel_id=1, source_target_pairs={{0,8},{4,12},{8,0},{12,4},{1,9},{5,13},{9,1},{13,5},{2,10},{6,14},... | collective-permute-start | bytes 221192 | tf_op jit(solution)/shard_map/ppermute | solution.py:97
  15.8 6.3 %collective-permute-start.5 = (bf16[32,1152]{1,0:T(8,128)(2,1)S(1)}, bf16[32,1152]{1,0:T(8,128)(2,1)S(1)}, u32[]{:S(2)}, u32[]{:S(2)}) collective-permute-start(bf16[32,1152]{1,0:T(8,128)(2,1)S(1)} %attend.7), channel_id=1, source_target_pairs={{0,12},{4,8},{8,4},{12,0},{1,13},{5,9},{9,5},{13,1},{2,14},{6,10},... | collective-permute-start | bytes 221192 | tf_op jit(solution)/shard_map/ppermute | solution.py:97
  23.1 3.7 %collective-permute-start.6 = (bf16[32,512]{1,0:T(8,128)(2,1)S(1)}, bf16[32,512]{1,0:T(8,128)(2,1)S(1)}, u32[]{:S(2)}, u32[]{:S(2)}) collective-permute-start(bf16[32,512]{1,0:T(8,128)(2,1)S(1)} %get-tuple-element.37), channel_id=1, source_target_pairs={{0,3},{1,2},{2,1},{3,0},{4,7},{5,6},{6,5},{7,4},{8,11},{9,10},{10,... | collective-permute-start | bytes 98312 | tf_op jit(solution)/shard_map/ppermute | solution.py:97
  23.2 4.0 %collective-permute-start.7 = (bf16[32,512]{1,0:T(8,128)(2,1)S(1)}, bf16[32,512]{1,0:T(8,128)(2,1)S(1)}, u32[]{:S(2)}, u32[]{:S(2)}) collective-permute-start(bf16[32,512]{1,0:T(8,128)(2,1)S(1)} %get-tuple-element.38), channel_id=1, source_target_pairs={{0,2},{1,3},{2,0},{3,1},{4,6},{5,7},{6,4},{7,5},{8,10},{9,11},{10,... | collective-permute-start | bytes 98312 | tf_op jit(solution)/shard_map/ppermute | solution.py:97
  24.7 2.5 %collective-permute-start.8 = (bf16[32,512]{1,0:T(8,128)(2,1)S(1)}, bf16[32,512]{1,0:T(8,128)(2,1)S(1)}, u32[]{:S(2)}, u32[]{:S(2)}) collective-permute-start(bf16[32,512]{1,0:T(8,128)(2,1)S(1)} %get-tuple-element.39), channel_id=1, source_target_pairs={{0,1},{1,0},{2,3},{3,2},{4,5},{5,4},{6,7},{7,6},{8,9},{9,8},{10,11... | collective-permute-start | bytes 98312 | tf_op jit(solution)/shard_map/ppermute | solution.py:97
  27.3 4.1 %collective-permute-start.9 = (bf16[32,640]{1,0:T(8,128)(2,1)S(1)}, bf16[32,640]{1,0:T(8,128)(2,1)S(1)}, u32[]{:S(2)}, u32[]{:S(2)}) collective-permute-start(bf16[32,640]{1,0:T(8,128)(2,1)S(1)} %get-tuple-element.43.refs_0_), channel_id=1, source_target_pairs={{0,4},{4,0},{8,12},{12,8},{1,5},{5,1},{9,13},{13,9},{2,6},{6,2},{1... | collective-permute-start | bytes 122888 | tf_op jit(solution)/shard_map/ppermute | solution.py:97
  28.7 5.8 %collective-permute-start.13 = (bf16[32,640]{1,0:T(8,128)(2,1)S(1)}, bf16[32,640]{1,0:T(8,128)(2,1)S(1)}, u32[]{:S(2)}, u32[]{:S(2)}) collective-permute-start(bf16[32,640]{1,0:T(8,128)(2,1)S(1)} %get-tuple-element.43.refs_0_), channel_id=1, source_target_pairs={{0,12},{4,8},{8,4},{12,0},{1,13},{5,9},{9,5},{13,1},{2,14},{6,10},... | collective-permute-start | bytes 122888 | tf_op jit(solution)/shard_map/ppermute | solution.py:97
  29.5 6.2 %collective-permute-start.12 = (bf16[32,640]{1,0:T(8,128)(2,1)S(1)}, bf16[32,640]{1,0:T(8,128)(2,1)S(1)}, u32[]{:S(2)}, u32[]{:S(2)}) collective-permute-start(bf16[32,640]{1,0:T(8,128)(2,1)S(1)} %get-tuple-element.43.refs_0_), channel_id=1, source_target_pairs={{0,8},{4,12},{8,0},{12,4},{1,9},{5,13},{9,1},{13,5},{2,10},{6,14},... | collective-permute-start | bytes 122888 | tf_op jit(solution)/shard_map/ppermute | solution.py:97
  34.4 2.9 %collective-permute-start.10 = (bf16[64,1664]{1,0:T(8,128)(2,1)S(1)}, bf16[64,1664]{1,0:T(8,128)(2,1)S(1)}, u32[]{:S(2)}, u32[]{:S(2)}) collective-permute-start(bf16[64,1664]{1,0:T(8,128)(2,1)S(1)} %get-tuple-element.45), channel_id=1, source_target_pairs={{0,1},{1,0},{2,3},{3,2},{4,5},{5,4},{6,7},{7,6},{8,9},{9,8},{10,11... | collective-permute-start | bytes 638984 | tf_op jit(solution)/shard_map/ppermute | solution.py:97
  36.8 3.2 %collective-permute-start.14 = (bf16[64,1664]{1,0:T(8,128)(2,1)S(1)}, bf16[64,1664]{1,0:T(8,128)(2,1)S(1)}, u32[]{:S(2)}, u32[]{:S(2)}) collective-permute-start(bf16[64,1664]{1,0:T(8,128)(2,1)S(1)} %gate_up.7), channel_id=1, source_target_pairs={{0,1},{1,0},{2,3},{3,2},{4,5},{5,4},{6,7},{7,6},{8,9},{9,8},{10,11... | collective-permute-start | bytes 638984 | tf_op jit(solution)/shard_map/ppermute | solution.py:97
  36.8 8.0 %collective-permute-start.15 = (bf16[64,1664]{1,0:T(8,128)(2,1)S(1)}, bf16[64,1664]{1,0:T(8,128)(2,1)S(1)}, u32[]{:S(2)}, u32[]{:S(2)}) collective-permute-start(bf16[64,1664]{1,0:T(8,128)(2,1)S(1)} %get-tuple-element.53), channel_id=1, source_target_pairs={{0,1},{1,0},{2,3},{3,2},{4,5},{5,4},{6,7},{7,6},{8,9},{9,8},{10,11... | collective-permute-start | bytes 638984 | tf_op jit(solution)/shard_map/ppermute | solution.py:97
  37.5 7.3 %collective-permute-start.11 = (bf16[64,1664]{1,0:T(8,128)(2,1)S(1)}, bf16[64,1664]{1,0:T(8,128)(2,1)S(1)}, u32[]{:S(2)}, u32[]{:S(2)}) collective-permute-start(bf16[64,1664]{1,0:T(8,128)(2,1)S(1)} %join.2), channel_id=1, source_target_pairs={{0,2},{2,0},{1,3},{3,1},{4,6},{6,4},{5,7},{7,5},{8,10},{10,8},{9,1... | collective-permute-start | bytes 638984 | tf_op jit(solution)/shard_map/ppermute | solution.py:97
  42.4 4.0 %collective-permute-start.18 = (bf16[64,1664]{1,0:T(8,128)(2,1)S(1)}, bf16[64,1664]{1,0:T(8,128)(2,1)S(1)}, u32[]{:S(2)}, u32[]{:S(2)}) collective-permute-start(bf16[64,1664]{1,0:T(8,128)(2,1)S(1)} %get-tuple-element.55), channel_id=1, source_target_pairs={{0,1},{1,0},{2,3},{3,2},{4,5},{5,4},{6,7},{7,6},{8,9},{9,8},{10,11... | collective-permute-start | bytes 638984 | tf_op jit(solution)/shard_map/ppermute | solution.py:97
  42.4 8.1 %collective-permute-start.19 = (bf16[64,1664]{1,0:T(8,128)(2,1)S(1)}, bf16[64,1664]{1,0:T(8,128)(2,1)S(1)}, u32[]{:S(2)}, u32[]{:S(2)}) collective-permute-start(bf16[64,1664]{1,0:T(8,128)(2,1)S(1)} %join.3), channel_id=1, source_target_pairs={{0,2},{2,0},{1,3},{3,1},{4,6},{6,4},{5,7},{7,5},{8,10},{10,8},{9,1... | collective-permute-start | bytes 638984 | tf_op jit(solution)/shard_map/ppermute | solution.py:97
  45.0 7.1 %collective-permute-start.21 = (bf16[64,768]{1,0:T(8,128)(2,1)S(1)}, bf16[64,768]{1,0:T(8,128)(2,1)S(1)}, u32[]{:S(2)}, u32[]{:S(2)}) collective-permute-start(bf16[64,768]{1,0:T(8,128)(2,1)S(1)} %hidden.2.refs_0_), channel_id=1, source_target_pairs={{0,1},{1,0},{2,3},{3,2},{4,5},{5,4},{6,7},{7,6},{8,9},{9,8},{10,11... | collective-permute-start | bytes 294920 | tf_op jit(solution)/shard_map/ppermute | solution.py:97
  45.1 7.0 %collective-permute-start.16 = (bf16[64,768]{1,0:T(8,128)(2,1)S(1)}, bf16[64,768]{1,0:T(8,128)(2,1)S(1)}, u32[]{:S(2)}, u32[]{:S(2)}) collective-permute-start(bf16[64,768]{1,0:T(8,128)(2,1)S(1)} %hidden.2.refs_0_), channel_id=1, source_target_pairs={{0,2},{2,0},{1,3},{3,1},{4,6},{6,4},{5,7},{7,5},{8,10},{10,8},{9,1... | collective-permute-start | bytes 294920 | tf_op jit(solution)/shard_map/ppermute | solution.py:97
  50.8 5.2 %collective-permute-start.20 = (bf16[64,768]{1,0:T(8,128)(2,1)S(1)}, bf16[64,768]{1,0:T(8,128)(2,1)S(1)}, u32[]{:S(2)}, u32[]{:S(2)}) collective-permute-start(bf16[64,768]{1,0:T(8,128)(2,1)S(1)} %hidden.3.refs_1_), channel_id=1, source_target_pairs={{0,2},{2,0},{1,3},{3,1},{4,6},{6,4},{5,7},{7,5},{8,10},{10,8},{9,1... | collective-permute-start | bytes 294920 | tf_op jit(solution)/shard_map/ppermute | solution.py:97
  58.3 5.9 %collective-permute-start.24 = (bf16[32,512]{1,0:T(8,128)(2,1)S(1)}, bf16[32,512]{1,0:T(8,128)(2,1)S(1)}, u32[]{:S(2)}, u32[]{:S(2)}) collective-permute-start(bf16[32,512]{1,0:T(8,128)(2,1)S(1)} %get-tuple-element.60), channel_id=1, source_target_pairs={{0,12},{4,8},{8,4},{12,0},{1,13},{5,9},{9,5},{13,1},{2,14},{6,10},... | collective-permute-start | bytes 98312 | tf_op jit(solution)/shard_map/ppermute | solution.py:97
  60.3 5.0 %collective-permute-start.25 = (bf16[32,512]{1,0:T(8,128)(2,1)S(1)}, bf16[32,512]{1,0:T(8,128)(2,1)S(1)}, u32[]{:S(2)}, u32[]{:S(2)}) collective-permute-start(bf16[32,512]{1,0:T(8,128)(2,1)S(1)} %get-tuple-element.61), channel_id=1, source_target_pairs={{0,8},{4,12},{8,0},{12,4},{1,9},{5,13},{9,1},{13,5},{2,10},{6,14},... | collective-permute-start | bytes 98312 | tf_op jit(solution)/shard_map/ppermute | solution.py:97
  60.7 4.6 %collective-permute-start.26 = (bf16[32,512]{1,0:T(8,128)(2,1)S(1)}, bf16[32,512]{1,0:T(8,128)(2,1)S(1)}, u32[]{:S(2)}, u32[]{:S(2)}) collective-permute-start(bf16[32,512]{1,0:T(8,128)(2,1)S(1)} %get-tuple-element.62), channel_id=1, source_target_pairs={{0,4},{4,0},{8,12},{12,8},{1,5},{5,1},{9,13},{13,9},{2,6},{6,2},{1... | collective-permute-start | bytes 98312 | tf_op jit(solution)/shard_map/ppermute | solution.py:97
  (19 other events, 182.5 us)

commit v11 on v9

--- a/solution.py
+++ b/solution.py
@@ -350,18 +350,20 @@
     return jnp.where(lane == 0, high, jnp.where(lane == 1, low, 0.0))
 
 
-def gate_up(names, layout, place, rows, weight):
+def gate_up(names, layout, place, sources, weight):
     _, width, ff_pair = weight.shape
     each = layout.rows // layout.experts
-    row_count = len(rows)
+    cells = sorted({name[2] for name in names})
+    count = len(sources[0])
 
     def kernel(place_ref, weight_ref, *refs):
-        for name, out_ref in zip(names, refs[row_count:]):
+        for name, out_ref in zip(names, refs[len(cells) * count :]):
             at, first = layout.cell(*name)
+            turn = cells.index(name[2])
             picked = 0.0
-            for i, ref in enumerate(refs[:row_count]):
-                count = ref.shape[0]
-                here = place_ref[at, i * count : (i + 1) * count, :]
+            for i, ref in enumerate(refs[turn * count : (turn + 1) * count]):
+                tokens = ref.shape[0]
+                here = place_ref[at, i * tokens : (i + 1) * tokens, :]
                 picked = picked + dot(here, ref[...], ((0,), (0,)))
             picked = picked.astype(bf16)
             for i in range(layout.experts):
@@ -377,7 +379,7 @@
         compiler_params=params(8),
         cost_estimate=cost(2 * layout.rows * width * ff_pair, 2 * layout.rows * ff_pair),
         name="gate_up",
-    )(place, weight, *rows)
+    )(place, weight, *[value for cell in cells for value in sources[cell]])
 
 
 def join_kernel(left_ref, right_ref, out_ref):
@@ -549,29 +551,30 @@
     half = ctx_count // CELLS
     sources = [[rows[k] for k in range(half * i, half * (i + 1))] for i in range(CELLS)]
 
-    def first_half(k, cell, flips):
-        names = [(flip, k, cell) for flip in flips]
-        return gate_up(names, layout, place, sources[cell], gate_up_weight)
+    def first_half(*names):
+        return gate_up(names, layout, place, sources, gate_up_weight)
 
     crossed = [[] for _ in range(CELLS)]
     for k in far_first(exp_count):
-        away, mine = first_half(k, 0, (1, 0))
+        away, mine = first_half((1, k, 0), (0, k, 0))
         here = [swapped(away, "tp", 1)]
         sources[1] = list(lax.optimization_barrier(tuple(sources[1]) + (mine,)))[:-1]
-        here.append(swapped(first_half(k, 1, (1,))[0], "tp", 1))
+        here.append(swapped(first_half((1, k, 1))[0], "tp", 1))
         for cell in range(CELLS):
             if cell:
-                mine = first_half(k, cell, (0,))[0]
+                mine = first_half((0, k, cell))[0]
             joined = join(mine, here[cell])
             place = after(place, joined)
             crossed[cell].append(swapped(joined, "exp", k))
+    arrived = [swapped(first_half((1, 0, 0))[0], "tp", 1)]
+    kept = list(first_half((0, 0, 0), (0, 0, 1)))
     own_hidden = []
     for cell in range(CELLS):
-        arrived = swapped(first_half(0, cell, (1,))[0], "tp", 1)
-        kept = first_half(0, cell, (0,))[0]
-        crossed[cell], kept = lax.optimization_barrier((crossed[cell], kept))
-        beside = [gate_up_weight] if cell == CELLS - 1 else []
-        hidden = hidden_of([kept, arrived] + crossed[cell], ff_width, model_width, beside)
+        if cell:
+            arrived.append(swapped(first_half((1, 0, cell))[0], "tp", 1))
+        crossed[cell], kept[cell] = lax.optimization_barrier((crossed[cell], kept[cell]))
+        beside = [out_matrix] * 3
+        hidden = hidden_of([kept[cell], arrived[cell]] + crossed[cell], ff_width, model_width, beside)
         place = after(place, hidden)
         own_hidden.append(hidden)
 

time: 64.7 us -> 64.7 us (level)
  waiting for transfers between devices: 15.1 us -> 16.5 us
  local copies, waits for them, and re-layouts: 1.42 us -> 0.08 us
    ppermute x27, waiting for transfers between devices: 15.1 us -> 16.5 us  [swapped(): return lax.ppermute(value, axes, pairs)]
    unnamed x32, local copies, waits for them, and re-layouts: 1.42 us -> 0.08 us
    pallas_call x7 -> x6, Pallas kernels: 8.86 us -> 8.72 us  [gate_up(): pl.pallas_call(kernel, out_shape=[out] * len(names), compiler_params=para...]
  transfers between devices with their start and end apart: 27 -> 27, of which waited for: 14 -> 16; matrix products, arithmetic and copies ran while one was open for 0% -> 0% of each run, Pallas kernels for 29% -> 28%
where the time goes in v11:
time: 64.7 us; the launch traced here: 64.6 us
  starting transfers between devices  25.7 us (40%)
  Pallas kernels  22 us (34%)
  waiting for transfers between devices  16.5 us (26%)
    ppermute x27, starting transfers between devices, swapped(): return lax.ppermute(value, axes, pairs)  25.7 us
    ppermute x27, waiting for transfers between devices, swapped(): return lax.ppermute(value, axes, pairs)  16.5 us
    pallas_call x6, Pallas kernels, gate_up(): pl.pallas_call(kernel, out_shape=[out] * len(names), compiler_params=para...  8.72 us
    pallas_call x4, Pallas kernels, attend(): pl.pallas_call(functools.partial(attend_kernel, heads, scale, layout, k),...  5.04 us
    pallas_call x3, Pallas kernels, down(): pl.pallas_call(kernel, out_shape=[jax.ShapeDtypeStruct((rows, piece_width...  3.23 us
  transfers between devices with their start and end apart: 27, of which 16 were waited for; matrix products, arithmetic and copies ran while one was open for 0% of the time, Pallas kernels for 28%

profile of v11, /device:TPU:0, one launch (start us, length us, event | category | flops | bytes accessed | tf_op | source)
XLA Modules:
  0.0 64.6 jit_solution(1575617562616728045)
XLA Ops:
  1.0 3.1 %collective-permute-start = (bf16[32,1152]{1,0:T(8,128)(2,1)S(1)}, bf16[32,1152]{1,0:T(8,128)(2,1)S(1)}, u32[]{:S(2)}, u32[]{:S(2)}) collective-permute-start(bf16[32,1152]{1,0:T(8,128)(2,1)S(1)} %pack.1.queries_ref.refs_0_), channel_id=1, source_target_pairs={{0,4},{4,0},{8,12},{12,8},{1,5},{5,1},{9,13},{13,9},{2,6},{6,2},{1... | collective-permute-start | bytes 221192 | tf_op jit(solution)/shard_map/ppermute | solution.py:97
  4.2 2.6 %collective-permute-start.2 = (bf16[32,1152]{1,0:T(8,128)(2,1)S(1)}, bf16[32,1152]{1,0:T(8,128)(2,1)S(1)}, u32[]{:S(2)}, u32[]{:S(2)}) collective-permute-start(bf16[32,1152]{1,0:T(8,128)(2,1)S(1)} %pack.1.queries_ref.refs_0_), channel_id=1, source_target_pairs={{0,8},{4,12},{8,0},{12,4},{1,9},{5,13},{9,1},{13,5},{2,10},{6,14},... | collective-permute-start | bytes 221192 | tf_op jit(solution)/shard_map/ppermute | solution.py:97
  7.4 1.3 %attend.5 = bf16[32,1152]{1,0:T(8,128)(2,1)S(1)} custom-call(bf16[32,1152]{1,0:T(8,128)(2,1)S(1)} %collective-permute-done.queries_ref.refs_1_, bf16[2048,128]{1,0:T(8,128)(2,1)S(1)} %bitcast.20, bf16[2048,128]{1,0:T(8,128)(2,1)S(1)} %bitcast.24, bf16[64,2048]{1,0:T(8,128)(2,1)S(1)} %sight.1.sight_ref, bf16[16,512,1536]{2,1,0:T(8,128)(2,1)} %weight_ref.14), custom_call_target="tpu_custom_call" | custom-call | flops 536870912 | bytes 1048576 | tf_op jit(solution)/shard_map/attend/pallas_call | solution.py:219
  9.8 2.1 %collective-permute-done.2.queries_ref.refs_2_ = bf16[32,1152]{1,0:T(8,128)(2,1)S(1)} collective-permute-done((bf16[32,1152]{1,0:T(8,128)(2,1)S(1)}, bf16[32,1152]{1,0:T(8,128)(2,1)S(1)}, u32[]{:S(2)}, u32[]{:S(2)}) %collective-permute-start.2) | collective-permute-done | bytes 73760 | tf_op jit(solution)/shard_map/ppermute | solution.py:97
  11.9 1.3 %attend.6 = bf16[32,1152]{1,0:T(8,128)(2,1)S(1)} custom-call(bf16[32,1152]{1,0:T(8,128)(2,1)S(1)} %collective-permute-done.2.queries_ref.refs_2_, bf16[2048,128]{1,0:T(8,128)(2,1)S(1)} %bitcast.21, bf16[2048,128]{1,0:T(8,128)(2,1)S(1)} %bitcast.25, bf16[64,2048]{1,0:T(8,128)(2,1)S(1)} %sight.1.sight_ref, bf16[16,512,1536]{2,1,0:T(8,128)(2,1)} %weight_ref.14), custom_call_target="tpu_custom_call" | custom-call | flops 536870912 | bytes 1048576 | tf_op jit(solution)/shard_map/attend/pallas_call | solution.py:219
  13.2 1.3 %collective-permute-start.3 = (bf16[32,1152]{1,0:T(8,128)(2,1)S(1)}, bf16[32,1152]{1,0:T(8,128)(2,1)S(1)}, u32[]{:S(2)}, u32[]{:S(2)}) collective-permute-start(bf16[32,1152]{1,0:T(8,128)(2,1)S(1)} %attend.6), channel_id=1, source_target_pairs={{0,8},{4,12},{8,0},{12,4},{1,9},{5,13},{9,1},{13,5},{2,10},{6,14},... | collective-permute-start | bytes 221192 | tf_op jit(solution)/shard_map/ppermute | solution.py:97
  14.5 1.3 %attend.7 = bf16[32,1152]{1,0:T(8,128)(2,1)S(1)} custom-call(bf16[32,1152]{1,0:T(8,128)(2,1)S(1)} %collective-permute-done.4.queries_ref.refs_3_, bf16[2048,128]{1,0:T(8,128)(2,1)S(1)} %bitcast.22, bf16[2048,128]{1,0:T(8,128)(2,1)S(1)} %bitcast.26, bf16[64,2048]{1,0:T(8,128)(2,1)S(1)} %sight.1.sight_ref, bf16[16,512,1536]{2,1,0:T(8,128)(2,1)} %weight_ref.14), custom_call_target="tpu_custom_call" | custom-call | flops 536870912 | bytes 1048576 | tf_op jit(solution)/shard_map/attend/pallas_call | solution.py:219
  15.8 2.2 %collective-permute-start.5 = (bf16[32,1152]{1,0:T(8,128)(2,1)S(1)}, bf16[32,1152]{1,0:T(8,128)(2,1)S(1)}, u32[]{:S(2)}, u32[]{:S(2)}) collective-permute-start(bf16[32,1152]{1,0:T(8,128)(2,1)S(1)} %attend.7), channel_id=1, source_target_pairs={{0,12},{4,8},{8,4},{12,0},{1,13},{5,9},{9,5},{13,1},{2,14},{6,10},... | collective-permute-start | bytes 221192 | tf_op jit(solution)/shard_map/ppermute | solution.py:97
  18.0 1.3 %attend.4.refs_0_ = bf16[32,1152]{1,0:T(8,128)(2,1)S(1)} custom-call(bf16[32,1152]{1,0:T(8,128)(2,1)S(1)} %pack.1.queries_ref.refs_0_, bf16[2048,128]{1,0:T(8,128)(2,1)S(1)} %bitcast.23, bf16[2048,128]{1,0:T(8,128)(2,1)S(1)} %bitcast.27, bf16[64,2048]{1,0:T(8,128)(2,1)S(1)} %sight.1.sight_ref, bf16[16,512,1536]{2,1,0:T(8,128)(2,1)} %weight_ref.14), custom_call_target="tpu_custom_call" | custom-call | flops 536870912 | bytes 1048576 | tf_op jit(solution)/shard_map/attend/pallas_call | solution.py:219
  20.1 2.0 %collective-permute-done.5.refs_3_ = bf16[32,1152]{1,0:T(8,128)(2,1)S(1)} collective-permute-done((bf16[32,1152]{1,0:T(8,128)(2,1)S(1)}, bf16[32,1152]{1,0:T(8,128)(2,1)S(1)}, u32[]{:S(2)}, u32[]{:S(2)}) %collective-permute-start.5) | collective-permute-done | bytes 73760 | tf_op jit(solution)/shard_map/ppermute | solution.py:97
  23.2 1.5 %collective-permute-start.7 = (bf16[32,512]{1,0:T(8,128)(2,1)S(1)}, bf16[32,512]{1,0:T(8,128)(2,1)S(1)}, u32[]{:S(2)}, u32[]{:S(2)}) collective-permute-start(bf16[32,512]{1,0:T(8,128)(2,1)S(1)} %get-tuple-element.38), channel_id=1, source_target_pairs={{0,2},{1,3},{2,0},{3,1},{4,6},{5,7},{6,4},{7,5},{8,10},{9,11},{10,... | collective-permute-start | bytes 98312 | tf_op jit(solution)/shard_map/ppermute | solution.py:97
  25.0 1.8 %collective-permute-done.6.refs_1_ = bf16[32,512]{1,0:T(8,128)(2,1)S(1)} collective-permute-done((bf16[32,512]{1,0:T(8,128)(2,1)S(1)}, bf16[32,512]{1,0:T(8,128)(2,1)S(1)}, u32[]{:S(2)}, u32[]{:S(2)}) %collective-permute-start.6) | collective-permute-done | bytes 32800 | tf_op jit(solution)/shard_map/ppermute | solution.py:97
  27.3 1.4 %collective-permute-start.9 = (bf16[32,640]{1,0:T(8,128)(2,1)S(1)}, bf16[32,640]{1,0:T(8,128)(2,1)S(1)}, u32[]{:S(2)}, u32[]{:S(2)}) collective-permute-start(bf16[32,640]{1,0:T(8,128)(2,1)S(1)} %get-tuple-element.43.refs_0_), channel_id=1, source_target_pairs={{0,4},{4,0},{8,12},{12,8},{1,5},{5,1},{9,13},{13,9},{2,6},{6,2},{1... | collective-permute-start | bytes 122888 | tf_op jit(solution)/shard_map/ppermute | solution.py:97
  29.5 1.3 %collective-permute-start.12 = (bf16[32,640]{1,0:T(8,128)(2,1)S(1)}, bf16[32,640]{1,0:T(8,128)(2,1)S(1)}, u32[]{:S(2)}, u32[]{:S(2)}) collective-permute-start(bf16[32,640]{1,0:T(8,128)(2,1)S(1)} %get-tuple-element.43.refs_0_), channel_id=1, source_target_pairs={{0,8},{4,12},{8,0},{12,4},{1,9},{5,13},{9,1},{13,5},{2,10},{6,14},... | collective-permute-start | bytes 122888 | tf_op jit(solution)/shard_map/ppermute | solution.py:97
  31.4 2.1 %gate_up.6 = (bf16[64,1664]{1,0:T(8,128)(2,1)S(1)}, bf16[64,1664]{1,0:T(8,128)(2,1)S(1)}) custom-call(bf16[8,64,64]{2,1,0:T(8,128)(2,1)S(1)} %get-tuple-element.55.place_ref, bf16[16,512,1536]{2,1,0:T(8,128)(2,1)S(1)} %bitcast.10, bf16[32,640]{1,0:T(8,128)(2,1)S(1)} %get-tuple-element.43.refs_0_, bf16[32,640]{1,0:T(8,128)(2,1)S(1)} %collective-permute-done.9.refs_1_), custom_call_target="tpu_custom_call" | custom-call | flops 100663296 | bytes 196608 | tf_op jit(solution)/shard_map/gate_up/pallas_call | solution.py:376
  37.0 1.3 %collective-permute-start.11 = (bf16[64,1664]{1,0:T(8,128)(2,1)S(1)}, bf16[64,1664]{1,0:T(8,128)(2,1)S(1)}, u32[]{:S(2)}, u32[]{:S(2)}) collective-permute-start(bf16[64,1664]{1,0:T(8,128)(2,1)S(1)} %join.2), channel_id=1, source_target_pairs={{0,2},{2,0},{1,3},{3,1},{4,6},{6,4},{5,7},{7,5},{8,10},{10,8},{9,1... | collective-permute-start | bytes 638984 | tf_op jit(solution)/shard_map/ppermute | solution.py:97
  41.8 2.2 %gate_up.9 = (bf16[64,1664]{1,0:T(8,128)(2,1)S(1)}, bf16[64,1664]{1,0:T(8,128)(2,1)S(1)}) custom-call(bf16[8,64,64]{2,1,0:T(8,128)(2,1)S(1)} %get-tuple-element.55.place_ref, bf16[16,512,1536]{2,1,0:T(8,128)(2,1)S(1)} %bitcast.10, bf16[32,640]{1,0:T(8,128)(2,1)S(1)} %get-tuple-element.43.refs_0_, bf16[32,640]{1,0:T(8,128)(2,1)S(1)} %collective-permute-done.9.refs_1_, ...), custom_call_target="tpu_custom_call" | custom-call | flops 100663296 | bytes 196608 | tf_op jit(solution)/shard_map/gate_up/pallas_call | solution.py:376
  47.0 1.2 %collective-permute-start.16 = (bf16[64,768]{1,0:T(8,128)(2,1)S(1)}, bf16[64,768]{1,0:T(8,128)(2,1)S(1)}, u32[]{:S(2)}, u32[]{:S(2)}) collective-permute-start(bf16[64,768]{1,0:T(8,128)(2,1)S(1)} %hidden.2.refs_0_), channel_id=1, source_target_pairs={{0,2},{2,0},{1,3},{3,1},{4,6},{6,4},{5,7},{7,5},{8,10},{10,8},{9,1... | collective-permute-start | bytes 294920 | tf_op jit(solution)/shard_map/ppermute | solution.py:97
  49.6 1.3 %collective-permute-start.20 = (bf16[64,768]{1,0:T(8,128)(2,1)S(1)}, bf16[64,768]{1,0:T(8,128)(2,1)S(1)}, u32[]{:S(2)}, u32[]{:S(2)}) collective-permute-start(bf16[64,768]{1,0:T(8,128)(2,1)S(1)} %hidden.3.refs_1_), channel_id=1, source_target_pairs={{0,2},{2,0},{1,3},{3,1},{4,6},{6,4},{5,7},{7,5},{8,10},{10,8},{9,1... | collective-permute-start | bytes 294920 | tf_op jit(solution)/shard_map/ppermute | solution.py:97
  51.8 1.6 %down.3.refs_2_ = f32[128,512]{1,0:T(8,128)S(1)} custom-call(bf16[16,768,512]{2,1,0:T(8,128)(2,1)S(1)} %bitcast.19, bf16[8,64,64]{2,1,0:T(8,128)(2,1)S(1)} %get-tuple-element.41.high_ref, bf16[8,64,64]{2,1,0:T(8,128)(2,1)S(1)} %get-tuple-element.42.low_ref, bf16[64,768]{1,0:T(8,128)(2,1)S(1)} %hidden.2.refs_0_, bf16[64,768]{1,0:T(8,128)(2,1)S(1)} %hidden.3.refs_1_, ...), custom_call_target="tpu_custom_call" | custom-call | flops 100663296 | bytes 1048576 | tf_op jit(solution)/shard_map/down/pallas_call | solution.py:458
  53.4 1.5 %collective-permute-done.20.refs_1_ = bf16[64,768]{1,0:T(8,128)(2,1)S(1)} collective-permute-done((bf16[64,768]{1,0:T(8,128)(2,1)S(1)}, bf16[64,768]{1,0:T(8,128)(2,1)S(1)}, u32[]{:S(2)}, u32[]{:S(2)}) %collective-permute-start.20) | collective-permute-done | bytes 98336 | tf_op jit(solution)/shard_map/ppermute | solution.py:97
  57.0 1.8 %collective-permute-start.24 = (bf16[32,512]{1,0:T(8,128)(2,1)S(1)}, bf16[32,512]{1,0:T(8,128)(2,1)S(1)}, u32[]{:S(2)}, u32[]{:S(2)}) collective-permute-start(bf16[32,512]{1,0:T(8,128)(2,1)S(1)} %get-tuple-element.60), channel_id=1, source_target_pairs={{0,12},{4,8},{8,4},{12,0},{1,13},{5,9},{9,5},{13,1},{2,14},{6,10},... | collective-permute-start | bytes 98312 | tf_op jit(solution)/shard_map/ppermute | solution.py:97
  58.8 2.7 %collective-permute-start.26 = (bf16[32,512]{1,0:T(8,128)(2,1)S(1)}, bf16[32,512]{1,0:T(8,128)(2,1)S(1)}, u32[]{:S(2)}, u32[]{:S(2)}) collective-permute-start(bf16[32,512]{1,0:T(8,128)(2,1)S(1)} %get-tuple-element.62), channel_id=1, source_target_pairs={{0,4},{4,0},{8,12},{12,8},{1,5},{5,1},{9,13},{13,9},{2,6},{6,2},{1... | collective-permute-start | bytes 98312 | tf_op jit(solution)/shard_map/ppermute | solution.py:97
  61.4 1.3 %collective-permute-done.24.refs_1_ = bf16[32,512]{1,0:T(8,128)(2,1)S(1)} collective-permute-done((bf16[32,512]{1,0:T(8,128)(2,1)S(1)}, bf16[32,512]{1,0:T(8,128)(2,1)S(1)}, u32[]{:S(2)}, u32[]{:S(2)}) %collective-permute-start.24) | collective-permute-done | bytes 32800 | tf_op jit(solution)/shard_map/ppermute | solution.py:97
  (88 shorter events, 22.9 us)
Async XLA Ops:
  1.0 6.3 %collective-permute-start = (bf16[32,1152]{1,0:T(8,128)(2,1)S(1)}, bf16[32,1152]{1,0:T(8,128)(2,1)S(1)}, u32[]{:S(2)}, u32[]{:S(2)}) collective-permute-start(bf16[32,1152]{1,0:T(8,128)(2,1)S(1)} %pack.1.queries_ref.refs_0_), channel_id=1, source_target_pairs={{0,4},{4,0},{8,12},{12,8},{1,5},{5,1},{9,13},{13,9},{2,6},{6,2},{1... | collective-permute-start | bytes 221192 | tf_op jit(solution)/shard_map/ppermute | solution.py:97
  4.2 7.8 %collective-permute-start.2 = (bf16[32,1152]{1,0:T(8,128)(2,1)S(1)}, bf16[32,1152]{1,0:T(8,128)(2,1)S(1)}, u32[]{:S(2)}, u32[]{:S(2)}) collective-permute-start(bf16[32,1152]{1,0:T(8,128)(2,1)S(1)} %pack.1.queries_ref.refs_0_), channel_id=1, source_target_pairs={{0,8},{4,12},{8,0},{12,4},{1,9},{5,13},{9,1},{13,5},{2,10},{6,14},... | collective-permute-start | bytes 221192 | tf_op jit(solution)/shard_map/ppermute | solution.py:97
  6.7 7.8 %collective-permute-start.4 = (bf16[32,1152]{1,0:T(8,128)(2,1)S(1)}, bf16[32,1152]{1,0:T(8,128)(2,1)S(1)}, u32[]{:S(2)}, u32[]{:S(2)}) collective-permute-start(bf16[32,1152]{1,0:T(8,128)(2,1)S(1)} %pack.1.queries_ref.refs_0_), channel_id=1, source_target_pairs={{0,12},{4,8},{8,4},{12,0},{1,13},{5,9},{9,5},{13,1},{2,14},{6,10},... | collective-permute-start | bytes 221192 | tf_op jit(solution)/shard_map/ppermute | solution.py:97
  8.7 11.3 %collective-permute-start.1 = (bf16[32,1152]{1,0:T(8,128)(2,1)S(1)}, bf16[32,1152]{1,0:T(8,128)(2,1)S(1)}, u32[]{:S(2)}, u32[]{:S(2)}) collective-permute-start(bf16[32,1152]{1,0:T(8,128)(2,1)S(1)} %attend.5), channel_id=1, source_target_pairs={{0,4},{4,0},{8,12},{12,8},{1,5},{5,1},{9,13},{13,9},{2,6},{6,2},{1... | collective-permute-start | bytes 221192 | tf_op jit(solution)/shard_map/ppermute | solution.py:97
  13.2 6.9 %collective-permute-start.3 = (bf16[32,1152]{1,0:T(8,128)(2,1)S(1)}, bf16[32,1152]{1,0:T(8,128)(2,1)S(1)}, u32[]{:S(2)}, u32[]{:S(2)}) collective-permute-start(bf16[32,1152]{1,0:T(8,128)(2,1)S(1)} %attend.6), channel_id=1, source_target_pairs={{0,8},{4,12},{8,0},{12,4},{1,9},{5,13},{9,1},{13,5},{2,10},{6,14},... | collective-permute-start | bytes 221192 | tf_op jit(solution)/shard_map/ppermute | solution.py:97
  15.8 6.3 %collective-permute-start.5 = (bf16[32,1152]{1,0:T(8,128)(2,1)S(1)}, bf16[32,1152]{1,0:T(8,128)(2,1)S(1)}, u32[]{:S(2)}, u32[]{:S(2)}) collective-permute-start(bf16[32,1152]{1,0:T(8,128)(2,1)S(1)} %attend.7), channel_id=1, source_target_pairs={{0,12},{4,8},{8,4},{12,0},{1,13},{5,9},{9,5},{13,1},{2,14},{6,10},... | collective-permute-start | bytes 221192 | tf_op jit(solution)/shard_map/ppermute | solution.py:97
  23.1 3.7 %collective-permute-start.6 = (bf16[32,512]{1,0:T(8,128)(2,1)S(1)}, bf16[32,512]{1,0:T(8,128)(2,1)S(1)}, u32[]{:S(2)}, u32[]{:S(2)}) collective-permute-start(bf16[32,512]{1,0:T(8,128)(2,1)S(1)} %get-tuple-element.37), channel_id=1, source_target_pairs={{0,3},{1,2},{2,1},{3,0},{4,7},{5,6},{6,5},{7,4},{8,11},{9,10},{10,... | collective-permute-start | bytes 98312 | tf_op jit(solution)/shard_map/ppermute | solution.py:97
  23.2 4.0 %collective-permute-start.7 = (bf16[32,512]{1,0:T(8,128)(2,1)S(1)}, bf16[32,512]{1,0:T(8,128)(2,1)S(1)}, u32[]{:S(2)}, u32[]{:S(2)}) collective-permute-start(bf16[32,512]{1,0:T(8,128)(2,1)S(1)} %get-tuple-element.38), channel_id=1, source_target_pairs={{0,2},{1,3},{2,0},{3,1},{4,6},{5,7},{6,4},{7,5},{8,10},{9,11},{10,... | collective-permute-start | bytes 98312 | tf_op jit(solution)/shard_map/ppermute | solution.py:97
  27.3 4.1 %collective-permute-start.9 = (bf16[32,640]{1,0:T(8,128)(2,1)S(1)}, bf16[32,640]{1,0:T(8,128)(2,1)S(1)}, u32[]{:S(2)}, u32[]{:S(2)}) collective-permute-start(bf16[32,640]{1,0:T(8,128)(2,1)S(1)} %get-tuple-element.43.refs_0_), channel_id=1, source_target_pairs={{0,4},{4,0},{8,12},{12,8},{1,5},{5,1},{9,13},{13,9},{2,6},{6,2},{1... | collective-permute-start | bytes 122888 | tf_op jit(solution)/shard_map/ppermute | solution.py:97
  28.7 5.8 %collective-permute-start.13 = (bf16[32,640]{1,0:T(8,128)(2,1)S(1)}, bf16[32,640]{1,0:T(8,128)(2,1)S(1)}, u32[]{:S(2)}, u32[]{:S(2)}) collective-permute-start(bf16[32,640]{1,0:T(8,128)(2,1)S(1)} %get-tuple-element.43.refs_0_), channel_id=1, source_target_pairs={{0,12},{4,8},{8,4},{12,0},{1,13},{5,9},{9,5},{13,1},{2,14},{6,10},... | collective-permute-start | bytes 122888 | tf_op jit(solution)/shard_map/ppermute | solution.py:97
  29.5 6.2 %collective-permute-start.12 = (bf16[32,640]{1,0:T(8,128)(2,1)S(1)}, bf16[32,640]{1,0:T(8,128)(2,1)S(1)}, u32[]{:S(2)}, u32[]{:S(2)}) collective-permute-start(bf16[32,640]{1,0:T(8,128)(2,1)S(1)} %get-tuple-element.43.refs_0_), channel_id=1, source_target_pairs={{0,8},{4,12},{8,0},{12,4},{1,9},{5,13},{9,1},{13,5},{2,10},{6,14},... | collective-permute-start | bytes 122888 | tf_op jit(solution)/shard_map/ppermute | solution.py:97
  33.5 3.3 %collective-permute-start.10 = (bf16[64,1664]{1,0:T(8,128)(2,1)S(1)}, bf16[64,1664]{1,0:T(8,128)(2,1)S(1)}, u32[]{:S(2)}, u32[]{:S(2)}) collective-permute-start(bf16[64,1664]{1,0:T(8,128)(2,1)S(1)} %get-tuple-element.45), channel_id=1, source_target_pairs={{0,1},{1,0},{2,3},{3,2},{4,5},{5,4},{6,7},{7,6},{8,9},{9,8},{10,11... | collective-permute-start | bytes 638984 | tf_op jit(solution)/shard_map/ppermute | solution.py:97
  36.8 2.7 %collective-permute-start.14 = (bf16[64,1664]{1,0:T(8,128)(2,1)S(1)}, bf16[64,1664]{1,0:T(8,128)(2,1)S(1)}, u32[]{:S(2)}, u32[]{:S(2)}) collective-permute-start(bf16[64,1664]{1,0:T(8,128)(2,1)S(1)} %gate_up.8), channel_id=1, source_target_pairs={{0,1},{1,0},{2,3},{3,2},{4,5},{5,4},{6,7},{7,6},{8,9},{9,8},{10,11... | collective-permute-start | bytes 638984 | tf_op jit(solution)/shard_map/ppermute | solution.py:97
  37.0 8.1 %collective-permute-start.11 = (bf16[64,1664]{1,0:T(8,128)(2,1)S(1)}, bf16[64,1664]{1,0:T(8,128)(2,1)S(1)}, u32[]{:S(2)}, u32[]{:S(2)}) collective-permute-start(bf16[64,1664]{1,0:T(8,128)(2,1)S(1)} %join.2), channel_id=1, source_target_pairs={{0,2},{2,0},{1,3},{3,1},{4,6},{6,4},{5,7},{7,5},{8,10},{10,8},{9,1... | collective-permute-start | bytes 638984 | tf_op jit(solution)/shard_map/ppermute | solution.py:97
  40.8 4.4 %collective-permute-start.15 = (bf16[64,1664]{1,0:T(8,128)(2,1)S(1)}, bf16[64,1664]{1,0:T(8,128)(2,1)S(1)}, u32[]{:S(2)}, u32[]{:S(2)}) collective-permute-start(bf16[64,1664]{1,0:T(8,128)(2,1)S(1)} %gate_up.10), channel_id=1, source_target_pairs={{0,1},{1,0},{2,3},{3,2},{4,5},{5,4},{6,7},{7,6},{8,9},{9,8},{10,11... | collective-permute-start | bytes 638984 | tf_op jit(solution)/shard_map/ppermute | solution.py:97
  41.0 8.3 %collective-permute-start.18 = (bf16[64,1664]{1,0:T(8,128)(2,1)S(1)}, bf16[64,1664]{1,0:T(8,128)(2,1)S(1)}, u32[]{:S(2)}, u32[]{:S(2)}) collective-permute-start(bf16[64,1664]{1,0:T(8,128)(2,1)S(1)} %join.3), channel_id=1, source_target_pairs={{0,2},{2,0},{1,3},{3,1},{4,6},{6,4},{5,7},{7,5},{8,10},{10,8},{9,1... | collective-permute-start | bytes 638984 | tf_op jit(solution)/shard_map/ppermute | solution.py:97
  46.5 2.8 %collective-permute-start.19 = (bf16[64,1664]{1,0:T(8,128)(2,1)S(1)}, bf16[64,1664]{1,0:T(8,128)(2,1)S(1)}, u32[]{:S(2)}, u32[]{:S(2)}) collective-permute-start(bf16[64,1664]{1,0:T(8,128)(2,1)S(1)} %gate_up.11), channel_id=1, source_target_pairs={{0,1},{1,0},{2,3},{3,2},{4,5},{5,4},{6,7},{7,6},{8,9},{9,8},{10,11... | collective-permute-start | bytes 638984 | tf_op jit(solution)/shard_map/ppermute | solution.py:97
  46.5 5.3 %collective-permute-start.21 = (bf16[64,768]{1,0:T(8,128)(2,1)S(1)}, bf16[64,768]{1,0:T(8,128)(2,1)S(1)}, u32[]{:S(2)}, u32[]{:S(2)}) collective-permute-start(bf16[64,768]{1,0:T(8,128)(2,1)S(1)} %hidden.2.refs_0_), channel_id=1, source_target_pairs={{0,1},{1,0},{2,3},{3,2},{4,5},{5,4},{6,7},{7,6},{8,9},{9,8},{10,11... | collective-permute-start | bytes 294920 | tf_op jit(solution)/shard_map/ppermute | solution.py:97
  47.0 4.8 %collective-permute-start.16 = (bf16[64,768]{1,0:T(8,128)(2,1)S(1)}, bf16[64,768]{1,0:T(8,128)(2,1)S(1)}, u32[]{:S(2)}, u32[]{:S(2)}) collective-permute-start(bf16[64,768]{1,0:T(8,128)(2,1)S(1)} %hidden.2.refs_0_), channel_id=1, source_target_pairs={{0,2},{2,0},{1,3},{3,1},{4,6},{6,4},{5,7},{7,5},{8,10},{10,8},{9,1... | collective-permute-start | bytes 294920 | tf_op jit(solution)/shard_map/ppermute | solution.py:97
  49.6 5.2 %collective-permute-start.20 = (bf16[64,768]{1,0:T(8,128)(2,1)S(1)}, bf16[64,768]{1,0:T(8,128)(2,1)S(1)}, u32[]{:S(2)}, u32[]{:S(2)}) collective-permute-start(bf16[64,768]{1,0:T(8,128)(2,1)S(1)} %hidden.3.refs_1_), channel_id=1, source_target_pairs={{0,2},{2,0},{1,3},{3,1},{4,6},{6,4},{5,7},{7,5},{8,10},{10,8},{9,1... | collective-permute-start | bytes 294920 | tf_op jit(solution)/shard_map/ppermute | solution.py:97
  51.8 3.9 %collective-permute-start.17 = (bf16[64,768]{1,0:T(8,128)(2,1)S(1)}, bf16[64,768]{1,0:T(8,128)(2,1)S(1)}, u32[]{:S(2)}, u32[]{:S(2)}) collective-permute-start(bf16[64,768]{1,0:T(8,128)(2,1)S(1)} %collective-permute-done.16.refs_0_), channel_id=1, source_target_pairs={{0,1},{1,0},{2,3},{3,2},{4,5},{5,4},{6,7},{7,6},{8,9},{9,8},{10,11... | collective-permute-start | bytes 294920 | tf_op jit(solution)/shard_map/ppermute | solution.py:97
  57.0 5.8 %collective-permute-start.24 = (bf16[32,512]{1,0:T(8,128)(2,1)S(1)}, bf16[32,512]{1,0:T(8,128)(2,1)S(1)}, u32[]{:S(2)}, u32[]{:S(2)}) collective-permute-start(bf16[32,512]{1,0:T(8,128)(2,1)S(1)} %get-tuple-element.60), channel_id=1, source_target_pairs={{0,12},{4,8},{8,4},{12,0},{1,13},{5,9},{9,5},{13,1},{2,14},{6,10},... | collective-permute-start | bytes 98312 | tf_op jit(solution)/shard_map/ppermute | solution.py:97
  58.8 5.0 %collective-permute-start.25 = (bf16[32,512]{1,0:T(8,128)(2,1)S(1)}, bf16[32,512]{1,0:T(8,128)(2,1)S(1)}, u32[]{:S(2)}, u32[]{:S(2)}) collective-permute-start(bf16[32,512]{1,0:T(8,128)(2,1)S(1)} %get-tuple-element.61), channel_id=1, source_target_pairs={{0,8},{4,12},{8,0},{12,4},{1,9},{5,13},{9,1},{13,5},{2,10},{6,14},... | collective-permute-start | bytes 98312 | tf_op jit(solution)/shard_map/ppermute | solution.py:97
  58.8 5.1 %collective-permute-start.26 = (bf16[32,512]{1,0:T(8,128)(2,1)S(1)}, bf16[32,512]{1,0:T(8,128)(2,1)S(1)}, u32[]{:S(2)}, u32[]{:S(2)}) collective-permute-start(bf16[32,512]{1,0:T(8,128)(2,1)S(1)} %get-tuple-element.62), channel_id=1, source_target_pairs={{0,4},{4,0},{8,12},{12,8},{1,5},{5,1},{9,13},{13,9},{2,6},{6,2},{1... | collective-permute-start | bytes 98312 | tf_op jit(solution)/shard_map/ppermute | solution.py:97
  (19 other events, 173.9 us)

commit v12 on v11

--- a/solution.py
+++ b/solution.py
@@ -523,7 +523,7 @@
     values = cached_values.reshape(key_count, head_size)
     out_matrix = out_weight.reshape(width, model_width)
     parts = {}
-    for k in list(range(1, ctx_count)) + [0]:
+    for k in far_first(ctx_count) + [0]:
         part = attend(
             layout, k, gathered[k], keys, values, sight, heads, scale, gate_up_weight
         )
@@ -536,7 +536,7 @@
 
     projected = project(
         layout,
-        [parts[k] for k in range(ctx_count)],
+        list(parts.values()),
         after(out_matrix, place),
         heads,
         scale,

time: 64.7 us -> 65.2 us (level)
  starting transfers between devices: 25.7 us -> 28.1 us
  waiting for transfers between devices: 16.5 us -> 14.6 us
    ppermute x27, starting transfers between devices: 25.7 us -> 28.1 us  [swapped(): return lax.ppermute(value, axes, pairs)]
    ppermute x27, waiting for transfers between devices: 16.5 us -> 14.6 us  [swapped(): return lax.ppermute(value, axes, pairs)]
  transfers between devices with their start and end apart: 27 -> 27, of which waited for: 16 -> 15; matrix products, arithmetic and copies ran while one was open for 0% -> 0% of each run, Pallas kernels for 28% -> 28%
where the time goes in v12:
time: 65.2 us; the launch traced here: 65.1 us
  starting transfers between devices  28.1 us (43%)
  Pallas kernels  22 us (34%)
  waiting for transfers between devices  14.6 us (22%)
    ppermute x27, starting transfers between devices, swapped(): return lax.ppermute(value, axes, pairs)  28.1 us
    ppermute x27, waiting for transfers between devices, swapped(): return lax.ppermute(value, axes, pairs)  14.6 us
    pallas_call x6, Pallas kernels, gate_up(): pl.pallas_call(kernel, out_shape=[out] * len(names), compiler_params=para...  8.72 us
    pallas_call x4, Pallas kernels, attend(): pl.pallas_call(functools.partial(attend_kernel, heads, scale, layout, k),...  5.05 us
    pallas_call x3, Pallas kernels, down(): pl.pallas_call(kernel, out_shape=[jax.ShapeDtypeStruct((rows, piece_width...  3.21 us
  transfers between devices with their start and end apart: 27, of which 15 were waited for; matrix products, arithmetic and copies ran while one was open for 0% of the time, Pallas kernels for 28%

profile of v12, /device:TPU:0, one launch (start us, length us, event | category | flops | bytes accessed | tf_op | source)
XLA Modules:
  0.0 65.1 jit_solution(6869541503597975587)
XLA Ops:
  1.0 5.1 %collective-permute-start = (bf16[32,1152]{1,0:T(8,128)(2,1)S(1)}, bf16[32,1152]{1,0:T(8,128)(2,1)S(1)}, u32[]{:S(2)}, u32[]{:S(2)}) collective-permute-start(bf16[32,1152]{1,0:T(8,128)(2,1)S(1)} %pack.1.queries_ref.refs_0_), channel_id=1, source_target_pairs={{0,12},{4,8},{8,4},{12,0},{1,13},{5,9},{9,5},{13,1},{2,14},{6,10},... | collective-permute-start | bytes 221192 | tf_op jit(solution)/shard_map/ppermute | solution.py:97
  7.5 1.5 %collective-permute-done.queries_ref.refs_3_ = bf16[32,1152]{1,0:T(8,128)(2,1)S(1)} collective-permute-done((bf16[32,1152]{1,0:T(8,128)(2,1)S(1)}, bf16[32,1152]{1,0:T(8,128)(2,1)S(1)}, u32[]{:S(2)}, u32[]{:S(2)}) %collective-permute-start) | collective-permute-done | bytes 73760 | tf_op jit(solution)/shard_map/ppermute | solution.py:97
  8.9 1.3 %attend.4 = bf16[32,1152]{1,0:T(8,128)(2,1)S(1)} custom-call(bf16[32,1152]{1,0:T(8,128)(2,1)S(1)} %collective-permute-done.queries_ref.refs_3_, bf16[2048,128]{1,0:T(8,128)(2,1)S(1)} %bitcast.20, bf16[2048,128]{1,0:T(8,128)(2,1)S(1)} %bitcast.24, bf16[64,2048]{1,0:T(8,128)(2,1)S(1)} %sight.1.sight_ref, bf16[16,512,1536]{2,1,0:T(8,128)(2,1)} %weight_ref.14), custom_call_target="tpu_custom_call" | custom-call | flops 536870912 | bytes 1048576 | tf_op jit(solution)/shard_map/attend/pallas_call | solution.py:219
  10.2 4.3 %collective-permute-start.1 = (bf16[32,1152]{1,0:T(8,128)(2,1)S(1)}, bf16[32,1152]{1,0:T(8,128)(2,1)S(1)}, u32[]{:S(2)}, u32[]{:S(2)}) collective-permute-start(bf16[32,1152]{1,0:T(8,128)(2,1)S(1)} %attend.4), channel_id=1, source_target_pairs={{0,12},{4,8},{8,4},{12,0},{1,13},{5,9},{9,5},{13,1},{2,14},{6,10},... | collective-permute-start | bytes 221192 | tf_op jit(solution)/shard_map/ppermute | solution.py:97
  14.5 1.3 %attend.5 = bf16[32,1152]{1,0:T(8,128)(2,1)S(1)} custom-call(bf16[32,1152]{1,0:T(8,128)(2,1)S(1)} %collective-permute-done.2.queries_ref.refs_2_, bf16[2048,128]{1,0:T(8,128)(2,1)S(1)} %bitcast.21, bf16[2048,128]{1,0:T(8,128)(2,1)S(1)} %bitcast.25, bf16[64,2048]{1,0:T(8,128)(2,1)S(1)} %sight.1.sight_ref, bf16[16,512,1536]{2,1,0:T(8,128)(2,1)} %weight_ref.14), custom_call_target="tpu_custom_call" | custom-call | flops 536870912 | bytes 1048576 | tf_op jit(solution)/shard_map/attend/pallas_call | solution.py:219
  16.2 1.3 %attend.6 = bf16[32,1152]{1,0:T(8,128)(2,1)S(1)} custom-call(bf16[32,1152]{1,0:T(8,128)(2,1)S(1)} %collective-permute-done.4.queries_ref.refs_1_, bf16[2048,128]{1,0:T(8,128)(2,1)S(1)} %bitcast.22, bf16[2048,128]{1,0:T(8,128)(2,1)S(1)} %bitcast.26, bf16[64,2048]{1,0:T(8,128)(2,1)S(1)} %sight.1.sight_ref, bf16[16,512,1536]{2,1,0:T(8,128)(2,1)} %weight_ref.14), custom_call_target="tpu_custom_call" | custom-call | flops 536870912 | bytes 1048576 | tf_op jit(solution)/shard_map/attend/pallas_call | solution.py:219
  17.5 1.6 %collective-permute-start.5 = (bf16[32,1152]{1,0:T(8,128)(2,1)S(1)}, bf16[32,1152]{1,0:T(8,128)(2,1)S(1)}, u32[]{:S(2)}, u32[]{:S(2)}) collective-permute-start(bf16[32,1152]{1,0:T(8,128)(2,1)S(1)} %attend.6), channel_id=1, source_target_pairs={{0,4},{4,0},{8,12},{12,8},{1,5},{5,1},{9,13},{13,9},{2,6},{6,2},{1... | collective-permute-start | bytes 221192 | tf_op jit(solution)/shard_map/ppermute | solution.py:97
  19.2 1.3 %attend.7.refs_3_ = bf16[32,1152]{1,0:T(8,128)(2,1)S(1)} custom-call(bf16[32,1152]{1,0:T(8,128)(2,1)S(1)} %pack.1.queries_ref.refs_0_, bf16[2048,128]{1,0:T(8,128)(2,1)S(1)} %bitcast.23, bf16[2048,128]{1,0:T(8,128)(2,1)S(1)} %bitcast.27, bf16[64,2048]{1,0:T(8,128)(2,1)S(1)} %sight.1.sight_ref, bf16[16,512,1536]{2,1,0:T(8,128)(2,1)} %weight_ref.14), custom_call_target="tpu_custom_call" | custom-call | flops 536870912 | bytes 1048576 | tf_op jit(solution)/shard_map/attend/pallas_call | solution.py:219
  23.4 1.3 %collective-permute-start.7 = (bf16[32,512]{1,0:T(8,128)(2,1)S(1)}, bf16[32,512]{1,0:T(8,128)(2,1)S(1)}, u32[]{:S(2)}, u32[]{:S(2)}) collective-permute-start(bf16[32,512]{1,0:T(8,128)(2,1)S(1)} %get-tuple-element.38), channel_id=1, source_target_pairs={{0,2},{1,3},{2,0},{3,1},{4,6},{5,7},{6,4},{7,5},{8,10},{9,11},{10,... | collective-permute-start | bytes 98312 | tf_op jit(solution)/shard_map/ppermute | solution.py:97
  25.3 1.6 %collective-permute-done.6.refs_1_ = bf16[32,512]{1,0:T(8,128)(2,1)S(1)} collective-permute-done((bf16[32,512]{1,0:T(8,128)(2,1)S(1)}, bf16[32,512]{1,0:T(8,128)(2,1)S(1)}, u32[]{:S(2)}, u32[]{:S(2)}) %collective-permute-start.6) | collective-permute-done | bytes 32800 | tf_op jit(solution)/shard_map/ppermute | solution.py:97
  27.5 1.3 %collective-permute-start.9 = (bf16[32,640]{1,0:T(8,128)(2,1)S(1)}, bf16[32,640]{1,0:T(8,128)(2,1)S(1)}, u32[]{:S(2)}, u32[]{:S(2)}) collective-permute-start(bf16[32,640]{1,0:T(8,128)(2,1)S(1)} %get-tuple-element.43.refs_0_), channel_id=1, source_target_pairs={{0,4},{4,0},{8,12},{12,8},{1,5},{5,1},{9,13},{13,9},{2,6},{6,2},{1... | collective-permute-start | bytes 122888 | tf_op jit(solution)/shard_map/ppermute | solution.py:97
  28.8 2.4 %collective-permute-start.13 = (bf16[32,640]{1,0:T(8,128)(2,1)S(1)}, bf16[32,640]{1,0:T(8,128)(2,1)S(1)}, u32[]{:S(2)}, u32[]{:S(2)}) collective-permute-start(bf16[32,640]{1,0:T(8,128)(2,1)S(1)} %get-tuple-element.43.refs_0_), channel_id=1, source_target_pairs={{0,12},{4,8},{8,4},{12,0},{1,13},{5,9},{9,5},{13,1},{2,14},{6,10},... | collective-permute-start | bytes 122888 | tf_op jit(solution)/shard_map/ppermute | solution.py:97
  31.6 2.1 %gate_up.6 = (bf16[64,1664]{1,0:T(8,128)(2,1)S(1)}, bf16[64,1664]{1,0:T(8,128)(2,1)S(1)}) custom-call(bf16[8,64,64]{2,1,0:T(8,128)(2,1)S(1)} %get-tuple-element.55.place_ref, bf16[16,512,1536]{2,1,0:T(8,128)(2,1)S(1)} %bitcast.10, bf16[32,640]{1,0:T(8,128)(2,1)S(1)} %get-tuple-element.43.refs_0_, bf16[32,640]{1,0:T(8,128)(2,1)S(1)} %collective-permute-done.9.refs_1_), custom_call_target="tpu_custom_call" | custom-call | flops 100663296 | bytes 196608 | tf_op jit(solution)/shard_map/gate_up/pallas_call | solution.py:376
  34.6 1.5 %collective-permute-done.12.refs_0_.refs_2_ = bf16[32,640]{1,0:T(8,128)(2,1)S(1)} collective-permute-done((bf16[32,640]{1,0:T(8,128)(2,1)S(1)}, bf16[32,640]{1,0:T(8,128)(2,1)S(1)}, u32[]{:S(2)}, u32[]{:S(2)}) %collective-permute-start.12) | collective-permute-done | bytes 40992 | tf_op jit(solution)/shard_map/ppermute | solution.py:97
  37.4 1.6 %collective-permute-start.11 = (bf16[64,1664]{1,0:T(8,128)(2,1)S(1)}, bf16[64,1664]{1,0:T(8,128)(2,1)S(1)}, u32[]{:S(2)}, u32[]{:S(2)}) collective-permute-start(bf16[64,1664]{1,0:T(8,128)(2,1)S(1)} %join.2), channel_id=1, source_target_pairs={{0,2},{2,0},{1,3},{3,1},{4,6},{6,4},{5,7},{7,5},{8,10},{10,8},{9,1... | collective-permute-start | bytes 638984 | tf_op jit(solution)/shard_map/ppermute | solution.py:97
  42.2 2.2 %gate_up.9 = (bf16[64,1664]{1,0:T(8,128)(2,1)S(1)}, bf16[64,1664]{1,0:T(8,128)(2,1)S(1)}) custom-call(bf16[8,64,64]{2,1,0:T(8,128)(2,1)S(1)} %get-tuple-element.55.place_ref, bf16[16,512,1536]{2,1,0:T(8,128)(2,1)S(1)} %bitcast.10, bf16[32,640]{1,0:T(8,128)(2,1)S(1)} %get-tuple-element.43.refs_0_, bf16[32,640]{1,0:T(8,128)(2,1)S(1)} %collective-permute-done.9.refs_1_, ...), custom_call_target="tpu_custom_call" | custom-call | flops 100663296 | bytes 196608 | tf_op jit(solution)/shard_map/gate_up/pallas_call | solution.py:376
  47.4 1.5 %collective-permute-start.16 = (bf16[64,768]{1,0:T(8,128)(2,1)S(1)}, bf16[64,768]{1,0:T(8,128)(2,1)S(1)}, u32[]{:S(2)}, u32[]{:S(2)}) collective-permute-start(bf16[64,768]{1,0:T(8,128)(2,1)S(1)} %hidden.2.refs_0_), channel_id=1, source_target_pairs={{0,2},{2,0},{1,3},{3,1},{4,6},{6,4},{5,7},{7,5},{8,10},{10,8},{9,1... | collective-permute-start | bytes 294920 | tf_op jit(solution)/shard_map/ppermute | solution.py:97
  50.0 1.6 %collective-permute-start.20 = (bf16[64,768]{1,0:T(8,128)(2,1)S(1)}, bf16[64,768]{1,0:T(8,128)(2,1)S(1)}, u32[]{:S(2)}, u32[]{:S(2)}) collective-permute-start(bf16[64,768]{1,0:T(8,128)(2,1)S(1)} %hidden.3.refs_1_), channel_id=1, source_target_pairs={{0,2},{2,0},{1,3},{3,1},{4,6},{6,4},{5,7},{7,5},{8,10},{10,8},{9,1... | collective-permute-start | bytes 294920 | tf_op jit(solution)/shard_map/ppermute | solution.py:97
  52.2 1.5 %down.3.refs_2_ = f32[128,512]{1,0:T(8,128)S(1)} custom-call(bf16[16,768,512]{2,1,0:T(8,128)(2,1)S(1)} %bitcast.19, bf16[8,64,64]{2,1,0:T(8,128)(2,1)S(1)} %get-tuple-element.41.high_ref, bf16[8,64,64]{2,1,0:T(8,128)(2,1)S(1)} %get-tuple-element.42.low_ref, bf16[64,768]{1,0:T(8,128)(2,1)S(1)} %hidden.2.refs_0_, bf16[64,768]{1,0:T(8,128)(2,1)S(1)} %hidden.3.refs_1_, ...), custom_call_target="tpu_custom_call" | custom-call | flops 100663296 | bytes 1048576 | tf_op jit(solution)/shard_map/down/pallas_call | solution.py:458
  53.8 1.5 %collective-permute-done.20.refs_1_ = bf16[64,768]{1,0:T(8,128)(2,1)S(1)} collective-permute-done((bf16[64,768]{1,0:T(8,128)(2,1)S(1)}, bf16[64,768]{1,0:T(8,128)(2,1)S(1)}, u32[]{:S(2)}, u32[]{:S(2)}) %collective-permute-start.20) | collective-permute-done | bytes 98336 | tf_op jit(solution)/shard_map/ppermute | solution.py:97
  57.4 2.2 %collective-permute-start.24 = (bf16[32,512]{1,0:T(8,128)(2,1)S(1)}, bf16[32,512]{1,0:T(8,128)(2,1)S(1)}, u32[]{:S(2)}, u32[]{:S(2)}) collective-permute-start(bf16[32,512]{1,0:T(8,128)(2,1)S(1)} %get-tuple-element.60), channel_id=1, source_target_pairs={{0,12},{4,8},{8,4},{12,0},{1,13},{5,9},{9,5},{13,1},{2,14},{6,10},... | collective-permute-start | bytes 98312 | tf_op jit(solution)/shard_map/ppermute | solution.py:97
  59.6 2.2 %collective-permute-start.26 = (bf16[32,512]{1,0:T(8,128)(2,1)S(1)}, bf16[32,512]{1,0:T(8,128)(2,1)S(1)}, u32[]{:S(2)}, u32[]{:S(2)}) collective-permute-start(bf16[32,512]{1,0:T(8,128)(2,1)S(1)} %get-tuple-element.62), channel_id=1, source_target_pairs={{0,4},{4,0},{8,12},{12,8},{1,5},{5,1},{9,13},{13,9},{2,6},{6,2},{1... | collective-permute-start | bytes 98312 | tf_op jit(solution)/shard_map/ppermute | solution.py:97
  61.9 1.3 %collective-permute-done.24.refs_1_ = bf16[32,512]{1,0:T(8,128)(2,1)S(1)} collective-permute-done((bf16[32,512]{1,0:T(8,128)(2,1)S(1)}, bf16[32,512]{1,0:T(8,128)(2,1)S(1)}, u32[]{:S(2)}, u32[]{:S(2)}) %collective-permute-start.24) | collective-permute-done | bytes 32800 | tf_op jit(solution)/shard_map/ppermute | solution.py:97
  63.2 1.3 %collective-permute-done.25.refs_2_ = bf16[32,512]{1,0:T(8,128)(2,1)S(1)} collective-permute-done((bf16[32,512]{1,0:T(8,128)(2,1)S(1)}, bf16[32,512]{1,0:T(8,128)(2,1)S(1)}, u32[]{:S(2)}, u32[]{:S(2)}) %collective-permute-start.25) | collective-permute-done | bytes 32800 | tf_op jit(solution)/shard_map/ppermute | solution.py:97
  (88 shorter events, 20.1 us)
Async XLA Ops:
  1.0 7.9 %collective-permute-start = (bf16[32,1152]{1,0:T(8,128)(2,1)S(1)}, bf16[32,1152]{1,0:T(8,128)(2,1)S(1)}, u32[]{:S(2)}, u32[]{:S(2)}) collective-permute-start(bf16[32,1152]{1,0:T(8,128)(2,1)S(1)} %pack.1.queries_ref.refs_0_), channel_id=1, source_target_pairs={{0,12},{4,8},{8,4},{12,0},{1,13},{5,9},{9,5},{13,1},{2,14},{6,10},... | collective-permute-start | bytes 221192 | tf_op jit(solution)/shard_map/ppermute | solution.py:97
  6.2 8.3 %collective-permute-start.2 = (bf16[32,1152]{1,0:T(8,128)(2,1)S(1)}, bf16[32,1152]{1,0:T(8,128)(2,1)S(1)}, u32[]{:S(2)}, u32[]{:S(2)}) collective-permute-start(bf16[32,1152]{1,0:T(8,128)(2,1)S(1)} %pack.1.queries_ref.refs_0_), channel_id=1, source_target_pairs={{0,8},{4,12},{8,0},{12,4},{1,9},{5,13},{9,1},{13,5},{2,10},{6,14},... | collective-permute-start | bytes 221192 | tf_op jit(solution)/shard_map/ppermute | solution.py:97
  6.2 10.0 %collective-permute-start.4 = (bf16[32,1152]{1,0:T(8,128)(2,1)S(1)}, bf16[32,1152]{1,0:T(8,128)(2,1)S(1)}, u32[]{:S(2)}, u32[]{:S(2)}) collective-permute-start(bf16[32,1152]{1,0:T(8,128)(2,1)S(1)} %pack.1.queries_ref.refs_0_), channel_id=1, source_target_pairs={{0,4},{4,0},{8,12},{12,8},{1,5},{5,1},{9,13},{13,9},{2,6},{6,2},{1... | collective-permute-start | bytes 221192 | tf_op jit(solution)/shard_map/ppermute | solution.py:97
  10.2 10.9 %collective-permute-start.1 = (bf16[32,1152]{1,0:T(8,128)(2,1)S(1)}, bf16[32,1152]{1,0:T(8,128)(2,1)S(1)}, u32[]{:S(2)}, u32[]{:S(2)}) collective-permute-start(bf16[32,1152]{1,0:T(8,128)(2,1)S(1)} %attend.4), channel_id=1, source_target_pairs={{0,12},{4,8},{8,4},{12,0},{1,13},{5,9},{9,5},{13,1},{2,14},{6,10},... | collective-permute-start | bytes 221192 | tf_op jit(solution)/shard_map/ppermute | solution.py:97
  15.7 6.1 %collective-permute-start.3 = (bf16[32,1152]{1,0:T(8,128)(2,1)S(1)}, bf16[32,1152]{1,0:T(8,128)(2,1)S(1)}, u32[]{:S(2)}, u32[]{:S(2)}) collective-permute-start(bf16[32,1152]{1,0:T(8,128)(2,1)S(1)} %attend.5), channel_id=1, source_target_pairs={{0,8},{4,12},{8,0},{12,4},{1,9},{5,13},{9,1},{13,5},{2,10},{6,14},... | collective-permute-start | bytes 221192 | tf_op jit(solution)/shard_map/ppermute | solution.py:97
  17.5 4.8 %collective-permute-start.5 = (bf16[32,1152]{1,0:T(8,128)(2,1)S(1)}, bf16[32,1152]{1,0:T(8,128)(2,1)S(1)}, u32[]{:S(2)}, u32[]{:S(2)}) collective-permute-start(bf16[32,1152]{1,0:T(8,128)(2,1)S(1)} %attend.6), channel_id=1, source_target_pairs={{0,4},{4,0},{8,12},{12,8},{1,5},{5,1},{9,13},{13,9},{2,6},{6,2},{1... | collective-permute-start | bytes 221192 | tf_op jit(solution)/shard_map/ppermute | solution.py:97
  23.4 3.5 %collective-permute-start.6 = (bf16[32,512]{1,0:T(8,128)(2,1)S(1)}, bf16[32,512]{1,0:T(8,128)(2,1)S(1)}, u32[]{:S(2)}, u32[]{:S(2)}) collective-permute-start(bf16[32,512]{1,0:T(8,128)(2,1)S(1)} %get-tuple-element.37), channel_id=1, source_target_pairs={{0,3},{1,2},{2,1},{3,0},{4,7},{5,6},{6,5},{7,4},{8,11},{9,10},{10,... | collective-permute-start | bytes 98312 | tf_op jit(solution)/shard_map/ppermute | solution.py:97
  23.4 4.0 %collective-permute-start.7 = (bf16[32,512]{1,0:T(8,128)(2,1)S(1)}, bf16[32,512]{1,0:T(8,128)(2,1)S(1)}, u32[]{:S(2)}, u32[]{:S(2)}) collective-permute-start(bf16[32,512]{1,0:T(8,128)(2,1)S(1)} %get-tuple-element.38), channel_id=1, source_target_pairs={{0,2},{1,3},{2,0},{3,1},{4,6},{5,7},{6,4},{7,5},{8,10},{9,11},{10,... | collective-permute-start | bytes 98312 | tf_op jit(solution)/shard_map/ppermute | solution.py:97
  27.5 4.1 %collective-permute-start.9 = (bf16[32,640]{1,0:T(8,128)(2,1)S(1)}, bf16[32,640]{1,0:T(8,128)(2,1)S(1)}, u32[]{:S(2)}, u32[]{:S(2)}) collective-permute-start(bf16[32,640]{1,0:T(8,128)(2,1)S(1)} %get-tuple-element.43.refs_0_), channel_id=1, source_target_pairs={{0,4},{4,0},{8,12},{12,8},{1,5},{5,1},{9,13},{13,9},{2,6},{6,2},{1... | collective-permute-start | bytes 122888 | tf_op jit(solution)/shard_map/ppermute | solution.py:97
  28.8 5.8 %collective-permute-start.13 = (bf16[32,640]{1,0:T(8,128)(2,1)S(1)}, bf16[32,640]{1,0:T(8,128)(2,1)S(1)}, u32[]{:S(2)}, u32[]{:S(2)}) collective-permute-start(bf16[32,640]{1,0:T(8,128)(2,1)S(1)} %get-tuple-element.43.refs_0_), channel_id=1, source_target_pairs={{0,12},{4,8},{8,4},{12,0},{1,13},{5,9},{9,5},{13,1},{2,14},{6,10},... | collective-permute-start | bytes 122888 | tf_op jit(solution)/shard_map/ppermute | solution.py:97
  31.2 4.9 %collective-permute-start.12 = (bf16[32,640]{1,0:T(8,128)(2,1)S(1)}, bf16[32,640]{1,0:T(8,128)(2,1)S(1)}, u32[]{:S(2)}, u32[]{:S(2)}) collective-permute-start(bf16[32,640]{1,0:T(8,128)(2,1)S(1)} %get-tuple-element.43.refs_0_), channel_id=1, source_target_pairs={{0,8},{4,12},{8,0},{12,4},{1,9},{5,13},{9,1},{13,5},{2,10},{6,14},... | collective-permute-start | bytes 122888 | tf_op jit(solution)/shard_map/ppermute | solution.py:97
  33.7 3.5 %collective-permute-start.10 = (bf16[64,1664]{1,0:T(8,128)(2,1)S(1)}, bf16[64,1664]{1,0:T(8,128)(2,1)S(1)}, u32[]{:S(2)}, u32[]{:S(2)}) collective-permute-start(bf16[64,1664]{1,0:T(8,128)(2,1)S(1)} %get-tuple-element.45), channel_id=1, source_target_pairs={{0,1},{1,0},{2,3},{3,2},{4,5},{5,4},{6,7},{7,6},{8,9},{9,8},{10,11... | collective-permute-start | bytes 638984 | tf_op jit(solution)/shard_map/ppermute | solution.py:97
  37.2 2.9 %collective-permute-start.14 = (bf16[64,1664]{1,0:T(8,128)(2,1)S(1)}, bf16[64,1664]{1,0:T(8,128)(2,1)S(1)}, u32[]{:S(2)}, u32[]{:S(2)}) collective-permute-start(bf16[64,1664]{1,0:T(8,128)(2,1)S(1)} %gate_up.8), channel_id=1, source_target_pairs={{0,1},{1,0},{2,3},{3,2},{4,5},{5,4},{6,7},{7,6},{8,9},{9,8},{10,11... | collective-permute-start | bytes 638984 | tf_op jit(solution)/shard_map/ppermute | solution.py:97
  37.4 8.1 %collective-permute-start.11 = (bf16[64,1664]{1,0:T(8,128)(2,1)S(1)}, bf16[64,1664]{1,0:T(8,128)(2,1)S(1)}, u32[]{:S(2)}, u32[]{:S(2)}) collective-permute-start(bf16[64,1664]{1,0:T(8,128)(2,1)S(1)} %join.2), channel_id=1, source_target_pairs={{0,2},{2,0},{1,3},{3,1},{4,6},{6,4},{5,7},{7,5},{8,10},{10,8},{9,1... | collective-permute-start | bytes 638984 | tf_op jit(solution)/shard_map/ppermute | solution.py:97
  41.4 4.1 %collective-permute-start.15 = (bf16[64,1664]{1,0:T(8,128)(2,1)S(1)}, bf16[64,1664]{1,0:T(8,128)(2,1)S(1)}, u32[]{:S(2)}, u32[]{:S(2)}) collective-permute-start(bf16[64,1664]{1,0:T(8,128)(2,1)S(1)} %gate_up.10), channel_id=1, source_target_pairs={{0,1},{1,0},{2,3},{3,2},{4,5},{5,4},{6,7},{7,6},{8,9},{9,8},{10,11... | collective-permute-start | bytes 638984 | tf_op jit(solution)/shard_map/ppermute | solution.py:97
  41.7 8.1 %collective-permute-start.18 = (bf16[64,1664]{1,0:T(8,128)(2,1)S(1)}, bf16[64,1664]{1,0:T(8,128)(2,1)S(1)}, u32[]{:S(2)}, u32[]{:S(2)}) collective-permute-start(bf16[64,1664]{1,0:T(8,128)(2,1)S(1)} %join.3), channel_id=1, source_target_pairs={{0,2},{2,0},{1,3},{3,1},{4,6},{6,4},{5,7},{7,5},{8,10},{10,8},{9,1... | collective-permute-start | bytes 638984 | tf_op jit(solution)/shard_map/ppermute | solution.py:97
  46.9 2.8 %collective-permute-start.19 = (bf16[64,1664]{1,0:T(8,128)(2,1)S(1)}, bf16[64,1664]{1,0:T(8,128)(2,1)S(1)}, u32[]{:S(2)}, u32[]{:S(2)}) collective-permute-start(bf16[64,1664]{1,0:T(8,128)(2,1)S(1)} %gate_up.11), channel_id=1, source_target_pairs={{0,1},{1,0},{2,3},{3,2},{4,5},{5,4},{6,7},{7,6},{8,9},{9,8},{10,11... | collective-permute-start | bytes 638984 | tf_op jit(solution)/shard_map/ppermute | solution.py:97
  46.9 5.3 %collective-permute-start.21 = (bf16[64,768]{1,0:T(8,128)(2,1)S(1)}, bf16[64,768]{1,0:T(8,128)(2,1)S(1)}, u32[]{:S(2)}, u32[]{:S(2)}) collective-permute-start(bf16[64,768]{1,0:T(8,128)(2,1)S(1)} %hidden.2.refs_0_), channel_id=1, source_target_pairs={{0,1},{1,0},{2,3},{3,2},{4,5},{5,4},{6,7},{7,6},{8,9},{9,8},{10,11... | collective-permute-start | bytes 294920 | tf_op jit(solution)/shard_map/ppermute | solution.py:97
  47.4 4.8 %collective-permute-start.16 = (bf16[64,768]{1,0:T(8,128)(2,1)S(1)}, bf16[64,768]{1,0:T(8,128)(2,1)S(1)}, u32[]{:S(2)}, u32[]{:S(2)}) collective-permute-start(bf16[64,768]{1,0:T(8,128)(2,1)S(1)} %hidden.2.refs_0_), channel_id=1, source_target_pairs={{0,2},{2,0},{1,3},{3,1},{4,6},{6,4},{5,7},{7,5},{8,10},{10,8},{9,1... | collective-permute-start | bytes 294920 | tf_op jit(solution)/shard_map/ppermute | solution.py:97
  50.0 5.2 %collective-permute-start.20 = (bf16[64,768]{1,0:T(8,128)(2,1)S(1)}, bf16[64,768]{1,0:T(8,128)(2,1)S(1)}, u32[]{:S(2)}, u32[]{:S(2)}) collective-permute-start(bf16[64,768]{1,0:T(8,128)(2,1)S(1)} %hidden.3.refs_1_), channel_id=1, source_target_pairs={{0,2},{2,0},{1,3},{3,1},{4,6},{6,4},{5,7},{7,5},{8,10},{10,8},{9,1... | collective-permute-start | bytes 294920 | tf_op jit(solution)/shard_map/ppermute | solution.py:97
  52.2 3.9 %collective-permute-start.17 = (bf16[64,768]{1,0:T(8,128)(2,1)S(1)}, bf16[64,768]{1,0:T(8,128)(2,1)S(1)}, u32[]{:S(2)}, u32[]{:S(2)}) collective-permute-start(bf16[64,768]{1,0:T(8,128)(2,1)S(1)} %collective-permute-done.16.refs_0_), channel_id=1, source_target_pairs={{0,1},{1,0},{2,3},{3,2},{4,5},{5,4},{6,7},{7,6},{8,9},{9,8},{10,11... | collective-permute-start | bytes 294920 | tf_op jit(solution)/shard_map/ppermute | solution.py:97
  57.4 5.8 %collective-permute-start.24 = (bf16[32,512]{1,0:T(8,128)(2,1)S(1)}, bf16[32,512]{1,0:T(8,128)(2,1)S(1)}, u32[]{:S(2)}, u32[]{:S(2)}) collective-permute-start(bf16[32,512]{1,0:T(8,128)(2,1)S(1)} %get-tuple-element.60), channel_id=1, source_target_pairs={{0,12},{4,8},{8,4},{12,0},{1,13},{5,9},{9,5},{13,1},{2,14},{6,10},... | collective-permute-start | bytes 98312 | tf_op jit(solution)/shard_map/ppermute | solution.py:97
  59.6 4.8 %collective-permute-start.25 = (bf16[32,512]{1,0:T(8,128)(2,1)S(1)}, bf16[32,512]{1,0:T(8,128)(2,1)S(1)}, u32[]{:S(2)}, u32[]{:S(2)}) collective-permute-start(bf16[32,512]{1,0:T(8,128)(2,1)S(1)} %get-tuple-element.61), channel_id=1, source_target_pairs={{0,8},{4,12},{8,0},{12,4},{1,9},{5,13},{9,1},{13,5},{2,10},{6,14},... | collective-permute-start | bytes 98312 | tf_op jit(solution)/shard_map/ppermute | solution.py:97
  59.6 4.8 %collective-permute-start.26 = (bf16[32,512]{1,0:T(8,128)(2,1)S(1)}, bf16[32,512]{1,0:T(8,128)(2,1)S(1)}, u32[]{:S(2)}, u32[]{:S(2)}) collective-permute-start(bf16[32,512]{1,0:T(8,128)(2,1)S(1)} %get-tuple-element.62), channel_id=1, source_target_pairs={{0,4},{4,0},{8,12},{12,8},{1,5},{5,1},{9,13},{13,9},{2,6},{6,2},{1... | collective-permute-start | bytes 98312 | tf_op jit(solution)/shard_map/ppermute | solution.py:97
  (19 other events, 164.0 us)

commit v13 on v11

--- a/solution.py
+++ b/solution.py
@@ -515,19 +515,29 @@
     packed = pack(
         queries.reshape(query_rows, width), query_seg, expert_ids, route_weight, gate_up_weight
     )
-    gathered = {0: packed}
-    for k in far_first(ctx_count):
-        gathered[k] = swapped(packed, "ctx", k)
     sight = sight_of(parent, key_seg)
     keys = cached_keys.reshape(key_count, head_size)
     values = cached_values.reshape(key_count, head_size)
     out_matrix = out_weight.reshape(width, model_width)
-    parts = {}
-    for k in list(range(1, ctx_count)) + [0]:
-        part = attend(
+
+    def attend_block(k):
+        return attend(
             layout, k, gathered[k], keys, values, sight, heads, scale, gate_up_weight
         )
-        parts[k] = swapped(part, "ctx", k) if k else part
+
+    gathered = {0: packed}
+    for k in range(1, ctx_count):
+        if k == 1 or k % 2 == 0:
+            gathered[k] = swapped(packed, "ctx", k)
+    parts = {1: attend_block(1)}
+    for k in range(3, ctx_count, 2):
+        gathered[k] = swapped(
+            lax.optimization_barrier((gathered[k - 1], parts[1]))[0], "ctx", 1
+        )
+    for k in list(range(2, ctx_count)) + [0]:
+        parts[k] = attend_block(k)
+    for k in range(1, ctx_count):
+        parts[k] = swapped(parts[k], "ctx", k)
     place, combine_high, combine_low = route(
         layout, [gathered[k] for k in range(ctx_count)], width, choices
     )

time: 64.7 us -> 65.7 us (1.015)
  starting transfers between devices: 25.7 us -> 28.1 us
  waiting for transfers between devices: 16.5 us -> 15.1 us
    ppermute x27, starting transfers between devices: 25.7 us -> 28.1 us  [swapped(): return lax.ppermute(value, axes, pairs)]
    ppermute x27, waiting for transfers between devices: 16.5 us -> 15.1 us  [swapped(): return lax.ppermute(value, axes, pairs)]
  transfers between devices with their start and end apart: 27 -> 27, of which waited for: 16 -> 13; matrix products, arithmetic and copies ran while one was open for 0% -> 0% of each run, Pallas kernels for 28% -> 28%
where the time goes in v13:
time: 65.7 us; the launch traced here: 65.6 us
  starting transfers between devices  28.1 us (43%)
  Pallas kernels  22 us (33%)
  waiting for transfers between devices  15.1 us (23%)
    ppermute x27, starting transfers between devices, swapped(): return lax.ppermute(value, axes, pairs)  28.1 us
    ppermute x27, waiting for transfers between devices, swapped(): return lax.ppermute(value, axes, pairs)  15.1 us
    pallas_call x6, Pallas kernels, gate_up(): pl.pallas_call(kernel, out_shape=[out] * len(names), compiler_params=para...  8.72 us
    pallas_call x4, Pallas kernels, attend(): pl.pallas_call(functools.partial(attend_kernel, heads, scale, layout, k),...  5.05 us
    pallas_call x3, Pallas kernels, down(): pl.pallas_call(kernel, out_shape=[jax.ShapeDtypeStruct((rows, piece_width...  3.21 us
  transfers between devices with their start and end apart: 27, of which 13 were waited for; matrix products, arithmetic and copies ran while one was open for 0% of the time, Pallas kernels for 28%

profile of v13, /device:TPU:0, one launch (start us, length us, event | category | flops | bytes accessed | tf_op | source)
XLA Modules:
  0.0 65.6 jit_solution(762617638379335974)
XLA Ops:
  1.0 3.1 %collective-permute-start = (bf16[32,1152]{1,0:T(8,128)(2,1)S(1)}, bf16[32,1152]{1,0:T(8,128)(2,1)S(1)}, u32[]{:S(2)}, u32[]{:S(2)}) collective-permute-start(bf16[32,1152]{1,0:T(8,128)(2,1)S(1)} %pack.1.queries_ref.refs_0_), channel_id=1, source_target_pairs={{0,4},{4,0},{8,12},{12,8},{1,5},{5,1},{9,13},{13,9},{2,6},{6,2},{1... | collective-permute-start | bytes 221192 | tf_op jit(solution)/shard_map/ppermute | solution.py:97
  4.2 2.6 %collective-permute-start.2 = (bf16[32,1152]{1,0:T(8,128)(2,1)S(1)}, bf16[32,1152]{1,0:T(8,128)(2,1)S(1)}, u32[]{:S(2)}, u32[]{:S(2)}) collective-permute-start(bf16[32,1152]{1,0:T(8,128)(2,1)S(1)} %pack.1.queries_ref.refs_0_), channel_id=1, source_target_pairs={{0,8},{4,12},{8,0},{12,4},{1,9},{5,13},{9,1},{13,5},{2,10},{6,14},... | collective-permute-start | bytes 221192 | tf_op jit(solution)/shard_map/ppermute | solution.py:97
  7.4 1.3 %attend.5 = bf16[32,1152]{1,0:T(8,128)(2,1)S(1)} custom-call(bf16[32,1152]{1,0:T(8,128)(2,1)S(1)} %collective-permute-done.queries_ref.refs_1_, bf16[2048,128]{1,0:T(8,128)(2,1)S(1)} %bitcast.20, bf16[2048,128]{1,0:T(8,128)(2,1)S(1)} %bitcast.24, bf16[64,2048]{1,0:T(8,128)(2,1)S(1)} %sight.1.sight_ref, bf16[16,512,1536]{2,1,0:T(8,128)(2,1)} %weight_ref.14), custom_call_target="tpu_custom_call" | custom-call | flops 536870912 | bytes 1048576 | tf_op jit(solution)/shard_map/attend/pallas_call | solution.py:219
  8.7 1.7 %collective-permute-done.2.queries_ref.refs_2_ = bf16[32,1152]{1,0:T(8,128)(2,1)S(1)} collective-permute-done((bf16[32,1152]{1,0:T(8,128)(2,1)S(1)}, bf16[32,1152]{1,0:T(8,128)(2,1)S(1)}, u32[]{:S(2)}, u32[]{:S(2)}) %collective-permute-start.2) | collective-permute-done | bytes 73760 | tf_op jit(solution)/shard_map/ppermute | solution.py:97
  10.8 1.7 %collective-permute-start.1 = (bf16[32,1152]{1,0:T(8,128)(2,1)S(1)}, bf16[32,1152]{1,0:T(8,128)(2,1)S(1)}, u32[]{:S(2)}, u32[]{:S(2)}) collective-permute-start(bf16[32,1152]{1,0:T(8,128)(2,1)S(1)} %attend.5), channel_id=1, source_target_pairs={{0,4},{4,0},{8,12},{12,8},{1,5},{5,1},{9,13},{13,9},{2,6},{6,2},{1... | collective-permute-start | bytes 221192 | tf_op jit(solution)/shard_map/ppermute | solution.py:97
  13.7 1.8 %collective-permute-start.3 = (bf16[32,1152]{1,0:T(8,128)(2,1)S(1)}, bf16[32,1152]{1,0:T(8,128)(2,1)S(1)}, u32[]{:S(2)}, u32[]{:S(2)}) collective-permute-start(bf16[32,1152]{1,0:T(8,128)(2,1)S(1)} %attend.6), channel_id=1, source_target_pairs={{0,8},{4,12},{8,0},{12,4},{1,9},{5,13},{9,1},{13,5},{2,10},{6,14},... | collective-permute-start | bytes 221192 | tf_op jit(solution)/shard_map/ppermute | solution.py:97
  15.5 1.3 %attend.7 = bf16[32,1152]{1,0:T(8,128)(2,1)S(1)} custom-call(bf16[32,1152]{1,0:T(8,128)(2,1)S(1)} %collective-permute-done.4.queries_ref.refs_3_, bf16[2048,128]{1,0:T(8,128)(2,1)S(1)} %bitcast.22, bf16[2048,128]{1,0:T(8,128)(2,1)S(1)} %bitcast.26, bf16[64,2048]{1,0:T(8,128)(2,1)S(1)} %sight.1.sight_ref, bf16[16,512,1536]{2,1,0:T(8,128)(2,1)} %weight_ref.14), custom_call_target="tpu_custom_call" | custom-call | flops 536870912 | bytes 1048576 | tf_op jit(solution)/shard_map/attend/pallas_call | solution.py:219
  16.8 2.8 %collective-permute-start.5 = (bf16[32,1152]{1,0:T(8,128)(2,1)S(1)}, bf16[32,1152]{1,0:T(8,128)(2,1)S(1)}, u32[]{:S(2)}, u32[]{:S(2)}) collective-permute-start(bf16[32,1152]{1,0:T(8,128)(2,1)S(1)} %attend.7), channel_id=1, source_target_pairs={{0,12},{4,8},{8,4},{12,0},{1,13},{5,9},{9,5},{13,1},{2,14},{6,10},... | collective-permute-start | bytes 221192 | tf_op jit(solution)/shard_map/ppermute | solution.py:97
  21.6 1.4 %collective-permute-done.5.refs_3_ = bf16[32,1152]{1,0:T(8,128)(2,1)S(1)} collective-permute-done((bf16[32,1152]{1,0:T(8,128)(2,1)S(1)}, bf16[32,1152]{1,0:T(8,128)(2,1)S(1)}, u32[]{:S(2)}, u32[]{:S(2)}) %collective-permute-start.5) | collective-permute-done | bytes 73760 | tf_op jit(solution)/shard_map/ppermute | solution.py:97
  24.1 1.5 %collective-permute-start.7 = (bf16[32,512]{1,0:T(8,128)(2,1)S(1)}, bf16[32,512]{1,0:T(8,128)(2,1)S(1)}, u32[]{:S(2)}, u32[]{:S(2)}) collective-permute-start(bf16[32,512]{1,0:T(8,128)(2,1)S(1)} %get-tuple-element.40), channel_id=1, source_target_pairs={{0,2},{1,3},{2,0},{3,1},{4,6},{5,7},{6,4},{7,5},{8,10},{9,11},{10,... | collective-permute-start | bytes 98312 | tf_op jit(solution)/shard_map/ppermute | solution.py:97
  25.9 1.8 %collective-permute-done.6.refs_1_ = bf16[32,512]{1,0:T(8,128)(2,1)S(1)} collective-permute-done((bf16[32,512]{1,0:T(8,128)(2,1)S(1)}, bf16[32,512]{1,0:T(8,128)(2,1)S(1)}, u32[]{:S(2)}, u32[]{:S(2)}) %collective-permute-start.6) | collective-permute-done | bytes 32800 | tf_op jit(solution)/shard_map/ppermute | solution.py:97
  28.3 2.8 %collective-permute-start.13 = (bf16[32,640]{1,0:T(8,128)(2,1)S(1)}, bf16[32,640]{1,0:T(8,128)(2,1)S(1)}, u32[]{:S(2)}, u32[]{:S(2)}) collective-permute-start(bf16[32,640]{1,0:T(8,128)(2,1)S(1)} %get-tuple-element.45.refs_0_), channel_id=1, source_target_pairs={{0,12},{4,8},{8,4},{12,0},{1,13},{5,9},{9,5},{13,1},{2,14},{6,10},... | collective-permute-start | bytes 122888 | tf_op jit(solution)/shard_map/ppermute | solution.py:97
  32.3 2.1 %gate_up.6 = (bf16[64,1664]{1,0:T(8,128)(2,1)S(1)}, bf16[64,1664]{1,0:T(8,128)(2,1)S(1)}) custom-call(bf16[8,64,64]{2,1,0:T(8,128)(2,1)S(1)} %get-tuple-element.57.place_ref, bf16[16,512,1536]{2,1,0:T(8,128)(2,1)S(1)} %bitcast.10, bf16[32,640]{1,0:T(8,128)(2,1)S(1)} %get-tuple-element.45.refs_0_, bf16[32,640]{1,0:T(8,128)(2,1)S(1)} %collective-permute-done.9.refs_1_), custom_call_target="tpu_custom_call" | custom-call | flops 100663296 | bytes 196608 | tf_op jit(solution)/shard_map/gate_up/pallas_call | solution.py:376
  34.4 1.6 %collective-permute-done.12.refs_0_.refs_2_ = bf16[32,640]{1,0:T(8,128)(2,1)S(1)} collective-permute-done((bf16[32,640]{1,0:T(8,128)(2,1)S(1)}, bf16[32,640]{1,0:T(8,128)(2,1)S(1)}, u32[]{:S(2)}, u32[]{:S(2)}) %collective-permute-start.12) | collective-permute-done | bytes 40992 | tf_op jit(solution)/shard_map/ppermute | solution.py:97
  37.3 1.6 %collective-permute-start.11 = (bf16[64,1664]{1,0:T(8,128)(2,1)S(1)}, bf16[64,1664]{1,0:T(8,128)(2,1)S(1)}, u32[]{:S(2)}, u32[]{:S(2)}) collective-permute-start(bf16[64,1664]{1,0:T(8,128)(2,1)S(1)} %join.2), channel_id=1, source_target_pairs={{0,2},{2,0},{1,3},{3,1},{4,6},{6,4},{5,7},{7,5},{8,10},{10,8},{9,1... | collective-permute-start | bytes 638984 | tf_op jit(solution)/shard_map/ppermute | solution.py:97
  42.1 2.2 %gate_up.9 = (bf16[64,1664]{1,0:T(8,128)(2,1)S(1)}, bf16[64,1664]{1,0:T(8,128)(2,1)S(1)}) custom-call(bf16[8,64,64]{2,1,0:T(8,128)(2,1)S(1)} %get-tuple-element.57.place_ref, bf16[16,512,1536]{2,1,0:T(8,128)(2,1)S(1)} %bitcast.10, bf16[32,640]{1,0:T(8,128)(2,1)S(1)} %get-tuple-element.45.refs_0_, bf16[32,640]{1,0:T(8,128)(2,1)S(1)} %collective-permute-done.9.refs_1_, ...), custom_call_target="tpu_custom_call" | custom-call | flops 100663296 | bytes 196608 | tf_op jit(solution)/shard_map/gate_up/pallas_call | solution.py:376
  47.3 1.5 %collective-permute-start.16 = (bf16[64,768]{1,0:T(8,128)(2,1)S(1)}, bf16[64,768]{1,0:T(8,128)(2,1)S(1)}, u32[]{:S(2)}, u32[]{:S(2)}) collective-permute-start(bf16[64,768]{1,0:T(8,128)(2,1)S(1)} %hidden.2.refs_0_), channel_id=1, source_target_pairs={{0,2},{2,0},{1,3},{3,1},{4,6},{6,4},{5,7},{7,5},{8,10},{10,8},{9,1... | collective-permute-start | bytes 294920 | tf_op jit(solution)/shard_map/ppermute | solution.py:97
  49.9 1.6 %collective-permute-start.20 = (bf16[64,768]{1,0:T(8,128)(2,1)S(1)}, bf16[64,768]{1,0:T(8,128)(2,1)S(1)}, u32[]{:S(2)}, u32[]{:S(2)}) collective-permute-start(bf16[64,768]{1,0:T(8,128)(2,1)S(1)} %hidden.3.refs_1_), channel_id=1, source_target_pairs={{0,2},{2,0},{1,3},{3,1},{4,6},{6,4},{5,7},{7,5},{8,10},{10,8},{9,1... | collective-permute-start | bytes 294920 | tf_op jit(solution)/shard_map/ppermute | solution.py:97
  52.1 1.5 %down.3.refs_2_ = f32[128,512]{1,0:T(8,128)S(1)} custom-call(bf16[16,768,512]{2,1,0:T(8,128)(2,1)S(1)} %bitcast.19, bf16[8,64,64]{2,1,0:T(8,128)(2,1)S(1)} %get-tuple-element.43.high_ref, bf16[8,64,64]{2,1,0:T(8,128)(2,1)S(1)} %get-tuple-element.44.low_ref, bf16[64,768]{1,0:T(8,128)(2,1)S(1)} %hidden.2.refs_0_, bf16[64,768]{1,0:T(8,128)(2,1)S(1)} %hidden.3.refs_1_, ...), custom_call_target="tpu_custom_call" | custom-call | flops 100663296 | bytes 1048576 | tf_op jit(solution)/shard_map/down/pallas_call | solution.py:458
  53.7 1.5 %collective-permute-done.20.refs_1_ = bf16[64,768]{1,0:T(8,128)(2,1)S(1)} collective-permute-done((bf16[64,768]{1,0:T(8,128)(2,1)S(1)}, bf16[64,768]{1,0:T(8,128)(2,1)S(1)}, u32[]{:S(2)}, u32[]{:S(2)}) %collective-permute-start.20) | collective-permute-done | bytes 98336 | tf_op jit(solution)/shard_map/ppermute | solution.py:97
  57.3 2.9 %collective-permute-start.24 = (bf16[32,512]{1,0:T(8,128)(2,1)S(1)}, bf16[32,512]{1,0:T(8,128)(2,1)S(1)}, u32[]{:S(2)}, u32[]{:S(2)}) collective-permute-start(bf16[32,512]{1,0:T(8,128)(2,1)S(1)} %get-tuple-element.62), channel_id=1, source_target_pairs={{0,12},{4,8},{8,4},{12,0},{1,13},{5,9},{9,5},{13,1},{2,14},{6,10},... | collective-permute-start | bytes 98312 | tf_op jit(solution)/shard_map/ppermute | solution.py:97
  60.1 1.6 %collective-permute-start.26 = (bf16[32,512]{1,0:T(8,128)(2,1)S(1)}, bf16[32,512]{1,0:T(8,128)(2,1)S(1)}, u32[]{:S(2)}, u32[]{:S(2)}) collective-permute-start(bf16[32,512]{1,0:T(8,128)(2,1)S(1)} %get-tuple-element.64), channel_id=1, source_target_pairs={{0,4},{4,0},{8,12},{12,8},{1,5},{5,1},{9,13},{13,9},{2,6},{6,2},{1... | collective-permute-start | bytes 98312 | tf_op jit(solution)/shard_map/ppermute | solution.py:97
  61.7 1.4 %collective-permute-done.24.refs_1_ = bf16[32,512]{1,0:T(8,128)(2,1)S(1)} collective-permute-done((bf16[32,512]{1,0:T(8,128)(2,1)S(1)}, bf16[32,512]{1,0:T(8,128)(2,1)S(1)}, u32[]{:S(2)}, u32[]{:S(2)}) %collective-permute-start.24) | collective-permute-done | bytes 32800 | tf_op jit(solution)/shard_map/ppermute | solution.py:97
  63.2 1.8 %collective-permute-done.25.refs_2_ = bf16[32,512]{1,0:T(8,128)(2,1)S(1)} collective-permute-done((bf16[32,512]{1,0:T(8,128)(2,1)S(1)}, bf16[32,512]{1,0:T(8,128)(2,1)S(1)}, u32[]{:S(2)}, u32[]{:S(2)}) %collective-permute-start.25) | collective-permute-done | bytes 32800 | tf_op jit(solution)/shard_map/ppermute | solution.py:97
  (88 shorter events, 20.3 us)
Async XLA Ops:
  1.0 6.3 %collective-permute-start = (bf16[32,1152]{1,0:T(8,128)(2,1)S(1)}, bf16[32,1152]{1,0:T(8,128)(2,1)S(1)}, u32[]{:S(2)}, u32[]{:S(2)}) collective-permute-start(bf16[32,1152]{1,0:T(8,128)(2,1)S(1)} %pack.1.queries_ref.refs_0_), channel_id=1, source_target_pairs={{0,4},{4,0},{8,12},{12,8},{1,5},{5,1},{9,13},{13,9},{2,6},{6,2},{1... | collective-permute-start | bytes 221192 | tf_op jit(solution)/shard_map/ppermute | solution.py:97
  4.2 6.3 %collective-permute-start.2 = (bf16[32,1152]{1,0:T(8,128)(2,1)S(1)}, bf16[32,1152]{1,0:T(8,128)(2,1)S(1)}, u32[]{:S(2)}, u32[]{:S(2)}) collective-permute-start(bf16[32,1152]{1,0:T(8,128)(2,1)S(1)} %pack.1.queries_ref.refs_0_), channel_id=1, source_target_pairs={{0,8},{4,12},{8,0},{12,4},{1,9},{5,13},{9,1},{13,5},{2,10},{6,14},... | collective-permute-start | bytes 221192 | tf_op jit(solution)/shard_map/ppermute | solution.py:97
  10.4 5.1 %collective-permute-start.4 = (bf16[32,1152]{1,0:T(8,128)(2,1)S(1)}, bf16[32,1152]{1,0:T(8,128)(2,1)S(1)}, u32[]{:S(2)}, u32[]{:S(2)}) collective-permute-start(bf16[32,1152]{1,0:T(8,128)(2,1)S(1)} %collective-permute-done.2.queries_ref.refs_2_), channel_id=1, source_target_pairs={{0,4},{4,0},{8,12},{12,8},{1,5},{5,1},{9,13},{13,9},{2,6},{6,2},{1... | collective-permute-start | bytes 221192 | tf_op jit(solution)/shard_map/ppermute | solution.py:97
  10.8 10.8 %collective-permute-start.1 = (bf16[32,1152]{1,0:T(8,128)(2,1)S(1)}, bf16[32,1152]{1,0:T(8,128)(2,1)S(1)}, u32[]{:S(2)}, u32[]{:S(2)}) collective-permute-start(bf16[32,1152]{1,0:T(8,128)(2,1)S(1)} %attend.5), channel_id=1, source_target_pairs={{0,4},{4,0},{8,12},{12,8},{1,5},{5,1},{9,13},{13,9},{2,6},{6,2},{1... | collective-permute-start | bytes 221192 | tf_op jit(solution)/shard_map/ppermute | solution.py:97
  13.7 7.9 %collective-permute-start.3 = (bf16[32,1152]{1,0:T(8,128)(2,1)S(1)}, bf16[32,1152]{1,0:T(8,128)(2,1)S(1)}, u32[]{:S(2)}, u32[]{:S(2)}) collective-permute-start(bf16[32,1152]{1,0:T(8,128)(2,1)S(1)} %attend.6), channel_id=1, source_target_pairs={{0,8},{4,12},{8,0},{12,4},{1,9},{5,13},{9,1},{13,5},{2,10},{6,14},... | collective-permute-start | bytes 221192 | tf_op jit(solution)/shard_map/ppermute | solution.py:97
  16.8 6.2 %collective-permute-start.5 = (bf16[32,1152]{1,0:T(8,128)(2,1)S(1)}, bf16[32,1152]{1,0:T(8,128)(2,1)S(1)}, u32[]{:S(2)}, u32[]{:S(2)}) collective-permute-start(bf16[32,1152]{1,0:T(8,128)(2,1)S(1)} %attend.7), channel_id=1, source_target_pairs={{0,12},{4,8},{8,4},{12,0},{1,13},{5,9},{9,5},{13,1},{2,14},{6,10},... | collective-permute-start | bytes 221192 | tf_op jit(solution)/shard_map/ppermute | solution.py:97
  24.0 3.7 %collective-permute-start.6 = (bf16[32,512]{1,0:T(8,128)(2,1)S(1)}, bf16[32,512]{1,0:T(8,128)(2,1)S(1)}, u32[]{:S(2)}, u32[]{:S(2)}) collective-permute-start(bf16[32,512]{1,0:T(8,128)(2,1)S(1)} %get-tuple-element.39), channel_id=1, source_target_pairs={{0,3},{1,2},{2,1},{3,0},{4,7},{5,6},{6,5},{7,4},{8,11},{9,10},{10,... | collective-permute-start | bytes 98312 | tf_op jit(solution)/shard_map/ppermute | solution.py:97
  24.1 4.0 %collective-permute-start.7 = (bf16[32,512]{1,0:T(8,128)(2,1)S(1)}, bf16[32,512]{1,0:T(8,128)(2,1)S(1)}, u32[]{:S(2)}, u32[]{:S(2)}) collective-permute-start(bf16[32,512]{1,0:T(8,128)(2,1)S(1)} %get-tuple-element.40), channel_id=1, source_target_pairs={{0,2},{1,3},{2,0},{3,1},{4,6},{5,7},{6,4},{7,5},{8,10},{9,11},{10,... | collective-permute-start | bytes 98312 | tf_op jit(solution)/shard_map/ppermute | solution.py:97
  28.2 4.1 %collective-permute-start.9 = (bf16[32,640]{1,0:T(8,128)(2,1)S(1)}, bf16[32,640]{1,0:T(8,128)(2,1)S(1)}, u32[]{:S(2)}, u32[]{:S(2)}) collective-permute-start(bf16[32,640]{1,0:T(8,128)(2,1)S(1)} %get-tuple-element.45.refs_0_), channel_id=1, source_target_pairs={{0,4},{4,0},{8,12},{12,8},{1,5},{5,1},{9,13},{13,9},{2,6},{6,2},{1... | collective-permute-start | bytes 122888 | tf_op jit(solution)/shard_map/ppermute | solution.py:97
  28.3 6.1 %collective-permute-start.13 = (bf16[32,640]{1,0:T(8,128)(2,1)S(1)}, bf16[32,640]{1,0:T(8,128)(2,1)S(1)}, u32[]{:S(2)}, u32[]{:S(2)}) collective-permute-start(bf16[32,640]{1,0:T(8,128)(2,1)S(1)} %get-tuple-element.45.refs_0_), channel_id=1, source_target_pairs={{0,12},{4,8},{8,4},{12,0},{1,13},{5,9},{9,5},{13,1},{2,14},{6,10},... | collective-permute-start | bytes 122888 | tf_op jit(solution)/shard_map/ppermute | solution.py:97
  31.1 4.9 %collective-permute-start.12 = (bf16[32,640]{1,0:T(8,128)(2,1)S(1)}, bf16[32,640]{1,0:T(8,128)(2,1)S(1)}, u32[]{:S(2)}, u32[]{:S(2)}) collective-permute-start(bf16[32,640]{1,0:T(8,128)(2,1)S(1)} %get-tuple-element.45.refs_0_), channel_id=1, source_target_pairs={{0,8},{4,12},{8,0},{12,4},{1,9},{5,13},{9,1},{13,5},{2,10},{6,14},... | collective-permute-start | bytes 122888 | tf_op jit(solution)/shard_map/ppermute | solution.py:97
  34.4 2.7 %collective-permute-start.10 = (bf16[64,1664]{1,0:T(8,128)(2,1)S(1)}, bf16[64,1664]{1,0:T(8,128)(2,1)S(1)}, u32[]{:S(2)}, u32[]{:S(2)}) collective-permute-start(bf16[64,1664]{1,0:T(8,128)(2,1)S(1)} %get-tuple-element.47), channel_id=1, source_target_pairs={{0,1},{1,0},{2,3},{3,2},{4,5},{5,4},{6,7},{7,6},{8,9},{9,8},{10,11... | collective-permute-start | bytes 638984 | tf_op jit(solution)/shard_map/ppermute | solution.py:97
  37.1 2.9 %collective-permute-start.14 = (bf16[64,1664]{1,0:T(8,128)(2,1)S(1)}, bf16[64,1664]{1,0:T(8,128)(2,1)S(1)}, u32[]{:S(2)}, u32[]{:S(2)}) collective-permute-start(bf16[64,1664]{1,0:T(8,128)(2,1)S(1)} %gate_up.8), channel_id=1, source_target_pairs={{0,1},{1,0},{2,3},{3,2},{4,5},{5,4},{6,7},{7,6},{8,9},{9,8},{10,11... | collective-permute-start | bytes 638984 | tf_op jit(solution)/shard_map/ppermute | solution.py:97
  37.3 8.1 %collective-permute-start.11 = (bf16[64,1664]{1,0:T(8,128)(2,1)S(1)}, bf16[64,1664]{1,0:T(8,128)(2,1)S(1)}, u32[]{:S(2)}, u32[]{:S(2)}) collective-permute-start(bf16[64,1664]{1,0:T(8,128)(2,1)S(1)} %join.2), channel_id=1, source_target_pairs={{0,2},{2,0},{1,3},{3,1},{4,6},{6,4},{5,7},{7,5},{8,10},{10,8},{9,1... | collective-permute-start | bytes 638984 | tf_op jit(solution)/shard_map/ppermute | solution.py:97
  41.3 4.1 %collective-permute-start.15 = (bf16[64,1664]{1,0:T(8,128)(2,1)S(1)}, bf16[64,1664]{1,0:T(8,128)(2,1)S(1)}, u32[]{:S(2)}, u32[]{:S(2)}) collective-permute-start(bf16[64,1664]{1,0:T(8,128)(2,1)S(1)} %gate_up.10), channel_id=1, source_target_pairs={{0,1},{1,0},{2,3},{3,2},{4,5},{5,4},{6,7},{7,6},{8,9},{9,8},{10,11... | collective-permute-start | bytes 638984 | tf_op jit(solution)/shard_map/ppermute | solution.py:97
  41.6 8.1 %collective-permute-start.18 = (bf16[64,1664]{1,0:T(8,128)(2,1)S(1)}, bf16[64,1664]{1,0:T(8,128)(2,1)S(1)}, u32[]{:S(2)}, u32[]{:S(2)}) collective-permute-start(bf16[64,1664]{1,0:T(8,128)(2,1)S(1)} %join.3), channel_id=1, source_target_pairs={{0,2},{2,0},{1,3},{3,1},{4,6},{6,4},{5,7},{7,5},{8,10},{10,8},{9,1... | collective-permute-start | bytes 638984 | tf_op jit(solution)/shard_map/ppermute | solution.py:97
  46.8 2.8 %collective-permute-start.19 = (bf16[64,1664]{1,0:T(8,128)(2,1)S(1)}, bf16[64,1664]{1,0:T(8,128)(2,1)S(1)}, u32[]{:S(2)}, u32[]{:S(2)}) collective-permute-start(bf16[64,1664]{1,0:T(8,128)(2,1)S(1)} %gate_up.11), channel_id=1, source_target_pairs={{0,1},{1,0},{2,3},{3,2},{4,5},{5,4},{6,7},{7,6},{8,9},{9,8},{10,11... | collective-permute-start | bytes 638984 | tf_op jit(solution)/shard_map/ppermute | solution.py:97
  46.8 5.3 %collective-permute-start.21 = (bf16[64,768]{1,0:T(8,128)(2,1)S(1)}, bf16[64,768]{1,0:T(8,128)(2,1)S(1)}, u32[]{:S(2)}, u32[]{:S(2)}) collective-permute-start(bf16[64,768]{1,0:T(8,128)(2,1)S(1)} %hidden.2.refs_0_), channel_id=1, source_target_pairs={{0,1},{1,0},{2,3},{3,2},{4,5},{5,4},{6,7},{7,6},{8,9},{9,8},{10,11... | collective-permute-start | bytes 294920 | tf_op jit(solution)/shard_map/ppermute | solution.py:97
  47.3 4.8 %collective-permute-start.16 = (bf16[64,768]{1,0:T(8,128)(2,1)S(1)}, bf16[64,768]{1,0:T(8,128)(2,1)S(1)}, u32[]{:S(2)}, u32[]{:S(2)}) collective-permute-start(bf16[64,768]{1,0:T(8,128)(2,1)S(1)} %hidden.2.refs_0_), channel_id=1, source_target_pairs={{0,2},{2,0},{1,3},{3,1},{4,6},{6,4},{5,7},{7,5},{8,10},{10,8},{9,1... | collective-permute-start | bytes 294920 | tf_op jit(solution)/shard_map/ppermute | solution.py:97
  49.9 5.2 %collective-permute-start.20 = (bf16[64,768]{1,0:T(8,128)(2,1)S(1)}, bf16[64,768]{1,0:T(8,128)(2,1)S(1)}, u32[]{:S(2)}, u32[]{:S(2)}) collective-permute-start(bf16[64,768]{1,0:T(8,128)(2,1)S(1)} %hidden.3.refs_1_), channel_id=1, source_target_pairs={{0,2},{2,0},{1,3},{3,1},{4,6},{6,4},{5,7},{7,5},{8,10},{10,8},{9,1... | collective-permute-start | bytes 294920 | tf_op jit(solution)/shard_map/ppermute | solution.py:97
  52.1 3.9 %collective-permute-start.17 = (bf16[64,768]{1,0:T(8,128)(2,1)S(1)}, bf16[64,768]{1,0:T(8,128)(2,1)S(1)}, u32[]{:S(2)}, u32[]{:S(2)}) collective-permute-start(bf16[64,768]{1,0:T(8,128)(2,1)S(1)} %collective-permute-done.16.refs_0_), channel_id=1, source_target_pairs={{0,1},{1,0},{2,3},{3,2},{4,5},{5,4},{6,7},{7,6},{8,9},{9,8},{10,11... | collective-permute-start | bytes 294920 | tf_op jit(solution)/shard_map/ppermute | solution.py:97
  57.3 5.9 %collective-permute-start.24 = (bf16[32,512]{1,0:T(8,128)(2,1)S(1)}, bf16[32,512]{1,0:T(8,128)(2,1)S(1)}, u32[]{:S(2)}, u32[]{:S(2)}) collective-permute-start(bf16[32,512]{1,0:T(8,128)(2,1)S(1)} %get-tuple-element.62), channel_id=1, source_target_pairs={{0,12},{4,8},{8,4},{12,0},{1,13},{5,9},{9,5},{13,1},{2,14},{6,10},... | collective-permute-start | bytes 98312 | tf_op jit(solution)/shard_map/ppermute | solution.py:97
  60.1 4.8 %collective-permute-start.25 = (bf16[32,512]{1,0:T(8,128)(2,1)S(1)}, bf16[32,512]{1,0:T(8,128)(2,1)S(1)}, u32[]{:S(2)}, u32[]{:S(2)}) collective-permute-start(bf16[32,512]{1,0:T(8,128)(2,1)S(1)} %get-tuple-element.63), channel_id=1, source_target_pairs={{0,8},{4,12},{8,0},{12,4},{1,9},{5,13},{9,1},{13,5},{2,10},{6,14},... | collective-permute-start | bytes 98312 | tf_op jit(solution)/shard_map/ppermute | solution.py:97
  60.1 4.8 %collective-permute-start.26 = (bf16[32,512]{1,0:T(8,128)(2,1)S(1)}, bf16[32,512]{1,0:T(8,128)(2,1)S(1)}, u32[]{:S(2)}, u32[]{:S(2)}) collective-permute-start(bf16[32,512]{1,0:T(8,128)(2,1)S(1)} %get-tuple-element.64), channel_id=1, source_target_pairs={{0,4},{4,0},{8,12},{12,8},{1,5},{5,1},{9,13},{13,9},{2,6},{6,2},{1... | collective-permute-start | bytes 98312 | tf_op jit(solution)/shard_map/ppermute | solution.py:97
  (19 other events, 173.4 us)

commit v14 on v11

--- a/solution.py
+++ b/solution.py
@@ -272,16 +272,11 @@
 
 def mix_kernel(residual_ref, gain_ref, *refs):
     parts_refs, (mixed_ref, sent_ref) = refs[:-2], refs[-2:]
-    rows, width = mixed_ref.shape
     mixed = residual_ref[...].astype(f32)
     for ref in parts_refs:
         mixed = mixed + ref[...].astype(f32)
     mixed_ref[...] = mixed
-    sent_ref[:, :width] = (mixed * gain_ref[...].astype(f32)).astype(bf16)
-    high, low = in_two(jnp.sum(mixed * mixed, axis=1, keepdims=True))
-    lane = lane_ids((rows, LANES))
-    squares = jnp.where(lane == 0, high, jnp.where(lane == 1, low, 0.0))
-    sent_ref[:, width:] = squares.astype(bf16)
+    sent_ref[...] = (mixed * gain_ref[...].astype(f32)).astype(bf16)
 
 
 def mix(residual, gain, parts):
@@ -290,7 +285,7 @@
         mix_kernel,
         out_shape=(
             jax.ShapeDtypeStruct((rows, width), f32),
-            jax.ShapeDtypeStruct((rows, width + LANES), bf16),
+            jax.ShapeDtypeStruct((rows, width), bf16),
         ),
         compiler_params=params(4),
         name="mix",
@@ -350,13 +345,14 @@
     return jnp.where(lane == 0, high, jnp.where(lane == 1, low, 0.0))
 
 
-def gate_up(names, layout, place, sources, weight):
+def gate_up(names, layout, place, sources, weight, gain):
     _, width, ff_pair = weight.shape
     each = layout.rows // layout.experts
     cells = sorted({name[2] for name in names})
     count = len(sources[0])
 
-    def kernel(place_ref, weight_ref, *refs):
+    def kernel(place_ref, gain_ref, weight_ref, *refs):
+        inverse_gain = 1.0 / gain_ref[...].astype(f32)
         for name, out_ref in zip(names, refs[len(cells) * count :]):
             at, first = layout.cell(*name)
             turn = cells.index(name[2])
@@ -368,9 +364,12 @@
             picked = picked.astype(bf16)
             for i in range(layout.experts):
                 here = slice(i * each, (i + 1) * each)
-                product = dot(picked[here, :width], weight_ref[first + i])
-                out_ref[here, :ff_pair] = product.astype(bf16)
-            out_ref[:, ff_pair:] = picked[:, width:]
+                out_ref[here, :ff_pair] = dot(picked[here, :], weight_ref[first + i]).astype(bf16)
+            mixed = picked.astype(f32) * inverse_gain
+            high, low = in_two(jnp.sum(mixed * mixed, axis=1, keepdims=True))
+            lane = lane_ids((layout.rows, LANES))
+            squares = jnp.where(lane == 0, high, jnp.where(lane == 1, low, 0.0))
+            out_ref[:, ff_pair:] = squares.astype(bf16)
 
     out = jax.ShapeDtypeStruct((layout.rows, ff_pair + LANES), bf16)
     return pl.pallas_call(
@@ -379,7 +378,7 @@
         compiler_params=params(8),
         cost_estimate=cost(2 * layout.rows * width * ff_pair, 2 * layout.rows * ff_pair),
         name="gate_up",
-    )(place, weight, *[value for cell in cells for value in sources[cell]])
+    )(place, gain, weight, *[value for cell in cells for value in sources[cell]])
 
 
 def join_kernel(left_ref, right_ref, out_ref):
@@ -552,7 +551,7 @@
     sources = [[rows[k] for k in range(half * i, half * (i + 1))] for i in range(CELLS)]
 
     def first_half(*names):
-        return gate_up(names, layout, place, sources, gate_up_weight)
+        return gate_up(names, layout, place, sources, gate_up_weight, norm_gain[None, :])
 
     crossed = [[] for _ in range(CELLS)]
     for k in far_first(exp_count):

time: 64.7 us -> 64.2 us (level)
  transfers between devices with their start and end apart: 27 -> 27, of which waited for: 16 -> 15; matrix products, arithmetic and copies ran while one was open for 0% -> 0% of each run, Pallas kernels for 28% -> 29%
where the time goes in v14:
time: 64.2 us; the launch traced here: 64 us
  starting transfers between devices  25.9 us (40%)
  Pallas kernels  21.8 us (34%)
  waiting for transfers between devices  15.9 us (25%)
    ppermute x27, starting transfers between devices, swapped(): return lax.ppermute(value, axes, pairs)  25.9 us
    ppermute x27, waiting for transfers between devices, swapped(): return lax.ppermute(value, axes, pairs)  15.9 us
    pallas_call x6, Pallas kernels, gate_up(): pl.pallas_call(kernel, out_shape=[out] * len(names), compiler_params=para...  8.61 us
    pallas_call x4, Pallas kernels, attend(): pl.pallas_call(functools.partial(attend_kernel, heads, scale, layout, k),...  5.04 us
    pallas_call x3, Pallas kernels, down(): pl.pallas_call(kernel, out_shape=[jax.ShapeDtypeStruct((rows, piece_width...  3.24 us
  transfers between devices with their start and end apart: 27, of which 15 were waited for; matrix products, arithmetic and copies ran while one was open for 0% of the time, Pallas kernels for 29%

profile of v14, /device:TPU:0, one launch (start us, length us, event | category | flops | bytes accessed | tf_op | source)
XLA Modules:
  0.0 64.0 jit_solution(4502742901228870070)
XLA Ops:
  1.0 3.1 %collective-permute-start = (bf16[32,1152]{1,0:T(8,128)(2,1)S(1)}, bf16[32,1152]{1,0:T(8,128)(2,1)S(1)}, u32[]{:S(2)}, u32[]{:S(2)}) collective-permute-start(bf16[32,1152]{1,0:T(8,128)(2,1)S(1)} %pack.1.queries_ref.refs_0_), channel_id=1, source_target_pairs={{0,4},{4,0},{8,12},{12,8},{1,5},{5,1},{9,13},{13,9},{2,6},{6,2},{1... | collective-permute-start | bytes 221192 | tf_op jit(solution)/shard_map/ppermute | solution.py:97
  4.2 2.6 %collective-permute-start.2 = (bf16[32,1152]{1,0:T(8,128)(2,1)S(1)}, bf16[32,1152]{1,0:T(8,128)(2,1)S(1)}, u32[]{:S(2)}, u32[]{:S(2)}) collective-permute-start(bf16[32,1152]{1,0:T(8,128)(2,1)S(1)} %pack.1.queries_ref.refs_0_), channel_id=1, source_target_pairs={{0,8},{4,12},{8,0},{12,4},{1,9},{5,13},{9,1},{13,5},{2,10},{6,14},... | collective-permute-start | bytes 221192 | tf_op jit(solution)/shard_map/ppermute | solution.py:97
  7.4 1.3 %attend.5 = bf16[32,1152]{1,0:T(8,128)(2,1)S(1)} custom-call(bf16[32,1152]{1,0:T(8,128)(2,1)S(1)} %collective-permute-done.queries_ref.refs_1_, bf16[2048,128]{1,0:T(8,128)(2,1)S(1)} %bitcast.20, bf16[2048,128]{1,0:T(8,128)(2,1)S(1)} %bitcast.24, bf16[64,2048]{1,0:T(8,128)(2,1)S(1)} %sight.1.sight_ref, bf16[16,512,1536]{2,1,0:T(8,128)(2,1)} %weight_ref.14), custom_call_target="tpu_custom_call" | custom-call | flops 536870912 | bytes 1048576 | tf_op jit(solution)/shard_map/attend/pallas_call | solution.py:219
  9.8 2.1 %collective-permute-done.2.queries_ref.refs_2_ = bf16[32,1152]{1,0:T(8,128)(2,1)S(1)} collective-permute-done((bf16[32,1152]{1,0:T(8,128)(2,1)S(1)}, bf16[32,1152]{1,0:T(8,128)(2,1)S(1)}, u32[]{:S(2)}, u32[]{:S(2)}) %collective-permute-start.2) | collective-permute-done | bytes 73760 | tf_op jit(solution)/shard_map/ppermute | solution.py:97
  11.9 1.3 %attend.6 = bf16[32,1152]{1,0:T(8,128)(2,1)S(1)} custom-call(bf16[32,1152]{1,0:T(8,128)(2,1)S(1)} %collective-permute-done.2.queries_ref.refs_2_, bf16[2048,128]{1,0:T(8,128)(2,1)S(1)} %bitcast.21, bf16[2048,128]{1,0:T(8,128)(2,1)S(1)} %bitcast.25, bf16[64,2048]{1,0:T(8,128)(2,1)S(1)} %sight.1.sight_ref, bf16[16,512,1536]{2,1,0:T(8,128)(2,1)} %weight_ref.14), custom_call_target="tpu_custom_call" | custom-call | flops 536870912 | bytes 1048576 | tf_op jit(solution)/shard_map/attend/pallas_call | solution.py:219
  13.2 1.3 %collective-permute-start.3 = (bf16[32,1152]{1,0:T(8,128)(2,1)S(1)}, bf16[32,1152]{1,0:T(8,128)(2,1)S(1)}, u32[]{:S(2)}, u32[]{:S(2)}) collective-permute-start(bf16[32,1152]{1,0:T(8,128)(2,1)S(1)} %attend.6), channel_id=1, source_target_pairs={{0,8},{4,12},{8,0},{12,4},{1,9},{5,13},{9,1},{13,5},{2,10},{6,14},... | collective-permute-start | bytes 221192 | tf_op jit(solution)/shard_map/ppermute | solution.py:97
  14.5 1.3 %attend.7 = bf16[32,1152]{1,0:T(8,128)(2,1)S(1)} custom-call(bf16[32,1152]{1,0:T(8,128)(2,1)S(1)} %collective-permute-done.4.queries_ref.refs_3_, bf16[2048,128]{1,0:T(8,128)(2,1)S(1)} %bitcast.22, bf16[2048,128]{1,0:T(8,128)(2,1)S(1)} %bitcast.26, bf16[64,2048]{1,0:T(8,128)(2,1)S(1)} %sight.1.sight_ref, bf16[16,512,1536]{2,1,0:T(8,128)(2,1)} %weight_ref.14), custom_call_target="tpu_custom_call" | custom-call | flops 536870912 | bytes 1048576 | tf_op jit(solution)/shard_map/attend/pallas_call | solution.py:219
  15.8 2.2 %collective-permute-start.5 = (bf16[32,1152]{1,0:T(8,128)(2,1)S(1)}, bf16[32,1152]{1,0:T(8,128)(2,1)S(1)}, u32[]{:S(2)}, u32[]{:S(2)}) collective-permute-start(bf16[32,1152]{1,0:T(8,128)(2,1)S(1)} %attend.7), channel_id=1, source_target_pairs={{0,12},{4,8},{8,4},{12,0},{1,13},{5,9},{9,5},{13,1},{2,14},{6,10},... | collective-permute-start | bytes 221192 | tf_op jit(solution)/shard_map/ppermute | solution.py:97
  18.0 1.3 %attend.4.refs_0_ = bf16[32,1152]{1,0:T(8,128)(2,1)S(1)} custom-call(bf16[32,1152]{1,0:T(8,128)(2,1)S(1)} %pack.1.queries_ref.refs_0_, bf16[2048,128]{1,0:T(8,128)(2,1)S(1)} %bitcast.23, bf16[2048,128]{1,0:T(8,128)(2,1)S(1)} %bitcast.27, bf16[64,2048]{1,0:T(8,128)(2,1)S(1)} %sight.1.sight_ref, bf16[16,512,1536]{2,1,0:T(8,128)(2,1)} %weight_ref.14), custom_call_target="tpu_custom_call" | custom-call | flops 536870912 | bytes 1048576 | tf_op jit(solution)/shard_map/attend/pallas_call | solution.py:219
  20.1 2.0 %collective-permute-done.5.refs_3_ = bf16[32,1152]{1,0:T(8,128)(2,1)S(1)} collective-permute-done((bf16[32,1152]{1,0:T(8,128)(2,1)S(1)}, bf16[32,1152]{1,0:T(8,128)(2,1)S(1)}, u32[]{:S(2)}, u32[]{:S(2)}) %collective-permute-start.5) | collective-permute-done | bytes 73760 | tf_op jit(solution)/shard_map/ppermute | solution.py:97
  23.2 1.5 %collective-permute-start.7 = (bf16[32,512]{1,0:T(8,128)(2,1)S(1)}, bf16[32,512]{1,0:T(8,128)(2,1)S(1)}, u32[]{:S(2)}, u32[]{:S(2)}) collective-permute-start(bf16[32,512]{1,0:T(8,128)(2,1)S(1)} %get-tuple-element.38), channel_id=1, source_target_pairs={{0,2},{1,3},{2,0},{3,1},{4,6},{5,7},{6,4},{7,5},{8,10},{9,11},{10,... | collective-permute-start | bytes 98312 | tf_op jit(solution)/shard_map/ppermute | solution.py:97
  25.0 1.8 %collective-permute-done.6.refs_1_ = bf16[32,512]{1,0:T(8,128)(2,1)S(1)} collective-permute-done((bf16[32,512]{1,0:T(8,128)(2,1)S(1)}, bf16[32,512]{1,0:T(8,128)(2,1)S(1)}, u32[]{:S(2)}, u32[]{:S(2)}) %collective-permute-start.6) | collective-permute-done | bytes 32800 | tf_op jit(solution)/shard_map/ppermute | solution.py:97
  27.2 1.4 %collective-permute-start.9 = (bf16[32,512]{1,0:T(8,128)(2,1)S(1)}, bf16[32,512]{1,0:T(8,128)(2,1)S(1)}, u32[]{:S(2)}, u32[]{:S(2)}) collective-permute-start(bf16[32,512]{1,0:T(8,128)(2,1)S(1)} %get-tuple-element.43.refs_0_), channel_id=1, source_target_pairs={{0,4},{4,0},{8,12},{12,8},{1,5},{5,1},{9,13},{13,9},{2,6},{6,2},{1... | collective-permute-start | bytes 98312 | tf_op jit(solution)/shard_map/ppermute | solution.py:97
  29.4 1.3 %collective-permute-start.12 = (bf16[32,512]{1,0:T(8,128)(2,1)S(1)}, bf16[32,512]{1,0:T(8,128)(2,1)S(1)}, u32[]{:S(2)}, u32[]{:S(2)}) collective-permute-start(bf16[32,512]{1,0:T(8,128)(2,1)S(1)} %get-tuple-element.43.refs_0_), channel_id=1, source_target_pairs={{0,8},{4,12},{8,0},{12,4},{1,9},{5,13},{9,1},{13,5},{2,10},{6,14},... | collective-permute-start | bytes 98312 | tf_op jit(solution)/shard_map/ppermute | solution.py:97
  31.3 2.0 %gate_up.6 = (bf16[64,1664]{1,0:T(8,128)(2,1)S(1)}, bf16[64,1664]{1,0:T(8,128)(2,1)S(1)}) custom-call(bf16[8,64,64]{2,1,0:T(8,128)(2,1)S(1)} %get-tuple-element.55.place_ref, bf16[1,512]{1,0:T(2,128)(2,1)S(1)} %broadcast_in_dim.8.gain_ref, bf16[16,512,1536]{2,1,0:T(8,128)(2,1)S(1)} %bitcast.10, bf16[32,512]{1,0:T(8,128)(2,1)S(1)} %get-tuple-element.43.refs_0_, ...), custom_call_target="tpu_custom_call" | custom-call | flops 100663296 | bytes 196608 | tf_op jit(solution)/shard_map/gate_up/pallas_call | solution.py:375
  36.4 1.4 %collective-permute-start.11 = (bf16[64,1664]{1,0:T(8,128)(2,1)S(1)}, bf16[64,1664]{1,0:T(8,128)(2,1)S(1)}, u32[]{:S(2)}, u32[]{:S(2)}) collective-permute-start(bf16[64,1664]{1,0:T(8,128)(2,1)S(1)} %join.2), channel_id=1, source_target_pairs={{0,2},{2,0},{1,3},{3,1},{4,6},{6,4},{5,7},{7,5},{8,10},{10,8},{9,1... | collective-permute-start | bytes 638984 | tf_op jit(solution)/shard_map/ppermute | solution.py:97
  41.2 2.2 %gate_up.9 = (bf16[64,1664]{1,0:T(8,128)(2,1)S(1)}, bf16[64,1664]{1,0:T(8,128)(2,1)S(1)}) custom-call(bf16[8,64,64]{2,1,0:T(8,128)(2,1)S(1)} %get-tuple-element.55.place_ref, bf16[1,512]{1,0:T(2,128)(2,1)S(1)} %broadcast_in_dim.8.gain_ref, bf16[16,512,1536]{2,1,0:T(8,128)(2,1)S(1)} %bitcast.10, bf16[32,512]{1,0:T(8,128)(2,1)S(1)} %get-tuple-element.43.refs_0_, ...), custom_call_target="tpu_custom_call" | custom-call | flops 100663296 | bytes 196608 | tf_op jit(solution)/shard_map/gate_up/pallas_call | solution.py:375
  46.4 1.4 %collective-permute-start.16 = (bf16[64,768]{1,0:T(8,128)(2,1)S(1)}, bf16[64,768]{1,0:T(8,128)(2,1)S(1)}, u32[]{:S(2)}, u32[]{:S(2)}) collective-permute-start(bf16[64,768]{1,0:T(8,128)(2,1)S(1)} %hidden.2.refs_0_), channel_id=1, source_target_pairs={{0,2},{2,0},{1,3},{3,1},{4,6},{6,4},{5,7},{7,5},{8,10},{10,8},{9,1... | collective-permute-start | bytes 294920 | tf_op jit(solution)/shard_map/ppermute | solution.py:97
  49.0 1.4 %collective-permute-start.20 = (bf16[64,768]{1,0:T(8,128)(2,1)S(1)}, bf16[64,768]{1,0:T(8,128)(2,1)S(1)}, u32[]{:S(2)}, u32[]{:S(2)}) collective-permute-start(bf16[64,768]{1,0:T(8,128)(2,1)S(1)} %hidden.3.refs_1_), channel_id=1, source_target_pairs={{0,2},{2,0},{1,3},{3,1},{4,6},{6,4},{5,7},{7,5},{8,10},{10,8},{9,1... | collective-permute-start | bytes 294920 | tf_op jit(solution)/shard_map/ppermute | solution.py:97
  51.2 1.6 %down.3.refs_2_ = f32[128,512]{1,0:T(8,128)S(1)} custom-call(bf16[16,768,512]{2,1,0:T(8,128)(2,1)S(1)} %bitcast.19, bf16[8,64,64]{2,1,0:T(8,128)(2,1)S(1)} %get-tuple-element.41.high_ref, bf16[8,64,64]{2,1,0:T(8,128)(2,1)S(1)} %get-tuple-element.42.low_ref, bf16[64,768]{1,0:T(8,128)(2,1)S(1)} %hidden.2.refs_0_, bf16[64,768]{1,0:T(8,128)(2,1)S(1)} %hidden.3.refs_1_, ...), custom_call_target="tpu_custom_call" | custom-call | flops 100663296 | bytes 1048576 | tf_op jit(solution)/shard_map/down/pallas_call | solution.py:457
  52.8 1.5 %collective-permute-done.20.refs_1_ = bf16[64,768]{1,0:T(8,128)(2,1)S(1)} collective-permute-done((bf16[64,768]{1,0:T(8,128)(2,1)S(1)}, bf16[64,768]{1,0:T(8,128)(2,1)S(1)}, u32[]{:S(2)}, u32[]{:S(2)}) %collective-permute-start.20) | collective-permute-done | bytes 98336 | tf_op jit(solution)/shard_map/ppermute | solution.py:97
  56.4 2.2 %collective-permute-start.24 = (bf16[32,512]{1,0:T(8,128)(2,1)S(1)}, bf16[32,512]{1,0:T(8,128)(2,1)S(1)}, u32[]{:S(2)}, u32[]{:S(2)}) collective-permute-start(bf16[32,512]{1,0:T(8,128)(2,1)S(1)} %get-tuple-element.60), channel_id=1, source_target_pairs={{0,12},{4,8},{8,4},{12,0},{1,13},{5,9},{9,5},{13,1},{2,14},{6,10},... | collective-permute-start | bytes 98312 | tf_op jit(solution)/shard_map/ppermute | solution.py:97
  58.6 2.2 %collective-permute-start.26 = (bf16[32,512]{1,0:T(8,128)(2,1)S(1)}, bf16[32,512]{1,0:T(8,128)(2,1)S(1)}, u32[]{:S(2)}, u32[]{:S(2)}) collective-permute-start(bf16[32,512]{1,0:T(8,128)(2,1)S(1)} %get-tuple-element.62), channel_id=1, source_target_pairs={{0,4},{4,0},{8,12},{12,8},{1,5},{5,1},{9,13},{13,9},{2,6},{6,2},{1... | collective-permute-start | bytes 98312 | tf_op jit(solution)/shard_map/ppermute | solution.py:97
  60.8 1.3 %collective-permute-done.24.refs_1_ = bf16[32,512]{1,0:T(8,128)(2,1)S(1)} collective-permute-done((bf16[32,512]{1,0:T(8,128)(2,1)S(1)}, bf16[32,512]{1,0:T(8,128)(2,1)S(1)}, u32[]{:S(2)}, u32[]{:S(2)}) %collective-permute-start.24) | collective-permute-done | bytes 32800 | tf_op jit(solution)/shard_map/ppermute | solution.py:97
  (88 shorter events, 22.2 us)
Async XLA Ops:
  1.0 6.3 %collective-permute-start = (bf16[32,1152]{1,0:T(8,128)(2,1)S(1)}, bf16[32,1152]{1,0:T(8,128)(2,1)S(1)}, u32[]{:S(2)}, u32[]{:S(2)}) collective-permute-start(bf16[32,1152]{1,0:T(8,128)(2,1)S(1)} %pack.1.queries_ref.refs_0_), channel_id=1, source_target_pairs={{0,4},{4,0},{8,12},{12,8},{1,5},{5,1},{9,13},{13,9},{2,6},{6,2},{1... | collective-permute-start | bytes 221192 | tf_op jit(solution)/shard_map/ppermute | solution.py:97
  4.2 7.8 %collective-permute-start.2 = (bf16[32,1152]{1,0:T(8,128)(2,1)S(1)}, bf16[32,1152]{1,0:T(8,128)(2,1)S(1)}, u32[]{:S(2)}, u32[]{:S(2)}) collective-permute-start(bf16[32,1152]{1,0:T(8,128)(2,1)S(1)} %pack.1.queries_ref.refs_0_), channel_id=1, source_target_pairs={{0,8},{4,12},{8,0},{12,4},{1,9},{5,13},{9,1},{13,5},{2,10},{6,14},... | collective-permute-start | bytes 221192 | tf_op jit(solution)/shard_map/ppermute | solution.py:97
  6.7 7.8 %collective-permute-start.4 = (bf16[32,1152]{1,0:T(8,128)(2,1)S(1)}, bf16[32,1152]{1,0:T(8,128)(2,1)S(1)}, u32[]{:S(2)}, u32[]{:S(2)}) collective-permute-start(bf16[32,1152]{1,0:T(8,128)(2,1)S(1)} %pack.1.queries_ref.refs_0_), channel_id=1, source_target_pairs={{0,12},{4,8},{8,4},{12,0},{1,13},{5,9},{9,5},{13,1},{2,14},{6,10},... | collective-permute-start | bytes 221192 | tf_op jit(solution)/shard_map/ppermute | solution.py:97
  8.7 11.3 %collective-permute-start.1 = (bf16[32,1152]{1,0:T(8,128)(2,1)S(1)}, bf16[32,1152]{1,0:T(8,128)(2,1)S(1)}, u32[]{:S(2)}, u32[]{:S(2)}) collective-permute-start(bf16[32,1152]{1,0:T(8,128)(2,1)S(1)} %attend.5), channel_id=1, source_target_pairs={{0,4},{4,0},{8,12},{12,8},{1,5},{5,1},{9,13},{13,9},{2,6},{6,2},{1... | collective-permute-start | bytes 221192 | tf_op jit(solution)/shard_map/ppermute | solution.py:97
  13.2 6.9 %collective-permute-start.3 = (bf16[32,1152]{1,0:T(8,128)(2,1)S(1)}, bf16[32,1152]{1,0:T(8,128)(2,1)S(1)}, u32[]{:S(2)}, u32[]{:S(2)}) collective-permute-start(bf16[32,1152]{1,0:T(8,128)(2,1)S(1)} %attend.6), channel_id=1, source_target_pairs={{0,8},{4,12},{8,0},{12,4},{1,9},{5,13},{9,1},{13,5},{2,10},{6,14},... | collective-permute-start | bytes 221192 | tf_op jit(solution)/shard_map/ppermute | solution.py:97
  15.8 6.3 %collective-permute-start.5 = (bf16[32,1152]{1,0:T(8,128)(2,1)S(1)}, bf16[32,1152]{1,0:T(8,128)(2,1)S(1)}, u32[]{:S(2)}, u32[]{:S(2)}) collective-permute-start(bf16[32,1152]{1,0:T(8,128)(2,1)S(1)} %attend.7), channel_id=1, source_target_pairs={{0,12},{4,8},{8,4},{12,0},{1,13},{5,9},{9,5},{13,1},{2,14},{6,10},... | collective-permute-start | bytes 221192 | tf_op jit(solution)/shard_map/ppermute | solution.py:97
  23.1 3.7 %collective-permute-start.6 = (bf16[32,512]{1,0:T(8,128)(2,1)S(1)}, bf16[32,512]{1,0:T(8,128)(2,1)S(1)}, u32[]{:S(2)}, u32[]{:S(2)}) collective-permute-start(bf16[32,512]{1,0:T(8,128)(2,1)S(1)} %get-tuple-element.37), channel_id=1, source_target_pairs={{0,3},{1,2},{2,1},{3,0},{4,7},{5,6},{6,5},{7,4},{8,11},{9,10},{10,... | collective-permute-start | bytes 98312 | tf_op jit(solution)/shard_map/ppermute | solution.py:97
  23.2 4.0 %collective-permute-start.7 = (bf16[32,512]{1,0:T(8,128)(2,1)S(1)}, bf16[32,512]{1,0:T(8,128)(2,1)S(1)}, u32[]{:S(2)}, u32[]{:S(2)}) collective-permute-start(bf16[32,512]{1,0:T(8,128)(2,1)S(1)} %get-tuple-element.38), channel_id=1, source_target_pairs={{0,2},{1,3},{2,0},{3,1},{4,6},{5,7},{6,4},{7,5},{8,10},{9,11},{10,... | collective-permute-start | bytes 98312 | tf_op jit(solution)/shard_map/ppermute | solution.py:97
  27.2 4.0 %collective-permute-start.9 = (bf16[32,512]{1,0:T(8,128)(2,1)S(1)}, bf16[32,512]{1,0:T(8,128)(2,1)S(1)}, u32[]{:S(2)}, u32[]{:S(2)}) collective-permute-start(bf16[32,512]{1,0:T(8,128)(2,1)S(1)} %get-tuple-element.43.refs_0_), channel_id=1, source_target_pairs={{0,4},{4,0},{8,12},{12,8},{1,5},{5,1},{9,13},{13,9},{2,6},{6,2},{1... | collective-permute-start | bytes 98312 | tf_op jit(solution)/shard_map/ppermute | solution.py:97
  28.6 5.7 %collective-permute-start.13 = (bf16[32,512]{1,0:T(8,128)(2,1)S(1)}, bf16[32,512]{1,0:T(8,128)(2,1)S(1)}, u32[]{:S(2)}, u32[]{:S(2)}) collective-permute-start(bf16[32,512]{1,0:T(8,128)(2,1)S(1)} %get-tuple-element.43.refs_0_), channel_id=1, source_target_pairs={{0,12},{4,8},{8,4},{12,0},{1,13},{5,9},{9,5},{13,1},{2,14},{6,10},... | collective-permute-start | bytes 98312 | tf_op jit(solution)/shard_map/ppermute | solution.py:97
  29.4 5.6 %collective-permute-start.12 = (bf16[32,512]{1,0:T(8,128)(2,1)S(1)}, bf16[32,512]{1,0:T(8,128)(2,1)S(1)}, u32[]{:S(2)}, u32[]{:S(2)}) collective-permute-start(bf16[32,512]{1,0:T(8,128)(2,1)S(1)} %get-tuple-element.43.refs_0_), channel_id=1, source_target_pairs={{0,8},{4,12},{8,0},{12,4},{1,9},{5,13},{9,1},{13,5},{2,10},{6,14},... | collective-permute-start | bytes 98312 | tf_op jit(solution)/shard_map/ppermute | solution.py:97
  33.3 2.9 %collective-permute-start.10 = (bf16[64,1664]{1,0:T(8,128)(2,1)S(1)}, bf16[64,1664]{1,0:T(8,128)(2,1)S(1)}, u32[]{:S(2)}, u32[]{:S(2)}) collective-permute-start(bf16[64,1664]{1,0:T(8,128)(2,1)S(1)} %get-tuple-element.45), channel_id=1, source_target_pairs={{0,1},{1,0},{2,3},{3,2},{4,5},{5,4},{6,7},{7,6},{8,9},{9,8},{10,11... | collective-permute-start | bytes 638984 | tf_op jit(solution)/shard_map/ppermute | solution.py:97
  36.2 2.8 %collective-permute-start.14 = (bf16[64,1664]{1,0:T(8,128)(2,1)S(1)}, bf16[64,1664]{1,0:T(8,128)(2,1)S(1)}, u32[]{:S(2)}, u32[]{:S(2)}) collective-permute-start(bf16[64,1664]{1,0:T(8,128)(2,1)S(1)} %gate_up.8), channel_id=1, source_target_pairs={{0,1},{1,0},{2,3},{3,2},{4,5},{5,4},{6,7},{7,6},{8,9},{9,8},{10,11... | collective-permute-start | bytes 638984 | tf_op jit(solution)/shard_map/ppermute | solution.py:97
  36.4 8.1 %collective-permute-start.11 = (bf16[64,1664]{1,0:T(8,128)(2,1)S(1)}, bf16[64,1664]{1,0:T(8,128)(2,1)S(1)}, u32[]{:S(2)}, u32[]{:S(2)}) collective-permute-start(bf16[64,1664]{1,0:T(8,128)(2,1)S(1)} %join.2), channel_id=1, source_target_pairs={{0,2},{2,0},{1,3},{3,1},{4,6},{6,4},{5,7},{7,5},{8,10},{10,8},{9,1... | collective-permute-start | bytes 638984 | tf_op jit(solution)/shard_map/ppermute | solution.py:97
  40.3 4.3 %collective-permute-start.15 = (bf16[64,1664]{1,0:T(8,128)(2,1)S(1)}, bf16[64,1664]{1,0:T(8,128)(2,1)S(1)}, u32[]{:S(2)}, u32[]{:S(2)}) collective-permute-start(bf16[64,1664]{1,0:T(8,128)(2,1)S(1)} %gate_up.10), channel_id=1, source_target_pairs={{0,1},{1,0},{2,3},{3,2},{4,5},{5,4},{6,7},{7,6},{8,9},{9,8},{10,11... | collective-permute-start | bytes 638984 | tf_op jit(solution)/shard_map/ppermute | solution.py:97
  40.5 8.2 %collective-permute-start.18 = (bf16[64,1664]{1,0:T(8,128)(2,1)S(1)}, bf16[64,1664]{1,0:T(8,128)(2,1)S(1)}, u32[]{:S(2)}, u32[]{:S(2)}) collective-permute-start(bf16[64,1664]{1,0:T(8,128)(2,1)S(1)} %join.3), channel_id=1, source_target_pairs={{0,2},{2,0},{1,3},{3,1},{4,6},{6,4},{5,7},{7,5},{8,10},{10,8},{9,1... | collective-permute-start | bytes 638984 | tf_op jit(solution)/shard_map/ppermute | solution.py:97
  45.9 2.8 %collective-permute-start.19 = (bf16[64,1664]{1,0:T(8,128)(2,1)S(1)}, bf16[64,1664]{1,0:T(8,128)(2,1)S(1)}, u32[]{:S(2)}, u32[]{:S(2)}) collective-permute-start(bf16[64,1664]{1,0:T(8,128)(2,1)S(1)} %gate_up.11), channel_id=1, source_target_pairs={{0,1},{1,0},{2,3},{3,2},{4,5},{5,4},{6,7},{7,6},{8,9},{9,8},{10,11... | collective-permute-start | bytes 638984 | tf_op jit(solution)/shard_map/ppermute | solution.py:97
  45.9 5.3 %collective-permute-start.21 = (bf16[64,768]{1,0:T(8,128)(2,1)S(1)}, bf16[64,768]{1,0:T(8,128)(2,1)S(1)}, u32[]{:S(2)}, u32[]{:S(2)}) collective-permute-start(bf16[64,768]{1,0:T(8,128)(2,1)S(1)} %hidden.2.refs_0_), channel_id=1, source_target_pairs={{0,1},{1,0},{2,3},{3,2},{4,5},{5,4},{6,7},{7,6},{8,9},{9,8},{10,11... | collective-permute-start | bytes 294920 | tf_op jit(solution)/shard_map/ppermute | solution.py:97
  46.4 4.8 %collective-permute-start.16 = (bf16[64,768]{1,0:T(8,128)(2,1)S(1)}, bf16[64,768]{1,0:T(8,128)(2,1)S(1)}, u32[]{:S(2)}, u32[]{:S(2)}) collective-permute-start(bf16[64,768]{1,0:T(8,128)(2,1)S(1)} %hidden.2.refs_0_), channel_id=1, source_target_pairs={{0,2},{2,0},{1,3},{3,1},{4,6},{6,4},{5,7},{7,5},{8,10},{10,8},{9,1... | collective-permute-start | bytes 294920 | tf_op jit(solution)/shard_map/ppermute | solution.py:97
  49.0 5.2 %collective-permute-start.20 = (bf16[64,768]{1,0:T(8,128)(2,1)S(1)}, bf16[64,768]{1,0:T(8,128)(2,1)S(1)}, u32[]{:S(2)}, u32[]{:S(2)}) collective-permute-start(bf16[64,768]{1,0:T(8,128)(2,1)S(1)} %hidden.3.refs_1_), channel_id=1, source_target_pairs={{0,2},{2,0},{1,3},{3,1},{4,6},{6,4},{5,7},{7,5},{8,10},{10,8},{9,1... | collective-permute-start | bytes 294920 | tf_op jit(solution)/shard_map/ppermute | solution.py:97
  51.2 3.9 %collective-permute-start.17 = (bf16[64,768]{1,0:T(8,128)(2,1)S(1)}, bf16[64,768]{1,0:T(8,128)(2,1)S(1)}, u32[]{:S(2)}, u32[]{:S(2)}) collective-permute-start(bf16[64,768]{1,0:T(8,128)(2,1)S(1)} %collective-permute-done.16.refs_0_), channel_id=1, source_target_pairs={{0,1},{1,0},{2,3},{3,2},{4,5},{5,4},{6,7},{7,6},{8,9},{9,8},{10,11... | collective-permute-start | bytes 294920 | tf_op jit(solution)/shard_map/ppermute | solution.py:97
  56.4 5.8 %collective-permute-start.24 = (bf16[32,512]{1,0:T(8,128)(2,1)S(1)}, bf16[32,512]{1,0:T(8,128)(2,1)S(1)}, u32[]{:S(2)}, u32[]{:S(2)}) collective-permute-start(bf16[32,512]{1,0:T(8,128)(2,1)S(1)} %get-tuple-element.60), channel_id=1, source_target_pairs={{0,12},{4,8},{8,4},{12,0},{1,13},{5,9},{9,5},{13,1},{2,14},{6,10},... | collective-permute-start | bytes 98312 | tf_op jit(solution)/shard_map/ppermute | solution.py:97
  58.6 4.8 %collective-permute-start.25 = (bf16[32,512]{1,0:T(8,128)(2,1)S(1)}, bf16[32,512]{1,0:T(8,128)(2,1)S(1)}, u32[]{:S(2)}, u32[]{:S(2)}) collective-permute-start(bf16[32,512]{1,0:T(8,128)(2,1)S(1)} %get-tuple-element.61), channel_id=1, source_target_pairs={{0,8},{4,12},{8,0},{12,4},{1,9},{5,13},{9,1},{13,5},{2,10},{6,14},... | collective-permute-start | bytes 98312 | tf_op jit(solution)/shard_map/ppermute | solution.py:97
  58.6 4.8 %collective-permute-start.26 = (bf16[32,512]{1,0:T(8,128)(2,1)S(1)}, bf16[32,512]{1,0:T(8,128)(2,1)S(1)}, u32[]{:S(2)}, u32[]{:S(2)}) collective-permute-start(bf16[32,512]{1,0:T(8,128)(2,1)S(1)} %get-tuple-element.62), channel_id=1, source_target_pairs={{0,4},{4,0},{8,12},{12,8},{1,5},{5,1},{9,13},{13,9},{2,6},{6,2},{1... | collective-permute-start | bytes 98312 | tf_op jit(solution)/shard_map/ppermute | solution.py:97
  (19 other events, 172.9 us)

commit v15 on v14

--- a/solution.py
+++ b/solution.py
@@ -593,7 +593,7 @@
         last[1, k] = [swapped(hidden, "tp", 1) for hidden in far[k]]
         total = add({(0, k): far[k]}, total)[0]
     totals = add(last, total, ctx_count)
-    returned = [totals[0]] + [swapped(totals[k], "ctx", k) for k in far_first(ctx_count)]
+    returned = [totals[0]] + [swapped(totals[k], "ctx", k) for k in range(1, ctx_count)]
     return finish(mixed, returned)
 
 

time: 64.2 us -> 65.6 us (1.022)
  waiting for transfers between devices: 15.9 us -> 17.4 us
    ppermute x27, waiting for transfers between devices: 15.9 us -> 17.4 us  [swapped(): return lax.ppermute(value, axes, pairs)]
  transfers between devices with their start and end apart: 27 -> 27, of which waited for: 15 -> 15; matrix products, arithmetic and copies ran while one was open for 0% -> 0% of each run, Pallas kernels for 29% -> 28%
where the time goes in v15:
time: 65.6 us; the launch traced here: 65.5 us
  starting transfers between devices  25.9 us (39%)
  Pallas kernels  21.8 us (33%)
  waiting for transfers between devices  17.4 us (27%)
    ppermute x27, starting transfers between devices, swapped(): return lax.ppermute(value, axes, pairs)  25.9 us
    ppermute x27, waiting for transfers between devices, swapped(): return lax.ppermute(value, axes, pairs)  17.4 us
    pallas_call x6, Pallas kernels, gate_up(): pl.pallas_call(kernel, out_shape=[out] * len(names), compiler_params=para...  8.61 us
    pallas_call x4, Pallas kernels, attend(): pl.pallas_call(functools.partial(attend_kernel, heads, scale, layout, k),...  5.04 us
    pallas_call x3, Pallas kernels, down(): pl.pallas_call(kernel, out_shape=[jax.ShapeDtypeStruct((rows, piece_width...  3.24 us
  transfers between devices with their start and end apart: 27, of which 15 were waited for; matrix products, arithmetic and copies ran while one was open for 0% of the time, Pallas kernels for 28%

profile of v15, /device:TPU:0, one launch (start us, length us, event | category | flops | bytes accessed | tf_op | source)
XLA Modules:
  0.0 65.5 jit_solution(2654872636357269750)
XLA Ops:
  1.0 3.1 %collective-permute-start = (bf16[32,1152]{1,0:T(8,128)(2,1)S(1)}, bf16[32,1152]{1,0:T(8,128)(2,1)S(1)}, u32[]{:S(2)}, u32[]{:S(2)}) collective-permute-start(bf16[32,1152]{1,0:T(8,128)(2,1)S(1)} %pack.1.queries_ref.refs_0_), channel_id=1, source_target_pairs={{0,4},{4,0},{8,12},{12,8},{1,5},{5,1},{9,13},{13,9},{2,6},{6,2},{1... | collective-permute-start | bytes 221192 | tf_op jit(solution)/shard_map/ppermute | solution.py:97
  4.2 2.6 %collective-permute-start.2 = (bf16[32,1152]{1,0:T(8,128)(2,1)S(1)}, bf16[32,1152]{1,0:T(8,128)(2,1)S(1)}, u32[]{:S(2)}, u32[]{:S(2)}) collective-permute-start(bf16[32,1152]{1,0:T(8,128)(2,1)S(1)} %pack.1.queries_ref.refs_0_), channel_id=1, source_target_pairs={{0,8},{4,12},{8,0},{12,4},{1,9},{5,13},{9,1},{13,5},{2,10},{6,14},... | collective-permute-start | bytes 221192 | tf_op jit(solution)/shard_map/ppermute | solution.py:97
  7.4 1.3 %attend.5 = bf16[32,1152]{1,0:T(8,128)(2,1)S(1)} custom-call(bf16[32,1152]{1,0:T(8,128)(2,1)S(1)} %collective-permute-done.queries_ref.refs_1_, bf16[2048,128]{1,0:T(8,128)(2,1)S(1)} %bitcast.20, bf16[2048,128]{1,0:T(8,128)(2,1)S(1)} %bitcast.24, bf16[64,2048]{1,0:T(8,128)(2,1)S(1)} %sight.1.sight_ref, bf16[16,512,1536]{2,1,0:T(8,128)(2,1)} %weight_ref.14), custom_call_target="tpu_custom_call" | custom-call | flops 536870912 | bytes 1048576 | tf_op jit(solution)/shard_map/attend/pallas_call | solution.py:219
  9.8 2.1 %collective-permute-done.2.queries_ref.refs_2_ = bf16[32,1152]{1,0:T(8,128)(2,1)S(1)} collective-permute-done((bf16[32,1152]{1,0:T(8,128)(2,1)S(1)}, bf16[32,1152]{1,0:T(8,128)(2,1)S(1)}, u32[]{:S(2)}, u32[]{:S(2)}) %collective-permute-start.2) | collective-permute-done | bytes 73760 | tf_op jit(solution)/shard_map/ppermute | solution.py:97
  11.9 1.3 %attend.6 = bf16[32,1152]{1,0:T(8,128)(2,1)S(1)} custom-call(bf16[32,1152]{1,0:T(8,128)(2,1)S(1)} %collective-permute-done.2.queries_ref.refs_2_, bf16[2048,128]{1,0:T(8,128)(2,1)S(1)} %bitcast.21, bf16[2048,128]{1,0:T(8,128)(2,1)S(1)} %bitcast.25, bf16[64,2048]{1,0:T(8,128)(2,1)S(1)} %sight.1.sight_ref, bf16[16,512,1536]{2,1,0:T(8,128)(2,1)} %weight_ref.14), custom_call_target="tpu_custom_call" | custom-call | flops 536870912 | bytes 1048576 | tf_op jit(solution)/shard_map/attend/pallas_call | solution.py:219
  13.2 1.3 %collective-permute-start.3 = (bf16[32,1152]{1,0:T(8,128)(2,1)S(1)}, bf16[32,1152]{1,0:T(8,128)(2,1)S(1)}, u32[]{:S(2)}, u32[]{:S(2)}) collective-permute-start(bf16[32,1152]{1,0:T(8,128)(2,1)S(1)} %attend.6), channel_id=1, source_target_pairs={{0,8},{4,12},{8,0},{12,4},{1,9},{5,13},{9,1},{13,5},{2,10},{6,14},... | collective-permute-start | bytes 221192 | tf_op jit(solution)/shard_map/ppermute | solution.py:97
  14.5 1.3 %attend.7 = bf16[32,1152]{1,0:T(8,128)(2,1)S(1)} custom-call(bf16[32,1152]{1,0:T(8,128)(2,1)S(1)} %collective-permute-done.4.queries_ref.refs_3_, bf16[2048,128]{1,0:T(8,128)(2,1)S(1)} %bitcast.22, bf16[2048,128]{1,0:T(8,128)(2,1)S(1)} %bitcast.26, bf16[64,2048]{1,0:T(8,128)(2,1)S(1)} %sight.1.sight_ref, bf16[16,512,1536]{2,1,0:T(8,128)(2,1)} %weight_ref.14), custom_call_target="tpu_custom_call" | custom-call | flops 536870912 | bytes 1048576 | tf_op jit(solution)/shard_map/attend/pallas_call | solution.py:219
  15.8 2.2 %collective-permute-start.5 = (bf16[32,1152]{1,0:T(8,128)(2,1)S(1)}, bf16[32,1152]{1,0:T(8,128)(2,1)S(1)}, u32[]{:S(2)}, u32[]{:S(2)}) collective-permute-start(bf16[32,1152]{1,0:T(8,128)(2,1)S(1)} %attend.7), channel_id=1, source_target_pairs={{0,12},{4,8},{8,4},{12,0},{1,13},{5,9},{9,5},{13,1},{2,14},{6,10},... | collective-permute-start | bytes 221192 | tf_op jit(solution)/shard_map/ppermute | solution.py:97
  20.1 2.0 %collective-permute-done.5.refs_3_ = bf16[32,1152]{1,0:T(8,128)(2,1)S(1)} collective-permute-done((bf16[32,1152]{1,0:T(8,128)(2,1)S(1)}, bf16[32,1152]{1,0:T(8,128)(2,1)S(1)}, u32[]{:S(2)}, u32[]{:S(2)}) %collective-permute-start.5) | collective-permute-done | bytes 73760 | tf_op jit(solution)/shard_map/ppermute | solution.py:97
  23.2 1.5 %collective-permute-start.7 = (bf16[32,512]{1,0:T(8,128)(2,1)S(1)}, bf16[32,512]{1,0:T(8,128)(2,1)S(1)}, u32[]{:S(2)}, u32[]{:S(2)}) collective-permute-start(bf16[32,512]{1,0:T(8,128)(2,1)S(1)} %get-tuple-element.38), channel_id=1, source_target_pairs={{0,2},{1,3},{2,0},{3,1},{4,6},{5,7},{6,4},{7,5},{8,10},{9,11},{10,... | collective-permute-start | bytes 98312 | tf_op jit(solution)/shard_map/ppermute | solution.py:97
  25.0 1.8 %collective-permute-done.6.refs_1_ = bf16[32,512]{1,0:T(8,128)(2,1)S(1)} collective-permute-done((bf16[32,512]{1,0:T(8,128)(2,1)S(1)}, bf16[32,512]{1,0:T(8,128)(2,1)S(1)}, u32[]{:S(2)}, u32[]{:S(2)}) %collective-permute-start.6) | collective-permute-done | bytes 32800 | tf_op jit(solution)/shard_map/ppermute | solution.py:97
  27.2 1.4 %collective-permute-start.9 = (bf16[32,512]{1,0:T(8,128)(2,1)S(1)}, bf16[32,512]{1,0:T(8,128)(2,1)S(1)}, u32[]{:S(2)}, u32[]{:S(2)}) collective-permute-start(bf16[32,512]{1,0:T(8,128)(2,1)S(1)} %get-tuple-element.43.refs_0_), channel_id=1, source_target_pairs={{0,4},{4,0},{8,12},{12,8},{1,5},{5,1},{9,13},{13,9},{2,6},{6,2},{1... | collective-permute-start | bytes 98312 | tf_op jit(solution)/shard_map/ppermute | solution.py:97
  29.4 1.3 %collective-permute-start.12 = (bf16[32,512]{1,0:T(8,128)(2,1)S(1)}, bf16[32,512]{1,0:T(8,128)(2,1)S(1)}, u32[]{:S(2)}, u32[]{:S(2)}) collective-permute-start(bf16[32,512]{1,0:T(8,128)(2,1)S(1)} %get-tuple-element.43.refs_0_), channel_id=1, source_target_pairs={{0,8},{4,12},{8,0},{12,4},{1,9},{5,13},{9,1},{13,5},{2,10},{6,14},... | collective-permute-start | bytes 98312 | tf_op jit(solution)/shard_map/ppermute | solution.py:97
  31.3 2.0 %gate_up.6 = (bf16[64,1664]{1,0:T(8,128)(2,1)S(1)}, bf16[64,1664]{1,0:T(8,128)(2,1)S(1)}) custom-call(bf16[8,64,64]{2,1,0:T(8,128)(2,1)S(1)} %get-tuple-element.55.place_ref, bf16[1,512]{1,0:T(2,128)(2,1)S(1)} %broadcast_in_dim.8.gain_ref, bf16[16,512,1536]{2,1,0:T(8,128)(2,1)S(1)} %bitcast.10, bf16[32,512]{1,0:T(8,128)(2,1)S(1)} %get-tuple-element.43.refs_0_, ...), custom_call_target="tpu_custom_call" | custom-call | flops 100663296 | bytes 196608 | tf_op jit(solution)/shard_map/gate_up/pallas_call | solution.py:375
  36.4 1.4 %collective-permute-start.11 = (bf16[64,1664]{1,0:T(8,128)(2,1)S(1)}, bf16[64,1664]{1,0:T(8,128)(2,1)S(1)}, u32[]{:S(2)}, u32[]{:S(2)}) collective-permute-start(bf16[64,1664]{1,0:T(8,128)(2,1)S(1)} %join.2), channel_id=1, source_target_pairs={{0,2},{2,0},{1,3},{3,1},{4,6},{6,4},{5,7},{7,5},{8,10},{10,8},{9,1... | collective-permute-start | bytes 638984 | tf_op jit(solution)/shard_map/ppermute | solution.py:97
  41.2 2.2 %gate_up.9 = (bf16[64,1664]{1,0:T(8,128)(2,1)S(1)}, bf16[64,1664]{1,0:T(8,128)(2,1)S(1)}) custom-call(bf16[8,64,64]{2,1,0:T(8,128)(2,1)S(1)} %get-tuple-element.55.place_ref, bf16[1,512]{1,0:T(2,128)(2,1)S(1)} %broadcast_in_dim.8.gain_ref, bf16[16,512,1536]{2,1,0:T(8,128)(2,1)S(1)} %bitcast.10, bf16[32,512]{1,0:T(8,128)(2,1)S(1)} %get-tuple-element.43.refs_0_, ...), custom_call_target="tpu_custom_call" | custom-call | flops 100663296 | bytes 196608 | tf_op jit(solution)/shard_map/gate_up/pallas_call | solution.py:375
  46.4 1.4 %collective-permute-start.16 = (bf16[64,768]{1,0:T(8,128)(2,1)S(1)}, bf16[64,768]{1,0:T(8,128)(2,1)S(1)}, u32[]{:S(2)}, u32[]{:S(2)}) collective-permute-start(bf16[64,768]{1,0:T(8,128)(2,1)S(1)} %hidden.2.refs_0_), channel_id=1, source_target_pairs={{0,2},{2,0},{1,3},{3,1},{4,6},{6,4},{5,7},{7,5},{8,10},{10,8},{9,1... | collective-permute-start | bytes 294920 | tf_op jit(solution)/shard_map/ppermute | solution.py:97
  49.0 1.4 %collective-permute-start.20 = (bf16[64,768]{1,0:T(8,128)(2,1)S(1)}, bf16[64,768]{1,0:T(8,128)(2,1)S(1)}, u32[]{:S(2)}, u32[]{:S(2)}) collective-permute-start(bf16[64,768]{1,0:T(8,128)(2,1)S(1)} %hidden.3.refs_1_), channel_id=1, source_target_pairs={{0,2},{2,0},{1,3},{3,1},{4,6},{6,4},{5,7},{7,5},{8,10},{10,8},{9,1... | collective-permute-start | bytes 294920 | tf_op jit(solution)/shard_map/ppermute | solution.py:97
  51.2 1.6 %down.3.refs_2_ = f32[128,512]{1,0:T(8,128)S(1)} custom-call(bf16[16,768,512]{2,1,0:T(8,128)(2,1)S(1)} %bitcast.19, bf16[8,64,64]{2,1,0:T(8,128)(2,1)S(1)} %get-tuple-element.41.high_ref, bf16[8,64,64]{2,1,0:T(8,128)(2,1)S(1)} %get-tuple-element.42.low_ref, bf16[64,768]{1,0:T(8,128)(2,1)S(1)} %hidden.2.refs_0_, bf16[64,768]{1,0:T(8,128)(2,1)S(1)} %hidden.3.refs_1_, ...), custom_call_target="tpu_custom_call" | custom-call | flops 100663296 | bytes 1048576 | tf_op jit(solution)/shard_map/down/pallas_call | solution.py:457
  52.8 1.5 %collective-permute-done.20.refs_1_ = bf16[64,768]{1,0:T(8,128)(2,1)S(1)} collective-permute-done((bf16[64,768]{1,0:T(8,128)(2,1)S(1)}, bf16[64,768]{1,0:T(8,128)(2,1)S(1)}, u32[]{:S(2)}, u32[]{:S(2)}) %collective-permute-start.20) | collective-permute-done | bytes 98336 | tf_op jit(solution)/shard_map/ppermute | solution.py:97
  56.7 2.5 %collective-permute-start.25 = (bf16[32,512]{1,0:T(8,128)(2,1)S(1)}, bf16[32,512]{1,0:T(8,128)(2,1)S(1)}, u32[]{:S(2)}, u32[]{:S(2)}) collective-permute-start(bf16[32,512]{1,0:T(8,128)(2,1)S(1)} %get-tuple-element.61), channel_id=1, source_target_pairs={{0,8},{4,12},{8,0},{12,4},{1,9},{5,13},{9,1},{13,5},{2,10},{6,14},... | collective-permute-start | bytes 98312 | tf_op jit(solution)/shard_map/ppermute | solution.py:97
  59.2 1.7 %collective-permute-start.26 = (bf16[32,512]{1,0:T(8,128)(2,1)S(1)}, bf16[32,512]{1,0:T(8,128)(2,1)S(1)}, u32[]{:S(2)}, u32[]{:S(2)}) collective-permute-start(bf16[32,512]{1,0:T(8,128)(2,1)S(1)} %get-tuple-element.62), channel_id=1, source_target_pairs={{0,12},{4,8},{8,4},{12,0},{1,13},{5,9},{9,5},{13,1},{2,14},{6,10},... | collective-permute-start | bytes 98312 | tf_op jit(solution)/shard_map/ppermute | solution.py:97
  60.8 1.3 %collective-permute-done.25.refs_2_ = bf16[32,512]{1,0:T(8,128)(2,1)S(1)} collective-permute-done((bf16[32,512]{1,0:T(8,128)(2,1)S(1)}, bf16[32,512]{1,0:T(8,128)(2,1)S(1)}, u32[]{:S(2)}, u32[]{:S(2)}) %collective-permute-start.25) | collective-permute-done | bytes 32800 | tf_op jit(solution)/shard_map/ppermute | solution.py:97
  62.2 2.7 %collective-permute-done.26.refs_3_ = bf16[32,512]{1,0:T(8,128)(2,1)S(1)} collective-permute-done((bf16[32,512]{1,0:T(8,128)(2,1)S(1)}, bf16[32,512]{1,0:T(8,128)(2,1)S(1)}, u32[]{:S(2)}, u32[]{:S(2)}) %collective-permute-start.26) | collective-permute-done | bytes 32800 | tf_op jit(solution)/shard_map/ppermute | solution.py:97
  (88 shorter events, 22.5 us)
Async XLA Ops:
  1.0 6.3 %collective-permute-start = (bf16[32,1152]{1,0:T(8,128)(2,1)S(1)}, bf16[32,1152]{1,0:T(8,128)(2,1)S(1)}, u32[]{:S(2)}, u32[]{:S(2)}) collective-permute-start(bf16[32,1152]{1,0:T(8,128)(2,1)S(1)} %pack.1.queries_ref.refs_0_), channel_id=1, source_target_pairs={{0,4},{4,0},{8,12},{12,8},{1,5},{5,1},{9,13},{13,9},{2,6},{6,2},{1... | collective-permute-start | bytes 221192 | tf_op jit(solution)/shard_map/ppermute | solution.py:97
  4.2 7.8 %collective-permute-start.2 = (bf16[32,1152]{1,0:T(8,128)(2,1)S(1)}, bf16[32,1152]{1,0:T(8,128)(2,1)S(1)}, u32[]{:S(2)}, u32[]{:S(2)}) collective-permute-start(bf16[32,1152]{1,0:T(8,128)(2,1)S(1)} %pack.1.queries_ref.refs_0_), channel_id=1, source_target_pairs={{0,8},{4,12},{8,0},{12,4},{1,9},{5,13},{9,1},{13,5},{2,10},{6,14},... | collective-permute-start | bytes 221192 | tf_op jit(solution)/shard_map/ppermute | solution.py:97
  6.7 7.8 %collective-permute-start.4 = (bf16[32,1152]{1,0:T(8,128)(2,1)S(1)}, bf16[32,1152]{1,0:T(8,128)(2,1)S(1)}, u32[]{:S(2)}, u32[]{:S(2)}) collective-permute-start(bf16[32,1152]{1,0:T(8,128)(2,1)S(1)} %pack.1.queries_ref.refs_0_), channel_id=1, source_target_pairs={{0,12},{4,8},{8,4},{12,0},{1,13},{5,9},{9,5},{13,1},{2,14},{6,10},... | collective-permute-start | bytes 221192 | tf_op jit(solution)/shard_map/ppermute | solution.py:97
  8.7 11.3 %collective-permute-start.1 = (bf16[32,1152]{1,0:T(8,128)(2,1)S(1)}, bf16[32,1152]{1,0:T(8,128)(2,1)S(1)}, u32[]{:S(2)}, u32[]{:S(2)}) collective-permute-start(bf16[32,1152]{1,0:T(8,128)(2,1)S(1)} %attend.5), channel_id=1, source_target_pairs={{0,4},{4,0},{8,12},{12,8},{1,5},{5,1},{9,13},{13,9},{2,6},{6,2},{1... | collective-permute-start | bytes 221192 | tf_op jit(solution)/shard_map/ppermute | solution.py:97
  13.2 6.9 %collective-permute-start.3 = (bf16[32,1152]{1,0:T(8,128)(2,1)S(1)}, bf16[32,1152]{1,0:T(8,128)(2,1)S(1)}, u32[]{:S(2)}, u32[]{:S(2)}) collective-permute-start(bf16[32,1152]{1,0:T(8,128)(2,1)S(1)} %attend.6), channel_id=1, source_target_pairs={{0,8},{4,12},{8,0},{12,4},{1,9},{5,13},{9,1},{13,5},{2,10},{6,14},... | collective-permute-start | bytes 221192 | tf_op jit(solution)/shard_map/ppermute | solution.py:97
  15.8 6.3 %collective-permute-start.5 = (bf16[32,1152]{1,0:T(8,128)(2,1)S(1)}, bf16[32,1152]{1,0:T(8,128)(2,1)S(1)}, u32[]{:S(2)}, u32[]{:S(2)}) collective-permute-start(bf16[32,1152]{1,0:T(8,128)(2,1)S(1)} %attend.7), channel_id=1, source_target_pairs={{0,12},{4,8},{8,4},{12,0},{1,13},{5,9},{9,5},{13,1},{2,14},{6,10},... | collective-permute-start | bytes 221192 | tf_op jit(solution)/shard_map/ppermute | solution.py:97
  23.1 3.7 %collective-permute-start.6 = (bf16[32,512]{1,0:T(8,128)(2,1)S(1)}, bf16[32,512]{1,0:T(8,128)(2,1)S(1)}, u32[]{:S(2)}, u32[]{:S(2)}) collective-permute-start(bf16[32,512]{1,0:T(8,128)(2,1)S(1)} %get-tuple-element.37), channel_id=1, source_target_pairs={{0,3},{1,2},{2,1},{3,0},{4,7},{5,6},{6,5},{7,4},{8,11},{9,10},{10,... | collective-permute-start | bytes 98312 | tf_op jit(solution)/shard_map/ppermute | solution.py:97
  23.2 4.0 %collective-permute-start.7 = (bf16[32,512]{1,0:T(8,128)(2,1)S(1)}, bf16[32,512]{1,0:T(8,128)(2,1)S(1)}, u32[]{:S(2)}, u32[]{:S(2)}) collective-permute-start(bf16[32,512]{1,0:T(8,128)(2,1)S(1)} %get-tuple-element.38), channel_id=1, source_target_pairs={{0,2},{1,3},{2,0},{3,1},{4,6},{5,7},{6,4},{7,5},{8,10},{9,11},{10,... | collective-permute-start | bytes 98312 | tf_op jit(solution)/shard_map/ppermute | solution.py:97
  27.2 4.0 %collective-permute-start.9 = (bf16[32,512]{1,0:T(8,128)(2,1)S(1)}, bf16[32,512]{1,0:T(8,128)(2,1)S(1)}, u32[]{:S(2)}, u32[]{:S(2)}) collective-permute-start(bf16[32,512]{1,0:T(8,128)(2,1)S(1)} %get-tuple-element.43.refs_0_), channel_id=1, source_target_pairs={{0,4},{4,0},{8,12},{12,8},{1,5},{5,1},{9,13},{13,9},{2,6},{6,2},{1... | collective-permute-start | bytes 98312 | tf_op jit(solution)/shard_map/ppermute | solution.py:97
  28.6 5.7 %collective-permute-start.13 = (bf16[32,512]{1,0:T(8,128)(2,1)S(1)}, bf16[32,512]{1,0:T(8,128)(2,1)S(1)}, u32[]{:S(2)}, u32[]{:S(2)}) collective-permute-start(bf16[32,512]{1,0:T(8,128)(2,1)S(1)} %get-tuple-element.43.refs_0_), channel_id=1, source_target_pairs={{0,12},{4,8},{8,4},{12,0},{1,13},{5,9},{9,5},{13,1},{2,14},{6,10},... | collective-permute-start | bytes 98312 | tf_op jit(solution)/shard_map/ppermute | solution.py:97
  29.4 5.6 %collective-permute-start.12 = (bf16[32,512]{1,0:T(8,128)(2,1)S(1)}, bf16[32,512]{1,0:T(8,128)(2,1)S(1)}, u32[]{:S(2)}, u32[]{:S(2)}) collective-permute-start(bf16[32,512]{1,0:T(8,128)(2,1)S(1)} %get-tuple-element.43.refs_0_), channel_id=1, source_target_pairs={{0,8},{4,12},{8,0},{12,4},{1,9},{5,13},{9,1},{13,5},{2,10},{6,14},... | collective-permute-start | bytes 98312 | tf_op jit(solution)/shard_map/ppermute | solution.py:97
  33.3 2.9 %collective-permute-start.10 = (bf16[64,1664]{1,0:T(8,128)(2,1)S(1)}, bf16[64,1664]{1,0:T(8,128)(2,1)S(1)}, u32[]{:S(2)}, u32[]{:S(2)}) collective-permute-start(bf16[64,1664]{1,0:T(8,128)(2,1)S(1)} %get-tuple-element.45), channel_id=1, source_target_pairs={{0,1},{1,0},{2,3},{3,2},{4,5},{5,4},{6,7},{7,6},{8,9},{9,8},{10,11... | collective-permute-start | bytes 638984 | tf_op jit(solution)/shard_map/ppermute | solution.py:97
  36.2 2.8 %collective-permute-start.14 = (bf16[64,1664]{1,0:T(8,128)(2,1)S(1)}, bf16[64,1664]{1,0:T(8,128)(2,1)S(1)}, u32[]{:S(2)}, u32[]{:S(2)}) collective-permute-start(bf16[64,1664]{1,0:T(8,128)(2,1)S(1)} %gate_up.8), channel_id=1, source_target_pairs={{0,1},{1,0},{2,3},{3,2},{4,5},{5,4},{6,7},{7,6},{8,9},{9,8},{10,11... | collective-permute-start | bytes 638984 | tf_op jit(solution)/shard_map/ppermute | solution.py:97
  36.4 8.1 %collective-permute-start.11 = (bf16[64,1664]{1,0:T(8,128)(2,1)S(1)}, bf16[64,1664]{1,0:T(8,128)(2,1)S(1)}, u32[]{:S(2)}, u32[]{:S(2)}) collective-permute-start(bf16[64,1664]{1,0:T(8,128)(2,1)S(1)} %join.2), channel_id=1, source_target_pairs={{0,2},{2,0},{1,3},{3,1},{4,6},{6,4},{5,7},{7,5},{8,10},{10,8},{9,1... | collective-permute-start | bytes 638984 | tf_op jit(solution)/shard_map/ppermute | solution.py:97
  40.3 4.3 %collective-permute-start.15 = (bf16[64,1664]{1,0:T(8,128)(2,1)S(1)}, bf16[64,1664]{1,0:T(8,128)(2,1)S(1)}, u32[]{:S(2)}, u32[]{:S(2)}) collective-permute-start(bf16[64,1664]{1,0:T(8,128)(2,1)S(1)} %gate_up.10), channel_id=1, source_target_pairs={{0,1},{1,0},{2,3},{3,2},{4,5},{5,4},{6,7},{7,6},{8,9},{9,8},{10,11... | collective-permute-start | bytes 638984 | tf_op jit(solution)/shard_map/ppermute | solution.py:97
  40.5 8.2 %collective-permute-start.18 = (bf16[64,1664]{1,0:T(8,128)(2,1)S(1)}, bf16[64,1664]{1,0:T(8,128)(2,1)S(1)}, u32[]{:S(2)}, u32[]{:S(2)}) collective-permute-start(bf16[64,1664]{1,0:T(8,128)(2,1)S(1)} %join.3), channel_id=1, source_target_pairs={{0,2},{2,0},{1,3},{3,1},{4,6},{6,4},{5,7},{7,5},{8,10},{10,8},{9,1... | collective-permute-start | bytes 638984 | tf_op jit(solution)/shard_map/ppermute | solution.py:97
  45.9 2.8 %collective-permute-start.19 = (bf16[64,1664]{1,0:T(8,128)(2,1)S(1)}, bf16[64,1664]{1,0:T(8,128)(2,1)S(1)}, u32[]{:S(2)}, u32[]{:S(2)}) collective-permute-start(bf16[64,1664]{1,0:T(8,128)(2,1)S(1)} %gate_up.11), channel_id=1, source_target_pairs={{0,1},{1,0},{2,3},{3,2},{4,5},{5,4},{6,7},{7,6},{8,9},{9,8},{10,11... | collective-permute-start | bytes 638984 | tf_op jit(solution)/shard_map/ppermute | solution.py:97
  45.9 5.3 %collective-permute-start.21 = (bf16[64,768]{1,0:T(8,128)(2,1)S(1)}, bf16[64,768]{1,0:T(8,128)(2,1)S(1)}, u32[]{:S(2)}, u32[]{:S(2)}) collective-permute-start(bf16[64,768]{1,0:T(8,128)(2,1)S(1)} %hidden.2.refs_0_), channel_id=1, source_target_pairs={{0,1},{1,0},{2,3},{3,2},{4,5},{5,4},{6,7},{7,6},{8,9},{9,8},{10,11... | collective-permute-start | bytes 294920 | tf_op jit(solution)/shard_map/ppermute | solution.py:97
  46.4 4.8 %collective-permute-start.16 = (bf16[64,768]{1,0:T(8,128)(2,1)S(1)}, bf16[64,768]{1,0:T(8,128)(2,1)S(1)}, u32[]{:S(2)}, u32[]{:S(2)}) collective-permute-start(bf16[64,768]{1,0:T(8,128)(2,1)S(1)} %hidden.2.refs_0_), channel_id=1, source_target_pairs={{0,2},{2,0},{1,3},{3,1},{4,6},{6,4},{5,7},{7,5},{8,10},{10,8},{9,1... | collective-permute-start | bytes 294920 | tf_op jit(solution)/shard_map/ppermute | solution.py:97
  49.0 5.2 %collective-permute-start.20 = (bf16[64,768]{1,0:T(8,128)(2,1)S(1)}, bf16[64,768]{1,0:T(8,128)(2,1)S(1)}, u32[]{:S(2)}, u32[]{:S(2)}) collective-permute-start(bf16[64,768]{1,0:T(8,128)(2,1)S(1)} %hidden.3.refs_1_), channel_id=1, source_target_pairs={{0,2},{2,0},{1,3},{3,1},{4,6},{6,4},{5,7},{7,5},{8,10},{10,8},{9,1... | collective-permute-start | bytes 294920 | tf_op jit(solution)/shard_map/ppermute | solution.py:97
  51.2 3.9 %collective-permute-start.17 = (bf16[64,768]{1,0:T(8,128)(2,1)S(1)}, bf16[64,768]{1,0:T(8,128)(2,1)S(1)}, u32[]{:S(2)}, u32[]{:S(2)}) collective-permute-start(bf16[64,768]{1,0:T(8,128)(2,1)S(1)} %collective-permute-done.16.refs_0_), channel_id=1, source_target_pairs={{0,1},{1,0},{2,3},{3,2},{4,5},{5,4},{6,7},{7,6},{8,9},{9,8},{10,11... | collective-permute-start | bytes 294920 | tf_op jit(solution)/shard_map/ppermute | solution.py:97
  56.4 4.5 %collective-permute-start.24 = (bf16[32,512]{1,0:T(8,128)(2,1)S(1)}, bf16[32,512]{1,0:T(8,128)(2,1)S(1)}, u32[]{:S(2)}, u32[]{:S(2)}) collective-permute-start(bf16[32,512]{1,0:T(8,128)(2,1)S(1)} %get-tuple-element.60), channel_id=1, source_target_pairs={{0,4},{4,0},{8,12},{12,8},{1,5},{5,1},{9,13},{13,9},{2,6},{6,2},{1... | collective-permute-start | bytes 98312 | tf_op jit(solution)/shard_map/ppermute | solution.py:97
  56.7 5.5 %collective-permute-start.25 = (bf16[32,512]{1,0:T(8,128)(2,1)S(1)}, bf16[32,512]{1,0:T(8,128)(2,1)S(1)}, u32[]{:S(2)}, u32[]{:S(2)}) collective-permute-start(bf16[32,512]{1,0:T(8,128)(2,1)S(1)} %get-tuple-element.61), channel_id=1, source_target_pairs={{0,8},{4,12},{8,0},{12,4},{1,9},{5,13},{9,1},{13,5},{2,10},{6,14},... | collective-permute-start | bytes 98312 | tf_op jit(solution)/shard_map/ppermute | solution.py:97
  59.2 5.7 %collective-permute-start.26 = (bf16[32,512]{1,0:T(8,128)(2,1)S(1)}, bf16[32,512]{1,0:T(8,128)(2,1)S(1)}, u32[]{:S(2)}, u32[]{:S(2)}) collective-permute-start(bf16[32,512]{1,0:T(8,128)(2,1)S(1)} %get-tuple-element.62), channel_id=1, source_target_pairs={{0,12},{4,8},{8,4},{12,0},{1,13},{5,9},{9,5},{13,1},{2,14},{6,10},... | collective-permute-start | bytes 98312 | tf_op jit(solution)/shard_map/ppermute | solution.py:97
  (19 other events, 172.9 us)

commit v16 on v15

--- a/solution.py
+++ b/solution.py
@@ -593,7 +593,9 @@
         last[1, k] = [swapped(hidden, "tp", 1) for hidden in far[k]]
         total = add({(0, k): far[k]}, total)[0]
     totals = add(last, total, ctx_count)
-    returned = [totals[0]] + [swapped(totals[k], "ctx", k) for k in range(1, ctx_count)]
+    order = far_first(ctx_count)
+    order = order[:1] + order[:0:-1]
+    returned = [totals[0]] + [swapped(totals[k], "ctx", k) for k in order]
     return finish(mixed, returned)
 
 

time: 65.6 us -> 64.5 us (0.983)
  waiting for transfers between devices: 17.4 us -> 16.3 us
    ppermute x27, waiting for transfers between devices: 17.4 us -> 16.3 us  [swapped(): return lax.ppermute(value, axes, pairs)]
  transfers between devices with their start and end apart: 27 -> 27, of which waited for: 15 -> 16; matrix products, arithmetic and copies ran while one was open for 0% -> 0% of each run, Pallas kernels for 28% -> 28%
where the time goes in v16:
time: 64.5 us; the launch traced here: 64.4 us
  starting transfers between devices  25.9 us (40%)
  Pallas kernels  21.8 us (34%)
  waiting for transfers between devices  16.3 us (25%)
    ppermute x27, starting transfers between devices, swapped(): return lax.ppermute(value, axes, pairs)  25.9 us
    ppermute x27, waiting for transfers between devices, swapped(): return lax.ppermute(value, axes, pairs)  16.3 us
    pallas_call x6, Pallas kernels, gate_up(): pl.pallas_call(kernel, out_shape=[out] * len(names), compiler_params=para...  8.61 us
    pallas_call x4, Pallas kernels, attend(): pl.pallas_call(functools.partial(attend_kernel, heads, scale, layout, k),...  5.04 us
    pallas_call x3, Pallas kernels, down(): pl.pallas_call(kernel, out_shape=[jax.ShapeDtypeStruct((rows, piece_width...  3.24 us
  transfers between devices with their start and end apart: 27, of which 16 were waited for; matrix products, arithmetic and copies ran while one was open for 0% of the time, Pallas kernels for 28%

profile of v16, /device:TPU:0, one launch (start us, length us, event | category | flops | bytes accessed | tf_op | source)
XLA Modules:
  0.0 64.4 jit_solution(11227712323493500687)
XLA Ops:
  1.0 3.1 %collective-permute-start = (bf16[32,1152]{1,0:T(8,128)(2,1)S(1)}, bf16[32,1152]{1,0:T(8,128)(2,1)S(1)}, u32[]{:S(2)}, u32[]{:S(2)}) collective-permute-start(bf16[32,1152]{1,0:T(8,128)(2,1)S(1)} %pack.1.queries_ref.refs_0_), channel_id=1, source_target_pairs={{0,4},{4,0},{8,12},{12,8},{1,5},{5,1},{9,13},{13,9},{2,6},{6,2},{1... | collective-permute-start | bytes 221192 | tf_op jit(solution)/shard_map/ppermute | solution.py:97
  4.2 2.6 %collective-permute-start.2 = (bf16[32,1152]{1,0:T(8,128)(2,1)S(1)}, bf16[32,1152]{1,0:T(8,128)(2,1)S(1)}, u32[]{:S(2)}, u32[]{:S(2)}) collective-permute-start(bf16[32,1152]{1,0:T(8,128)(2,1)S(1)} %pack.1.queries_ref.refs_0_), channel_id=1, source_target_pairs={{0,8},{4,12},{8,0},{12,4},{1,9},{5,13},{9,1},{13,5},{2,10},{6,14},... | collective-permute-start | bytes 221192 | tf_op jit(solution)/shard_map/ppermute | solution.py:97
  7.4 1.3 %attend.5 = bf16[32,1152]{1,0:T(8,128)(2,1)S(1)} custom-call(bf16[32,1152]{1,0:T(8,128)(2,1)S(1)} %collective-permute-done.queries_ref.refs_1_, bf16[2048,128]{1,0:T(8,128)(2,1)S(1)} %bitcast.20, bf16[2048,128]{1,0:T(8,128)(2,1)S(1)} %bitcast.24, bf16[64,2048]{1,0:T(8,128)(2,1)S(1)} %sight.1.sight_ref, bf16[16,512,1536]{2,1,0:T(8,128)(2,1)} %weight_ref.14), custom_call_target="tpu_custom_call" | custom-call | flops 536870912 | bytes 1048576 | tf_op jit(solution)/shard_map/attend/pallas_call | solution.py:219
  9.8 2.1 %collective-permute-done.2.queries_ref.refs_2_ = bf16[32,1152]{1,0:T(8,128)(2,1)S(1)} collective-permute-done((bf16[32,1152]{1,0:T(8,128)(2,1)S(1)}, bf16[32,1152]{1,0:T(8,128)(2,1)S(1)}, u32[]{:S(2)}, u32[]{:S(2)}) %collective-permute-start.2) | collective-permute-done | bytes 73760 | tf_op jit(solution)/shard_map/ppermute | solution.py:97
  11.9 1.3 %attend.6 = bf16[32,1152]{1,0:T(8,128)(2,1)S(1)} custom-call(bf16[32,1152]{1,0:T(8,128)(2,1)S(1)} %collective-permute-done.2.queries_ref.refs_2_, bf16[2048,128]{1,0:T(8,128)(2,1)S(1)} %bitcast.21, bf16[2048,128]{1,0:T(8,128)(2,1)S(1)} %bitcast.25, bf16[64,2048]{1,0:T(8,128)(2,1)S(1)} %sight.1.sight_ref, bf16[16,512,1536]{2,1,0:T(8,128)(2,1)} %weight_ref.14), custom_call_target="tpu_custom_call" | custom-call | flops 536870912 | bytes 1048576 | tf_op jit(solution)/shard_map/attend/pallas_call | solution.py:219
  13.2 1.3 %collective-permute-start.3 = (bf16[32,1152]{1,0:T(8,128)(2,1)S(1)}, bf16[32,1152]{1,0:T(8,128)(2,1)S(1)}, u32[]{:S(2)}, u32[]{:S(2)}) collective-permute-start(bf16[32,1152]{1,0:T(8,128)(2,1)S(1)} %attend.6), channel_id=1, source_target_pairs={{0,8},{4,12},{8,0},{12,4},{1,9},{5,13},{9,1},{13,5},{2,10},{6,14},... | collective-permute-start | bytes 221192 | tf_op jit(solution)/shard_map/ppermute | solution.py:97
  14.5 1.3 %attend.7 = bf16[32,1152]{1,0:T(8,128)(2,1)S(1)} custom-call(bf16[32,1152]{1,0:T(8,128)(2,1)S(1)} %collective-permute-done.4.queries_ref.refs_3_, bf16[2048,128]{1,0:T(8,128)(2,1)S(1)} %bitcast.22, bf16[2048,128]{1,0:T(8,128)(2,1)S(1)} %bitcast.26, bf16[64,2048]{1,0:T(8,128)(2,1)S(1)} %sight.1.sight_ref, bf16[16,512,1536]{2,1,0:T(8,128)(2,1)} %weight_ref.14), custom_call_target="tpu_custom_call" | custom-call | flops 536870912 | bytes 1048576 | tf_op jit(solution)/shard_map/attend/pallas_call | solution.py:219
  15.8 2.2 %collective-permute-start.5 = (bf16[32,1152]{1,0:T(8,128)(2,1)S(1)}, bf16[32,1152]{1,0:T(8,128)(2,1)S(1)}, u32[]{:S(2)}, u32[]{:S(2)}) collective-permute-start(bf16[32,1152]{1,0:T(8,128)(2,1)S(1)} %attend.7), channel_id=1, source_target_pairs={{0,12},{4,8},{8,4},{12,0},{1,13},{5,9},{9,5},{13,1},{2,14},{6,10},... | collective-permute-start | bytes 221192 | tf_op jit(solution)/shard_map/ppermute | solution.py:97
  18.0 1.3 %attend.4.refs_0_ = bf16[32,1152]{1,0:T(8,128)(2,1)S(1)} custom-call(bf16[32,1152]{1,0:T(8,128)(2,1)S(1)} %pack.1.queries_ref.refs_0_, bf16[2048,128]{1,0:T(8,128)(2,1)S(1)} %bitcast.23, bf16[2048,128]{1,0:T(8,128)(2,1)S(1)} %bitcast.27, bf16[64,2048]{1,0:T(8,128)(2,1)S(1)} %sight.1.sight_ref, bf16[16,512,1536]{2,1,0:T(8,128)(2,1)} %weight_ref.14), custom_call_target="tpu_custom_call" | custom-call | flops 536870912 | bytes 1048576 | tf_op jit(solution)/shard_map/attend/pallas_call | solution.py:219
  20.1 2.0 %collective-permute-done.5.refs_3_ = bf16[32,1152]{1,0:T(8,128)(2,1)S(1)} collective-permute-done((bf16[32,1152]{1,0:T(8,128)(2,1)S(1)}, bf16[32,1152]{1,0:T(8,128)(2,1)S(1)}, u32[]{:S(2)}, u32[]{:S(2)}) %collective-permute-start.5) | collective-permute-done | bytes 73760 | tf_op jit(solution)/shard_map/ppermute | solution.py:97
  23.2 1.5 %collective-permute-start.7 = (bf16[32,512]{1,0:T(8,128)(2,1)S(1)}, bf16[32,512]{1,0:T(8,128)(2,1)S(1)}, u32[]{:S(2)}, u32[]{:S(2)}) collective-permute-start(bf16[32,512]{1,0:T(8,128)(2,1)S(1)} %get-tuple-element.38), channel_id=1, source_target_pairs={{0,2},{1,3},{2,0},{3,1},{4,6},{5,7},{6,4},{7,5},{8,10},{9,11},{10,... | collective-permute-start | bytes 98312 | tf_op jit(solution)/shard_map/ppermute | solution.py:97
  25.0 1.8 %collective-permute-done.6.refs_1_ = bf16[32,512]{1,0:T(8,128)(2,1)S(1)} collective-permute-done((bf16[32,512]{1,0:T(8,128)(2,1)S(1)}, bf16[32,512]{1,0:T(8,128)(2,1)S(1)}, u32[]{:S(2)}, u32[]{:S(2)}) %collective-permute-start.6) | collective-permute-done | bytes 32800 | tf_op jit(solution)/shard_map/ppermute | solution.py:97
  27.2 1.4 %collective-permute-start.9 = (bf16[32,512]{1,0:T(8,128)(2,1)S(1)}, bf16[32,512]{1,0:T(8,128)(2,1)S(1)}, u32[]{:S(2)}, u32[]{:S(2)}) collective-permute-start(bf16[32,512]{1,0:T(8,128)(2,1)S(1)} %get-tuple-element.43.refs_0_), channel_id=1, source_target_pairs={{0,4},{4,0},{8,12},{12,8},{1,5},{5,1},{9,13},{13,9},{2,6},{6,2},{1... | collective-permute-start | bytes 98312 | tf_op jit(solution)/shard_map/ppermute | solution.py:97
  29.4 1.3 %collective-permute-start.12 = (bf16[32,512]{1,0:T(8,128)(2,1)S(1)}, bf16[32,512]{1,0:T(8,128)(2,1)S(1)}, u32[]{:S(2)}, u32[]{:S(2)}) collective-permute-start(bf16[32,512]{1,0:T(8,128)(2,1)S(1)} %get-tuple-element.43.refs_0_), channel_id=1, source_target_pairs={{0,8},{4,12},{8,0},{12,4},{1,9},{5,13},{9,1},{13,5},{2,10},{6,14},... | collective-permute-start | bytes 98312 | tf_op jit(solution)/shard_map/ppermute | solution.py:97
  31.3 2.0 %gate_up.6 = (bf16[64,1664]{1,0:T(8,128)(2,1)S(1)}, bf16[64,1664]{1,0:T(8,128)(2,1)S(1)}) custom-call(bf16[8,64,64]{2,1,0:T(8,128)(2,1)S(1)} %get-tuple-element.55.place_ref, bf16[1,512]{1,0:T(2,128)(2,1)S(1)} %broadcast_in_dim.8.gain_ref, bf16[16,512,1536]{2,1,0:T(8,128)(2,1)S(1)} %bitcast.10, bf16[32,512]{1,0:T(8,128)(2,1)S(1)} %get-tuple-element.43.refs_0_, ...), custom_call_target="tpu_custom_call" | custom-call | flops 100663296 | bytes 196608 | tf_op jit(solution)/shard_map/gate_up/pallas_call | solution.py:375
  36.4 1.4 %collective-permute-start.11 = (bf16[64,1664]{1,0:T(8,128)(2,1)S(1)}, bf16[64,1664]{1,0:T(8,128)(2,1)S(1)}, u32[]{:S(2)}, u32[]{:S(2)}) collective-permute-start(bf16[64,1664]{1,0:T(8,128)(2,1)S(1)} %join.2), channel_id=1, source_target_pairs={{0,2},{2,0},{1,3},{3,1},{4,6},{6,4},{5,7},{7,5},{8,10},{10,8},{9,1... | collective-permute-start | bytes 638984 | tf_op jit(solution)/shard_map/ppermute | solution.py:97
  41.2 2.2 %gate_up.9 = (bf16[64,1664]{1,0:T(8,128)(2,1)S(1)}, bf16[64,1664]{1,0:T(8,128)(2,1)S(1)}) custom-call(bf16[8,64,64]{2,1,0:T(8,128)(2,1)S(1)} %get-tuple-element.55.place_ref, bf16[1,512]{1,0:T(2,128)(2,1)S(1)} %broadcast_in_dim.8.gain_ref, bf16[16,512,1536]{2,1,0:T(8,128)(2,1)S(1)} %bitcast.10, bf16[32,512]{1,0:T(8,128)(2,1)S(1)} %get-tuple-element.43.refs_0_, ...), custom_call_target="tpu_custom_call" | custom-call | flops 100663296 | bytes 196608 | tf_op jit(solution)/shard_map/gate_up/pallas_call | solution.py:375
  46.4 1.4 %collective-permute-start.16 = (bf16[64,768]{1,0:T(8,128)(2,1)S(1)}, bf16[64,768]{1,0:T(8,128)(2,1)S(1)}, u32[]{:S(2)}, u32[]{:S(2)}) collective-permute-start(bf16[64,768]{1,0:T(8,128)(2,1)S(1)} %hidden.2.refs_0_), channel_id=1, source_target_pairs={{0,2},{2,0},{1,3},{3,1},{4,6},{6,4},{5,7},{7,5},{8,10},{10,8},{9,1... | collective-permute-start | bytes 294920 | tf_op jit(solution)/shard_map/ppermute | solution.py:97
  49.0 1.4 %collective-permute-start.20 = (bf16[64,768]{1,0:T(8,128)(2,1)S(1)}, bf16[64,768]{1,0:T(8,128)(2,1)S(1)}, u32[]{:S(2)}, u32[]{:S(2)}) collective-permute-start(bf16[64,768]{1,0:T(8,128)(2,1)S(1)} %hidden.3.refs_1_), channel_id=1, source_target_pairs={{0,2},{2,0},{1,3},{3,1},{4,6},{6,4},{5,7},{7,5},{8,10},{10,8},{9,1... | collective-permute-start | bytes 294920 | tf_op jit(solution)/shard_map/ppermute | solution.py:97
  51.2 1.6 %down.3.refs_2_ = f32[128,512]{1,0:T(8,128)S(1)} custom-call(bf16[16,768,512]{2,1,0:T(8,128)(2,1)S(1)} %bitcast.19, bf16[8,64,64]{2,1,0:T(8,128)(2,1)S(1)} %get-tuple-element.41.high_ref, bf16[8,64,64]{2,1,0:T(8,128)(2,1)S(1)} %get-tuple-element.42.low_ref, bf16[64,768]{1,0:T(8,128)(2,1)S(1)} %hidden.2.refs_0_, bf16[64,768]{1,0:T(8,128)(2,1)S(1)} %hidden.3.refs_1_, ...), custom_call_target="tpu_custom_call" | custom-call | flops 100663296 | bytes 1048576 | tf_op jit(solution)/shard_map/down/pallas_call | solution.py:457
  52.8 1.5 %collective-permute-done.20.refs_1_ = bf16[64,768]{1,0:T(8,128)(2,1)S(1)} collective-permute-done((bf16[64,768]{1,0:T(8,128)(2,1)S(1)}, bf16[64,768]{1,0:T(8,128)(2,1)S(1)}, u32[]{:S(2)}, u32[]{:S(2)}) %collective-permute-start.20) | collective-permute-done | bytes 98336 | tf_op jit(solution)/shard_map/ppermute | solution.py:97
  56.4 2.2 %collective-permute-start.24 = (bf16[32,512]{1,0:T(8,128)(2,1)S(1)}, bf16[32,512]{1,0:T(8,128)(2,1)S(1)}, u32[]{:S(2)}, u32[]{:S(2)}) collective-permute-start(bf16[32,512]{1,0:T(8,128)(2,1)S(1)} %get-tuple-element.60), channel_id=1, source_target_pairs={{0,12},{4,8},{8,4},{12,0},{1,13},{5,9},{9,5},{13,1},{2,14},{6,10},... | collective-permute-start | bytes 98312 | tf_op jit(solution)/shard_map/ppermute | solution.py:97
  58.6 2.2 %collective-permute-start.26 = (bf16[32,512]{1,0:T(8,128)(2,1)S(1)}, bf16[32,512]{1,0:T(8,128)(2,1)S(1)}, u32[]{:S(2)}, u32[]{:S(2)}) collective-permute-start(bf16[32,512]{1,0:T(8,128)(2,1)S(1)} %get-tuple-element.62), channel_id=1, source_target_pairs={{0,8},{4,12},{8,0},{12,4},{1,9},{5,13},{9,1},{13,5},{2,10},{6,14},... | collective-permute-start | bytes 98312 | tf_op jit(solution)/shard_map/ppermute | solution.py:97
  60.8 1.3 %collective-permute-done.24.refs_1_ = bf16[32,512]{1,0:T(8,128)(2,1)S(1)} collective-permute-done((bf16[32,512]{1,0:T(8,128)(2,1)S(1)}, bf16[32,512]{1,0:T(8,128)(2,1)S(1)}, u32[]{:S(2)}, u32[]{:S(2)}) %collective-permute-start.24) | collective-permute-done | bytes 32800 | tf_op jit(solution)/shard_map/ppermute | solution.py:97
  (88 shorter events, 22.5 us)
Async XLA Ops:
  1.0 6.3 %collective-permute-start = (bf16[32,1152]{1,0:T(8,128)(2,1)S(1)}, bf16[32,1152]{1,0:T(8,128)(2,1)S(1)}, u32[]{:S(2)}, u32[]{:S(2)}) collective-permute-start(bf16[32,1152]{1,0:T(8,128)(2,1)S(1)} %pack.1.queries_ref.refs_0_), channel_id=1, source_target_pairs={{0,4},{4,0},{8,12},{12,8},{1,5},{5,1},{9,13},{13,9},{2,6},{6,2},{1... | collective-permute-start | bytes 221192 | tf_op jit(solution)/shard_map/ppermute | solution.py:97
  4.2 7.8 %collective-permute-start.2 = (bf16[32,1152]{1,0:T(8,128)(2,1)S(1)}, bf16[32,1152]{1,0:T(8,128)(2,1)S(1)}, u32[]{:S(2)}, u32[]{:S(2)}) collective-permute-start(bf16[32,1152]{1,0:T(8,128)(2,1)S(1)} %pack.1.queries_ref.refs_0_), channel_id=1, source_target_pairs={{0,8},{4,12},{8,0},{12,4},{1,9},{5,13},{9,1},{13,5},{2,10},{6,14},... | collective-permute-start | bytes 221192 | tf_op jit(solution)/shard_map/ppermute | solution.py:97
  6.7 7.8 %collective-permute-start.4 = (bf16[32,1152]{1,0:T(8,128)(2,1)S(1)}, bf16[32,1152]{1,0:T(8,128)(2,1)S(1)}, u32[]{:S(2)}, u32[]{:S(2)}) collective-permute-start(bf16[32,1152]{1,0:T(8,128)(2,1)S(1)} %pack.1.queries_ref.refs_0_), channel_id=1, source_target_pairs={{0,12},{4,8},{8,4},{12,0},{1,13},{5,9},{9,5},{13,1},{2,14},{6,10},... | collective-permute-start | bytes 221192 | tf_op jit(solution)/shard_map/ppermute | solution.py:97
  8.7 11.3 %collective-permute-start.1 = (bf16[32,1152]{1,0:T(8,128)(2,1)S(1)}, bf16[32,1152]{1,0:T(8,128)(2,1)S(1)}, u32[]{:S(2)}, u32[]{:S(2)}) collective-permute-start(bf16[32,1152]{1,0:T(8,128)(2,1)S(1)} %attend.5), channel_id=1, source_target_pairs={{0,4},{4,0},{8,12},{12,8},{1,5},{5,1},{9,13},{13,9},{2,6},{6,2},{1... | collective-permute-start | bytes 221192 | tf_op jit(solution)/shard_map/ppermute | solution.py:97
  13.2 6.9 %collective-permute-start.3 = (bf16[32,1152]{1,0:T(8,128)(2,1)S(1)}, bf16[32,1152]{1,0:T(8,128)(2,1)S(1)}, u32[]{:S(2)}, u32[]{:S(2)}) collective-permute-start(bf16[32,1152]{1,0:T(8,128)(2,1)S(1)} %attend.6), channel_id=1, source_target_pairs={{0,8},{4,12},{8,0},{12,4},{1,9},{5,13},{9,1},{13,5},{2,10},{6,14},... | collective-permute-start | bytes 221192 | tf_op jit(solution)/shard_map/ppermute | solution.py:97
  15.8 6.3 %collective-permute-start.5 = (bf16[32,1152]{1,0:T(8,128)(2,1)S(1)}, bf16[32,1152]{1,0:T(8,128)(2,1)S(1)}, u32[]{:S(2)}, u32[]{:S(2)}) collective-permute-start(bf16[32,1152]{1,0:T(8,128)(2,1)S(1)} %attend.7), channel_id=1, source_target_pairs={{0,12},{4,8},{8,4},{12,0},{1,13},{5,9},{9,5},{13,1},{2,14},{6,10},... | collective-permute-start | bytes 221192 | tf_op jit(solution)/shard_map/ppermute | solution.py:97
  23.1 3.7 %collective-permute-start.6 = (bf16[32,512]{1,0:T(8,128)(2,1)S(1)}, bf16[32,512]{1,0:T(8,128)(2,1)S(1)}, u32[]{:S(2)}, u32[]{:S(2)}) collective-permute-start(bf16[32,512]{1,0:T(8,128)(2,1)S(1)} %get-tuple-element.37), channel_id=1, source_target_pairs={{0,3},{1,2},{2,1},{3,0},{4,7},{5,6},{6,5},{7,4},{8,11},{9,10},{10,... | collective-permute-start | bytes 98312 | tf_op jit(solution)/shard_map/ppermute | solution.py:97
  23.2 4.0 %collective-permute-start.7 = (bf16[32,512]{1,0:T(8,128)(2,1)S(1)}, bf16[32,512]{1,0:T(8,128)(2,1)S(1)}, u32[]{:S(2)}, u32[]{:S(2)}) collective-permute-start(bf16[32,512]{1,0:T(8,128)(2,1)S(1)} %get-tuple-element.38), channel_id=1, source_target_pairs={{0,2},{1,3},{2,0},{3,1},{4,6},{5,7},{6,4},{7,5},{8,10},{9,11},{10,... | collective-permute-start | bytes 98312 | tf_op jit(solution)/shard_map/ppermute | solution.py:97
  27.2 4.0 %collective-permute-start.9 = (bf16[32,512]{1,0:T(8,128)(2,1)S(1)}, bf16[32,512]{1,0:T(8,128)(2,1)S(1)}, u32[]{:S(2)}, u32[]{:S(2)}) collective-permute-start(bf16[32,512]{1,0:T(8,128)(2,1)S(1)} %get-tuple-element.43.refs_0_), channel_id=1, source_target_pairs={{0,4},{4,0},{8,12},{12,8},{1,5},{5,1},{9,13},{13,9},{2,6},{6,2},{1... | collective-permute-start | bytes 98312 | tf_op jit(solution)/shard_map/ppermute | solution.py:97
  28.6 5.7 %collective-permute-start.13 = (bf16[32,512]{1,0:T(8,128)(2,1)S(1)}, bf16[32,512]{1,0:T(8,128)(2,1)S(1)}, u32[]{:S(2)}, u32[]{:S(2)}) collective-permute-start(bf16[32,512]{1,0:T(8,128)(2,1)S(1)} %get-tuple-element.43.refs_0_), channel_id=1, source_target_pairs={{0,12},{4,8},{8,4},{12,0},{1,13},{5,9},{9,5},{13,1},{2,14},{6,10},... | collective-permute-start | bytes 98312 | tf_op jit(solution)/shard_map/ppermute | solution.py:97
  29.4 5.6 %collective-permute-start.12 = (bf16[32,512]{1,0:T(8,128)(2,1)S(1)}, bf16[32,512]{1,0:T(8,128)(2,1)S(1)}, u32[]{:S(2)}, u32[]{:S(2)}) collective-permute-start(bf16[32,512]{1,0:T(8,128)(2,1)S(1)} %get-tuple-element.43.refs_0_), channel_id=1, source_target_pairs={{0,8},{4,12},{8,0},{12,4},{1,9},{5,13},{9,1},{13,5},{2,10},{6,14},... | collective-permute-start | bytes 98312 | tf_op jit(solution)/shard_map/ppermute | solution.py:97
  33.3 2.9 %collective-permute-start.10 = (bf16[64,1664]{1,0:T(8,128)(2,1)S(1)}, bf16[64,1664]{1,0:T(8,128)(2,1)S(1)}, u32[]{:S(2)}, u32[]{:S(2)}) collective-permute-start(bf16[64,1664]{1,0:T(8,128)(2,1)S(1)} %get-tuple-element.45), channel_id=1, source_target_pairs={{0,1},{1,0},{2,3},{3,2},{4,5},{5,4},{6,7},{7,6},{8,9},{9,8},{10,11... | collective-permute-start | bytes 638984 | tf_op jit(solution)/shard_map/ppermute | solution.py:97
  36.2 2.8 %collective-permute-start.14 = (bf16[64,1664]{1,0:T(8,128)(2,1)S(1)}, bf16[64,1664]{1,0:T(8,128)(2,1)S(1)}, u32[]{:S(2)}, u32[]{:S(2)}) collective-permute-start(bf16[64,1664]{1,0:T(8,128)(2,1)S(1)} %gate_up.8), channel_id=1, source_target_pairs={{0,1},{1,0},{2,3},{3,2},{4,5},{5,4},{6,7},{7,6},{8,9},{9,8},{10,11... | collective-permute-start | bytes 638984 | tf_op jit(solution)/shard_map/ppermute | solution.py:97
  36.4 8.1 %collective-permute-start.11 = (bf16[64,1664]{1,0:T(8,128)(2,1)S(1)}, bf16[64,1664]{1,0:T(8,128)(2,1)S(1)}, u32[]{:S(2)}, u32[]{:S(2)}) collective-permute-start(bf16[64,1664]{1,0:T(8,128)(2,1)S(1)} %join.2), channel_id=1, source_target_pairs={{0,2},{2,0},{1,3},{3,1},{4,6},{6,4},{5,7},{7,5},{8,10},{10,8},{9,1... | collective-permute-start | bytes 638984 | tf_op jit(solution)/shard_map/ppermute | solution.py:97
  40.3 4.3 %collective-permute-start.15 = (bf16[64,1664]{1,0:T(8,128)(2,1)S(1)}, bf16[64,1664]{1,0:T(8,128)(2,1)S(1)}, u32[]{:S(2)}, u32[]{:S(2)}) collective-permute-start(bf16[64,1664]{1,0:T(8,128)(2,1)S(1)} %gate_up.10), channel_id=1, source_target_pairs={{0,1},{1,0},{2,3},{3,2},{4,5},{5,4},{6,7},{7,6},{8,9},{9,8},{10,11... | collective-permute-start | bytes 638984 | tf_op jit(solution)/shard_map/ppermute | solution.py:97
  40.5 8.2 %collective-permute-start.18 = (bf16[64,1664]{1,0:T(8,128)(2,1)S(1)}, bf16[64,1664]{1,0:T(8,128)(2,1)S(1)}, u32[]{:S(2)}, u32[]{:S(2)}) collective-permute-start(bf16[64,1664]{1,0:T(8,128)(2,1)S(1)} %join.3), channel_id=1, source_target_pairs={{0,2},{2,0},{1,3},{3,1},{4,6},{6,4},{5,7},{7,5},{8,10},{10,8},{9,1... | collective-permute-start | bytes 638984 | tf_op jit(solution)/shard_map/ppermute | solution.py:97
  45.9 2.8 %collective-permute-start.19 = (bf16[64,1664]{1,0:T(8,128)(2,1)S(1)}, bf16[64,1664]{1,0:T(8,128)(2,1)S(1)}, u32[]{:S(2)}, u32[]{:S(2)}) collective-permute-start(bf16[64,1664]{1,0:T(8,128)(2,1)S(1)} %gate_up.11), channel_id=1, source_target_pairs={{0,1},{1,0},{2,3},{3,2},{4,5},{5,4},{6,7},{7,6},{8,9},{9,8},{10,11... | collective-permute-start | bytes 638984 | tf_op jit(solution)/shard_map/ppermute | solution.py:97
  45.9 5.3 %collective-permute-start.21 = (bf16[64,768]{1,0:T(8,128)(2,1)S(1)}, bf16[64,768]{1,0:T(8,128)(2,1)S(1)}, u32[]{:S(2)}, u32[]{:S(2)}) collective-permute-start(bf16[64,768]{1,0:T(8,128)(2,1)S(1)} %hidden.2.refs_0_), channel_id=1, source_target_pairs={{0,1},{1,0},{2,3},{3,2},{4,5},{5,4},{6,7},{7,6},{8,9},{9,8},{10,11... | collective-permute-start | bytes 294920 | tf_op jit(solution)/shard_map/ppermute | solution.py:97
  46.4 4.8 %collective-permute-start.16 = (bf16[64,768]{1,0:T(8,128)(2,1)S(1)}, bf16[64,768]{1,0:T(8,128)(2,1)S(1)}, u32[]{:S(2)}, u32[]{:S(2)}) collective-permute-start(bf16[64,768]{1,0:T(8,128)(2,1)S(1)} %hidden.2.refs_0_), channel_id=1, source_target_pairs={{0,2},{2,0},{1,3},{3,1},{4,6},{6,4},{5,7},{7,5},{8,10},{10,8},{9,1... | collective-permute-start | bytes 294920 | tf_op jit(solution)/shard_map/ppermute | solution.py:97
  49.0 5.2 %collective-permute-start.20 = (bf16[64,768]{1,0:T(8,128)(2,1)S(1)}, bf16[64,768]{1,0:T(8,128)(2,1)S(1)}, u32[]{:S(2)}, u32[]{:S(2)}) collective-permute-start(bf16[64,768]{1,0:T(8,128)(2,1)S(1)} %hidden.3.refs_1_), channel_id=1, source_target_pairs={{0,2},{2,0},{1,3},{3,1},{4,6},{6,4},{5,7},{7,5},{8,10},{10,8},{9,1... | collective-permute-start | bytes 294920 | tf_op jit(solution)/shard_map/ppermute | solution.py:97
  51.2 3.9 %collective-permute-start.17 = (bf16[64,768]{1,0:T(8,128)(2,1)S(1)}, bf16[64,768]{1,0:T(8,128)(2,1)S(1)}, u32[]{:S(2)}, u32[]{:S(2)}) collective-permute-start(bf16[64,768]{1,0:T(8,128)(2,1)S(1)} %collective-permute-done.16.refs_0_), channel_id=1, source_target_pairs={{0,1},{1,0},{2,3},{3,2},{4,5},{5,4},{6,7},{7,6},{8,9},{9,8},{10,11... | collective-permute-start | bytes 294920 | tf_op jit(solution)/shard_map/ppermute | solution.py:97
  56.4 5.8 %collective-permute-start.24 = (bf16[32,512]{1,0:T(8,128)(2,1)S(1)}, bf16[32,512]{1,0:T(8,128)(2,1)S(1)}, u32[]{:S(2)}, u32[]{:S(2)}) collective-permute-start(bf16[32,512]{1,0:T(8,128)(2,1)S(1)} %get-tuple-element.60), channel_id=1, source_target_pairs={{0,12},{4,8},{8,4},{12,0},{1,13},{5,9},{9,5},{13,1},{2,14},{6,10},... | collective-permute-start | bytes 98312 | tf_op jit(solution)/shard_map/ppermute | solution.py:97
  58.6 4.3 %collective-permute-start.25 = (bf16[32,512]{1,0:T(8,128)(2,1)S(1)}, bf16[32,512]{1,0:T(8,128)(2,1)S(1)}, u32[]{:S(2)}, u32[]{:S(2)}) collective-permute-start(bf16[32,512]{1,0:T(8,128)(2,1)S(1)} %get-tuple-element.61), channel_id=1, source_target_pairs={{0,4},{4,0},{8,12},{12,8},{1,5},{5,1},{9,13},{13,9},{2,6},{6,2},{1... | collective-permute-start | bytes 98312 | tf_op jit(solution)/shard_map/ppermute | solution.py:97
  58.6 5.2 %collective-permute-start.26 = (bf16[32,512]{1,0:T(8,128)(2,1)S(1)}, bf16[32,512]{1,0:T(8,128)(2,1)S(1)}, u32[]{:S(2)}, u32[]{:S(2)}) collective-permute-start(bf16[32,512]{1,0:T(8,128)(2,1)S(1)} %get-tuple-element.62), channel_id=1, source_target_pairs={{0,8},{4,12},{8,0},{12,4},{1,9},{5,13},{9,1},{13,5},{2,10},{6,14},... | collective-permute-start | bytes 98312 | tf_op jit(solution)/shard_map/ppermute | solution.py:97
  (19 other events, 172.9 us)
